TPU v7x, 32 devices: a whole 2x2x4 slice. The times are simulated.
32 devices in a mesh: band: 8 (over z, core), img: 4 (over y, x).
Axes of the slice: x: 2, y: 2, z: 4, core: 2. Of those that a mesh axis runs over, the one named last changes fastest.
Arguments:
- x_small: bfloat16 [16, 24, 16, 512], P('img', 'band'), may hold values from -6 to 6
- x_medium: bfloat16 [24, 32, 24, 512], P('img', 'band'), may hold values from -6 to 6
- x_large: bfloat16 [8, 48, 32, 512], P('img', 'band'), may hold values from -6 to 6
- cot_small: bfloat16 [16, 24, 16, 512], P('img', 'band'), may hold values from -6 to 6
- cot_medium: bfloat16 [24, 32, 24, 512], P('img', 'band'), may hold values from -6 to 6
- cot_large: bfloat16 [8, 48, 32, 512], P('img', 'band'), may hold values from -6 to 6
- band_rows: int32 [3, 8], replicated, may hold values from 1 to 6, as said below
- params: float32 [11296, 512], P(('band', 'img'))
- first_moment: float32 [11296, 512], P(('band', 'img')), may hold values from -640 to 640
- second_moment: float32 [11296, 512], P(('band', 'img')), may hold values from 1000 to 100000
- step: int32 [1], replicated, may hold values from 1 to 9
- rate: float32 [1], replicated, may hold values from 0.001 to 0.01
Outputs:
- out_small: bfloat16 [16, 24, 16, 512], P('img', 'band')
- out_medium: bfloat16 [24, 32, 24, 512], P('img', 'band')
- out_large: bfloat16 [8, 48, 32, 512], P('img', 'band')
- again_small: bfloat16 [16, 24, 16, 512], P('img', 'band')
- again_medium: bfloat16 [24, 32, 24, 512], P('img', 'band')
- again_large: bfloat16 [8, 48, 32, 512], P('img', 'band')
- grad_small: bfloat16 [16, 24, 16, 512], P('img', 'band')
- grad_medium: bfloat16 [24, 32, 24, 512], P('img', 'band')
- grad_large: bfloat16 [8, 48, 32, 512], P('img', 'band')
- weight_update: float32 [11296, 512], P(('band', 'img'))
- new_first: float32 [11296, 512], P(('band', 'img'))
- new_second: float32 [11296, 512], P(('band', 'img'))
Inputs may be any that keep to these rules, and one draw needn't show every extreme that they name: Row s of band_rows belongs to the side in (16, 24, 32); its entries sum to that side and its largest entry is exactly (3, 4, 6) for that side, every entry at least 1.
All inputs are finite; a program needn't handle non-finite values.
Results may differ from a plain program's by a relative error of at most 0.017.
Values may be sent and summed in bfloat16 or wider, within the bound.
No kernel may reach another device: no remote copies, remote signals or barrier semaphores. Data moves between devices by JAX's collectives and lax.ppermute only.
A program may use at most 192 MiB of HBM per device.

v0:
```python
import jax
import jax.numpy as jnp
from jax import lax
from jax.sharding import PartitionSpec as P

GROUPS = 32


EPSILON = 1e-05
ADAM_EPSILON = 1e-08


def extended_2(cells, sides, width):
    for axis, dim in sides:
        count = lax.axis_size(axis)
        ends = count - 1
        head = lax.slice_in_dim(cells, 0, width, axis=dim)
        tail = lax.slice_in_dim(cells, cells.shape[dim] - width, cells.shape[dim], axis=dim)
        cells = jnp.concatenate(
            [
                lax.ppermute(tail, axis, [(i, (i + 1) % count) for i in range(ends)]),
                cells,
                lax.ppermute(head, axis, [((i + 1) % count, i) for i in range(ends)]),
            ],
            axis=dim,
        )
    return cells


def swish(value):
    return value * jax.nn.sigmoid(value)


def swish_slope(value):
    sigma = jax.nn.sigmoid(value)
    return sigma * (1.0 + value * (1.0 - sigma))


def unpack(gathered):
    channel_count = gathered.shape[1]
    conv_one = gathered[: 9 * channel_count].reshape(9, channel_count, channel_count)
    conv_two = gathered[9 * channel_count : 18 * channel_count].reshape(
        9, channel_count, channel_count
    )
    project = [
        gathered[(18 + offset) * channel_count : (19 + offset) * channel_count]
        for offset in range(4)
    ]
    small_band_rows = gathered[22 * channel_count : 22 * channel_count + 11].astype(jnp.float32)
    return (conv_one, conv_two, project, small_band_rows)


def fetch_weights(shard):
    return lax.all_gather(shard.astype(jnp.bfloat16), ("band", "img"), axis=0, tiled=True)


def group_sums(feature):
    num_img, num_rows, num_cols, channel_count = feature.shape
    return jnp.sum(
        feature.reshape(num_img, num_rows * num_cols, GROUPS, channel_count // GROUPS), axis=(1, 3)
    )


def broadcast_groups(stat, channel_count):
    return jnp.repeat(stat, channel_count // GROUPS, axis=1)[:, None, None, :]


def pixel_counts(features):
    return [
        feature.shape[2] * feature.shape[2] * (feature.shape[3] // GROUPS) for feature in features
    ]


def norm_forward(features, masks4, gain_row, shift_row):
    channel_count = features[0].shape[3]
    counts_all = pixel_counts(features)
    firsts = [group_sums(feature) for feature in features]
    firsts = lax.psum((firsts[0], firsts[1], firsts[2]), "band")
    centers = [firsts[member] / counts_all[member] for member in range(3)]
    deviations = [
        (features[member] - broadcast_groups(centers[member], channel_count)) * masks4[member]
        for member in range(3)
    ]
    squared = [group_sums(deviation * deviation) for deviation in deviations]
    seconds = lax.psum((squared[0], squared[1], squared[2]), "band")
    variances = [seconds[member] / counts_all[member] for member in range(3)]
    normeds, scaleds, rstds = ([], [], [])
    for member in range(3):
        rstd_full = broadcast_groups(lax.rsqrt(variances[member] + EPSILON), channel_count)
        normed = (
            (features[member] - broadcast_groups(centers[member], channel_count))
            * rstd_full
            * masks4[member]
        )
        normeds.append(normed)
        scaleds.append((normed * gain_row + shift_row) * masks4[member])
        rstds.append(rstd_full)
    return (normeds, scaleds, rstds)


def norm_backward(gradients, normeds, rstds, masks4, gain_row):
    channel_count = gradients[0].shape[3]
    counts_all = pixel_counts(gradients)
    weighted = [gradient * gain_row for gradient in gradients]
    ones_sums = [group_sums(weighted[member]) for member in range(3)]
    cross_sums = [group_sums(weighted[member] * normeds[member]) for member in range(3)]
    merged = lax.psum(
        (ones_sums[0], ones_sums[1], ones_sums[2], cross_sums[0], cross_sums[1], cross_sums[2]),
        "band",
    )
    results = []
    for member in range(3):
        first_mean = broadcast_groups(merged[member] / counts_all[member], channel_count)
        second_mean = broadcast_groups(merged[3 + member] / counts_all[member], channel_count)
        results.append(
            rstds[member]
            * (weighted[member] - first_mean - normeds[member] * second_mean)
            * masks4[member]
        )
    gain_grad = sum(
        (jnp.sum(gradients[member] * normeds[member], axis=(0, 1, 2)) for member in range(3))
    )
    shift_grad = sum((jnp.sum(gradients[member], axis=(0, 1, 2)) for member in range(3)))
    return (results, gain_grad, shift_grad)


def add_rims(features, lengths):
    tops, bottoms = ([], [])
    for feature, length in zip(features, lengths):
        num_img, num_rows, num_cols, channel_count = feature.shape
        tops.append(feature[:, 0].reshape(num_img * num_cols, channel_count))
        bottoms.append(
            lax.dynamic_index_in_dim(feature, length - 1, 1, keepdims=False).reshape(
                num_img * num_cols, channel_count
            )
        )
    stacked = jnp.stack([jnp.concatenate(tops, 0), jnp.concatenate(bottoms, 0)])
    edged = extended_2(stacked, (("band", 0),), 1)
    extended = []
    cursor = 0
    for feature, length in zip(features, lengths):
        num_img, num_rows, num_cols, channel_count = feature.shape
        upper_rim = edged[0, cursor : cursor + num_img * num_cols].reshape(
            num_img, 1, num_cols, channel_count
        )
        lower_rim = edged[3, cursor : cursor + num_img * num_cols].reshape(
            num_img, 1, num_cols, channel_count
        )
        cursor = cursor + num_img * num_cols
        filler = jnp.zeros((num_img, 1, num_cols, channel_count), feature.dtype)
        grown = jnp.concatenate([upper_rim, feature, filler], axis=1)
        grown = lax.dynamic_update_slice_in_dim(grown, lower_rim, length + 1, 1)
        extended.append(jnp.pad(grown, ((0, 0), (0, 0), (1, 1), (0, 0))))
    return extended


def apply_kernel(extended, kernel, mirrored):
    num_rows, num_cols = (extended.shape[1] - 2, extended.shape[2] - 2)
    summed = None
    for offset in range(9):
        row_shift, col_shift = (offset // 3, offset % 3)
        window = extended[:, row_shift : row_shift + num_rows, col_shift : col_shift + num_cols]
        if mirrored:
            term = jnp.einsum(
                "ahwd,cd->ahwc", window, kernel[8 - offset], preferred_element_type=jnp.float32
            )
        else:
            term = jnp.einsum(
                "ahwc,cd->ahwd", window, kernel[offset], preferred_element_type=jnp.float32
            )
        summed = term if summed is None else summed + term
    return summed


def kernel_grad(extended, gradient):
    num_rows, num_cols = (gradient.shape[1], gradient.shape[2])
    pieces = []
    for offset in range(9):
        row_shift, col_shift = (offset // 3, offset % 3)
        window = extended[:, row_shift : row_shift + num_rows, col_shift : col_shift + num_cols]
        pieces.append(
            jnp.einsum("ahwc,ahwd->cd", window, gradient, preferred_element_type=jnp.float32)
        )
    return jnp.stack(pieces)


def forward_pass(gathered, inputs, masks4, key_masks, lengths):
    conv_one, conv_two, project, small_band_rows = unpack(gathered)
    query_w, key_w, value_w, output_weight = project
    normed_one, scaled_one, rstd_one = norm_forward(
        inputs, masks4, small_band_rows[0], small_band_rows[1]
    )
    act_one = [
        (swish(scaled_one[member]) * masks4[member]).astype(jnp.bfloat16) for member in range(3)
    ]
    ext_one = add_rims(act_one, lengths)
    branch = [
        (apply_kernel(ext_one[member], conv_one, False) + small_band_rows[2]) * masks4[member]
        for member in range(3)
    ]
    normed_two, scaled_two, rstd_two = norm_forward(
        branch, masks4, small_band_rows[3], small_band_rows[4]
    )
    act_two = [
        (swish(scaled_two[member]) * masks4[member]).astype(jnp.bfloat16) for member in range(3)
    ]
    ext_two = add_rims(act_two, lengths)
    middle = [
        inputs[member]
        + (apply_kernel(ext_two[member], conv_two, False) + small_band_rows[5]) * masks4[member]
        for member in range(3)
    ]
    normed_three, scaled_three, rstd_three = norm_forward(
        middle, masks4, small_band_rows[6], small_band_rows[7]
    )
    normal_in = []
    for member in range(3):
        num_img, num_rows, num_cols, channel_count = scaled_three[member].shape
        normal_in.append(
            scaled_three[member]
            .astype(jnp.bfloat16)
            .reshape(num_img, num_rows * num_cols, channel_count)
        )
    query_block = [
        (
            jnp.einsum("aqc,cd->aqd", rows_in, query_w, preferred_element_type=jnp.float32)
            + small_band_rows[8]
        ).astype(jnp.bfloat16)
        for rows_in in normal_in
    ]
    key_row_block = [
        jnp.einsum("aqc,cd->aqd", rows_in, key_w, preferred_element_type=jnp.float32).astype(
            jnp.bfloat16
        )
        for rows_in in normal_in
    ]
    value_row_block = [
        (
            jnp.einsum("aqc,cd->aqd", rows_in, value_w, preferred_element_type=jnp.float32)
            + small_band_rows[9]
        ).astype(jnp.bfloat16)
        for rows_in in normal_in
    ]
    all_kv = (
        lax.all_gather(key_row_block[0], "band", axis=1, tiled=True),
        lax.all_gather(key_row_block[1], "band", axis=1, tiled=True),
        lax.all_gather(key_row_block[2], "band", axis=1, tiled=True),
        lax.all_gather(value_row_block[0], "band", axis=1, tiled=True),
        lax.all_gather(value_row_block[1], "band", axis=1, tiled=True),
        lax.all_gather(value_row_block[2], "band", axis=1, tiled=True),
    )
    scaling = gathered.shape[1] ** (-0.5)
    outputs, log_sums, mixed_list = ([], [], [])
    for member in range(3):
        attention_scores = (
            jnp.einsum(
                "aqc,akc->aqk",
                query_block[member],
                all_kv[member],
                preferred_element_type=jnp.float32,
            )
            * scaling
        )
        attention_scores = jnp.where(key_masks[member][None, None, :], attention_scores, -1e30)
        top = jnp.max(attention_scores, axis=2, keepdims=True)
        expo = jnp.exp(attention_scores - top)
        summed = jnp.sum(expo, axis=2, keepdims=True)
        attention_probabilities = (expo / summed).astype(jnp.bfloat16)
        log_sums.append((top + jnp.log(summed))[:, :, 0])
        attended_values = jnp.einsum(
            "aqk,akc->aqc",
            attention_probabilities,
            all_kv[3 + member],
            preferred_element_type=jnp.float32,
        ).astype(jnp.bfloat16)
        mixed_list.append(attended_values)
        projected_output = (
            jnp.einsum(
                "aqc,cd->aqd", attended_values, output_weight, preferred_element_type=jnp.float32
            )
            + small_band_rows[10]
        )
        outputs.append(
            (middle[member] + projected_output.reshape(middle[member].shape)) * masks4[member]
        )
    kept = (
        normed_one,
        scaled_one,
        rstd_one,
        ext_one,
        normed_two,
        scaled_two,
        rstd_two,
        ext_two,
        normed_three,
        rstd_three,
        normal_in,
        query_block,
        all_kv,
        log_sums,
        mixed_list,
    )
    return (outputs, kept)


def body(
    x_small,
    x_medium,
    x_large,
    cot_small,
    cot_medium,
    cot_large,
    band_rows,
    params,
    first_moment,
    second_moment,
    step,
    rate,
):
    num_bands = lax.axis_size("band")
    position = lax.axis_index("band")
    mine = lax.dynamic_index_in_dim(band_rows, position, 1, keepdims=False)
    raw_inputs = (x_small, x_medium, x_large)
    raw_cots = (cot_small, cot_medium, cot_large)
    lengths = [mine[member] for member in range(3)]
    masks4, key_masks, own_masks = ([], [], [])
    for member in range(3):
        num_img, num_rows, num_cols, channel_count = raw_inputs[member].shape
        row_mask = (jnp.arange(num_rows, dtype=jnp.int32) < lengths[member]).astype(jnp.float32)
        masks4.append(row_mask[None, :, None, None])
        own_masks.append(jnp.repeat(row_mask, num_cols)[None, :, None])
        slot_ids = jnp.arange(num_bands * num_rows, dtype=jnp.int32)
        key_valid = slot_ids % num_rows < band_rows[member][slot_ids // num_rows]
        key_masks.append(jnp.repeat(key_valid, num_cols))
    inputs = [raw_inputs[member].astype(jnp.float32) * masks4[member] for member in range(3)]
    gathered = fetch_weights(params)
    conv_one, conv_two, project, small_band_rows = unpack(gathered)
    query_w, key_w, value_w, output_weight = project
    outputs, kept = forward_pass(gathered, inputs, masks4, key_masks, lengths)
    (
        normed_one,
        scaled_one,
        rstd_one,
        ext_one,
        normed_two,
        scaled_two,
        rstd_two,
        ext_two,
        normed_three,
        rstd_three,
        normal_in,
        query_block,
        all_kv,
        log_sums,
        mixed_list,
    ) = kept
    channel_count = gathered.shape[1]
    scaling = channel_count ** (-0.5)
    cot_flat, d_mixed, dot_terms, d_query, key_parts, value_parts = ([], [], [], [], [], [])
    out_w_grad = jnp.zeros((channel_count, channel_count), jnp.float32)
    out_b_grad = jnp.zeros((channel_count,), jnp.float32)
    for member in range(3):
        num_img, num_rows, num_cols, channel_count = raw_cots[member].shape
        cot_rows = (
            (raw_cots[member].astype(jnp.float32) * masks4[member])
            .astype(jnp.bfloat16)
            .reshape(num_img, num_rows * num_cols, channel_count)
        )
        cot_flat.append(cot_rows)
        out_w_grad = out_w_grad + jnp.einsum(
            "aqc,aqd->cd", mixed_list[member], cot_rows, preferred_element_type=jnp.float32
        )
        out_b_grad = out_b_grad + jnp.sum(cot_rows.astype(jnp.float32), axis=(0, 1))
        grad_mixed = jnp.einsum(
            "aqd,cd->aqc", cot_rows, output_weight, preferred_element_type=jnp.float32
        ).astype(jnp.bfloat16)
        d_mixed.append(grad_mixed)
        attention_scores = (
            jnp.einsum(
                "aqc,akc->aqk",
                query_block[member],
                all_kv[member],
                preferred_element_type=jnp.float32,
            )
            * scaling
        )
        attention_scores = jnp.where(key_masks[member][None, None, :], attention_scores, -1e30)
        attention_probabilities = jnp.exp(attention_scores - log_sums[member][:, :, None])
        d_probs = jnp.einsum(
            "aqc,akc->aqk", grad_mixed, all_kv[3 + member], preferred_element_type=jnp.float32
        )
        dot_term = jnp.sum(attention_probabilities * d_probs, axis=2)
        dot_terms.append(dot_term)
        d_scores = (attention_probabilities * (d_probs - dot_term[:, :, None])).astype(jnp.bfloat16)
        d_query.append(
            (
                scaling
                * jnp.einsum(
                    "aqk,akc->aqc", d_scores, all_kv[member], preferred_element_type=jnp.float32
                )
            ).astype(jnp.bfloat16)
        )
        key_parts.append(
            scaling
            * jnp.einsum(
                "aqk,aqc->akc", d_scores, query_block[member], preferred_element_type=jnp.float32
            )
        )
        value_parts.append(
            jnp.einsum(
                "aqk,aqc->akc",
                attention_probabilities.astype(jnp.bfloat16),
                grad_mixed,
                preferred_element_type=jnp.float32,
            )
        )
    own_sums = (
        lax.psum_scatter(
            key_parts[0].astype(jnp.bfloat16), "band", scatter_dimension=1, tiled=True
        ).astype(jnp.float32),
        lax.psum_scatter(
            key_parts[1].astype(jnp.bfloat16), "band", scatter_dimension=1, tiled=True
        ).astype(jnp.float32),
        lax.psum_scatter(
            key_parts[2].astype(jnp.bfloat16), "band", scatter_dimension=1, tiled=True
        ).astype(jnp.float32),
        lax.psum_scatter(
            value_parts[0].astype(jnp.bfloat16), "band", scatter_dimension=1, tiled=True
        ).astype(jnp.float32),
        lax.psum_scatter(
            value_parts[1].astype(jnp.bfloat16), "band", scatter_dimension=1, tiled=True
        ).astype(jnp.float32),
        lax.psum_scatter(
            value_parts[2].astype(jnp.bfloat16), "band", scatter_dimension=1, tiled=True
        ).astype(jnp.float32),
    )
    key_own = [own_sums[member] for member in range(3)]
    value_own = [own_sums[3 + member] for member in range(3)]
    query_w_grad = jnp.zeros((channel_count, channel_count), jnp.float32)
    key_w_grad = jnp.zeros((channel_count, channel_count), jnp.float32)
    value_w_grad = jnp.zeros((channel_count, channel_count), jnp.float32)
    query_b_grad = jnp.zeros((channel_count,), jnp.float32)
    value_b_grad = jnp.zeros((channel_count,), jnp.float32)
    d_normal = []
    for member in range(3):
        key_grad_b = (key_own[member] * own_masks[member]).astype(jnp.bfloat16)
        value_grad_b = (value_own[member] * own_masks[member]).astype(jnp.bfloat16)
        rows_in = normal_in[member]
        query_w_grad = query_w_grad + jnp.einsum(
            "aqc,aqd->cd", rows_in, d_query[member], preferred_element_type=jnp.float32
        )
        key_w_grad = key_w_grad + jnp.einsum(
            "aqc,aqd->cd", rows_in, key_grad_b, preferred_element_type=jnp.float32
        )
        value_w_grad = value_w_grad + jnp.einsum(
            "aqc,aqd->cd", rows_in, value_grad_b, preferred_element_type=jnp.float32
        )
        query_b_grad = query_b_grad + jnp.sum(d_query[member].astype(jnp.float32), axis=(0, 1))
        value_b_grad = value_b_grad + jnp.sum(value_grad_b.astype(jnp.float32), axis=(0, 1))
        grad_rows = jnp.einsum(
            "aqd,cd->aqc", d_query[member], query_w, preferred_element_type=jnp.float32
        )
        grad_rows = grad_rows + jnp.einsum(
            "aqd,cd->aqc", key_grad_b, key_w, preferred_element_type=jnp.float32
        )
        grad_rows = grad_rows + jnp.einsum(
            "aqd,cd->aqc", value_grad_b, value_w, preferred_element_type=jnp.float32
        )
        d_normal.append(grad_rows.reshape(raw_cots[member].shape) * masks4[member])
    back_three, gain_three_grad, shift_three_grad = norm_backward(
        d_normal, normed_three, rstd_three, masks4, small_band_rows[6]
    )
    d_middle = [
        raw_cots[member].astype(jnp.float32) * masks4[member] + back_three[member]
        for member in range(3)
    ]
    branch_two = [d_middle[member].astype(jnp.bfloat16) for member in range(3)]
    bias_two_grad = sum(
        (jnp.sum(branch_two[member].astype(jnp.float32), axis=(0, 1, 2)) for member in range(3))
    )
    conv_two_grad = sum((kernel_grad(ext_two[member], branch_two[member]) for member in range(3)))
    rim_two = add_rims(branch_two, lengths)
    d_scaled_two = [
        apply_kernel(rim_two[member], conv_two, True)
        * swish_slope(scaled_two[member])
        * masks4[member]
        for member in range(3)
    ]
    back_two, gain_two_grad, shift_two_grad = norm_backward(
        d_scaled_two, normed_two, rstd_two, masks4, small_band_rows[3]
    )
    branch_one = [back_two[member].astype(jnp.bfloat16) for member in range(3)]
    bias_one_grad = sum(
        (jnp.sum(branch_one[member].astype(jnp.float32), axis=(0, 1, 2)) for member in range(3))
    )
    conv_one_grad = sum((kernel_grad(ext_one[member], branch_one[member]) for member in range(3)))
    rim_one = add_rims(branch_one, lengths)
    d_scaled_one = [
        apply_kernel(rim_one[member], conv_one, True)
        * swish_slope(scaled_one[member])
        * masks4[member]
        for member in range(3)
    ]
    back_one, gain_one_grad, shift_one_grad = norm_backward(
        d_scaled_one, normed_one, rstd_one, masks4, small_band_rows[0]
    )
    input_grads = [
        ((d_middle[member] + back_one[member]) * masks4[member]).astype(jnp.bfloat16)
        for member in range(3)
    ]
    small_grads = jnp.stack(
        [
            gain_one_grad,
            shift_one_grad,
            bias_one_grad,
            gain_two_grad,
            shift_two_grad,
            bias_two_grad,
            gain_three_grad,
            shift_three_grad,
            query_b_grad,
            value_b_grad,
            out_b_grad,
        ]
    )
    total_rows = gathered.shape[0]
    grad_full = jnp.concatenate(
        [
            conv_one_grad.reshape(9 * channel_count, channel_count),
            conv_two_grad.reshape(9 * channel_count, channel_count),
            query_w_grad,
            key_w_grad,
            value_w_grad,
            out_w_grad,
            small_grads,
            jnp.zeros((total_rows - 22 * channel_count - 11, channel_count), jnp.float32),
        ],
        axis=0,
    )
    grad_shard = lax.psum_scatter(grad_full, ("band", "img"), scatter_dimension=0, tiled=True)
    step_count = step[0].astype(jnp.float32)
    new_first = 0.5 * first_moment + 0.5 * grad_shard
    new_second = 0.9 * second_moment + 0.1 * grad_shard * grad_shard
    weight_update = (
        rate[0]
        * (new_first / (1.0 - jnp.power(0.5, step_count)))
        / (jnp.sqrt(new_second / (1.0 - jnp.power(0.9, step_count))) + ADAM_EPSILON)
    )
    new_params = params - weight_update
    again, unused_kept = forward_pass(fetch_weights(new_params), inputs, masks4, key_masks, lengths)
    first_out = [outputs[member].astype(jnp.bfloat16) for member in range(3)]
    second_out = [again[member].astype(jnp.bfloat16) for member in range(3)]
    return (
        first_out[0],
        first_out[1],
        first_out[2],
        second_out[0],
        second_out[1],
        second_out[2],
        input_grads[0],
        input_grads[1],
        input_grads[2],
        weight_update,
        new_first,
        new_second,
    )


def solution(mesh):
    return jax.shard_map(
        body,
        mesh=mesh,
        in_specs=(
            P("img", "band", None, None),
            P("img", "band", None, None),
            P("img", "band", None, None),
            P("img", "band", None, None),
            P("img", "band", None, None),
            P("img", "band", None, None),
            P(),
            P(("band", "img"), None),
            P(("band", "img"), None),
            P(("band", "img"), None),
            P(),
            P(),
        ),
        out_specs=(
            P("img", "band", None, None),
            P("img", "band", None, None),
            P("img", "band", None, None),
            P("img", "band", None, None),
            P("img", "band", None, None),
            P("img", "band", None, None),
            P("img", "band", None, None),
            P("img", "band", None, None),
            P("img", "band", None, None),
            P(("band", "img"), None),
            P(("band", "img"), None),
            P(("band", "img"), None),
        ),
        check_vma=False,
    )
```

profile of v0, /device:TPU:0, one launch (start us, length us, event | category | flops | bytes accessed | tf_op | source)
XLA Modules:
  0.0 2157.1 jit_solution(11057064079500898311)
XLA Ops:
  17.6 18.5 all-reduce.31
  38.0 14.4 all-reduce.30
  53.0 53.9 %all-gather.41.cloned.1.call-done = bf16[32,353,512]{2,1,0:T(8,128)(2,1)} async-done(((bf16[1,353,512]{2,1,0:T(8,128)(2,1)}), bf16[32,353,512]{2,1,0:T(8,128)(2,1)}) %all-gather.41.cloned.1.call-update) | async-done | bytes 11567120 | tf_op jit(solution)/shard_map/all_gather | solution.py:54
  106.9 10.0 reshape.964
  174.2 18.0 all-reduce.29
  198.1 14.0 all-reduce.28
  261.0 18.2 all-reduce.27
  280.9 13.9 all-reduce.26
  314.0 5.9 all-gather.17.cloned.1.call-done
  322.7 23.9 %all-gather.19.cloned.1.call-done = bf16[4,384,512]{2,1,0:T(8,128)(2,1)} async-done(((bf16[4,48,512]{2,1,0:T(8,128)(2,1)}), bf16[4,384,512]{2,1,0:T(8,128)(2,1)}) %all-gather.19.cloned.1.call-update) | async-done | bytes 1572880 | tf_op jit(solution)/shard_map/all_gather | solution.py:248
  353.4 5.0 fusion.306
  363.5 22.9 %all-gather.25.cloned.1.call-done = bf16[2,1536,512]{2,1,0:T(8,128)(2,1)} async-done(((bf16[2,192,512]{2,1,0:T(8,128)(2,1)}), bf16[2,1536,512]{2,1,0:T(8,128)(2,1)}) %all-gather.25.cloned.1.call-update) | async-done | bytes 3145744 | tf_op jit(solution)/shard_map/all_gather | solution.py:247
  391.5 33.6 %all-gather.27.cloned.1.call-done = bf16[2,1536,512]{2,1,0:T(8,128)(2,1)} async-done(((bf16[2,192,512]{2,1,0:T(8,128)(2,1)}), bf16[2,1536,512]{2,1,0:T(8,128)(2,1)}) %all-gather.27.cloned.1.call-update) | async-done | bytes 3145744 | tf_op jit(solution)/shard_map/all_gather | solution.py:250
  445.2 32.5 %all-gather.21.cloned.1.call-done = bf16[6,768,512]{2,1,0:T(8,128)(2,1)} async-done(((bf16[6,96,512]{2,1,0:T(8,128)(2,1)}), bf16[6,768,512]{2,1,0:T(8,128)(2,1)}) %all-gather.21.cloned.1.call-update) | async-done | bytes 4718608 | tf_op jit(solution)/shard_map/all_gather | solution.py:246
  477.7 4.2 fusion.510
  484.2 46.2 %all-gather.23.cloned.1.call-done = bf16[6,768,512]{2,1,0:T(8,128)(2,1)} async-done(((bf16[6,96,512]{2,1,0:T(8,128)(2,1)}), bf16[6,768,512]{2,1,0:T(8,128)(2,1)}) %all-gather.23.cloned.1.call-update) | async-done | bytes 4718608 | tf_op jit(solution)/shard_map/all_gather | solution.py:249
  530.4 4.9 multiply_reduce_fusion.1
  540.4 5.3 convolution_convert_fusion.1
  571.3 29.3 %reduce-scatter.11.cloned.1.call-done = bf16[4,48,512]{2,1,0:T(8,128)(2,1)} async-done(((bf16[4,384,512]{2,1,0:T(8,128)(2,1)}), bf16[4,48,512]{2,1,0:T(8,128)(2,1)}) %reduce-scatter.11.cloned.1.call-update) | async-done | bytes 196624 | tf_op jit(solution)/shard_map/reduce_scatter | solution.py:427
  623.2 17.8 reduce-scatter.17.cloned.1.call-done
  643.5 39.3 %reduce-scatter.19.cloned.1.call-done = bf16[2,192,512]{2,1,0:T(8,128)(2,1)} async-done(((bf16[2,1536,512]{2,1,0:T(8,128)(2,1)}), bf16[2,192,512]{2,1,0:T(8,128)(2,1)}) %reduce-scatter.19.cloned.1.call-update) | async-done | bytes 393232 | tf_op jit(solution)/shard_map/reduce_scatter | solution.py:433
  691.8 47.2 %reduce-scatter.13.cloned.1.call-done = bf16[6,96,512]{2,1,0:T(8,128)(2,1)} async-done(((bf16[6,768,512]{2,1,0:T(8,128)(2,1)}), bf16[6,96,512]{2,1,0:T(8,128)(2,1)}) %reduce-scatter.13.cloned.1.call-update) | async-done | bytes 589840 | tf_op jit(solution)/shard_map/reduce_scatter | solution.py:421
  742.1 52.5 %reduce-scatter.15.cloned.1.call-done = bf16[6,96,512]{2,1,0:T(8,128)(2,1)} async-done(((bf16[6,768,512]{2,1,0:T(8,128)(2,1)}), bf16[6,96,512]{2,1,0:T(8,128)(2,1)}) %reduce-scatter.15.cloned.1.call-update) | async-done | bytes 589840 | tf_op jit(solution)/shard_map/reduce_scatter | solution.py:430
  802.8 27.2 %all-reduce.25 = (f32[2,32]{1,0:T(2,128)}, f32[2,32]{1,0:T(2,128)}, f32[6,32]{1,0:T(8,128)S(1)}, f32[6,32]{1,0:T(8,128)S(1)}, f32[4,32]{1,0:T(4,128)}, /*index=5*/f32[4,32]{1,0:T(4,128)}) all-reduce(f32[2,32]{1,0:T(2,128)} %reduce_sum.1247, f32[2,32]{1,0:T(2,128)} %reduce_sum.1244, ...), channel_id=1, replica_groups=mesh['band'=8,'img'=4] {'band'}, use_global_device_ids=true, to_apply=%region_86.87 | all-reduce | flops 768 | bytes 6144 | tf_op jit(solution)/shard_map/psum | solution.py:107
  875.7 15.3 add_add_fusion
  930.0 4.2 multiply_reduce_fusion.6
  934.5 27.0 %all-reduce.24 = (f32[2,32]{1,0:T(2,128)}, f32[2,32]{1,0:T(2,128)}, f32[4,32]{1,0:T(4,128)}, f32[4,32]{1,0:T(4,128)}, f32[6,32]{1,0:T(8,128)S(1)}, /*index=5*/f32[6,32]{1,0:T(8,128)S(1)}) all-reduce(f32[2,32]{1,0:T(2,128)S(1)} %reduce_sum.1265, f32[2,32]{1,0:T(2,128)S(1)} %reduce_sum.1262, ...), channel_id=1, replica_groups=mesh['band'=8,'img'=4] {'band'}, use_global_device_ids=true, to_apply=%region_104.105 | all-reduce | flops 768 | bytes 6144 | tf_op jit(solution)/shard_map/psum | solution.py:107
  997.2 4.1 copy-done.44
  1001.4 15.1 add_add_fusion.1
  1035.9 57.3 %concatenate.113 = f32[11296,512]{1,0:T(8,128)} concatenate(f32[4608,512]{1,0:T(8,128)} %bitcast.1282, f32[4608,512]{1,0:T(8,128)} %bitcast.1281, f32[512,512]{1,0:T(8,128)} %fusion.99, f32[512,512]{1,0:T(8,128)} %fusion.101, f32[512,512]{1,0:T(8,128)} %fusion.103, f32[512,512]{1,0:T(8,128)S(1)} %copy-done.60, f32[1,512]{1,0:T(1,128)S(1)} %bitcast.1493, f32[1,512]{1,0:T(1,128)S(1)} %bitcast.1492, ...), dimensions={0} | concatenate | bytes 46268416 | tf_op jit(solution)/shard_map/concatenate | solution.py:527
  1093.2 493.8 %fusion = f32[360,512]{1,0:T(8,128)S(1)} fusion(f32[11296,512]{1,0:T(8,128)} %concatenate.113), kind=kCustom, calls=%all-reduce-scatter | all-reduce-scatter fusion | flops 5898241 | bytes 23871488
  1587.0 10.4 collective-permute-start.12
  1598.8 7.9 collective-permute-done.12
  1612.4 92.3 %all-gather.43.cloned.1.call-done = bf16[32,353,512]{2,1,0:T(8,128)(2,1)} async-done(((bf16[1,353,512]{2,1,0:T(8,128)(2,1)}), bf16[32,353,512]{2,1,0:T(8,128)(2,1)}) %all-gather.43.cloned.1.call-update) | async-done | bytes 11567120 | tf_op jit(solution)/shard_map/all_gather | solution.py:54
  1704.7 10.0 reshape.966
  1760.7 18.9 all-reduce.23
  1782.3 14.1 all-reduce.22
  1858.8 18.4 all-reduce.21
  1879.9 26.6 %all-reduce.20 = (f32[4,32]{1,0:T(4,128)S(1)}, f32[6,32]{1,0:T(8,128)S(1)}, f32[2,32]{1,0:T(2,128)S(1)}, f32[4,32]{1,0:T(4,128)S(1)}, f32[4,32]{1,0:T(4,128)S(1)...) all-reduce(f32[4,32]{1,0:T(4,128)S(1)} %reduce_sum.1322, ...), channel_id=1, replica_groups=mesh['band'=8,'img'=4] {'band'}, use_global_device_ids=true, to_apply=%region_162.163 | all-reduce | flops 1152 | bytes 9216 | tf_op jit(solution)/shard_map/psum | solution.py:85
  1936.4 24.1 %all-gather.31.cloned.1.call-done = bf16[4,384,512]{2,1,0:T(8,128)(2,1)} async-done(((bf16[4,48,512]{2,1,0:T(8,128)(2,1)}), bf16[4,384,512]{2,1,0:T(8,128)(2,1)}) %all-gather.31.cloned.1.call-update) | async-done | bytes 1572880 | tf_op jit(solution)/shard_map/all_gather | solution.py:248
  1963.4 36.3 %all-gather.37.cloned.1.call-done = bf16[2,1536,512]{2,1,0:T(8,128)(2,1)} async-done(((bf16[2,192,512]{2,1,0:T(8,128)(2,1)}), bf16[2,1536,512]{2,1,0:T(8,128)(2,1)}) %all-gather.37.cloned.1.call-update) | async-done | bytes 3145744 | tf_op jit(solution)/shard_map/all_gather | solution.py:247
  1999.8 5.0 fusion.5
  2007.7 30.7 %all-gather.39.cloned.1.call-done = bf16[2,1536,512]{2,1,0:T(8,128)(2,1)} async-done(((bf16[2,192,512]{2,1,0:T(8,128)(2,1)}), bf16[2,1536,512]{2,1,0:T(8,128)(2,1)}) %all-gather.39.cloned.1.call-update) | async-done | bytes 3145744 | tf_op jit(solution)/shard_map/all_gather | solution.py:250
  2038.4 5.7 convolution_add_fusion.62
  2046.2 44.4 %all-gather.33.cloned.1.call-done = bf16[6,768,512]{2,1,0:T(8,128)(2,1)} async-done(((bf16[6,96,512]{2,1,0:T(8,128)(2,1)}), bf16[6,768,512]{2,1,0:T(8,128)(2,1)}) %all-gather.33.cloned.1.call-update) | async-done | bytes 4718608 | tf_op jit(solution)/shard_map/all_gather | solution.py:246
  2090.6 4.4 fusion.155
  2095.5 47.1 %all-gather.35.cloned.1.call-done = bf16[6,768,512]{2,1,0:T(8,128)(2,1)} async-done(((bf16[6,96,512]{2,1,0:T(8,128)(2,1)}), bf16[6,768,512]{2,1,0:T(8,128)(2,1)}) %all-gather.35.cloned.1.call-update) | async-done | bytes 4718608 | tf_op jit(solution)/shard_map/all_gather | solution.py:249
  2142.6 5.1 convolution_add_fusion
  (1364 shorter events, 551.0 us)
Async XLA Ops:
  7.2 99.7 %all-gather.41.cloned.1.call-start = ((), (), s32[]{:S(2)}) async-start(), calls=%async_computation.24 | async-start | bytes 12165120 | tf_op jit(solution)/shard_map/all_gather | solution.py:54
  9.3 310.6 %all-gather.17.cloned.1.call-start = ((), (), s32[]{:S(2)}) async-start(), calls=%async_computation.6 | async-start | bytes 1769472 | tf_op jit(solution)/shard_map/all_gather | solution.py:245
  15.2 670.2 %copy-start.141 = (f32[6]{0:T(128)}, f32[6]{0:T(128)S(1)}, u32[]{:S(2)}) copy-start(f32[6]{0:T(128)S(1)} %compare_convert_fusion) | copy-start | bytes 76
  16.1 586.7 %copy-start.139 = (f32[3]{0:T(128)}, f32[3]{0:T(128)S(1)}, u32[]{:S(2)}) copy-start(f32[3]{0:T(128)S(1)} %compare_convert_fusion.2) | copy-start | bytes 40
  17.2 780.6 %copy-start.143 = (f32[4]{0:T(128)}, f32[4]{0:T(128)S(1)}, u32[]{:S(2)}) copy-start(f32[4]{0:T(128)S(1)} %compare_convert_fusion.1) | copy-start | bytes 52
  36.3 83.6 %copy-start.164 = (f32[2,512]{1,0:T(2,128)}, f32[2,512]{1,0:T(2,128)S(1)}, u32[]{:S(2)}) copy-start(f32[2,512]{1,0:T(2,128)S(1)} %sub.264) | copy-start | bytes 12292
  36.9 81.4 %copy-start.148 = (f32[4,512]{1,0:T(4,128)}, f32[4,512]{1,0:T(4,128)S(1)}, u32[]{:S(2)}) copy-start(f32[4,512]{1,0:T(4,128)S(1)} %sub.256) | copy-start | bytes 24580
  37.4 84.3 %copy-start.126 = (f32[6,512]{1,0:T(8,128)}, f32[6,512]{1,0:T(8,128)S(1)}, u32[]{:S(2)}) copy-start(f32[6,512]{1,0:T(8,128)S(1)} %sub.260) | copy-start | bytes 36868
  52.5 67.4 %copy-start.179 = (f32[2,512]{1,0:T(2,128)}, f32[2,512]{1,0:T(2,128)S(1)}, u32[]{:S(2)}) copy-start(f32[2,512]{1,0:T(2,128)S(1)} %mul.758) | copy-start | bytes 12292
  52.7 65.6 %copy-start.159 = (f32[4,512]{1,0:T(4,128)}, f32[4,512]{1,0:T(4,128)S(1)}, u32[]{:S(2)}) copy-start(f32[4,512]{1,0:T(4,128)S(1)} %mul.731) | copy-start | bytes 24580
  52.9 68.9 %copy-start.133 = (f32[6,512]{1,0:T(8,128)}, f32[6,512]{1,0:T(8,128)S(1)}, u32[]{:S(2)}) copy-start(f32[6,512]{1,0:T(8,128)S(1)} %mul.745) | copy-start | bytes 36868
  53.0 65.3 %copy-start.111 = (bf16[4,3,16,512]{3,2,1,0:T(8,128)(2,1)S(1)}, bf16[4,3,16,512]{3,2,1,0:T(8,128)(2,1)}, u32[]{:S(2)}) copy-start(bf16[4,3,16,512]{3,2,1,0:T(8,128)(2,1)} %param.15) | copy-start | bytes 589828
  53.0 66.9 %copy-start.103 = (bf16[2,6,32,512]{3,2,1,0:T(8,128)(2,1)S(1)}, bf16[2,6,32,512]{3,2,1,0:T(8,128)(2,1)}, u32[]{:S(2)}) copy-start(bf16[2,6,32,512]{3,2,1,0:T(8,128)(2,1)} %param.17) | copy-start | bytes 1179652
  118.3 97.4 %copy-start.171 = (f32[1,512]{1,0:T(1,128)}, f32[1,512]{1,0:T(1,128)S(1)}, u32[]{:S(2)}) copy-start(f32[1,512]{1,0:T(1,128)S(1)} %get-tuple-element.205) | copy-start | bytes 6148
  118.3 186.4 %copy-start.150 = (f32[1,512]{1,0:T(1,128)}, f32[1,512]{1,0:T(1,128)S(1)}, u32[]{:S(2)}) copy-start(f32[1,512]{1,0:T(1,128)S(1)} %get-tuple-element.202) | copy-start | bytes 6148
  124.0 7.8 collective-permute-start
  130.4 3.8 collective-permute-start.1
  216.3 3.5 collective-permute-start.2
  218.2 3.5 collective-permute-start.3
  297.3 49.3 %all-gather.19.cloned.1.call-start = ((), (), s32[]{:S(2)}) async-start(), calls=%async_computation.7 | async-start | bytes 1769472 | tf_op jit(solution)/shard_map/all_gather | solution.py:248
  299.4 87.1 %all-gather.25.cloned.1.call-start = ((), (), s32[]{:S(2)}) async-start(), calls=%async_computation.10 | async-start | bytes 3538944 | tf_op jit(solution)/shard_map/all_gather | solution.py:247
  299.9 61.5 %copy-start.47 = (bf16[2,6,32,512]{3,2,1,0:T(8,128)(2,1)}, bf16[2,6,32,512]{3,2,1,0:T(8,128)(2,1)S(1)}, u32[]{:S(2)}) copy-start(bf16[2,6,32,512]{3,2,1,0:T(8,128)(2,1)S(1)} %multiply_convert_fusion.26) | copy-start | bytes 1179652
  302.2 122.9 %all-gather.27.cloned.1.call-start = ((), (), s32[]{:S(2)}) async-start(), calls=%async_computation.11 | async-start | bytes 3538944 | tf_op jit(solution)/shard_map/all_gather | solution.py:250
  304.5 173.2 %all-gather.21.cloned.1.call-start = ((), (), s32[]{:S(2)}) async-start(), calls=%async_computation.8 | async-start | bytes 5308416 | tf_op jit(solution)/shard_map/all_gather | solution.py:246
  307.7 222.8 %all-gather.23.cloned.1.call-start = ((), (), s32[]{:S(2)}) async-start(), calls=%async_computation.9 | async-start | bytes 5308416 | tf_op jit(solution)/shard_map/all_gather | solution.py:249
  310.1 258.7 %reduce-scatter.9.cloned.1.call-start = ((), (), s32[]{:S(2)}) async-start(), calls=%async_computation.12 | async-start | bytes 1769472 | tf_op jit(solution)/shard_map/reduce_scatter | solution.py:418
  350.6 249.9 %reduce-scatter.11.cloned.1.call-start = ((), (), s32[]{:S(2)}) async-start(), calls=%async_computation.13 | async-start | bytes 1769472 | tf_op jit(solution)/shard_map/reduce_scatter | solution.py:427
  352.7 288.3 %reduce-scatter.17.cloned.1.call-start = ((), (), s32[]{:S(2)}) async-start(), calls=%async_computation.16 | async-start | bytes 3538944 | tf_op jit(solution)/shard_map/reduce_scatter | solution.py:424
  432.8 250.0 %reduce-scatter.19.cloned.1.call-start = ((), (), s32[]{:S(2)}) async-start(), calls=%async_computation.17 | async-start | bytes 3538944 | tf_op jit(solution)/shard_map/reduce_scatter | solution.py:433
  436.8 302.2 %reduce-scatter.13.cloned.1.call-start = ((), (), s32[]{:S(2)}) async-start(), calls=%async_computation.14 | async-start | bytes 5308416 | tf_op jit(solution)/shard_map/reduce_scatter | solution.py:421
  540.3 254.3 %reduce-scatter.15.cloned.1.call-start = ((), (), s32[]{:S(2)}) async-start(), calls=%async_computation.15 | async-start | bytes 5308416 | tf_op jit(solution)/shard_map/reduce_scatter | solution.py:430
  545.8 1158.9 %all-gather.43.cloned.1.call-start = ((), (), s32[]{:S(2)}) async-start(), calls=%async_computation.25 | async-start | bytes 12165120 | tf_op jit(solution)/shard_map/all_gather | solution.py:54
  742.1 56.6 %copy-start.138 = (f32[6,512]{1,0:T(8,128)S(1)}, f32[6,512]{1,0:T(8,128)}, u32[]{:S(2)}) copy-start(f32[6,512]{1,0:T(8,128)} %copy-done.137) | copy-start | bytes 36868
  848.2 48.3 %collective-permute-start.4 = (bf16[1,272,512]{2,1,0:T(8,128)(2,1)S(1)}, bf16[1,272,512]{2,1,0:T(8,128)(2,1)S(1)}, u32[]{:S(2)}, u32[]{:S(2)}) collective-permute-start(bf16[1,272,512]{2,1,0:T(8,128)(2,1)S(1)} %maximum_bitcast_fusion.4), channel_id=1, source_target_pairs={{0,4},{4,8},{8,12},{12,16},{16,20},{20,24},{24,28},{1,5},{5,9},{9,... | collective-permute-start | bytes 835592 | tf_op jit(solution)/shard_map/ppermute | solution.py:21
  849.5 47.1 %collective-permute-start.5 = (bf16[1,272,512]{2,1,0:T(8,128)(2,1)S(1)}, bf16[1,272,512]{2,1,0:T(8,128)(2,1)S(1)}, u32[]{:S(2)}, u32[]{:S(2)}) collective-permute-start(bf16[1,272,512]{2,1,0:T(8,128)(2,1)S(1)} %maximum_bitcast_fusion.5), channel_id=1, source_target_pairs={{4,0},{8,4},{12,8},{16,12},{20,16},{24,20},{28,24},{5,1},{9,5},{13... | collective-permute-start | bytes 835592 | tf_op jit(solution)/shard_map/ppermute | solution.py:23
  971.1 45.5 %collective-permute-start.6 = (bf16[1,272,512]{2,1,0:T(8,128)(2,1)S(1)}, bf16[1,272,512]{2,1,0:T(8,128)(2,1)S(1)}, u32[]{:S(2)}, u32[]{:S(2)}) collective-permute-start(bf16[1,272,512]{2,1,0:T(8,128)(2,1)S(1)} %maximum_bitcast_fusion.6), channel_id=1, source_target_pairs={{0,4},{4,8},{8,12},{12,16},{16,20},{20,24},{24,28},{1,5},{5,9},{9,... | collective-permute-start | bytes 835592 | tf_op jit(solution)/shard_map/ppermute | solution.py:21
  972.4 44.2 %collective-permute-start.7 = (bf16[1,272,512]{2,1,0:T(8,128)(2,1)S(1)}, bf16[1,272,512]{2,1,0:T(8,128)(2,1)S(1)}, u32[]{:S(2)}, u32[]{:S(2)}) collective-permute-start(bf16[1,272,512]{2,1,0:T(8,128)(2,1)S(1)} %maximum_bitcast_fusion.7), channel_id=1, source_target_pairs={{4,0},{8,4},{12,8},{16,12},{20,16},{24,20},{28,24},{5,1},{9,5},{13... | collective-permute-start | bytes 835592 | tf_op jit(solution)/shard_map/ppermute | solution.py:23
  1587.0 19.6 collective-permute-start.12
  1612.4 321.4 %all-gather.29.cloned.1.call-start = ((), (), s32[]{:S(2)}) async-start(), calls=%async_computation.18 | async-start | bytes 1769472 | tf_op jit(solution)/shard_map/all_gather | solution.py:245
  1717.5 3.9 collective-permute-start.8
  1720.1 3.7 collective-permute-start.9
  1801.0 4.1 collective-permute-start.10
  1803.8 3.5 collective-permute-start.11
  1911.3 49.1 %all-gather.31.cloned.1.call-start = ((), (), s32[]{:S(2)}) async-start(), calls=%async_computation.19 | async-start | bytes 1769472 | tf_op jit(solution)/shard_map/all_gather | solution.py:248
  1913.6 86.2 %all-gather.37.cloned.1.call-start = ((), (), s32[]{:S(2)}) async-start(), calls=%async_computation.22 | async-start | bytes 3538944 | tf_op jit(solution)/shard_map/all_gather | solution.py:247
  1919.9 118.5 %all-gather.39.cloned.1.call-start = ((), (), s32[]{:S(2)}) async-start(), calls=%async_computation.23 | async-start | bytes 3538944 | tf_op jit(solution)/shard_map/all_gather | solution.py:250
  1922.3 168.3 %all-gather.33.cloned.1.call-start = ((), (), s32[]{:S(2)}) async-start(), calls=%async_computation.20 | async-start | bytes 5308416 | tf_op jit(solution)/shard_map/all_gather | solution.py:246
  1929.4 213.2 %all-gather.35.cloned.1.call-start = ((), (), s32[]{:S(2)}) async-start(), calls=%async_computation.21 | async-start | bytes 5308416 | tf_op jit(solution)/shard_map/all_gather | solution.py:249
  (277 other events, 2459.2 us)
Sparse Core Ops, SparseCore 0:
  11.5 95.3 all-gather.40
  297.4 22.4 all-gather.16
  322.1 24.4 all-gather.18
  348.6 37.8 all-gather.24
  387.9 37.1 all-gather.26
  427.1 50.5 all-gather.20
  479.9 50.5 all-gather.22
  532.7 33.0 reduce-scatter.8
  568.2 32.3 reduce-scatter.10
  602.7 38.2 reduce-scatter.16
  643.3 39.4 reduce-scatter.18
  684.9 54.0 reduce-scatter.12
  741.3 53.3 reduce-scatter.14
  1612.5 92.1 all-gather.42
  1911.4 22.3 all-gather.28
  1935.8 24.5 all-gather.30
  1961.9 37.7 all-gather.36
  2001.2 37.1 all-gather.38
  2040.0 50.5 all-gather.32
  2092.0 50.5 all-gather.34
where the time goes:
time: 2170 us; the launch traced here: 2160 us
  blocking collectives  723 us (33%)
  waiting for transfers between devices  698 us (32%)
  matrix products  413 us (19%)
  local copies, waits for them, and re-layouts  141 us (6%)
  other arithmetic  121 us (6%)
  starting transfers between devices  31.1 us (1%)
  between operations  29.8 us (1%)
    unnamed x1, blocking collectives  494 us
    dot_general x108, matrix products, apply_kernel(): jnp.einsum('ahwc,cd->ahwd', window, kernel[offset], preferred_element_typ...  163 us
    all_gather x2, waiting for transfers between devices, fetch_weights(): lax.all_gather(shard.astype(jnp.bfloat16), ('band', 'img'), axis=0, tiled...  146 us
    all_gather x2, waiting for transfers between devices, forward_pass(): lax.all_gather(value_row_block[1], 'band', axis=1, tiled=True)  93.2 us
    psum x5, blocking collectives, norm_forward(): firsts = lax.psum((firsts[0], firsts[1], firsts[2]), 'band')  91.9 us
    psum x5, blocking collectives, norm_forward(): seconds = lax.psum((squared[0], squared[1], squared[2]), 'band')  83 us
    all_gather x2, waiting for transfers between devices, forward_pass(): lax.all_gather(key_row_block[1], 'band', axis=1, tiled=True)  76.9 us
    all_gather x2, waiting for transfers between devices, forward_pass(): lax.all_gather(value_row_block[2], 'band', axis=1, tiled=True)  64.3 us
  transfers between devices with their start and end apart: 33, of which 24 were waited for; matrix products, arithmetic and copies ran while one was open for 12% of the time, Pallas kernels for 0%

commit v1 on v0

v1 whole, which is shorter than its diff:
```python
import functools

import jax
import jax.numpy as jnp
import numpy as np
from jax import lax
from jax.experimental import pallas as pl
from jax.experimental.pallas import tpu as pltpu
from jax.sharding import PartitionSpec as P

GROUPS = 32
EPSILON = 1e-05
ADAM_EPSILON = 1e-08
C = 512
AXES = ("band", "img")
VMEM_BYTES = 58 * 1024 * 1024
F32, BF16 = jnp.float32, jnp.bfloat16

PIX = 1024
SEG_LINES = ((0, 24), (24, 32))
BUF_LINES = 36


class Plan:
    def __init__(self, shapes, n_band):
        (self.n_s, self.cap_s, self.side_s, _), (self.n_m, self.cap_m, self.side_m, _), (
            self.n_l,
            self.cap_l,
            self.side_l,
            _,
        ) = shapes
        assert (self.side_s, self.side_m, self.side_l) == (16, 24, 32)
        self.n_band = n_band
        self.n_chip = n_band // 2
        self.r_s, self.r_m, self.r_l = (
            self.cap_s * self.side_s,
            self.cap_m * self.side_m,
            self.cap_l * self.side_l,
        )
        holders = [dict() for _ in range(n_band)]
        for i in range(self.n_l):
            holders[2 * i]["l"] = i
        free = [b for b in range(n_band) if "l" not in holders[b]]
        for i in range(self.n_m):
            holders[free[i]]["m"] = i
        spots = [b for b in free if b >= 2 * self.n_l]
        for i in range(self.n_s):
            holders[spots[i]]["s"] = i
        self.holders = holders
        self.sizes = [
            (self.r_l if "l" in h else 0)
            + (self.r_m if "m" in h else 0)
            + (self.r_s if "s" in h else 0)
            for h in holders
        ]
        self.block = max(self.sizes[2 * j] + self.sizes[2 * j + 1] for j in range(self.n_chip))
        self.piece = max(self.sizes)
        self.offs = [0 if b % 2 == 0 else self.piece - self.sizes[b] for b in range(n_band)]
        self.is_l = np.array([int("l" in h) for h in holders], np.int32)
        self.has_m = np.array([int("m" in h) for h in holders], np.int32)
        self.has_s = np.array([int("s" in h) for h in holders], np.int32)
        self.off = np.array(self.offs, np.int32)


def pick(table, index):
    return lax.dynamic_index_in_dim(jnp.asarray(table), index, 0, keepdims=False)


def make_tables(plan, band_rows, position):
    nz = plan.n_chip
    z, core = position // 2, position % 2
    is_l, has_m, has_s, off = (pick(t, position) for t in (plan.is_l, plan.has_m, plan.has_s, plan.off))
    starts = jnp.cumsum(band_rows, axis=1) - band_rows
    zero_in = plan.n_band * plan.piece // 8

    def band_of(member, rows):
        return jnp.sum((starts[member][None, :] <= rows[:, None]).astype(jnp.int32), axis=1) - 1

    def place(member, rows):
        band = band_of(member, rows)
        onehot = band[:, None] == jnp.arange(plan.n_band)[None, :]
        start = jnp.sum(jnp.where(onehot, starts[member][None, :], 0), axis=1)
        k = (z - band // 2) % nz
        pos = jnp.where(band % 2 == core, k, nz + k)
        return pos * plan.piece + off, rows - start

    q = np.arange(128)
    base, r = place(2, jnp.asarray(q // 4, jnp.int32))
    src_l = (base + r * 32) // 8 + jnp.asarray(q % 4, jnp.int32)
    base, r = place(1, jnp.asarray(np.minimum(q // 4, 23), jnp.int32))
    src_m = (base + r * 24) // 8 + jnp.asarray(q % 4, jnp.int32)
    ok_m = jnp.asarray((q < 96) & (q % 4 < 3)) & (has_m == 1)
    line = np.clip((q - 96) // 4, 0, 7)
    base, r = place(0, jnp.asarray(line + 8 * (q % 4 // 2), jnp.int32))
    src_s = (base + has_m * plan.r_m + r * 16) // 8 + jnp.asarray(q % 2, jnp.int32)
    ok_s = jnp.asarray(q >= 96) & (has_s == 1)
    gather = jnp.where(
        is_l == 1, src_l, jnp.where(ok_m, src_m, jnp.where(ok_s, src_s, zero_in))
    ).astype(jnp.int32)

    per = plan.piece // 8
    p, t = np.divmod(np.arange(plan.n_band * per), per)
    k = jnp.asarray(p % nz, jnp.int32)
    c_src = jnp.where(jnp.asarray(p < nz), core, 1 - core)
    band = 2 * ((z - k) % nz) + c_src
    onehot = band[:, None] == jnp.arange(plan.n_band)[None, :]

    def of_band(row):
        return jnp.sum(jnp.where(onehot, row[None, :], 0), axis=1)

    within = jnp.asarray(t * 8, jnp.int32) - off
    wl = jnp.maximum(within, 0)
    r = wl // 32
    ok_l = (within >= 0) & (r < of_band(band_rows[2]))
    out_l = (of_band(starts[2]) + r) * 4 + wl % 32 // 8
    r = wl // 24
    in_m = (has_m == 1) & (wl < plan.r_m)
    ok_m = (within >= 0) & in_m & (r < of_band(band_rows[1]))
    out_m = (of_band(starts[1]) + r) * 4 + wl % 24 // 8
    ws = jnp.maximum(wl - has_m * plan.r_m, 0)
    r = ws // 16
    h = of_band(starts[0]) + r
    ok_s = (within >= 0) & (has_s == 1) & ~in_m & (r < of_band(band_rows[0]))
    out_s = 96 + (h % 8) * 4 + (h // 8) * 2 + ws % 16 // 8
    scatter = jnp.where(
        is_l == 1,
        jnp.where(ok_l, out_l, 128),
        jnp.where(ok_m, out_m, jnp.where(ok_s, out_s, 128)),
    ).astype(jnp.int32)
    flags = jnp.stack(
        [
            is_l,
            jnp.where(is_l == 1, 32, 24 * has_m),
            jnp.where(is_l == 1, 32, 32 * has_s),
            jnp.where(is_l == 1, 0, 16),
        ]
    ).astype(jnp.int32)
    return gather, scatter, flags


class Scalars:
    def __init__(self, flags):
        self.is_l = flags[0]
        self.lims = (flags[1], flags[2])
        self.split = flags[3]
        self.l_f = flags[0].astype(F32)
        large = flags[0] == 1
        self.inv = (
            jnp.where(large, 1.0 / (1024 * 16), 1.0 / (576 * 16)).astype(F32),
            jnp.where(large, 1.0 / (1024 * 16), 1.0 / (256 * 16)).astype(F32),
        )


def dot(a, b):
    return jnp.dot(a, b, preferred_element_type=F32)


def dot_nt(a, b):
    return lax.dot_general(a, b, (((1,), (1,)), ((), ())), preferred_element_type=F32)


def dot_tn(a, b):
    return lax.dot_general(a, b, (((0,), (0,)), ((), ())), preferred_element_type=F32)


def line_rows(line):
    return pl.ds(pl.multiple_of(line * 32, 32), 32)


def line_loop(body, carries, unroll=2):
    results = []
    for seg, (low, high) in enumerate(SEG_LINES):
        results.append(
            lax.fori_loop(
                low, high, lambda line, carry, seg=seg: body(seg, line, carry), carries[seg], unroll=unroll
            )
        )
    return results


def fold(value):
    return value.reshape(4, 8, C).sum(axis=0)


def columns():
    return lax.broadcasted_iota(jnp.int32, (32, C), 0)


def fill_group_matrix(gm_ref):
    row = lax.broadcasted_iota(jnp.int32, (C, C), 0) // (C // GROUPS)
    col = lax.broadcasted_iota(jnp.int32, (C, C), 1) // (C // GROUPS)
    gm_ref[...] = (row == col).astype(F32).astype(BF16)


def group_totals(gm_ref, scal, per_seg):
    stacked = jnp.concatenate(list(per_seg) + [jnp.zeros((8 - len(per_seg), C), F32)], axis=0)
    hi = stacked.astype(BF16)
    rest = stacked - hi.astype(F32)
    mid = rest.astype(BF16)
    low = (rest - mid.astype(F32)).astype(BF16)
    both = dot(jnp.concatenate([hi, mid, low, jnp.zeros((8, C), BF16)], axis=0), gm_ref[...])
    total = both[0:8] + both[8:16] + both[16:24]
    out = []
    for i in range(0, len(per_seg), 2):
        first, second = total[i : i + 1], total[i + 1 : i + 2]
        out.append((first + scal.l_f * second, second + scal.l_f * first))
    return out


def norm_stats(read, gm_ref, scal):
    zero = jnp.zeros((8, C), F32)
    sums = line_loop(lambda seg, line, acc: acc + fold(read(line)), (zero, zero))
    sums = [s.sum(axis=0, keepdims=True) for s in sums]
    (totals,) = group_totals(gm_ref, scal, sums)
    means = [totals[seg] * scal.inv[seg] for seg in range(2)]
    col = columns()

    def squares(seg, line, acc):
        dev = jnp.where(col < scal.lims[seg], read(line) - means[seg], 0.0)
        return acc + fold(dev * dev)

    sums = line_loop(squares, (zero, zero))
    sums = [s.sum(axis=0, keepdims=True) for s in sums]
    (totals,) = group_totals(gm_ref, scal, sums)
    rstds = [lax.rsqrt(totals[seg] * scal.inv[seg] + EPSILON) for seg in range(2)]
    return means, rstds


def store_shifted(buf_ref, scal, seg, line, value16):
    col = columns()
    value = value16.astype(F32)
    keep_left, keep_right = col != 0, col != 31
    if seg == 1:
        keep_left &= col != scal.split
        keep_right &= col != scal.split - 1
    left = jnp.where(keep_left, pltpu.roll(value, 1, 0), 0.0).astype(BF16)
    right = jnp.where(keep_right, pltpu.roll(value, 31, 0), 0.0).astype(BF16)
    at = line_rows(line + (1 if seg == 0 else 3))
    buf_ref[at, 0:C] = left
    buf_ref[at, C : 2 * C] = value16
    buf_ref[at, 2 * C : 3 * C] = right


def fill_halos(buf_ref, scal):
    zero = jnp.zeros((32, 3 * C), BF16)
    buf_ref[0:32, :] = zero
    buf_ref[25 * 32 : 26 * 32, :] = zero
    buf_ref[26 * 32 : 27 * 32, :] = zero
    buf_ref[35 * 32 : 36 * 32, :] = zero

    @pl.when(scal.is_l == 1)
    def _():
        buf_ref[25 * 32 : 26 * 32, :] = buf_ref[27 * 32 : 28 * 32, :]
        buf_ref[26 * 32 : 27 * 32, :] = buf_ref[24 * 32 : 25 * 32, :]

    @pl.when(scal.is_l == 0)
    def _():
        buf_ref[26 * 32 + 16 : 27 * 32, :] = buf_ref[34 * 32 : 34 * 32 + 16, :]
        buf_ref[35 * 32 : 35 * 32 + 16, :] = buf_ref[27 * 32 + 16 : 28 * 32, :]


def tile_rows(tile, shift):
    line = (8 * tile if tile < 3 else 26) + shift
    return slice(line * 32, line * 32 + 256)


def conv_tiles(buf_ref, w_ref, write):
    for tile in range(4):
        acc = None
        for shift in range(3):
            term = dot(buf_ref[tile_rows(tile, shift), :], w_ref[shift * 3 * C : (shift + 1) * 3 * C, :])
            acc = term if acc is None else acc + term
        write(tile, acc)


def gather_pieces(table_ref, src_ref, dst_ref, count):
    def step(i, carry):
        at = pl.multiple_of(table_ref[i] * 8, 8)
        dst_ref[pl.ds(pl.multiple_of(i * 8, 8), 8), :] = src_ref[pl.ds(at, 8), :]
        return carry

    lax.fori_loop(0, count, step, 0, unroll=4)


def slots_to_image(table_ref, own_ref, got_ref, slots_ref, image_ref):
    half = own_ref.shape[0]
    slots_ref[0:half, :] = own_ref[...].astype(F32)
    slots_ref[half : 2 * half, :] = got_ref[...].astype(F32)
    slots_ref[2 * half : 2 * half + 8, :] = jnp.zeros((8, C), F32)
    gather_pieces(table_ref, slots_ref, image_ref, 128)


def image_to_slots(table_ref, image_ref, slots_ref, own_ref, oth_ref):
    half = own_ref.shape[0]
    gather_pieces(table_ref, image_ref, slots_ref, 2 * half // 8)
    own_ref[...] = slots_ref[0:half, :].astype(BF16)
    oth_ref[...] = slots_ref[half : 2 * half, :].astype(BF16)


def swish_slope(value):
    sigma = jax.nn.sigmoid(value)
    return sigma * (1.0 + value * (1.0 - sigma))


def features_kernel(
    first,
    gather,
    flags,
    own,
    got,
    small,
    weights,
    *refs,
):
    if first:
        x_out, a1_out, h1_out, a2_out, y_out, z_out, q_out, k_out, v_out, stats_out = refs[:10]
        scratch = refs[10:]
    else:
        y_out, q_out, k_out, v_out = refs[:4]
        scratch = refs[4:]
    slots, x_ref, h_ref, z_ref, buf, w1, w2, wp, gm, sems = scratch
    copies = [
        pltpu.make_async_copy(weights.at[pl.ds(0, 9 * C)], w1, sems.at[0]),
        pltpu.make_async_copy(weights.at[pl.ds(9 * C, 9 * C)], w2, sems.at[1]),
        pltpu.make_async_copy(weights.at[pl.ds(18 * C, 3 * C)], wp, sems.at[2]),
    ]
    for copy in copies:
        copy.start()
    scal = Scalars(flags)
    fill_group_matrix(gm)
    slots_to_image(gather, own, got, slots, x_ref)
    col = columns()

    def row(i):
        return small[i : i + 1, :]

    def activate(read, means, rstds, gain, shift, keep):
        def body(seg, line, carry):
            normed = (read(line) - means[seg]) * rstds[seg] * gain + shift
            act = jnp.where(col < scal.lims[seg], normed * jax.nn.sigmoid(normed), 0.0).astype(BF16)
            if keep is not None:
                keep[line_rows(line), :] = act
            store_shifted(buf, scal, seg, line, act)
            return carry

        line_loop(body, (0, 0))
        fill_halos(buf, scal)

    def read_x(line):
        return x_ref[line_rows(line), :]

    means1, rstds1 = norm_stats(read_x, gm, scal)
    activate(read_x, means1, rstds1, row(0), row(1), a1_out if first else None)
    if first:

        def keep_x(seg, line, carry):
            x_out[line_rows(line), :] = read_x(line).astype(BF16)
            return carry

        line_loop(keep_x, (0, 0))

    copies[0].wait()

    def write_h(tile, acc):
        h_ref[tile * 256 : (tile + 1) * 256, :] = acc

    conv_tiles(buf, w1, write_h)

    def finish_h(seg, line, carry):
        value = jnp.where(col < scal.lims[seg], h_ref[line_rows(line), :] + row(2), 0.0)
        h_ref[line_rows(line), :] = value
        if first:
            h1_out[line_rows(line), :] = value
        return carry

    line_loop(finish_h, (0, 0))

    def read_h(line):
        return h_ref[line_rows(line), :]

    means2, rstds2 = norm_stats(read_h, gm, scal)
    activate(read_h, means2, rstds2, row(3), row(4), a2_out if first else None)
    copies[1].wait()
    conv_tiles(buf, w2, write_h)

    def finish_y(seg, line, carry):
        value = jnp.where(
            col < scal.lims[seg], read_x(line) + (h_ref[line_rows(line), :] + row(5)), 0.0
        )
        y_out[line_rows(line), :] = value
        return carry

    line_loop(finish_y, (0, 0))

    def read_y(line):
        return y_out[line_rows(line), :]

    means3, rstds3 = norm_stats(read_y, gm, scal)

    def third(seg, line, carry):
        normed = (read_y(line) - means3[seg]) * rstds3[seg] * row(6) + row(7)
        value = jnp.where(col < scal.lims[seg], normed, 0.0).astype(BF16)
        z_ref[line_rows(line), :] = value
        if first:
            z_out[line_rows(line), :] = value
        return carry

    line_loop(third, (0, 0))
    copies[2].wait()
    for tile in range(4):
        at = slice(tile * 256, (tile + 1) * 256)
        rows = z_ref[at, :]
        q_out[at, :] = (dot(rows, wp[0:C, :]) + row(8)).astype(BF16)
        k_out[at, :] = dot(rows, wp[C : 2 * C, :]).astype(BF16)
        v_out[at, :] = (dot(rows, wp[2 * C : 3 * C, :]) + row(9)).astype(BF16)
    if first:
        for i, pair in enumerate((means1, rstds1, means2, rstds2, means3, rstds3)):
            stats_out[2 * i : 2 * i + 1, :] = pair[0]
            stats_out[2 * i + 1 : 2 * i + 2, :] = pair[1]


def key_bias(scal):
    key = lax.broadcasted_iota(jnp.int32, (1, PIX), 1)
    column = key % 32
    in0 = key < 768
    ok0 = in0 & (column < scal.lims[0])
    ok1 = (~in0) & (column < scal.lims[1])
    large = scal.is_l == 1
    row0 = jnp.where(ok0 | (ok1 & large), 0.0, -1e30).astype(F32)
    row1 = jnp.where(ok1 | (ok0 & large), 0.0, -1e30).astype(F32)
    return row0, row1


def probabilities(q, k_ref, bias):
    scores = dot_nt(q, k_ref[...]) * (C**-0.5) + bias
    top = jnp.max(scores, axis=1, keepdims=True)
    expo = jnp.exp(scores - top)
    return expo * (1.0 / jnp.sum(expo, axis=1, keepdims=True))


def attend_kernel(scatter, flags, q, k, v, y, small, weights, own_out, oth_out, image, slots, wo, sems):
    copy = pltpu.make_async_copy(weights.at[pl.ds(21 * C, C)], wo, sems.at[0])
    copy.start()
    scal = Scalars(flags)
    biases = key_bias(scal)
    copy.wait()
    for tile in range(4):
        at = slice(tile * 256, (tile + 1) * 256)
        prob = probabilities(q[at, :], k, biases[tile // 3]).astype(BF16)
        mixed = dot(prob, v[...]).astype(BF16)
        image[at, :] = y[at, :] + (dot(mixed, wo[...]) + small[10:11, :])
    image[PIX : PIX + 8, :] = jnp.zeros((8, C), F32)
    image_to_slots(scatter, image, slots, own_out, oth_out)


def attend_both_kernel(
    gather,
    scatter,
    flags,
    q,
    k,
    v,
    y,
    z,
    cot_own,
    cot_got,
    stats,
    small,
    weights,
    own_out,
    oth_out,
    dy_out,
    dy16_out,
    grads_out,
    sums_out,
    image,
    slots,
    g_ref,
    o_ref,
    d_ref,
    dk_acc,
    dv_acc,
    wp,
    gm,
    sems,
):
    copy = pltpu.make_async_copy(weights.at[pl.ds(18 * C, 4 * C)], wp, sems.at[0])
    copy.start()
    scal = Scalars(flags)
    fill_group_matrix(gm)
    biases = key_bias(scal)
    slots_to_image(gather, cot_own, cot_got, slots, g_ref)
    copy.wait()
    scaling = C**-0.5
    for tile in range(4):
        at = slice(tile * 256, (tile + 1) * 256)
        q_t = q[at, :]
        prob = probabilities(q_t, k, biases[tile // 3])
        prob16 = prob.astype(BF16)
        mixed = dot(prob16, v[...]).astype(BF16)
        o_ref[at, :] = mixed
        image[at, :] = y[at, :] + (dot(mixed, wp[3 * C : 4 * C, :]) + small[10:11, :])
        d_mixed = dot_nt(g_ref[at, :].astype(BF16), wp[3 * C : 4 * C, :]).astype(BF16)
        d_prob = dot_nt(d_mixed, v[...])
        inner = jnp.sum(prob * d_prob, axis=1, keepdims=True)
        d_score = (prob * (d_prob - inner)).astype(BF16)
        d_ref[at, 0:C] = (scaling * dot(d_score, k[...])).astype(BF16)
        dk = dot_tn(d_score, q_t)
        dv = dot_tn(prob16, d_mixed)
        if tile == 0:
            dk_acc[...] = dk
            dv_acc[...] = dv
        else:
            dk_acc[...] += dk
            dv_acc[...] += dv
    d_ref[:, C : 2 * C] = (scaling * dk_acc[...]).astype(BF16)
    d_ref[:, 2 * C : 3 * C] = dv_acc[...].astype(BF16)
    image[PIX : PIX + 8, :] = jnp.zeros((8, C), F32)
    image_to_slots(scatter, image, slots, own_out, oth_out)
    for part in range(3):
        grads_out[part * C : (part + 1) * C, :] = dot_tn(
            z[...], d_ref[:, part * C : (part + 1) * C]
        ).astype(BF16)
    grads_out[3 * C : 4 * C, :] = dot_tn(o_ref[...], g_ref[...].astype(BF16)).astype(BF16)
    for tile in range(4):
        at = slice(tile * 256, (tile + 1) * 256)
        acc = dot_nt(d_ref[at, 0:C], wp[0:C, :])
        acc = acc + dot_nt(d_ref[at, C : 2 * C], wp[C : 2 * C, :])
        image[at, :] = acc + dot_nt(d_ref[at, 2 * C : 3 * C], wp[2 * C : 3 * C, :])
    col = columns()
    means = (stats[8:9, :], stats[9:10, :])
    rstds = (stats[10:11, :], stats[11:12, :])
    zero = jnp.zeros((8, C), F32)

    def sums(seg, line, acc):
        at = line_rows(line)
        d_norm = image[at, :]
        unit = (y[at, :] - means[seg]) * rstds[seg]
        d_all = d_ref[at, :].astype(F32)
        return (
            acc[0] + fold(d_norm),
            acc[1] + fold(d_norm * unit),
            acc[2] + fold(d_all[:, 0:C]),
            acc[3] + fold(d_all[:, 2 * C : 3 * C]),
            acc[4] + fold(g_ref[at, :]),
        )

    got = line_loop(sums, ((zero,) * 5, (zero,) * 5), unroll=1)
    got = [[part.sum(axis=0, keepdims=True) for part in seg] for seg in got]
    gain = small[6:7, :]
    ones, cross = group_totals(
        gm, scal, [got[0][0] * gain, got[1][0] * gain, got[0][1] * gain, got[1][1] * gain]
    )
    for i, part in enumerate((1, 0, 2, 3, 4)):
        sums_out[i : i + 1, :] = got[0][part] + got[1][part]
    sums_out[5:8, :] = jnp.zeros((3, C), F32)

    def back(seg, line, carry):
        at = line_rows(line)
        unit = (y[at, :] - means[seg]) * rstds[seg]
        d_in = rstds[seg] * (
            image[at, :] * gain - ones[seg] * scal.inv[seg] - unit * (cross[seg] * scal.inv[seg])
        )
        value = g_ref[at, :] + jnp.where(col < scal.lims[seg], d_in, 0.0)
        dy_out[at, :] = value
        dy16_out[at, :] = value.astype(BF16)
        return carry

    line_loop(back, (0, 0))


def fill_gradient_buffer(buf, scal, grad_ref):
    def body(seg, line, carry):
        store_shifted(buf, scal, seg, line, grad_ref[line_rows(line), :])
        return carry

    line_loop(body, (0, 0))
    fill_halos(buf, scal)


def weight_grad_kernel(flags, act, grad, w_out, sums_out, buf, act_t):
    scal = Scalars(flags)
    fill_gradient_buffer(buf, scal, grad)
    for tile in range(4):
        at = slice(tile * 256, (tile + 1) * 256)
        act_t[:, at] = act[at, :].T
    for shift in range(3):
        seg0 = slice(shift * 32, shift * 32 + 768)
        seg1 = slice((26 + shift) * 32, (26 + shift) * 32 + 256)
        for part in range(3):
            cols = slice(part * C, (part + 1) * C)
            value = dot(act_t[:, 0:768], buf[seg0, cols]) + dot(act_t[:, 768:1024], buf[seg1, cols])
            tap = 3 * (2 - shift) + (2 - part)
            w_out[tap * C : (tap + 1) * C, :] = value.astype(BF16)
    zero = jnp.zeros((8, C), F32)
    got = line_loop(
        lambda seg, line, acc: acc + fold(grad[line_rows(line), :].astype(F32)), (zero, zero)
    )
    sums_out[...] = jnp.zeros((8, C), F32)
    sums_out[0:1, :] = (got[0] + got[1]).sum(axis=0, keepdims=True)


def data_grad_kernel(last, conv, *refs):
    if last:
        scatter, flags, grad, feat, dy, stats, small, weights, own_out, oth_out, sums_out = refs[:11]
        dn, slots, buf, w, gm, sems = refs[11:]
    else:
        flags, grad, feat, stats, small, weights, grad_out, sums_out = refs[:8]
        dn, buf, w, gm, sems = refs[8:]
    copy = pltpu.make_async_copy(weights.at[pl.ds(conv * 9 * C, 9 * C)], w, sems.at[0])
    copy.start()
    scal = Scalars(flags)
    fill_group_matrix(gm)
    fill_gradient_buffer(buf, scal, grad)
    copy.wait()
    for tile in range(4):
        acc = None
        for shift in range(3):
            for part in range(3):
                tap = 3 * (2 - shift) + (2 - part)
                term = dot_nt(
                    buf[tile_rows(tile, shift), part * C : (part + 1) * C], w[tap * C : (tap + 1) * C, :]
                )
                acc = term if acc is None else acc + term
        dn[tile * 256 : (tile + 1) * 256, :] = acc
    base = 4 * conv
    means = (stats[base : base + 1, :], stats[base + 1 : base + 2, :])
    rstds = (stats[base + 2 : base + 3, :], stats[base + 3 : base + 4, :])
    gain, shift_row = small[3 * conv : 3 * conv + 1, :], small[3 * conv + 1 : 3 * conv + 2, :]
    col = columns()
    zero = jnp.zeros((8, C), F32)

    def sums(seg, line, acc):
        at = line_rows(line)
        unit = (feat[at, :].astype(F32) - means[seg]) * rstds[seg]
        value = dn[at, :] * swish_slope(unit * gain + shift_row)
        value = jnp.where(col < scal.lims[seg], value, 0.0)
        dn[at, :] = value
        return (acc[0] + fold(value), acc[1] + fold(value * unit))

    got = line_loop(sums, ((zero, zero), (zero, zero)))
    got = [[part.sum(axis=0, keepdims=True) for part in seg] for seg in got]
    ones, cross = group_totals(
        gm, scal, [got[0][0] * gain, got[1][0] * gain, got[0][1] * gain, got[1][1] * gain]
    )
    sums_out[...] = jnp.zeros((8, C), F32)
    sums_out[0:1, :] = got[0][1] + got[1][1]
    sums_out[1:2, :] = got[0][0] + got[1][0]

    def back(seg, line, carry):
        at = line_rows(line)
        unit = (feat[at, :].astype(F32) - means[seg]) * rstds[seg]
        value = rstds[seg] * (
            dn[at, :] * gain - ones[seg] * scal.inv[seg] - unit * (cross[seg] * scal.inv[seg])
        )
        value = jnp.where(col < scal.lims[seg], value, 0.0)
        if last:
            dn[at, :] = value + dy[at, :]
        else:
            grad_out[at, :] = value.astype(BF16)
        return carry

    line_loop(back, (0, 0))
    if last:
        dn[PIX : PIX + 8, :] = jnp.zeros((8, C), F32)
        image_to_slots(scatter, dn, slots, own_out, oth_out)


SMEM = pl.BlockSpec(memory_space=pltpu.SMEM)
VMEM = pl.BlockSpec(memory_space=pltpu.VMEM)
ANY = pl.BlockSpec(memory_space=pl.ANY)


def call(kernel, name, in_specs, outs, scratch, flops, args):
    moved = sum(int(np.prod(a.shape)) * a.dtype.itemsize for a in args)
    moved += sum(int(np.prod(s)) * jnp.dtype(d).itemsize for s, d in outs)
    return pl.pallas_call(
        kernel,
        name=name,
        out_shape=[jax.ShapeDtypeStruct(s, d) for s, d in outs],
        in_specs=in_specs,
        out_specs=[VMEM] * len(outs),
        scratch_shapes=scratch,
        compiler_params=pltpu.CompilerParams(vmem_limit_bytes=VMEM_BYTES),
        cost_estimate=pl.CostEstimate(flops=int(flops), bytes_accessed=moved, transcendentals=0),
    )(*args)


MAP, SLOT_PAD = (PIX, C), 8
CONV_FLOPS = 2 * PIX * 9 * C * C
PROJ_FLOPS = 2 * PIX * C * C
PAIR_FLOPS = 2 * PIX * PIX * C
BUF = pltpu.VMEM((BUF_LINES * 32, 3 * C), BF16)


def run_features(first, tables, slots_in, small, weights):
    gather, _, flags = tables
    rows = 2 * slots_in[0].shape[0] + SLOT_PAD
    outs = [(MAP, F32), (MAP, BF16), (MAP, BF16), (MAP, BF16)]
    if first:
        outs = [
            (MAP, BF16),
            (MAP, BF16),
            (MAP, F32),
            (MAP, BF16),
            (MAP, F32),
            (MAP, BF16),
            (MAP, BF16),
            (MAP, BF16),
            (MAP, BF16),
            ((16, C), F32),
        ]
    return call(
        functools.partial(features_kernel, first),
        "features_first" if first else "features_again",
        [SMEM, SMEM, VMEM, VMEM, VMEM, ANY],
        outs,
        [
            pltpu.VMEM((rows, C), F32),
            pltpu.VMEM(MAP, F32),
            pltpu.VMEM(MAP, F32),
            pltpu.VMEM(MAP, BF16),
            BUF,
            pltpu.VMEM((9 * C, C), BF16),
            pltpu.VMEM((9 * C, C), BF16),
            pltpu.VMEM((3 * C, C), BF16),
            pltpu.VMEM((C, C), BF16),
            pltpu.SemaphoreType.DMA((3,)),
        ],
        2 * CONV_FLOPS + 3 * PROJ_FLOPS,
        (gather, flags, slots_in[0], slots_in[1], small, weights),
    )


def run_attend(tables, q, k, v, y, small, weights, half):
    _, scatter, flags = tables
    return call(
        attend_kernel,
        "attend_again",
        [SMEM, SMEM, VMEM, VMEM, VMEM, VMEM, VMEM, ANY],
        [((half, C), BF16)] * 2,
        [
            pltpu.VMEM((PIX + 8, C), F32),
            pltpu.VMEM((2 * half, C), F32),
            pltpu.VMEM((C, C), BF16),
            pltpu.SemaphoreType.DMA((1,)),
        ],
        2 * PAIR_FLOPS + PROJ_FLOPS,
        (scatter, flags, q, k, v, y, small, weights),
    )


def run_attend_both(tables, q, k, v, y, z, cot, stats, small, weights):
    gather, scatter, flags = tables
    half = cot[0].shape[0]
    return call(
        attend_both_kernel,
        "attend_both",
        [SMEM, SMEM, SMEM] + [VMEM] * 9 + [ANY],
        [
            ((half, C), BF16),
            ((half, C), BF16),
            (MAP, F32),
            (MAP, BF16),
            ((4 * C, C), BF16),
            ((8, C), F32),
        ],
        [
            pltpu.VMEM((PIX + 8, C), F32),
            pltpu.VMEM((2 * half + SLOT_PAD, C), F32),
            pltpu.VMEM(MAP, F32),
            pltpu.VMEM(MAP, BF16),
            pltpu.VMEM((PIX, 3 * C), BF16),
            pltpu.VMEM(MAP, F32),
            pltpu.VMEM(MAP, F32),
            pltpu.VMEM((4 * C, C), BF16),
            pltpu.VMEM((C, C), BF16),
            pltpu.SemaphoreType.DMA((1,)),
        ],
        7 * PAIR_FLOPS + 9 * PROJ_FLOPS,
        (gather, scatter, flags, q, k, v, y, z, cot[0], cot[1], stats, small, weights),
    )


def run_weight_grad(tables, act, grad, name):
    return call(
        weight_grad_kernel,
        name,
        [SMEM, VMEM, VMEM],
        [((9 * C, C), BF16), ((8, C), F32)],
        [BUF, pltpu.VMEM((C, PIX), BF16)],
        CONV_FLOPS,
        (tables[2], act, grad),
    )


def run_data_grad(tables, conv, grad, feat, stats, small, weights, dy=None, half=None):
    last = dy is not None
    scratch = [BUF, pltpu.VMEM((9 * C, C), BF16), pltpu.VMEM((C, C), BF16), pltpu.SemaphoreType.DMA((1,))]
    if last:
        outs = [((half, C), BF16)] * 2
        scratch = [pltpu.VMEM((PIX + 8, C), F32), pltpu.VMEM((2 * half, C), F32)] + scratch
        args = (tables[1], tables[2], grad, feat, dy, stats, small, weights)
        specs = [SMEM, SMEM] + [VMEM] * 5 + [ANY]
    else:
        outs = [(MAP, BF16)]
        scratch = [pltpu.VMEM(MAP, F32)] + scratch
        args = (tables[2], grad, feat, stats, small, weights)
        specs = [SMEM] + [VMEM] * 4 + [ANY]
    return call(
        functools.partial(data_grad_kernel, last, conv),
        "data_grad_one" if conv == 0 else "data_grad_two",
        specs,
        outs + [((8, C), F32)],
        scratch,
        CONV_FLOPS,
        args,
    )


def z_shift(value, nz, k):
    return lax.ppermute(value, "band", [(2 * z + c, 2 * ((z + k) % nz) + c) for z in range(nz) for c in range(2)])


def core_swap(value, n_band):
    return lax.ppermute(value, "band", [(b, b ^ 1) for b in range(n_band)])


def to_holders(plan, position, arrays):
    z, core = position // 2, position % 2
    flat = [a.reshape(a.shape[0], -1, C) for a in arrays]
    blocks = []
    for chip in range(plan.n_chip):
        parts = []
        for c in range(2):
            h = plan.holders[2 * chip + c]
            mine = [flat[m][h[name]] for m, name in ((2, "l"), (1, "m"), (0, "s")) if name in h]
            if c == 1:
                used = plan.sizes[2 * chip] + plan.sizes[2 * chip + 1]
                if used < plan.block:
                    parts.append(jnp.zeros((plan.block - used, C), BF16))
            parts += mine
        blocks.append(jnp.concatenate(parts, axis=0))
    sent = jnp.stack(blocks)
    nz = plan.n_chip
    received = []
    for k in range(nz):
        block = lax.dynamic_index_in_dim(sent, (z + k) % nz, 0, keepdims=False)
        received.append(block if k == 0 else z_shift(block, nz, k))
    received = jnp.stack(received)
    slack = plan.block - plan.piece
    own = lax.dynamic_slice_in_dim(received, slack * core, plan.piece, 1)
    other = lax.dynamic_slice_in_dim(received, slack * (1 - core), plan.piece, 1)
    got = core_swap(other, plan.n_band)
    return own.reshape(-1, C), got.reshape(-1, C)


def from_holders(plan, position, own, other):
    z, core = position // 2, position % 2
    nz, slack = plan.n_chip, plan.block - plan.piece
    got = core_swap(other, plan.n_band).reshape(nz, plan.piece, C)
    own = own.reshape(nz, plan.piece, C)
    first, second = jnp.where(core == 0, own, got), jnp.where(core == 0, got, own)
    blocks = jnp.pad(first, ((0, 0), (0, slack), (0, 0))) + jnp.pad(second, ((0, 0), (slack, 0), (0, 0)))
    received = [blocks[0]] + [z_shift(blocks[k], nz, -k) for k in range(1, nz)]
    received = jnp.stack(received)
    images = [[None] * plan.n_s, [None] * plan.n_m, [None] * plan.n_l]
    for b, h in enumerate(plan.holders):
        chip = b // 2
        if not h:
            continue
        block = lax.dynamic_index_in_dim(received, (chip - z) % nz, 0, keepdims=False)
        at = plan.offs[b] + (slack if b % 2 else 0)
        for member, name, size in ((2, "l", plan.r_l), (1, "m", plan.r_m), (0, "s", plan.r_s)):
            if name in h:
                images[member][h[name]] = block[at : at + size]
                at += size
    sides = (plan.side_s, plan.side_m, plan.side_l)
    return [
        jnp.stack(images[m]).reshape(len(images[m]), -1, sides[m], C) for m in range(3)
    ]


def fetch_weights(shard):
    full = lax.all_gather(shard.astype(BF16), AXES, axis=0, tiled=True)
    small = full[22 * C : 22 * C + 16].astype(F32)
    return full, small


def swap_axis(value, n_band, which):
    if which == "core":
        return core_swap(value, n_band)
    bit = 1 if which == "x" else 2
    return lax.ppermute(value, "img", [(i, i ^ bit) for i in range(4)])


def reduce_pair(position, img, top, small):
    core, y, x = position % 2, img // 2, img % 2
    rows = top.shape[3]
    kept = lax.dynamic_index_in_dim(top, core, 1, keepdims=False)
    sent = lax.dynamic_index_in_dim(top, 1 - core, 1, keepdims=False)
    got = core_swap(sent, lax.axis_size("band"))
    both = (kept.astype(F32) + got.astype(F32)).astype(BF16).reshape(2, 2, 2, rows, C)

    def halve(value, axis, mine, which):
        keep = lax.dynamic_index_in_dim(value, mine, axis, keepdims=False)
        send = lax.dynamic_index_in_dim(value, 1 - mine, axis, keepdims=False)
        arrived = swap_axis(send, None, which)
        return (keep.astype(F32) + arrived.astype(F32)).astype(BF16)

    a = halve(both[0], 1, x, "x")
    b = halve(both[1], 0, y, "y")
    a = halve(a, 0, y, "y")
    b = halve(b, 0, x, "x")
    return a, b


def reduce_grads(position, img, high, low):
    z = position // 2
    planes = list(reduce_pair(position, img, low, None)) + list(reduce_pair(position, img, high, None))
    stacked = jnp.stack(planes)
    total = lax.dynamic_index_in_dim(stacked, z, 0, keepdims=False).astype(F32)
    for k in range(1, 4):
        sent = lax.dynamic_index_in_dim(stacked, (z + k) % 4, 0, keepdims=False)
        total = total + z_shift(sent, 4, k).astype(F32)
    return total


def shard_of_grads(position, img, w1, w2, proj, small_rows, rows):
    n_band, n_img = lax.axis_size("band"), lax.axis_size("img")
    count = n_band * n_img
    small_rows = jnp.pad(small_rows, ((0, rows * count - 22 * C - small_rows.shape[0]), (0, 0)))
    if n_band != 8 or n_img != 4:
        full = jnp.concatenate([w1, w2, proj, small_rows.astype(BF16)], axis=0)
        return lax.psum_scatter(full, AXES, scatter_dimension=0, tiled=True).astype(F32)
    block = 22 * C // count
    high = jnp.concatenate([w2[2 * C :], proj], axis=0).reshape(2, 2, 4, block, C)
    low = jnp.concatenate([w1, w2[: 2 * C]], axis=0).reshape(2, 2, 4, block, C)
    mine = reduce_grads(position, img, high, low)
    small_sum = lax.psum(small_rows, AXES)
    owner = position * n_img + img
    after = lax.ppermute(mine[:count], AXES, [(o, o - 1) for o in range(1, count)])
    after = jnp.where(owner == count - 1, small_sum, after)
    return lax.dynamic_slice_in_dim(jnp.concatenate([mine, after], axis=0), owner, rows, 0)


def body(
    x_small,
    x_medium,
    x_large,
    cot_small,
    cot_medium,
    cot_large,
    band_rows,
    params,
    first_moment,
    second_moment,
    step,
    rate,
):
    n_band = lax.axis_size("band")
    position, img = lax.axis_index("band"), lax.axis_index("img")
    plan = Plan([x_small.shape, x_medium.shape, x_large.shape], n_band)
    tables = make_tables(plan, band_rows, position)
    half = n_band // 2 * plan.piece

    x_slots = to_holders(plan, position, (x_small, x_medium, x_large))
    weights, small = fetch_weights(params)
    cot_slots = to_holders(plan, position, (cot_small, cot_medium, cot_large))
    x_img, a1, h1, a2, y, z, q, k, v, stats = run_features(True, tables, x_slots, small, weights)
    out_own, out_oth, dy, dy16, g_proj, sums3 = run_attend_both(
        tables, q, k, v, y, z, cot_slots, stats, small, weights
    )
    first_out = from_holders(plan, position, out_own, out_oth)
    g_w2, sums_b2 = run_weight_grad(tables, a2, dy16, "weight_grad_two")
    dh1, sums_n2 = run_data_grad(tables, 1, dy16, h1, stats, small, weights)
    g_w1, sums_b1 = run_weight_grad(tables, a1, dh1, "weight_grad_one")
    dx_own, dx_oth, sums_n1 = run_data_grad(
        tables, 0, dh1, x_img, stats, small, weights, dy=dy, half=half
    )
    input_grads = from_holders(plan, position, dx_own, dx_oth)
    small_rows = jnp.concatenate(
        [sums_n1[0:2], sums_b1[0:1], sums_n2[0:2], sums_b2[0:1], sums3[0:5]], axis=0
    )
    grad = shard_of_grads(position, img, g_w1, g_w2, g_proj, small_rows, params.shape[0])

    step_count = step[0].astype(F32)
    new_first = 0.5 * first_moment + 0.5 * grad
    new_second = 0.9 * second_moment + 0.1 * grad * grad
    weight_update = (
        rate[0]
        * (new_first / (1.0 - jnp.power(0.5, step_count)))
        / (jnp.sqrt(new_second / (1.0 - jnp.power(0.9, step_count))) + ADAM_EPSILON)
    )
    new_weights, new_small = fetch_weights(params - weight_update)
    y2, q2, k2, v2 = run_features(False, tables, x_slots, new_small, new_weights)
    again_own, again_oth = run_attend(tables, q2, k2, v2, y2, new_small, new_weights, half)
    second_out = from_holders(plan, position, again_own, again_oth)
    return (*first_out, *second_out, *input_grads, weight_update, new_first, new_second)


def solution(mesh):
    image = P("img", "band", None, None)
    shard = P(("band", "img"), None)
    return jax.shard_map(
        body,
        mesh=mesh,
        in_specs=(image,) * 6 + (P(),) + (shard,) * 3 + (P(), P()),
        out_specs=(image,) * 9 + (shard,) * 3,
        check_vma=False,
    )
```

time: 2170 us -> 685 us (0.32)
  blocking collectives: 723 us -> 0 us
  matrix products: 413 us -> 0 us
  waiting for transfers between devices: 698 us -> 409 us
  Pallas kernels: 0 us -> 128 us
  local copies, waits for them, and re-layouts: 141 us -> 46.5 us
  other arithmetic: 121 us -> 29.5 us
    unnamed x1 -> x0, blocking collectives: 494 us -> none
    all_gather x14 -> x2, waiting for transfers between devices: 496 us -> 77.9 us  [fetch_weights(): full = lax.all_gather(shard.astype(BF16), AXES, axis=0, tiled=True)]
    dot_general x282 -> x0, matrix products: 413 us -> none  [the longest x108 163 us: apply_kernel(): jnp.einsum('ahwc,cd->ahwd', window, kernel[offset], preferred_element_typ...]
    psum x12 -> x0, blocking collectives: 229 us -> none  [the longest x5 91.9 us: norm_forward(): firsts = lax.psum((firsts[0], firsts[1], firsts[2]), 'band')]
    ppermute x12 -> x34, waiting for transfers between devices: 8.17 us -> 209 us  [the longest x18 166 us: z_shift(): lax.ppermute(value, 'band', [(2 * z + c, 2 * ((z + k) % nz) + c) for z in...]
    reduce_scatter x6 -> x0, waiting for transfers between devices: 186 us -> none  [the longest x1 52.5 us: body(): lax.psum_scatter(value_parts[1].astype(jnp.bfloat16), 'band', scatter_dim...]
    pallas_call x0 -> x8, Pallas kernels: none -> 128 us  [call(): pl.pallas_call(kernel, name=name, out_shape=[jax.ShapeDtypeStruct(s, d) f...]
    psum x0 -> x1, waiting for transfers between devices: none -> 123 us  [shard_of_grads(): small_sum = lax.psum(small_rows, AXES)]
  transfers between devices with their start and end apart: 33 -> 37, of which waited for: 24 -> 20; matrix products, arithmetic and copies ran while one was open for 12% -> 6% of each run, Pallas kernels for 0% -> 6%
where the time goes in v1:
time: 685 us; the launch traced here: 676 us
  waiting for transfers between devices  409 us (60%)
  Pallas kernels  128 us (19%)
  local copies, waits for them, and re-layouts  46.5 us (7%)
  starting transfers between devices  42.5 us (6%)
  other arithmetic  29.5 us (4%)
  between operations  20.6 us (3%)
    ppermute x18, waiting for transfers between devices, z_shift(): lax.ppermute(value, 'band', [(2 * z + c, 2 * ((z + k) % nz) + c) for z in...  166 us
    pallas_call x8, Pallas kernels, call(): pl.pallas_call(kernel, name=name, out_shape=[jax.ShapeDtypeStruct(s, d) f...  128 us
    psum x1, waiting for transfers between devices, shard_of_grads(): small_sum = lax.psum(small_rows, AXES)  123 us
    all_gather x2, waiting for transfers between devices, fetch_weights(): full = lax.all_gather(shard.astype(BF16), AXES, axis=0, tiled=True)  77.9 us
    ppermute x8, waiting for transfers between devices, swap_axis(): return lax.ppermute(value, 'img', [(i, i ^ bit) for i in range(4)])  39.3 us
    ppermute x18, starting transfers between devices, z_shift(): lax.ppermute(value, 'band', [(2 * z + c, 2 * ((z + k) % nz) + c) for z in...  29.9 us
    unnamed x85, local copies, waits for them, and re-layouts  27.9 us
  transfers between devices with their start and end apart: 37, of which 20 were waited for; matrix products, arithmetic and copies ran while one was open for 6% of the time, Pallas kernels for 6%

profile of v1, /device:TPU:0, one launch (start us, length us, event | category | flops | bytes accessed | tf_op | source)
XLA Modules:
  0.0 676.0 jit_solution(17001990228098551628)
XLA Ops:
  7.2 2.0 convert_bitcast_fusion
  10.7 3.1 collective-permute-start.4
  13.8 2.6 collective-permute-start.5
  17.9 1.8 collective-permute-start.1
  19.7 1.9 collective-permute-start.2
  29.9 14.3 %collective-permute-done = bf16[288,512]{1,0:T(8,128)(2,1)S(1)} collective-permute-done((bf16[288,512]{1,0:T(8,128)(2,1)S(1)}, bf16[288,512]{1,0:T(8,128)(2,1)S(1)}, u32[]{:S(2)}, u32[]{:S(2)}) %collective-permute-start) | collective-permute-done | bytes 294944 | tf_op jit(solution)/shard_map/ppermute | solution.py:822
  44.2 18.2 %collective-permute-done.1 = bf16[288,512]{1,0:T(8,128)(2,1)S(1)} collective-permute-done((bf16[288,512]{1,0:T(8,128)(2,1)}, bf16[288,512]{1,0:T(8,128)(2,1)S(1)}, u32[]{:S(2)}, u32[]{:S(2)}) %collective-permute-start.1) | collective-permute-done | bytes 294944 | tf_op jit(solution)/shard_map/ppermute | solution.py:822
  66.1 23.0 %collective-permute-done.6 = bf16[288,512]{1,0:T(8,128)(2,1)S(1)} collective-permute-done((bf16[288,512]{1,0:T(8,128)(2,1)S(1)}, bf16[288,512]{1,0:T(8,128)(2,1)S(1)}, u32[]{:S(2)}, u32[]{:S(2)}) %collective-permute-start.6) | collective-permute-done | bytes 294944 | tf_op jit(solution)/shard_map/ppermute | solution.py:822
  90.2 41.5 %all-gather.5.cloned.1.call-done = bf16[32,353,512]{2,1,0:T(8,128)(2,1)} async-done(((bf16[1,353,512]{2,1,0:T(8,128)(2,1)}), bf16[32,353,512]{2,1,0:T(8,128)(2,1)}) %all-gather.5.cloned.1.call-update) | async-done | bytes 11567120 | tf_op jit(solution)/shard_map/all_gather | solution.py:885
  131.7 9.9 %reshape.315.weights.refs_5_.refs_7_ = bf16[11296,512]{1,0:T(8,128)(2,1)} reshape(bf16[32,353,512]{2,1,0:T(8,128)(2,1)} %all-gather.5.cloned.1.call-done) | data formatting | bytes 23134208
  143.0 23.5 %features_first.1 = (bf16[1024,512]{1,0:T(8,128)(2,1)}, bf16[1024,512]{1,0:T(8,128)(2,1)}, f32[1024,512]{1,0:T(8,128)}, bf16[1024,512]{1,0:T(8,128)(2,1)}, f32[1...) custom-call(s32[128]{0:T(128)} %broadcast_select_fusion.7.gather, ...), custom_call_target="tpu_custom_call" | custom-call | flops 11274289152 | bytes 24740368 | tf_op jit(solution)/shard_map/features_first/pallas_call | solution.py:677
  167.4 25.6 %attend_both.1 = (bf16[768,512]{1,0:T(8,128)(2,1)}, bf16[768,512]{1,0:T(8,128)(2,1)}, f32[1024,512]{1,0:T(8,128)}, bf16[1024,512]{1,0:T(8,128)(2,1)}, bf16[2048,512]{1,0:T(8,128)(2,1)}, /*index=5*/f32[8,512]{1,0:T(8,128)}) custom-call(s32[128]{0:T(128)} %broadcast_select_fusion.7.gather, s32[192]{0:T(256)} %fusion.48.scatter.refs_0_, ...), custom_call_target="tpu_custom_call" | custom-call | flops 12348030976 | bytes 26330384 | tf_op jit(solution)/shard_map/attend_both/pallas_call | solution.py:677
  193.0 9.7 %weight_grad_two.1 = (bf16[4608,512]{1,0:T(8,128)(2,1)}, f32[8,512]{1,0:T(8,128)}) custom-call(s32[4]{0:T(128)} %pad_add_fusion.3.flags.refs_0_.refs_1_, bf16[1024,512]{1,0:T(8,128)(2,1)} %get-tuple-element.56.act, bf16[1024,512]{1,0:T(8,128)(2,1)} %get-tuple-element.52.refs_1_.grad), custom_call_target="tpu_custom_call" | custom-call | flops 4831838208 | bytes 6832144 | tf_op jit(solution)/shard_map/weight_grad_two/pallas_call | solution.py:677
  204.0 2.3 slice.396
  206.3 12.4 %data_grad_two.1 = (bf16[1024,512]{1,0:T(8,128)(2,1)}, f32[8,512]{1,0:T(8,128)}) custom-call(s32[4]{0:T(128)} %pad_add_fusion.3.flags.refs_0_.refs_1_, bf16[1024,512]{1,0:T(8,128)(2,1)} %get-tuple-element.52.refs_1_.grad, f32[1024,512]{1,0:T(8,128)} %get-tuple-element.53.refs_2_, f32[16,512]{1,0:T(8,128)} %get-tuple-element.48.stats.refs_3_.refs_5_, ...), custom_call_target="tpu_custom_call" | custom-call | flops 4831838208 | bytes 15843344 | tf_op jit(solution)/shard_map/data_grad_two/pallas_call | solution.py:677
  218.8 9.9 %weight_grad_one.1 = (bf16[4608,512]{1,0:T(8,128)(2,1)}, f32[8,512]{1,0:T(8,128)}) custom-call(s32[4]{0:T(128)} %pad_add_fusion.3.flags.refs_0_.refs_1_, bf16[1024,512]{1,0:T(8,128)(2,1)} %get-tuple-element.51.act, bf16[1024,512]{1,0:T(8,128)(2,1)} %get-tuple-element.54.grad.refs_2_), custom_call_target="tpu_custom_call" | custom-call | flops 4831838208 | bytes 6832144 | tf_op jit(solution)/shard_map/weight_grad_one/pallas_call | solution.py:677
  228.7 2.7 pad_maximum_fusion
  231.4 1.9 dynamic-slice_bitcast_fusion.1
  233.3 1.7 copy-done.1
  235.6 2.1 dynamic-slice_bitcast_fusion
  240.6 3.7 fusion.1
  250.2 13.4 %collective-permute-done.13 = bf16[2,352,512]{2,1,0:T(8,128)(2,1)S(1)} collective-permute-done((bf16[2,352,512]{2,1,0:T(8,128)(2,1)S(1)}, bf16[2,352,512]{2,1,0:T(8,128)(2,1)S(1)}, u32[]{:S(2)}, u32[]{:S(2)}) %collective-permute-start.13) | collective-permute-done | bytes 720928 | tf_op jit(solution)/shard_map/ppermute | solution.py:894
  263.8 1.6 collective-permute-start.14
  266.3 12.8 %collective-permute-done.18 = bf16[2,352,512]{2,1,0:T(8,128)(2,1)S(1)} collective-permute-done((bf16[2,352,512]{2,1,0:T(8,128)(2,1)S(1)}, bf16[2,352,512]{2,1,0:T(8,128)(2,1)S(1)}, u32[]{:S(2)}, u32[]{:S(2)}) %collective-permute-start.18) | collective-permute-done | bytes 720928 | tf_op jit(solution)/shard_map/ppermute | solution.py:894
  279.3 1.6 collective-permute-start.19
  281.7 6.6 collective-permute-done.14
  288.6 6.5 collective-permute-done.19
  297.8 2.4 collective-permute-start.24
  300.2 8.7 %collective-permute-done.22 = bf16[352,512]{1,0:T(8,128)(2,1)S(1)} collective-permute-done((bf16[352,512]{1,0:T(8,128)(2,1)S(1)}, bf16[352,512]{1,0:T(8,128)(2,1)S(1)}, u32[]{:S(2)}, u32[]{:S(2)}) %collective-permute-start.22) | collective-permute-done | bytes 360480 | tf_op jit(solution)/shard_map/ppermute | solution.py:822
  308.9 13.6 %collective-permute-done.23 = bf16[352,512]{1,0:T(8,128)(2,1)S(1)} collective-permute-done((bf16[352,512]{1,0:T(8,128)(2,1)S(1)}, bf16[352,512]{1,0:T(8,128)(2,1)S(1)}, u32[]{:S(2)}, u32[]{:S(2)}) %collective-permute-start.23) | collective-permute-done | bytes 360480 | tf_op jit(solution)/shard_map/ppermute | solution.py:822
  325.0 14.1 %data_grad_one.1 = (bf16[768,512]{1,0:T(8,128)(2,1)}, bf16[768,512]{1,0:T(8,128)(2,1)}, f32[8,512]{1,0:T(8,128)}) custom-call(s32[192]{0:T(256)} %fusion.48.scatter.refs_0_, s32[4]{0:T(128)} %pad_add_fusion.3.flags.refs_0_.refs_1_, bf16[1024,512]{1,0:T(8,128)(2,1)} %get-tuple-element.54.grad.refs_2_, bf16[1024,512]{1,0:T(8,128)(2,1)} %get-tuple-element.59.refs_3_, ...), custom_call_target="tpu_custom_call" | custom-call | flops 4831838208 | bytes 17416976 | tf_op jit(solution)/shard_map/data_grad_one/pallas_call | solution.py:677
  344.2 122.6 %all-reduce.9.cloned.1.call-done = f32[32,512]{1,0:T(8,128)} async-done(((f32[32,512]{1,0:T(8,128)}), f32[32,512]{1,0:T(8,128)}) %all-reduce.9.cloned.1.call-update) | async-done | bytes 65552 | tf_op jit(solution)/shard_map/psum | solution.py:940
  466.8 3.5 fusion.14
  470.4 1.7 collective-permute-start.30
  472.1 2.0 collective-permute-done.30
  474.5 2.3 collective-permute-start.31
  478.8 3.0 collective-permute-start.9
  482.1 4.6 collective-permute-done.31
  486.7 4.8 collective-permute-start.11
  491.5 32.7 %collective-permute-done.32 = bf16[288,512]{1,0:T(8,128)(2,1)S(1)} collective-permute-done((bf16[288,512]{1,0:T(8,128)(2,1)S(1)}, bf16[288,512]{1,0:T(8,128)(2,1)S(1)}, u32[]{:S(2)}, u32[]{:S(2)}) %collective-permute-start.32) | collective-permute-done | bytes 294944 | tf_op jit(solution)/shard_map/ppermute | solution.py:822
  524.4 28.1 %collective-permute-done.10 = bf16[288,512]{1,0:T(8,128)(2,1)S(1)} collective-permute-done((bf16[288,512]{1,0:T(8,128)(2,1)S(1)}, bf16[288,512]{1,0:T(8,128)(2,1)S(1)}, u32[]{:S(2)}, u32[]{:S(2)}) %collective-permute-start.10) | collective-permute-done | bytes 294944 | tf_op jit(solution)/shard_map/ppermute | solution.py:822
  555.4 36.4 %all-gather.7.cloned.1.call-done = bf16[32,353,512]{2,1,0:T(8,128)(2,1)} async-done(((bf16[1,353,512]{2,1,0:T(8,128)(2,1)}), bf16[32,353,512]{2,1,0:T(8,128)(2,1)}) %all-gather.7.cloned.1.call-update) | async-done | bytes 11567120 | tf_op jit(solution)/shard_map/all_gather | solution.py:885
  591.8 9.9 %reshape.317.weights = bf16[11296,512]{1,0:T(8,128)(2,1)} reshape(bf16[32,353,512]{2,1,0:T(8,128)(2,1)} %all-gather.7.cloned.1.call-done) | data formatting | bytes 23134208
  603.1 22.2 %features_again.1 = (f32[1024,512]{1,0:T(8,128)}, bf16[1024,512]{1,0:T(8,128)(2,1)}, bf16[1024,512]{1,0:T(8,128)(2,1)}, bf16[1024,512]{1,0:T(8,128)(2,1)}) custom-call(s32[128]{0:T(128)} %broadcast_select_fusion.7.gather, s32[4]{0:T(128)} %pad_add_fusion.3.flags.refs_0_.refs_1_, bf16[768,512]{1,0:T(8,128)(2,1)} %bitcast.268, bf16[768,512]{1,0:T(8,128)(2,1)} %bitcast.39.got, ...), custom_call_target="tpu_custom_call" | custom-call | flops 11274289152 | bytes 18416144 | tf_op jit(solution)/shard_map/features_again/pallas_call | solution.py:677
  625.3 10.1 %attend_again.1 = (bf16[768,512]{1,0:T(8,128)(2,1)}, bf16[768,512]{1,0:T(8,128)(2,1)}) custom-call(s32[192]{0:T(256)} %fusion.48.scatter.refs_0_, s32[4]{0:T(128)} %pad_add_fusion.3.flags.refs_0_.refs_1_, bf16[1024,512]{1,0:T(8,128)(2,1)} %get-tuple-element.66.q, bf16[1024,512]{1,0:T(8,128)(2,1)} %get-tuple-element.67.k, ...), custom_call_target="tpu_custom_call" | custom-call | flops 2684354560 | bytes 18416400 | tf_op jit(solution)/shard_map/attend_again/pallas_call | solution.py:677
  638.3 1.7 collective-permute-start.27
  644.2 3.5 collective-permute-done.27
  647.7 19.3 %collective-permute-done.28 = bf16[288,512]{1,0:T(8,128)(2,1)S(1)} collective-permute-done((bf16[288,512]{1,0:T(8,128)(2,1)S(1)}, bf16[288,512]{1,0:T(8,128)(2,1)S(1)}, u32[]{:S(2)}, u32[]{:S(2)}) %collective-permute-start.28) | collective-permute-done | bytes 294944 | tf_op jit(solution)/shard_map/ppermute | solution.py:822
  (230 shorter events, 52.1 us)
Async XLA Ops:
  7.2 124.5 %all-gather.5.cloned.1.call-start = ((), (), s32[]{:S(2)}) async-start(), calls=%async_computation.1 | async-start | bytes 12165120 | tf_op jit(solution)/shard_map/all_gather | solution.py:885
  9.2 457.5 %all-reduce.9.cloned.1.call-start = ((), (), s32[]{:S(2)}) async-start(), calls=%async_computation | async-start | bytes 131072 | tf_op jit(solution)/shard_map/psum | solution.py:940
  10.7 55.4 %collective-permute-start.4 = (bf16[288,512]{1,0:T(8,128)(2,1)S(1)}, bf16[288,512]{1,0:T(8,128)(2,1)S(1)}, u32[]{:S(2)}, u32[]{:S(2)}) collective-permute-start(bf16[288,512]{1,0:T(8,128)(2,1)S(1)} %get-tuple-element.150), channel_id=1, source_target_pairs={{0,8},{4,12},{8,16},{12,20},{16,24},{20,28},{24,0},{28,4},{1,9},{5... | collective-permute-start | bytes 884744 | tf_op jit(solution)/shard_map/ppermute | solution.py:822
  13.8 52.3 %collective-permute-start.5 = (bf16[288,512]{1,0:T(8,128)(2,1)S(1)}, bf16[288,512]{1,0:T(8,128)(2,1)S(1)}, u32[]{:S(2)}, u32[]{:S(2)}) collective-permute-start(bf16[288,512]{1,0:T(8,128)(2,1)S(1)} %get-tuple-element.149), channel_id=1, source_target_pairs={{0,16},{4,20},{8,24},{12,28},{16,0},{20,4},{24,8},{28,12},{1,17},{... | collective-permute-start | bytes 884744 | tf_op jit(solution)/shard_map/ppermute | solution.py:822
  16.8 11.4 %copy-start.21 = (s32[128]{0:T(128)S(1)}, s32[128]{0:T(128)}, u32[]{:S(2)}) copy-start(s32[128]{0:T(128)} %constant.585.clone) | copy-start | bytes 1540
  16.8 11.5 %copy-start.22 = (s32[128]{0:T(128)S(1)}, s32[128]{0:T(128)}, u32[]{:S(2)}) copy-start(s32[128]{0:T(128)} %constant.581.clone) | copy-start | bytes 1540
  16.8 11.7 %copy-start.17 = (s32[192]{0:T(256)S(1)}, s32[192]{0:T(256)}, u32[]{:S(2)}) copy-start(s32[192]{0:T(256)} %constant.614) | copy-start | bytes 2308
  16.8 11.7 %copy-start.19 = (pred[192]{0:T(512)(128)(4,1)S(1)}, pred[192]{0:T(512)(128)(4,1)}, u32[]{:S(2)}) copy-start(pred[192]{0:T(512)(128)(4,1)} %constant.589.clone) | copy-start | bytes 580
  16.9 11.9 %copy-start.23 = (s32[128]{0:T(128)S(1)}, s32[128]{0:T(128)}, u32[]{:S(2)}) copy-start(s32[128]{0:T(128)} %constant.582.clone) | copy-start | bytes 1540
  16.9 11.9 %copy-start.24 = (pred[128]{0:T(512)(128)(4,1)S(1)}, pred[128]{0:T(512)(128)(4,1)}, u32[]{:S(2)}) copy-start(pred[128]{0:T(512)(128)(4,1)} %constant.584.clone) | copy-start | bytes 388
  16.9 11.9 %copy-start.25 = (s32[128]{0:T(128)S(1)}, s32[128]{0:T(128)}, u32[]{:S(2)}) copy-start(s32[128]{0:T(128)} %constant.586.clone) | copy-start | bytes 1540
  16.9 11.9 %copy-start.26 = (pred[128]{0:T(512)(128)(4,1)S(1)}, pred[128]{0:T(512)(128)(4,1)}, u32[]{:S(2)}) copy-start(pred[128]{0:T(512)(128)(4,1)} %constant.587.clone) | copy-start | bytes 388
  17.8 26.4 %collective-permute-start = (bf16[288,512]{1,0:T(8,128)(2,1)S(1)}, bf16[288,512]{1,0:T(8,128)(2,1)S(1)}, u32[]{:S(2)}, u32[]{:S(2)}) collective-permute-start(bf16[288,512]{1,0:T(8,128)(2,1)S(1)} %get-tuple-element.156), channel_id=1, source_target_pairs={{0,8},{4,12},{8,16},{12,20},{16,24},{20,28},{24,0},{28,4},{1,9},{5... | collective-permute-start | bytes 884744 | tf_op jit(solution)/shard_map/ppermute | solution.py:822
  17.9 44.5 %collective-permute-start.1 = (bf16[288,512]{1,0:T(8,128)(2,1)}, bf16[288,512]{1,0:T(8,128)(2,1)S(1)}, u32[]{:S(2)}, u32[]{:S(2)}) collective-permute-start(bf16[288,512]{1,0:T(8,128)(2,1)} %get-tuple-element.155), channel_id=1, source_target_pairs={{0,16},{4,20},{8,24},{12,28},{16,0},{20,4},{24,8},{28,12},{1,17},{... | collective-permute-start | bytes 884744 | tf_op jit(solution)/shard_map/ppermute | solution.py:822
  19.7 42.7 %collective-permute-start.2 = (bf16[288,512]{1,0:T(8,128)(2,1)}, bf16[288,512]{1,0:T(8,128)(2,1)S(1)}, u32[]{:S(2)}, u32[]{:S(2)}) collective-permute-start(bf16[288,512]{1,0:T(8,128)(2,1)} %get-tuple-element.154), channel_id=1, source_target_pairs={{0,24},{4,28},{8,0},{12,4},{16,8},{20,12},{24,16},{28,20},{1,25},{... | collective-permute-start | bytes 884744 | tf_op jit(solution)/shard_map/ppermute | solution.py:822
  44.2 44.8 %collective-permute-start.6 = (bf16[288,512]{1,0:T(8,128)(2,1)S(1)}, bf16[288,512]{1,0:T(8,128)(2,1)S(1)}, u32[]{:S(2)}, u32[]{:S(2)}) collective-permute-start(bf16[288,512]{1,0:T(8,128)(2,1)S(1)} %get-tuple-element.148), channel_id=1, source_target_pairs={{0,24},{4,28},{8,0},{12,4},{16,8},{20,12},{24,16},{28,20},{1,25},{... | collective-permute-start | bytes 884744 | tf_op jit(solution)/shard_map/ppermute | solution.py:822
  63.5 79.5 %collective-permute-start.3 = (bf16[4,192,512]{2,1,0:T(8,128)(2,1)S(1)}, bf16[4,192,512]{2,1,0:T(8,128)(2,1)}, u32[]{:S(2)}, u32[]{:S(2)}) collective-permute-start(bf16[4,192,512]{2,1,0:T(8,128)(2,1)S(1)} %get-tuple-element.151), channel_id=1, source_target_pairs={{0,4},{4,0},{8,12},{12,8},{16,20},{20,16},{24,28},{28,24},{1,5},{5... | collective-permute-start | bytes 2359304 | tf_op jit(solution)/shard_map/ppermute | solution.py:826
  90.2 76.3 %collective-permute-start.7 = (bf16[4,192,512]{2,1,0:T(8,128)(2,1)S(1)}, bf16[4,192,512]{2,1,0:T(8,128)(2,1)S(1)}, u32[]{:S(2)}, u32[]{:S(2)}) collective-permute-start(bf16[4,192,512]{2,1,0:T(8,128)(2,1)S(1)} %get-tuple-element.145), channel_id=1, source_target_pairs={{0,4},{4,0},{8,12},{12,8},{16,20},{20,16},{24,28},{28,24},{1,5},{5... | collective-permute-start | bytes 2359304 | tf_op jit(solution)/shard_map/ppermute | solution.py:826
  234.9 5.6 collective-permute-start.12
  238.8 7.9 %collective-permute-start.17 = (bf16[2,4,352,512]{3,2,1,0:T(8,128)(2,1)}, bf16[2,4,352,512]{3,2,1,0:T(8,128)(2,1)S(1)}, u32[]{:S(2)}, u32[]{:S(2)}) collective-permute-start(bf16[2,4,352,512]{3,2,1,0:T(8,128)(2,1)} %dynamic-slice_bitcast_fusion), channel_id=1, source_target_pairs={{0,4},{4,0},{8,12},{12,8},{16,20},{20,16},{24,28},{28,24},{1,5},{5... | collective-permute-start | bytes 8650760 | tf_op jit(solution)/shard_map/ppermute | solution.py:826
  244.6 19.0 %collective-permute-start.13 = (bf16[2,352,512]{2,1,0:T(8,128)(2,1)S(1)}, bf16[2,352,512]{2,1,0:T(8,128)(2,1)S(1)}, u32[]{:S(2)}, u32[]{:S(2)}) collective-permute-start(bf16[2,352,512]{2,1,0:T(8,128)(2,1)S(1)} %dynamic-slice_bitcast_fusion.5), channel_id=1, source_target_pairs={{0,1},{1,0},{2,3},{3,2},{4,5},{5,4},{6,7},{7,6},{8,9},{9,8},{10,11... | collective-permute-start | bytes 2162696 | tf_op jit(solution)/shard_map/ppermute | solution.py:894
  246.1 19.3 %collective-permute-start.15 = (bf16[2,352,512]{2,1,0:T(8,128)(2,1)S(1)}, bf16[2,352,512]{2,1,0:T(8,128)(2,1)S(1)}, u32[]{:S(2)}, u32[]{:S(2)}) collective-permute-start(bf16[2,352,512]{2,1,0:T(8,128)(2,1)S(1)} %dynamic-slice_bitcast_fusion.4), channel_id=1, source_target_pairs={{0,2},{1,3},{2,0},{3,1},{4,6},{5,7},{6,4},{7,5},{8,10},{9,11},{10,... | collective-permute-start | bytes 2162696 | tf_op jit(solution)/shard_map/ppermute | solution.py:894
  248.0 31.1 %collective-permute-start.18 = (bf16[2,352,512]{2,1,0:T(8,128)(2,1)S(1)}, bf16[2,352,512]{2,1,0:T(8,128)(2,1)S(1)}, u32[]{:S(2)}, u32[]{:S(2)}) collective-permute-start(bf16[2,352,512]{2,1,0:T(8,128)(2,1)S(1)} %dynamic-slice_bitcast_fusion.3), channel_id=1, source_target_pairs={{0,1},{1,0},{2,3},{3,2},{4,5},{5,4},{6,7},{7,6},{8,9},{9,8},{10,11... | collective-permute-start | bytes 2162696 | tf_op jit(solution)/shard_map/ppermute | solution.py:894
  249.6 31.3 %collective-permute-start.20 = (bf16[2,352,512]{2,1,0:T(8,128)(2,1)S(1)}, bf16[2,352,512]{2,1,0:T(8,128)(2,1)S(1)}, u32[]{:S(2)}, u32[]{:S(2)}) collective-permute-start(bf16[2,352,512]{2,1,0:T(8,128)(2,1)S(1)} %dynamic-slice_bitcast_fusion.2), channel_id=1, source_target_pairs={{0,2},{1,3},{2,0},{3,1},{4,6},{5,7},{6,4},{7,5},{8,10},{9,11},{10,... | collective-permute-start | bytes 2162696 | tf_op jit(solution)/shard_map/ppermute | solution.py:894
  263.8 24.5 %collective-permute-start.14 = (bf16[352,512]{1,0:T(8,128)(2,1)S(1)}, bf16[352,512]{1,0:T(8,128)(2,1)S(1)}, u32[]{:S(2)}, u32[]{:S(2)}) collective-permute-start(bf16[352,512]{1,0:T(8,128)(2,1)S(1)} %dynamic-slice_bitcast_fusion.12), channel_id=1, source_target_pairs={{0,2},{1,3},{2,0},{3,1},{4,6},{5,7},{6,4},{7,5},{8,10},{9,11},{10,... | collective-permute-start | bytes 1081352 | tf_op jit(solution)/shard_map/ppermute | solution.py:894
  265.6 22.8 %collective-permute-start.16 = (bf16[352,512]{1,0:T(8,128)(2,1)S(1)}, bf16[352,512]{1,0:T(8,128)(2,1)S(1)}, u32[]{:S(2)}, u32[]{:S(2)}) collective-permute-start(bf16[352,512]{1,0:T(8,128)(2,1)S(1)} %dynamic-slice_bitcast_fusion.11), channel_id=1, source_target_pairs={{0,1},{1,0},{2,3},{3,2},{4,5},{5,4},{6,7},{7,6},{8,9},{9,8},{10,11... | collective-permute-start | bytes 1081352 | tf_op jit(solution)/shard_map/ppermute | solution.py:894
  279.3 15.8 %collective-permute-start.19 = (bf16[352,512]{1,0:T(8,128)(2,1)S(1)}, bf16[352,512]{1,0:T(8,128)(2,1)S(1)}, u32[]{:S(2)}, u32[]{:S(2)}) collective-permute-start(bf16[352,512]{1,0:T(8,128)(2,1)S(1)} %dynamic-slice_bitcast_fusion.10), channel_id=1, source_target_pairs={{0,2},{1,3},{2,0},{3,1},{4,6},{5,7},{6,4},{7,5},{8,10},{9,11},{10,... | collective-permute-start | bytes 1081352 | tf_op jit(solution)/shard_map/ppermute | solution.py:894
  281.1 14.1 %collective-permute-start.21 = (bf16[352,512]{1,0:T(8,128)(2,1)S(1)}, bf16[352,512]{1,0:T(8,128)(2,1)S(1)}, u32[]{:S(2)}, u32[]{:S(2)}) collective-permute-start(bf16[352,512]{1,0:T(8,128)(2,1)S(1)} %dynamic-slice_bitcast_fusion.9), channel_id=1, source_target_pairs={{0,1},{1,0},{2,3},{3,2},{4,5},{5,4},{6,7},{7,6},{8,9},{9,8},{10,11... | collective-permute-start | bytes 1081352 | tf_op jit(solution)/shard_map/ppermute | solution.py:894
  295.6 13.3 %collective-permute-start.22 = (bf16[352,512]{1,0:T(8,128)(2,1)S(1)}, bf16[352,512]{1,0:T(8,128)(2,1)S(1)}, u32[]{:S(2)}, u32[]{:S(2)}) collective-permute-start(bf16[352,512]{1,0:T(8,128)(2,1)S(1)} %get-tuple-element.106), channel_id=1, source_target_pairs={{0,8},{4,12},{8,16},{12,20},{16,24},{20,28},{24,0},{28,4},{1,9},{5... | collective-permute-start | bytes 1081352 | tf_op jit(solution)/shard_map/ppermute | solution.py:822
  296.7 25.8 %collective-permute-start.23 = (bf16[352,512]{1,0:T(8,128)(2,1)S(1)}, bf16[352,512]{1,0:T(8,128)(2,1)S(1)}, u32[]{:S(2)}, u32[]{:S(2)}) collective-permute-start(bf16[352,512]{1,0:T(8,128)(2,1)S(1)} %get-tuple-element.108), channel_id=1, source_target_pairs={{0,16},{4,20},{8,24},{12,28},{16,0},{20,4},{24,8},{28,12},{1,17},{... | collective-permute-start | bytes 1081352 | tf_op jit(solution)/shard_map/ppermute | solution.py:822
  297.8 24.7 %collective-permute-start.24 = (bf16[352,512]{1,0:T(8,128)(2,1)S(1)}, bf16[352,512]{1,0:T(8,128)(2,1)}, u32[]{:S(2)}, u32[]{:S(2)}) collective-permute-start(bf16[352,512]{1,0:T(8,128)(2,1)S(1)} %get-tuple-element.107), channel_id=1, source_target_pairs={{0,24},{4,28},{8,0},{12,4},{16,8},{20,12},{24,16},{28,20},{1,25},{... | collective-permute-start | bytes 1081352 | tf_op jit(solution)/shard_map/ppermute | solution.py:822
  323.6 143.1 %collective-permute-start.25 = (f32[32,512]{1,0:T(8,128)S(1)}, f32[32,512]{1,0:T(8,128)S(1)}, u32[]{:S(2)}, u32[]{:S(2)}) collective-permute-start(f32[32,512]{1,0:T(8,128)S(1)} %slice.449), channel_id=1, source_target_pairs={{1,0},{2,1},{3,2},{4,3},{5,4},{6,5},{7,6},{8,7},{9,8},{10,9},{11,1... | collective-permute-start | bytes 196616 | tf_op jit(solution)/shard_map/ppermute | solution.py:942
  324.9 17.0 %copy-start.15 = (f32[8,512]{1,0:T(8,128)S(1)}, f32[8,512]{1,0:T(8,128)}, u32[]{:S(2)}) copy-start(f32[8,512]{1,0:T(8,128)} %get-tuple-element.65) | copy-start | bytes 49156
  325.0 141.9 %copy-start.2 = (f32[353,512]{1,0:T(8,128)S(1)}, f32[353,512]{1,0:T(8,128)}, u32[]{:S(2)}) copy-start(f32[353,512]{1,0:T(8,128)} %param.34) | copy-start | bytes 2168836
  342.8 249.0 %all-gather.7.cloned.1.call-start = ((), (), s32[]{:S(2)}) async-start(), calls=%async_computation.2 | async-start | bytes 12165120 | tf_op jit(solution)/shard_map/all_gather | solution.py:885
  470.4 3.8 collective-permute-start.30
  472.0 6.4 collective-permute-start.8
  474.5 12.2 %collective-permute-start.31 = (bf16[288,512]{1,0:T(8,128)(2,1)S(1)}, bf16[288,512]{1,0:T(8,128)(2,1)S(1)}, u32[]{:S(2)}, u32[]{:S(2)}) collective-permute-start(bf16[288,512]{1,0:T(8,128)(2,1)S(1)} %get-tuple-element.89), channel_id=1, source_target_pairs={{0,24},{4,28},{8,0},{12,4},{16,8},{20,12},{24,16},{28,20},{1,25},{... | collective-permute-start | bytes 884744 | tf_op jit(solution)/shard_map/ppermute | solution.py:822
  476.7 47.4 %collective-permute-start.32 = (bf16[288,512]{1,0:T(8,128)(2,1)S(1)}, bf16[288,512]{1,0:T(8,128)(2,1)S(1)}, u32[]{:S(2)}, u32[]{:S(2)}) collective-permute-start(bf16[288,512]{1,0:T(8,128)(2,1)S(1)} %get-tuple-element.91), channel_id=1, source_target_pairs={{0,16},{4,20},{8,24},{12,28},{16,0},{20,4},{24,8},{28,12},{1,17},{... | collective-permute-start | bytes 884744 | tf_op jit(solution)/shard_map/ppermute | solution.py:822
  477.5 46.6 %collective-permute-start.33 = (bf16[288,512]{1,0:T(8,128)(2,1)S(1)}, bf16[288,512]{1,0:T(8,128)(2,1)S(1)}, u32[]{:S(2)}, u32[]{:S(2)}) collective-permute-start(bf16[288,512]{1,0:T(8,128)(2,1)S(1)} %get-tuple-element.90), channel_id=1, source_target_pairs={{0,8},{4,12},{8,16},{12,20},{16,24},{20,28},{24,0},{28,4},{1,9},{5... | collective-permute-start | bytes 884744 | tf_op jit(solution)/shard_map/ppermute | solution.py:822
  478.8 45.6 %collective-permute-start.9 = (bf16[288,512]{1,0:T(8,128)(2,1)S(1)}, bf16[288,512]{1,0:T(8,128)(2,1)S(1)}, u32[]{:S(2)}, u32[]{:S(2)}) collective-permute-start(bf16[288,512]{1,0:T(8,128)(2,1)S(1)} %get-tuple-element.101), channel_id=1, source_target_pairs={{0,24},{4,28},{8,0},{12,4},{16,8},{20,12},{24,16},{28,20},{1,25},{... | collective-permute-start | bytes 884744 | tf_op jit(solution)/shard_map/ppermute | solution.py:822
  481.8 70.8 %collective-permute-start.10 = (bf16[288,512]{1,0:T(8,128)(2,1)S(1)}, bf16[288,512]{1,0:T(8,128)(2,1)S(1)}, u32[]{:S(2)}, u32[]{:S(2)}) collective-permute-start(bf16[288,512]{1,0:T(8,128)(2,1)S(1)} %get-tuple-element.103), channel_id=1, source_target_pairs={{0,16},{4,20},{8,24},{12,28},{16,0},{20,4},{24,8},{28,12},{1,17},{... | collective-permute-start | bytes 884744 | tf_op jit(solution)/shard_map/ppermute | solution.py:822
  486.7 65.8 %collective-permute-start.11 = (bf16[288,512]{1,0:T(8,128)(2,1)S(1)}, bf16[288,512]{1,0:T(8,128)(2,1)S(1)}, u32[]{:S(2)}, u32[]{:S(2)}) collective-permute-start(bf16[288,512]{1,0:T(8,128)(2,1)S(1)} %get-tuple-element.102), channel_id=1, source_target_pairs={{0,8},{4,12},{8,16},{12,20},{16,24},{20,28},{24,0},{28,4},{1,9},{5... | collective-permute-start | bytes 884744 | tf_op jit(solution)/shard_map/ppermute | solution.py:822
  553.4 48.3 %copy-start.13 = (bf16[6,4,24,512]{3,2,1,0:T(8,128)(2,1)}, bf16[6,4,24,512]{3,2,1,0:T(8,128)(2,1)S(1)}, u32[]{:S(2)}) copy-start(bf16[6,4,24,512]{3,2,1,0:T(8,128)(2,1)S(1)} %constant_dynamic-update-slice_fusion.12) | copy-start | bytes 1769476
  635.4 2.6 collective-permute-start.26
  638.3 9.4 %collective-permute-start.27 = (bf16[288,512]{1,0:T(8,128)(2,1)S(1)}, bf16[288,512]{1,0:T(8,128)(2,1)S(1)}, u32[]{:S(2)}, u32[]{:S(2)}) collective-permute-start(bf16[288,512]{1,0:T(8,128)(2,1)S(1)} %get-tuple-element.95), channel_id=1, source_target_pairs={{0,24},{4,28},{8,0},{12,4},{16,8},{20,12},{24,16},{28,20},{1,25},{... | collective-permute-start | bytes 884744 | tf_op jit(solution)/shard_map/ppermute | solution.py:822
  640.0 27.0 %collective-permute-start.28 = (bf16[288,512]{1,0:T(8,128)(2,1)S(1)}, bf16[288,512]{1,0:T(8,128)(2,1)S(1)}, u32[]{:S(2)}, u32[]{:S(2)}) collective-permute-start(bf16[288,512]{1,0:T(8,128)(2,1)S(1)} %get-tuple-element.97), channel_id=1, source_target_pairs={{0,16},{4,20},{8,24},{12,28},{16,0},{20,4},{24,8},{28,12},{1,17},{... | collective-permute-start | bytes 884744 | tf_op jit(solution)/shard_map/ppermute | solution.py:822
  640.8 26.1 %collective-permute-start.29 = (bf16[288,512]{1,0:T(8,128)(2,1)S(1)}, bf16[288,512]{1,0:T(8,128)(2,1)S(1)}, u32[]{:S(2)}, u32[]{:S(2)}) collective-permute-start(bf16[288,512]{1,0:T(8,128)(2,1)S(1)} %get-tuple-element.96), channel_id=1, source_target_pairs={{0,8},{4,12},{8,16},{12,20},{16,24},{20,28},{24,0},{28,4},{1,9},{5... | collective-permute-start | bytes 884744 | tf_op jit(solution)/shard_map/ppermute | solution.py:822
  (23 other events, 105.0 us)
Sparse Core Ops, SparseCore 0:
  11.5 120.2 all-gather.4
  342.9 123.8 all-reduce.8
  470.5 121.2 all-gather.6

commit v2 on v1

--- a/solution.py
+++ b/solution.py
@@ -133,6 +133,7 @@
             jnp.where(is_l == 1, 32, 24 * has_m),
             jnp.where(is_l == 1, 32, 32 * has_s),
             jnp.where(is_l == 1, 0, 16),
+            core,
         ]
     ).astype(jnp.int32)
     return gather, scatter, flags
@@ -143,6 +144,7 @@
         self.is_l = flags[0]
         self.lims = (flags[1], flags[2])
         self.split = flags[3]
+        self.core = flags[4]
         self.l_f = flags[0].astype(F32)
         large = flags[0] == 1
         self.inv = (
@@ -282,11 +284,12 @@
     lax.fori_loop(0, count, step, 0, unroll=4)
 
 
-def slots_to_image(table_ref, own_ref, got_ref, slots_ref, image_ref):
-    half = own_ref.shape[0]
-    slots_ref[0:half, :] = own_ref[...].astype(F32)
-    slots_ref[half : 2 * half, :] = got_ref[...].astype(F32)
-    slots_ref[2 * half : 2 * half + 8, :] = jnp.zeros((8, C), F32)
+def slots_to_image(table_ref, scal, blocks, slots_ref, image_ref):
+    piece = (slots_ref.shape[0] - 8) // len(blocks)
+    start = pl.multiple_of((blocks[0].shape[0] - piece) * scal.core, 16)
+    for i, block in enumerate(blocks):
+        slots_ref[i * piece : (i + 1) * piece, :] = block[pl.ds(start, piece), :].astype(F32)
+    slots_ref[len(blocks) * piece :, :] = jnp.zeros((8, C), F32)
     gather_pieces(table_ref, slots_ref, image_ref, 128)
 
 
@@ -302,33 +305,71 @@
     return sigma * (1.0 + value * (1.0 - sigma))
 
 
-def features_kernel(
-    first,
-    gather,
-    flags,
-    own,
-    got,
-    small,
-    weights,
-    *refs,
-):
+def load_weights(pieces, parts, table, w, small16, sems):
+    copies, last = [], len(parts) * len(pieces)
+    if len(pieces) == 1:
+        copies.append(pltpu.make_async_copy(pieces[0].at[pl.ds(0, 22 * C)], w, sems.at[0]))
+        copy = pltpu.make_async_copy(pieces[0].at[pl.ds(22 * C, 16)], small16, sems.at[1])
+        copies[0].start()
+        copy.start()
+        copy.wait()
+    else:
+        for i, piece in enumerate(pieces):
+            for start, count in parts:
+                e = len(copies)
+                at = pl.multiple_of(table[e] * 16, 16)
+                copy = pltpu.make_async_copy(
+                    piece.at[pl.ds(start, count)], w.at[pl.ds(at, count)], sems.at[e]
+                )
+                copy.start()
+                copies.append(copy)
+
+            @pl.when(table[last] == i)
+            def _():
+                copy = pltpu.make_async_copy(
+                    piece.at[pl.ds(parts[-1][0] + parts[-1][1], 16)], small16, sems.at[last]
+                )
+                copy.start()
+                copy.wait()
+
+    def wait():
+        for copy in copies:
+            copy.wait()
+
+    return wait
+
+
+def features_kernel(first, sources, count, parts, *refs):
     if first:
-        x_out, a1_out, h1_out, a2_out, y_out, z_out, q_out, k_out, v_out, stats_out = refs[:10]
-        scratch = refs[10:]
+        gather, flags, table = refs[:3]
+        blocks, refs = refs[3 : 3 + sources], refs[3 + sources :]
+        pieces, refs = refs[:count], refs[count:]
+        (
+            x_out,
+            a1_out,
+            h1_out,
+            a2_out,
+            y_ref,
+            z_out,
+            q_ref,
+            k_ref,
+            v_ref,
+            stats_out,
+            small,
+            w_out,
+        ) = refs[:12]
+        slots, x_ref, h_ref, z_ref, buf, w, gm, sems, small16 = refs[12:]
     else:
-        y_out, q_out, k_out, v_out = refs[:4]
-        scratch = refs[4:]
-    slots, x_ref, h_ref, z_ref, buf, w1, w2, wp, gm, sems = scratch
-    copies = [
-        pltpu.make_async_copy(weights.at[pl.ds(0, 9 * C)], w1, sems.at[0]),
-        pltpu.make_async_copy(weights.at[pl.ds(9 * C, 9 * C)], w2, sems.at[1]),
-        pltpu.make_async_copy(weights.at[pl.ds(18 * C, 3 * C)], wp, sems.at[2]),
-    ]
-    for copy in copies:
-        copy.start()
+        gather, scatter, flags, table = refs[:4]
+        blocks, refs = refs[4 : 4 + sources], refs[4 + sources :]
+        pieces, refs = refs[:count], refs[count:]
+        own_out, oth_out = refs[:2]
+        slots, x_ref, h_ref, z_ref, buf, w, gm, sems, small16, small, y_ref, q_ref, k_ref, v_ref = refs[2:]
+    wait_weights = load_weights(pieces, parts, table, w, small16, sems)
     scal = Scalars(flags)
     fill_group_matrix(gm)
-    slots_to_image(gather, own, got, slots, x_ref)
+    slots_to_image(gather, scal, blocks, slots, x_ref)
+    small[...] = small16[...].astype(F32)
     col = columns()
 
     def row(i):
@@ -359,12 +400,15 @@
 
         line_loop(keep_x, (0, 0))
 
-    copies[0].wait()
+    wait_weights()
+    if first:
+        save = pltpu.make_async_copy(w, w_out, sems.at[0])
+        save.start()
 
     def write_h(tile, acc):
         h_ref[tile * 256 : (tile + 1) * 256, :] = acc
 
-    conv_tiles(buf, w1, write_h)
+    conv_tiles(buf, w.at[0 : 9 * C], write_h)
 
     def finish_h(seg, line, carry):
         value = jnp.where(col < scal.lims[seg], h_ref[line_rows(line), :] + row(2), 0.0)
@@ -380,20 +424,19 @@
 
     means2, rstds2 = norm_stats(read_h, gm, scal)
     activate(read_h, means2, rstds2, row(3), row(4), a2_out if first else None)
-    copies[1].wait()
-    conv_tiles(buf, w2, write_h)
+    conv_tiles(buf, w.at[9 * C : 18 * C], write_h)
 
     def finish_y(seg, line, carry):
         value = jnp.where(
             col < scal.lims[seg], read_x(line) + (h_ref[line_rows(line), :] + row(5)), 0.0
         )
-        y_out[line_rows(line), :] = value
+        y_ref[line_rows(line), :] = value
         return carry
 
     line_loop(finish_y, (0, 0))
 
     def read_y(line):
-        return y_out[line_rows(line), :]
+        return y_ref[line_rows(line), :]
 
     means3, rstds3 = norm_stats(read_y, gm, scal)
 
@@ -406,17 +449,27 @@
         return carry
 
     line_loop(third, (0, 0))
-    copies[2].wait()
     for tile in range(4):
         at = slice(tile * 256, (tile + 1) * 256)
         rows = z_ref[at, :]
-        q_out[at, :] = (dot(rows, wp[0:C, :]) + row(8)).astype(BF16)
-        k_out[at, :] = dot(rows, wp[C : 2 * C, :]).astype(BF16)
-        v_out[at, :] = (dot(rows, wp[2 * C : 3 * C, :]) + row(9)).astype(BF16)
+        q_ref[at, :] = (dot(rows, w[18 * C : 19 * C, :]) + row(8)).astype(BF16)
+        k_ref[at, :] = dot(rows, w[19 * C : 20 * C, :]).astype(BF16)
+        v_ref[at, :] = (dot(rows, w[20 * C : 21 * C, :]) + row(9)).astype(BF16)
     if first:
         for i, pair in enumerate((means1, rstds1, means2, rstds2, means3, rstds3)):
             stats_out[2 * i : 2 * i + 1, :] = pair[0]
             stats_out[2 * i + 1 : 2 * i + 2, :] = pair[1]
+        stats_out[12:16, :] = jnp.zeros((4, C), F32)
+        save.wait()
+        return
+    biases = key_bias(scal)
+    for tile in range(4):
+        at = slice(tile * 256, (tile + 1) * 256)
+        prob = probabilities(q_ref[at, :], k_ref, biases[tile // 3]).astype(BF16)
+        mixed = dot(prob, v_ref[...]).astype(BF16)
+        y_ref[at, :] = y_ref[at, :] + (dot(mixed, w[21 * C : 22 * C, :]) + row(10))
+    y_ref[PIX : PIX + 8, :] = jnp.zeros((8, C), F32)
+    image_to_slots(scatter, y_ref, slots, own_out, oth_out)
 
 
 def key_bias(scal):
@@ -438,21 +491,6 @@
     return expo * (1.0 / jnp.sum(expo, axis=1, keepdims=True))
 
 
-def attend_kernel(scatter, flags, q, k, v, y, small, weights, own_out, oth_out, image, slots, wo, sems):
-    copy = pltpu.make_async_copy(weights.at[pl.ds(21 * C, C)], wo, sems.at[0])
-    copy.start()
-    scal = Scalars(flags)
-    biases = key_bias(scal)
-    copy.wait()
-    for tile in range(4):
-        at = slice(tile * 256, (tile + 1) * 256)
-        prob = probabilities(q[at, :], k, biases[tile // 3]).astype(BF16)
-        mixed = dot(prob, v[...]).astype(BF16)
-        image[at, :] = y[at, :] + (dot(mixed, wo[...]) + small[10:11, :])
-    image[PIX : PIX + 8, :] = jnp.zeros((8, C), F32)
-    image_to_slots(scatter, image, slots, own_out, oth_out)
-
-
 def attend_both_kernel(
     gather,
     scatter,
@@ -462,34 +500,20 @@
     v,
     y,
     z,
-    cot_own,
-    cot_got,
     stats,
     small,
     weights,
-    own_out,
-    oth_out,
-    dy_out,
-    dy16_out,
-    grads_out,
-    sums_out,
-    image,
-    slots,
-    g_ref,
-    o_ref,
-    d_ref,
-    dk_acc,
-    dv_acc,
-    wp,
-    gm,
-    sems,
+    *refs,
 ):
+    blocks = refs[:-16]
+    own_out, oth_out, dy_out, dy16_out, grads_out, sums_out = refs[-16:-10]
+    image, slots, g_ref, o_ref, d_ref, dk_acc, dv_acc, wp, gm, sems = refs[-10:]
     copy = pltpu.make_async_copy(weights.at[pl.ds(18 * C, 4 * C)], wp, sems.at[0])
     copy.start()
     scal = Scalars(flags)
     fill_group_matrix(gm)
     biases = key_bias(scal)
-    slots_to_image(gather, cot_own, cot_got, slots, g_ref)
+    slots_to_image(gather, scal, blocks, slots, g_ref)
     copy.wait()
     scaling = C**-0.5
     for tile in range(4):
@@ -578,8 +602,40 @@
     fill_halos(buf, scal)
 
 
-def weight_grad_kernel(flags, act, grad, w_out, sums_out, buf, act_t):
+def weight_grad_kernel(conv, split, *refs):
+    if not split:
+        flags, act, grad, w_out, sums_out, buf, act_t = refs
+    elif conv == 1:
+        flags, act, grad, proj, kept, sent, early, sums_out, buf, act_t = refs
+    else:
+        flags, act, grad, early, kept, sent, sums_out, buf, act_t = refs
     scal = Scalars(flags)
+
+    def put(unit, value16):
+        if split and conv == 1 and unit < 44:
+            early[(unit - 36) * 128 : (unit - 35) * 128, :] = value16
+            return
+        if not split:
+            unit -= 36 * conv
+            w_out[unit * 128 : (unit + 1) * 128, :] = value16
+            return
+        row = (unit // 22 % 2) * 1408 + unit % 11 * 128
+        mine = scal.core == unit % 22 // 11
+
+        @pl.when(mine)
+        def _():
+            kept[row : row + 128, :] = value16
+
+        @pl.when(jnp.logical_not(mine))
+        def _():
+            sent[row : row + 128, :] = value16
+
+    if split and conv == 1:
+        for i in range(16):
+            put(72 + i, proj[i * 128 : (i + 1) * 128, :])
+    elif split:
+        for i in range(8):
+            put(36 + i, early[i * 128 : (i + 1) * 128, :])
     fill_gradient_buffer(buf, scal, grad)
     for tile in range(4):
         at = slice(tile * 256, (tile + 1) * 256)
@@ -589,9 +645,11 @@
         seg1 = slice((26 + shift) * 32, (26 + shift) * 32 + 256)
         for part in range(3):
             cols = slice(part * C, (part + 1) * C)
+            tap = 3 * (2 - shift) + (2 - part)
             value = dot(act_t[:, 0:768], buf[seg0, cols]) + dot(act_t[:, 768:1024], buf[seg1, cols])
-            tap = 3 * (2 - shift) + (2 - part)
-            w_out[tap * C : (tap + 1) * C, :] = value.astype(BF16)
+            value16 = value.astype(BF16)
+            for i in range(4):
+                put(36 * conv + 4 * tap + i, value16[i * 128 : (i + 1) * 128])
     zero = jnp.zeros((8, C), F32)
     got = line_loop(
         lambda seg, line, acc: acc + fold(grad[line_rows(line), :].astype(F32)), (zero, zero)
@@ -671,7 +729,7 @@
 ANY = pl.BlockSpec(memory_space=pl.ANY)
 
 
-def call(kernel, name, in_specs, outs, scratch, flops, args):
+def call(kernel, name, in_specs, outs, scratch, flops, args, out_specs=None):
     moved = sum(int(np.prod(a.shape)) * a.dtype.itemsize for a in args)
     moved += sum(int(np.prod(s)) * jnp.dtype(d).itemsize for s, d in outs)
     return pl.pallas_call(
@@ -679,7 +737,7 @@
         name=name,
         out_shape=[jax.ShapeDtypeStruct(s, d) for s, d in outs],
         in_specs=in_specs,
-        out_specs=[VMEM] * len(outs),
+        out_specs=out_specs or [VMEM] * len(outs),
         scratch_shapes=scratch,
         compiler_params=pltpu.CompilerParams(vmem_limit_bytes=VMEM_BYTES),
         cost_estimate=pl.CostEstimate(flops=int(flops), bytes_accessed=moved, transcendentals=0),
@@ -687,16 +745,25 @@
 
 
 MAP, SLOT_PAD = (PIX, C), 8
-CONV_FLOPS = 2 * PIX * 9 * C * C
-PROJ_FLOPS = 2 * PIX * C * C
-PAIR_FLOPS = 2 * PIX * PIX * C
+MICROSECOND = 1_100_000_000
 BUF = pltpu.VMEM((BUF_LINES * 32, 3 * C), BF16)
 
 
-def run_features(first, tables, slots_in, small, weights):
-    gather, _, flags = tables
-    rows = 2 * slots_in[0].shape[0] + SLOT_PAD
-    outs = [(MAP, F32), (MAP, BF16), (MAP, BF16), (MAP, BF16)]
+def run_features(first, plan, tables, blocks, pieces, parts, table):
+    gather, scatter, flags = tables
+    slot_rows = plan.n_band * plan.piece
+    scratch = [
+        pltpu.VMEM((slot_rows + SLOT_PAD, C), F32),
+        pltpu.VMEM(MAP, F32),
+        pltpu.VMEM(MAP, F32),
+        pltpu.VMEM(MAP, BF16),
+        BUF,
+        pltpu.VMEM((22 * C, C), BF16),
+        pltpu.VMEM((C, C), BF16),
+        pltpu.SemaphoreType.DMA((len(parts) * len(pieces) + 1,)),
+        pltpu.VMEM((16, C), BF16),
+    ]
+    count = len(pieces)
     if first:
         outs = [
             (MAP, BF16),
@@ -709,57 +776,47 @@
             (MAP, BF16),
             (MAP, BF16),
             ((16, C), F32),
+            ((16, C), F32),
+            ((22 * C, C), BF16),
         ]
+        return call(
+            functools.partial(features_kernel, True, len(blocks), count, parts),
+            "features_first",
+            [SMEM] * 3 + [VMEM] * len(blocks) + [ANY] * count,
+            outs,
+            scratch,
+            26 * MICROSECOND,
+            (gather, flags, table, *blocks, *pieces),
+            out_specs=[VMEM] * 11 + [ANY],
+        )
     return call(
-        functools.partial(features_kernel, first),
-        "features_first" if first else "features_again",
-        [SMEM, SMEM, VMEM, VMEM, VMEM, ANY],
-        outs,
-        [
-            pltpu.VMEM((rows, C), F32),
-            pltpu.VMEM(MAP, F32),
-            pltpu.VMEM(MAP, F32),
+        functools.partial(features_kernel, False, len(blocks), count, parts),
+        "forward_again",
+        [SMEM] * 4 + [VMEM] * len(blocks) + [ANY] * count,
+        [((slot_rows // 2, C), BF16)] * 2,
+        scratch
+        + [
+            pltpu.VMEM((16, C), F32),
+            pltpu.VMEM((PIX + 8, C), F32),
             pltpu.VMEM(MAP, BF16),
-            BUF,
-            pltpu.VMEM((9 * C, C), BF16),
-            pltpu.VMEM((9 * C, C), BF16),
-            pltpu.VMEM((3 * C, C), BF16),
-            pltpu.VMEM((C, C), BF16),
-            pltpu.SemaphoreType.DMA((3,)),
+            pltpu.VMEM(MAP, BF16),
+            pltpu.VMEM(MAP, BF16),
         ],
-        2 * CONV_FLOPS + 3 * PROJ_FLOPS,
-        (gather, flags, slots_in[0], slots_in[1], small, weights),
+        28 * MICROSECOND,
+        (gather, scatter, flags, table, *blocks, *pieces),
     )
 
 
-def run_attend(tables, q, k, v, y, small, weights, half):
-    _, scatter, flags = tables
-    return call(
-        attend_kernel,
-        "attend_again",
-        [SMEM, SMEM, VMEM, VMEM, VMEM, VMEM, VMEM, ANY],
-        [((half, C), BF16)] * 2,
-        [
-            pltpu.VMEM((PIX + 8, C), F32),
-            pltpu.VMEM((2 * half, C), F32),
-            pltpu.VMEM((C, C), BF16),
-            pltpu.SemaphoreType.DMA((1,)),
-        ],
-        2 * PAIR_FLOPS + PROJ_FLOPS,
-        (scatter, flags, q, k, v, y, small, weights),
-    )
-
-
-def run_attend_both(tables, q, k, v, y, z, cot, stats, small, weights):
+def run_attend_both(plan, tables, q, k, v, y, z, blocks, stats, small, weights):
     gather, scatter, flags = tables
-    half = cot[0].shape[0]
+    slot_rows = plan.n_band * plan.piece
     return call(
         attend_both_kernel,
         "attend_both",
-        [SMEM, SMEM, SMEM] + [VMEM] * 9 + [ANY],
+        [SMEM] * 3 + [VMEM] * 7 + [ANY] + [VMEM] * len(blocks),
         [
-            ((half, C), BF16),
-            ((half, C), BF16),
+            ((slot_rows // 2, C), BF16),
+            ((slot_rows // 2, C), BF16),
             (MAP, F32),
             (MAP, BF16),
             ((4 * C, C), BF16),
@@ -767,7 +824,7 @@
         ],
         [
             pltpu.VMEM((PIX + 8, C), F32),
-            pltpu.VMEM((2 * half + SLOT_PAD, C), F32),
+            pltpu.VMEM((slot_rows + SLOT_PAD, C), F32),
             pltpu.VMEM(MAP, F32),
             pltpu.VMEM(MAP, BF16),
             pltpu.VMEM((PIX, 3 * C), BF16),
@@ -777,20 +834,24 @@
             pltpu.VMEM((C, C), BF16),
             pltpu.SemaphoreType.DMA((1,)),
         ],
-        7 * PAIR_FLOPS + 9 * PROJ_FLOPS,
-        (gather, scatter, flags, q, k, v, y, z, cot[0], cot[1], stats, small, weights),
+        24 * MICROSECOND,
+        (gather, scatter, flags, q, k, v, y, z, stats, small, weights, *blocks),
     )
 
 
-def run_weight_grad(tables, act, grad, name):
+def run_weight_grad(tables, conv, act, grad, more=None):
+    split = more is not None
+    outs = [((2816, C), BF16)] * 2 if split else [((9 * C, C), BF16)]
+    if split and conv == 1:
+        outs.append(((2 * C, C), BF16))
     return call(
-        weight_grad_kernel,
-        name,
-        [SMEM, VMEM, VMEM],
-        [((9 * C, C), BF16), ((8, C), F32)],
+        functools.partial(weight_grad_kernel, conv, split),
+        "weight_grad_one" if conv == 0 else "weight_grad_two",
+        [SMEM, VMEM, VMEM] + [VMEM] * split,
+        outs + [((8, C), F32)],
         [BUF, pltpu.VMEM((C, PIX), BF16)],
-        CONV_FLOPS,
-        (tables[2], act, grad),
+        12 * MICROSECOND,
+        (tables[2], act, grad) + ((more,) if split else ()),
     )
 
 
@@ -813,7 +874,7 @@
         specs,
         outs + [((8, C), F32)],
         scratch,
-        CONV_FLOPS,
+        12 * MICROSECOND,
         args,
     )
 
@@ -826,8 +887,11 @@
     return lax.ppermute(value, "band", [(b, b ^ 1) for b in range(n_band)])
 
 
-def to_holders(plan, position, arrays):
-    z, core = position // 2, position % 2
+def stage(values):
+    return lax.optimization_barrier(values)
+
+
+def pack_slots(plan, arrays):
     flat = [a.reshape(a.shape[0], -1, C) for a in arrays]
     blocks = []
     for chip in range(plan.n_chip):
@@ -841,28 +905,36 @@
                     parts.append(jnp.zeros((plan.block - used, C), BF16))
             parts += mine
         blocks.append(jnp.concatenate(parts, axis=0))
-    sent = jnp.stack(blocks)
-    nz = plan.n_chip
-    received = []
-    for k in range(nz):
-        block = lax.dynamic_index_in_dim(sent, (z + k) % nz, 0, keepdims=False)
-        received.append(block if k == 0 else z_shift(block, nz, k))
-    received = jnp.stack(received)
-    slack = plan.block - plan.piece
-    own = lax.dynamic_slice_in_dim(received, slack * core, plan.piece, 1)
-    other = lax.dynamic_slice_in_dim(received, slack * (1 - core), plan.piece, 1)
-    got = core_swap(other, plan.n_band)
-    return own.reshape(-1, C), got.reshape(-1, C)
-
-
-def from_holders(plan, position, own, other):
-    z, core = position // 2, position % 2
-    nz, slack = plan.n_chip, plan.block - plan.piece
-    got = core_swap(other, plan.n_band).reshape(nz, plan.piece, C)
-    own = own.reshape(nz, plan.piece, C)
+    return jnp.stack(blocks)
+
+
+def chip_blocks(plan, position, arrays):
+    z, nz = position // 2, plan.n_chip
+    sent = pack_slots(plan, arrays)
+    return [lax.dynamic_index_in_dim(sent, (z + k) % nz, 0, keepdims=False) for k in range(nz)]
+
+
+def to_chips(plan, blocks):
+    return [blocks[0]] + [z_shift(blocks[k], plan.n_chip, k) for k in range(1, plan.n_chip)]
+
+
+def to_cores(plan, received):
+    return [*received, *[core_swap(block, plan.n_band) for block in received]]
+
+
+def merge_cores(plan, position, own, got):
+    core, nz, slack = position % 2, plan.n_chip, plan.block - plan.piece
+    own, got = own.reshape(nz, plan.piece, C), got.reshape(nz, plan.piece, C)
     first, second = jnp.where(core == 0, own, got), jnp.where(core == 0, got, own)
-    blocks = jnp.pad(first, ((0, 0), (0, slack), (0, 0))) + jnp.pad(second, ((0, 0), (slack, 0), (0, 0)))
-    received = [blocks[0]] + [z_shift(blocks[k], nz, -k) for k in range(1, nz)]
+    return jnp.pad(first, ((0, 0), (0, slack), (0, 0))) + jnp.pad(second, ((0, 0), (slack, 0), (0, 0)))
+
+
+def from_chips(plan, blocks):
+    return [blocks[0]] + [z_shift(blocks[k], plan.n_chip, -k) for k in range(1, plan.n_chip)]
+
+
+def to_bands(plan, position, received):
+    z, nz, slack = position // 2, plan.n_chip, plan.block - plan.piece
     received = jnp.stack(received)
     images = [[None] * plan.n_s, [None] * plan.n_m, [None] * plan.n_l]
     for b, h in enumerate(plan.holders):
@@ -881,67 +953,158 @@
     ]
 
 
-def fetch_weights(shard):
-    full = lax.all_gather(shard.astype(BF16), AXES, axis=0, tiled=True)
-    small = full[22 * C : 22 * C + 16].astype(F32)
-    return full, small
-
-
-def swap_axis(value, n_band, which):
-    if which == "core":
-        return core_swap(value, n_band)
-    bit = 1 if which == "x" else 2
-    return lax.ppermute(value, "img", [(i, i ^ bit) for i in range(4)])
-
-
-def reduce_pair(position, img, top, small):
-    core, y, x = position % 2, img // 2, img % 2
-    rows = top.shape[3]
-    kept = lax.dynamic_index_in_dim(top, core, 1, keepdims=False)
-    sent = lax.dynamic_index_in_dim(top, 1 - core, 1, keepdims=False)
-    got = core_swap(sent, lax.axis_size("band"))
-    both = (kept.astype(F32) + got.astype(F32)).astype(BF16).reshape(2, 2, 2, rows, C)
-
-    def halve(value, axis, mine, which):
-        keep = lax.dynamic_index_in_dim(value, mine, axis, keepdims=False)
-        send = lax.dynamic_index_in_dim(value, 1 - mine, axis, keepdims=False)
-        arrived = swap_axis(send, None, which)
-        return (keep.astype(F32) + arrived.astype(F32)).astype(BF16)
-
-    a = halve(both[0], 1, x, "x")
-    b = halve(both[1], 0, y, "y")
-    a = halve(a, 0, y, "y")
-    b = halve(b, 0, x, "x")
-    return a, b
-
-
-def reduce_grads(position, img, high, low):
-    z = position // 2
-    planes = list(reduce_pair(position, img, low, None)) + list(reduce_pair(position, img, high, None))
-    stacked = jnp.stack(planes)
-    total = lax.dynamic_index_in_dim(stacked, z, 0, keepdims=False).astype(F32)
-    for k in range(1, 4):
-        sent = lax.dynamic_index_in_dim(stacked, (z + k) % 4, 0, keepdims=False)
-        total = total + z_shift(sent, 4, k).astype(F32)
+class Place:
+    def __init__(self):
+        self.n_band, self.n_img = lax.axis_size("band"), lax.axis_size("img")
+        self.count = self.n_band * self.n_img
+        self.position, self.img = lax.axis_index("band"), lax.axis_index("img")
+        self.owner = self.position * self.n_img + self.img
+        self.z, self.core = self.position // 2, self.position % 2
+        self.y, self.x = self.img // 2, self.img % 2
+        self.planes = self.n_band == 8 and self.n_img == 4
+
+
+def over_core(value):
+    return core_swap(value, lax.axis_size("band"))
+
+
+def over_x(value):
+    return lax.ppermute(value, "img", [(i, i ^ 1) for i in range(4)])
+
+
+def over_y(value):
+    return lax.ppermute(value, "img", [(i, i ^ 2) for i in range(4)])
+
+
+def along_z(value, pairs):
+    return lax.ppermute(value, "band", [(2 * a + c, 2 * b + c) for a, b in pairs for c in range(2)])
+
+
+def over_corner(value):
+    return lax.ppermute(value, "img", [(i, i ^ 3) for i in range(4)])
+
+
+class Gather:
+    def __init__(self, block):
+        self.block = block
+
+    def beside(self):
+        return [self.block, over_x(self.block), over_y(self.block)]
+
+    def first(self, got=None):
+        block, x0, y0 = got or self.beside()
+        return [block, x0, y0, over_corner(block), z_shift(block, 4, 1), z_shift(block, 4, 3)]
+
+    def second(self, values):
+        block, x0, y0, d0, up, down = values
+        across = z_shift(block, 4, 2)
+        return values + [over_x(up), over_y(up), over_x(down), over_y(down), across]
+
+    def third(self, values):
+        d0, up, down, x1, y1, x3, y3, across = values[3:]
+        return values + [over_x(across), over_y(across), z_shift(d0, 4, 2), over_y(x1), over_x(y3)]
+
+    def others(self, values, count):
+        return [over_core(value) for value in values[:count]]
+
+    def pieces(self, values, others):
+        def ordered(v):
+            block, x0, y0, d0, up, down, x1, y1, x3, y3, across, x2, y2, d2, c1, c3 = v
+            return [block, x0, y0, d0, up, x1, y1, c1, across, x2, y2, d2, down, x3, y3, c3]
+
+        return ordered(values) + ordered(others)
+
+
+GATHERED = [(side, k, flip) for side in range(2) for k in (0, 1, 2, 3) for flip in range(4)]
+
+
+def gather_table(here, block_rows):
+    side, k, flip = np.array(GATHERED, np.int32).T
+    core, z, img = here.core ^ side, (here.z - k) % 4, here.img ^ flip
+    last = (core == 1) & (z == 3) & (img == 3)
+    rows = jnp.stack(block_rows(z, 4 * core + img), axis=1).reshape(-1)
+    return jnp.concatenate([rows, jnp.argmax(last)[None]]).astype(jnp.int32)
+
+
+def part(value, axis, index):
+    return lax.dynamic_index_in_dim(value, index, axis, keepdims=False)
+
+
+def planes_of(rows):
+    return rows.reshape(2, 2, 2, 352, C)
+
+
+def add_part(kept, got, plane, axis, index):
+    both = part(planes_of(kept)[plane], axis, index).astype(F32)
+    return (both + part(planes_of(got)[plane], axis, index).astype(F32)).astype(BF16)
+
+
+def send_halves(here, kept, got):
+    return over_x(add_part(kept, got, 0, 1, 1 - here.x)), over_y(add_part(kept, got, 1, 0, 1 - here.y))
+
+
+def add_halves(here, kept, got, got_a, got_b):
+    a = add_part(kept, got, 0, 1, here.x).astype(F32) + got_a.astype(F32)
+    b = add_part(kept, got, 1, 0, here.y).astype(F32) + got_b.astype(F32)
+    return a.astype(BF16), b.astype(BF16)
+
+
+def quarters_to_send(here, a, b):
+    return part(a, 0, 1 - here.y), part(b, 0, 1 - here.x)
+
+
+def send_quarters(a, b):
+    return over_y(a), over_x(b)
+
+
+def add_quarters(here, a, b, got_a, got_b):
+    return (
+        part(a, 0, here.y).astype(F32) + got_a.astype(F32),
+        part(b, 0, here.x).astype(F32) + got_b.astype(F32),
+    )
+
+
+def by_plane(low_planes, first, second):
+    halves = [first[:176], second[:176], first[176:], second[176:]]
+    return jnp.stack(halves if low_planes else halves[2:] + halves[:2])
+
+
+def send_planes(here, planes, more=None):
+    planes16 = planes.astype(BF16)
+    sent = [part(planes16, 0, (here.z + k) % 4) for k in (1, 3, 2)]
+    if more is not None:
+        sent = [jnp.concatenate([value, more.astype(BF16)], axis=0) for value in sent]
+    return [z_shift(value, 4, k) for value, k in zip(sent, (1, 3, 2))]
+
+
+def add_planes(here, planes, got, more=None):
+    total = part(planes, 0, here.z)
+    if more is not None:
+        total = jnp.concatenate([total, more], axis=0)
+    for value in got:
+        total = total + value.astype(F32)
     return total
 
 
-def shard_of_grads(position, img, w1, w2, proj, small_rows, rows):
-    n_band, n_img = lax.axis_size("band"), lax.axis_size("img")
-    count = n_band * n_img
-    small_rows = jnp.pad(small_rows, ((0, rows * count - 22 * C - small_rows.shape[0]), (0, 0)))
-    if n_band != 8 or n_img != 4:
-        full = jnp.concatenate([w1, w2, proj, small_rows.astype(BF16)], axis=0)
-        return lax.psum_scatter(full, AXES, scatter_dimension=0, tiled=True).astype(F32)
-    block = 22 * C // count
-    high = jnp.concatenate([w2[2 * C :], proj], axis=0).reshape(2, 2, 4, block, C)
-    low = jnp.concatenate([w1, w2[: 2 * C]], axis=0).reshape(2, 2, 4, block, C)
-    mine = reduce_grads(position, img, high, low)
-    small_sum = lax.psum(small_rows, AXES)
-    owner = position * n_img + img
-    after = lax.ppermute(mine[:count], AXES, [(o, o - 1) for o in range(1, count)])
-    after = jnp.where(owner == count - 1, small_sum, after)
-    return lax.dynamic_slice_in_dim(jnp.concatenate([mine, after], axis=0), owner, rows, 0)
+def over_two_planes(value):
+    return along_z(value, [(0, 2), (2, 0), (1, 3), (3, 1)])
+
+
+def sum_over_plane(value):
+    value = value + over_core(value)
+    value = value + over_x(value)
+    return value + over_y(value)
+
+
+def adam(params, first, second, grad, step_count, rate):
+    new_first = 0.5 * first + 0.5 * grad
+    new_second = 0.9 * second + 0.1 * grad * grad
+    update = (
+        rate
+        * (new_first / (1.0 - jnp.power(0.5, step_count)))
+        / (jnp.sqrt(new_second / (1.0 - jnp.power(0.9, step_count))) + ADAM_EPSILON)
+    )
+    return update, new_first, new_second
 
 
 def body(
@@ -958,44 +1121,168 @@
     step,
     rate,
 ):
-    n_band = lax.axis_size("band")
-    position, img = lax.axis_index("band"), lax.axis_index("img")
+    here = Place()
+    n_band, position = here.n_band, here.position
     plan = Plan([x_small.shape, x_medium.shape, x_large.shape], n_band)
     tables = make_tables(plan, band_rows, position)
     half = n_band // 2 * plan.piece
-
-    x_slots = to_holders(plan, position, (x_small, x_medium, x_large))
-    weights, small = fetch_weights(params)
-    cot_slots = to_holders(plan, position, (cot_small, cot_medium, cot_large))
-    x_img, a1, h1, a2, y, z, q, k, v, stats = run_features(True, tables, x_slots, small, weights)
+    rows, count = params.shape[0], here.count
+    step_count, step_rate = step[0].astype(F32), rate[0]
+    last = count - 1
+    singles = 22 * C - last * rows
+
+    images, cots = (x_small, x_medium, x_large), (cot_small, cot_medium, cot_large)
+    if here.planes:
+        shard16 = params.astype(BF16)
+        before = lax.ppermute(shard16[rows - count :], AXES, [(o, o + 1) for o in range(last)])
+
+        def aligned(head, shard, size):
+            both = jnp.concatenate([head, shard], axis=0)
+            return lax.dynamic_slice_in_dim(both, count - here.owner, size, 0)
+
+        gather = Gather(jnp.concatenate([aligned(before, shard16, rows - 1), shard16[singles : singles + 16]], axis=0))
+        x_got = to_chips(plan, chip_blocks(plan, position, images))
+        values, x_got, band_rows, cots = stage((gather.beside(), x_got, band_rows, cots))
+        tables = make_tables(plan, band_rows, position)
+        cot_sent = chip_blocks(plan, position, cots)
+        table = gather_table(here, lambda z, place: [(8 * z + place) * 22])
+        values, x_blocks, cot_sent, tables, table = stage(
+            (gather.first(values), to_cores(plan, x_got), cot_sent, tables, table)
+        )
+        state = (params, first_moment, second_moment)
+        far = [lax.dynamic_slice_in_dim(rows_of, 176 - here.owner, 176, 0).astype(BF16) for rows_of in state]
+        values, far = stage((gather.second(values), jnp.concatenate(far, axis=1)))
+        values, others = stage((gather.third(values), gather.others(values, 4)))
+        cot_sent, values = stage((cot_sent, values))
+        cot_got = to_chips(plan, cot_sent)
+        pieces, parts = gather.pieces(values, others + gather.others(values[4:], 12)), ((0, rows - 1),)
+        pieces, x_blocks = stage((pieces, x_blocks))
+    else:
+        pieces, parts = [lax.all_gather(params.astype(BF16), AXES, axis=0, tiled=True)], ((0, rows),)
+        table = jnp.zeros((2,), jnp.int32)
+        tables = make_tables(plan, band_rows, position)
+        x_blocks = to_cores(plan, to_chips(plan, chip_blocks(plan, position, images)))
+        cot_got = to_chips(plan, chip_blocks(plan, position, cots))
+    x_img, a1, h1, a2, y, z, q, k, v, stats, small, weights = run_features(
+        True, plan, tables, x_blocks, pieces, parts, table
+    )
+    cot_got, y = stage((cot_got, y))
+    cot_blocks = to_cores(plan, cot_got)
+    if here.planes:
+        cot_blocks, far = stage((cot_blocks, far))
+        far = over_two_planes(far)
     out_own, out_oth, dy, dy16, g_proj, sums3 = run_attend_both(
-        tables, q, k, v, y, z, cot_slots, stats, small, weights
+        plan, tables, q, k, v, y, z, cot_blocks, stats, small, weights
     )
-    first_out = from_holders(plan, position, out_own, out_oth)
-    g_w2, sums_b2 = run_weight_grad(tables, a2, dy16, "weight_grad_two")
-    dh1, sums_n2 = run_data_grad(tables, 1, dy16, h1, stats, small, weights)
-    g_w1, sums_b1 = run_weight_grad(tables, a1, dh1, "weight_grad_one")
-    dx_own, dx_oth, sums_n1 = run_data_grad(
-        tables, 0, dh1, x_img, stats, small, weights, dy=dy, half=half
-    )
-    input_grads = from_holders(plan, position, dx_own, dx_oth)
-    small_rows = jnp.concatenate(
-        [sums_n1[0:2], sums_b1[0:1], sums_n2[0:2], sums_b2[0:1], sums3[0:5]], axis=0
-    )
-    grad = shard_of_grads(position, img, g_w1, g_w2, g_proj, small_rows, params.shape[0])
-
-    step_count = step[0].astype(F32)
-    new_first = 0.5 * first_moment + 0.5 * grad
-    new_second = 0.9 * second_moment + 0.1 * grad * grad
-    weight_update = (
-        rate[0]
-        * (new_first / (1.0 - jnp.power(0.5, step_count)))
-        / (jnp.sqrt(new_second / (1.0 - jnp.power(0.9, step_count))) + ADAM_EPSILON)
-    )
-    new_weights, new_small = fetch_weights(params - weight_update)
-    y2, q2, k2, v2 = run_features(False, tables, x_slots, new_small, new_weights)
-    again_own, again_oth = run_attend(tables, q2, k2, v2, y2, new_small, new_weights, half)
-    second_out = from_holders(plan, position, again_own, again_oth)
+    if here.planes:
+
+        def stepped(state, grad):
+            update, _, _ = adam(*state, grad, step_count, step_rate)
+            return (state[0] - update).astype(BF16)
+
+        dy16, far, out_oth = stage((dy16, far, out_oth))
+        out_got = over_core(out_oth)
+        kept, sent, early, sums_b2 = run_weight_grad(tables, 1, a2, dy16, g_proj)
+        dy16, kept, sent, out_got = stage((dy16, kept, sent, out_got))
+        got = over_core(sent)
+        out_got = from_chips(plan, merge_cores(plan, position, out_own, out_got))
+        dh1, sums_n2 = run_data_grad(tables, 1, dy16, h1, stats, small, weights)
+        dh1, kept, got = stage((dh1, kept, got))
+        halves = send_halves(here, kept, got)
+        high = kept, got
+        kept, sent, sums_b1 = run_weight_grad(tables, 0, a1, dh1, early)
+        kept, sent, high, halves, out_got = stage((kept, sent, high, halves, out_got))
+        got = over_core(sent)
+        high = add_halves(here, *high, *halves)
+        quarters = send_quarters(*quarters_to_send(here, *high))
+        kept, got, high = stage((kept, got, high))
+        low = kept, got
+        halves = send_halves(here, *low)
+        high, quarters, dh1 = stage((high, quarters, dh1))
+        high = by_plane(False, *add_quarters(here, *high, *quarters))
+        high, dh1, head = stage((high, dh1, [rows_of[rows - count :] for rows_of in state]))
+        high_got = send_planes(here, high)
+        dx_own, dx_oth, sums_n1 = run_data_grad(
+            tables, 0, dh1, x_img, stats, small, weights, dy=dy, half=out_own.shape[0]
+        )
+        low, halves, high, high_got, sums_n1, head = stage((low, halves, high, high_got, sums_n1, head))
+        low = add_halves(here, *low, *halves)
+        low, low_sent, sums_n1, head = stage((low, quarters_to_send(here, *low), sums_n1, head))
+        quarters = send_quarters(*low_sent)
+        before = lax.ppermute(jnp.concatenate(head, axis=1), AXES, [(o, o + 1) for o in range(last)])
+        small_rows = jnp.concatenate(
+            [sums_n1[0:2], sums_b1[0:1], sums_n2[0:2], sums_b2[0:1], sums3[0:5]], axis=0
+        )
+        small_sum = sum_over_plane(jnp.pad(small_rows, ((0, 5), (0, 0))))
+        low, quarters, small_sum, before = stage((low, quarters, small_sum, before))
+        low = by_plane(True, *add_quarters(here, *low, *quarters))
+        low_got = send_planes(here, low, small_sum)
+        low, low_got, before, far, high, high_got = stage((low, low_got, before, far, high, high_got))
+        low, high = add_planes(here, low, low_got, small_sum), add_planes(here, high, high_got)
+        low, small_sum = low[:176], low[176:]
+        own = [
+            aligned(before[:, i * C : (i + 1) * C], rows_of[:176], 176) for i, rows_of in enumerate(state)
+        ]
+        far = [far[:, i * C : (i + 1) * C].astype(F32) for i in range(3)]
+        first_two = here.z < 2
+        block = [
+            stepped([jnp.where(first_two, a, b) for a, b in zip(own, far)], low),
+            stepped([jnp.where(first_two, b, a) for a, b in zip(own, far)], high),
+            stepped([rows_of[singles : singles + 16] for rows_of in state], small_sum),
+        ]
+        gather = Gather(jnp.concatenate(block, axis=0))
+        values = stage(gather.first())
+        values, others, dx_oth = stage((gather.second(values), gather.others(values, 4), dx_oth))
+        values, more, dx_got = stage((gather.third(values), gather.others(values[4:], 6), over_core(dx_oth)))
+        others = others + more
+        dx_sent = merge_cores(plan, position, dx_own, dx_got)
+        pieces = gather.pieces(values, others + gather.others(values[10:], 6))
+        pieces, dx_sent = stage((pieces, dx_sent))
+        dx_got = from_chips(plan, dx_sent)
+        far = over_two_planes(jnp.where(here.z < 2, high, low).astype(BF16))
+        table = gather_table(
+            here,
+            lambda z, place: [
+                (8 * (z & 1) + place) * 22 + jnp.where(z < 2, 0, 11),
+                (8 * (z | 2) + place) * 22 + jnp.where(z < 2, 11, 0),
+            ],
+        )
+        parts = ((0, 176), (176, 176))
+    else:
+        out_got = from_chips(plan, merge_cores(plan, position, out_own, over_core(out_oth)))
+        g_w2, sums_b2 = run_weight_grad(tables, 1, a2, dy16)
+        dh1, sums_n2 = run_data_grad(tables, 1, dy16, h1, stats, small, weights)
+        g_w1, sums_b1 = run_weight_grad(tables, 0, a1, dh1)
+        dx_own, dx_oth, sums_n1 = run_data_grad(
+            tables, 0, dh1, x_img, stats, small, weights, dy=dy, half=out_own.shape[0]
+        )
+        dx_got = from_chips(plan, merge_cores(plan, position, dx_own, over_core(dx_oth)))
+        small_rows = jnp.concatenate(
+            [sums_n1[0:2], sums_b1[0:1], sums_n2[0:2], sums_b2[0:1], sums3[0:5]], axis=0
+        )
+        full = jnp.concatenate([g_w1, g_w2, g_proj, small_rows.astype(BF16)], axis=0)
+        full = jnp.pad(full, ((0, rows * count - full.shape[0]), (0, 0)))
+        grad = lax.psum_scatter(full, AXES, scatter_dimension=0, tiled=True).astype(F32)
+        weight_update, new_first, new_second = adam(
+            params, first_moment, second_moment, grad, step_count, step_rate
+        )
+        pieces = [lax.all_gather((params - weight_update).astype(BF16), AXES, axis=0, tiled=True)]
+    again_own, again_oth = run_features(False, plan, tables, x_blocks, pieces, parts, table)
+    if here.planes:
+        again_own, again_oth, out_got, dx_got, far = stage((again_own, again_oth, out_got, dx_got, far))
+    again = from_chips(plan, merge_cores(plan, position, again_own, over_core(again_oth)))
+    if here.planes:
+        mine = jnp.concatenate([jnp.where(here.z < 2, low, high), far.astype(F32)], axis=0)
+        follow = lax.ppermute(mine[:count], AXES, [(o, o - 1) for o in range(1, count)])
+        follow, dx_got, out_got = stage((follow, dx_got, out_got))
+        follow = jnp.where(here.owner == last, jnp.pad(small_sum, ((0, count - 16), (0, 0))), follow)
+        grad = lax.dynamic_slice_in_dim(jnp.concatenate([mine, follow], axis=0), here.owner, rows, 0)
+        weight_update, new_first, new_second = adam(
+            params, first_moment, second_moment, grad, step_count, step_rate
+        )
+    first_out = to_bands(plan, position, out_got)
+    input_grads = to_bands(plan, position, dx_got)
+    second_out = to_bands(plan, position, again)
     return (*first_out, *second_out, *input_grads, weight_update, new_first, new_second)
 
 

time: 685 us -> 490 us (0.72)
  waiting for transfers between devices: 409 us -> 142 us
  starting transfers between devices: 42.5 us -> 117 us
  Pallas kernels: 128 us -> 147 us
  between operations: 20.6 us -> 8.58 us
  local copies, waits for them, and re-layouts: 46.5 us -> 36.3 us
    psum x1 -> x0, waiting for transfers between devices: 123 us -> none  [shard_of_grads(): small_sum = lax.psum(small_rows, AXES)]
    ppermute x18 -> x29, waiting for transfers between devices: 166 us -> 64.4 us  [z_shift(): lax.ppermute(value, 'band', [(2 * z + c, 2 * ((z + k) % nz) + c) for z in...]
    all_gather x2 -> x0, waiting for transfers between devices: 77.9 us -> none  [fetch_weights(): full = lax.all_gather(shard.astype(BF16), AXES, axis=0, tiled=True)]
    ppermute x9 -> x37, starting transfers between devices: 9.98 us -> 47.3 us  [the longest x15 18.9 us: over_x(): return lax.ppermute(value, 'img', [(i, i ^ 1) for i in range(4)])]
    ppermute x18 -> x29, starting transfers between devices: 29.9 us -> 59.5 us  [z_shift(): lax.ppermute(value, 'band', [(2 * z + c, 2 * ((z + k) % nz) + c) for z in...]
    ppermute x9 -> x37, waiting for transfers between devices: 39.3 us -> 66.8 us  [the longest x15 46.8 us: over_x(): return lax.ppermute(value, 'img', [(i, i ^ 1) for i in range(4)])]
    unnamed x85 -> x255, local copies, waits for them, and re-layouts: 27.9 us -> 6.56 us
    pallas_call x8 -> x7, Pallas kernels: 128 us -> 147 us  [call(): pl.pallas_call(kernel, name=name, out_shape=[jax.ShapeDtypeStruct(s, d) f...]
  transfers between devices with their start and end apart: 37 -> 112, of which waited for: 20 -> 50; matrix products, arithmetic and copies ran while one was open for 6% -> 9% of each run, Pallas kernels for 6% -> 30%
where the time goes in v2:
time: 490 us; the launch traced here: 484 us
  Pallas kernels  147 us (30%)
  waiting for transfers between devices  142 us (29%)
  starting transfers between devices  117 us (24%)
  local copies, waits for them, and re-layouts  36.3 us (7%)
  other arithmetic  34.2 us (7%)
  between operations  8.58 us (2%)
    pallas_call x7, Pallas kernels, call(): pl.pallas_call(kernel, name=name, out_shape=[jax.ShapeDtypeStruct(s, d) f...  147 us
    ppermute x29, waiting for transfers between devices, z_shift(): lax.ppermute(value, 'band', [(2 * z + c, 2 * ((z + k) % nz) + c) for z in...  64.4 us
    ppermute x29, starting transfers between devices, z_shift(): lax.ppermute(value, 'band', [(2 * z + c, 2 * ((z + k) % nz) + c) for z in...  59.5 us
    ppermute x15, waiting for transfers between devices, over_x(): return lax.ppermute(value, 'img', [(i, i ^ 1) for i in range(4)])  46.8 us
    ppermute x15, waiting for transfers between devices, over_y(): return lax.ppermute(value, 'img', [(i, i ^ 2) for i in range(4)])  19.9 us
    ppermute x15, starting transfers between devices, over_x(): return lax.ppermute(value, 'img', [(i, i ^ 1) for i in range(4)])  18.9 us
    ppermute x15, starting transfers between devices, over_y(): return lax.ppermute(value, 'img', [(i, i ^ 2) for i in range(4)])  16.9 us
    ppermute x46, waiting for transfers between devices, core_swap(): return lax.ppermute(value, 'band', [(b, b ^ 1) for b in range(n_band)])  10.5 us
  transfers between devices with their start and end apart: 112, of which 50 were waited for; matrix products, arithmetic and copies ran while one was open for 9% of the time, Pallas kernels for 30%

profile of v2, /device:TPU:0, one launch (start us, length us, event | category | flops | bytes accessed | tf_op | source)
XLA Modules:
  0.0 484.5 jit_solution(6395134913439330802)
XLA Ops:
  3.3 3.0 collective-permute-start.3
  6.3 2.6 collective-permute-start.4
  10.3 3.5 collective-permute-start
  16.8 2.1 collective-permute-start.1
  34.1 12.7 %collective-permute-start.7 = (bf16[368,512]{1,0:T(8,128)(2,1)S(1)}, bf16[368,512]{1,0:T(8,128)(2,1)S(1)}, u32[]{:S(2)}, u32[]{:S(2)}) collective-permute-start(bf16[368,512]{1,0:T(8,128)(2,1)S(1)} %pad_maximum_fusion.11.refs_11_), channel_id=1, source_target_pairs={{0,8},{4,12},{8,16},{12,20},{16,24},{20,28},{24,0},{28,4},{1,9},{5... | collective-permute-start | bytes 1130504 | tf_op jit(solution)/shard_map/ppermute | solution.py:883
  49.4 2.4 collective-permute-start.10
  55.8 6.6 %collective-permute-done.8.refs_23_ = bf16[368,512]{1,0:T(8,128)(2,1)S(1)} collective-permute-done((bf16[368,512]{1,0:T(8,128)(2,1)S(1)}, bf16[368,512]{1,0:T(8,128)(2,1)S(1)}, u32[]{:S(2)}, u32[]{:S(2)}) %collective-permute-start.8) | collective-permute-done | bytes 376864 | tf_op jit(solution)/shard_map/ppermute | solution.py:883
  64.4 2.0 collective-permute-start.16
  66.4 7.5 %collective-permute-start.17 = (bf16[368,512]{1,0:T(8,128)(2,1)S(1)}, bf16[368,512]{1,0:T(8,128)(2,1)S(1)}, u32[]{:S(2)}, u32[]{:S(2)}) collective-permute-start(bf16[368,512]{1,0:T(8,128)(2,1)S(1)} %pad_maximum_fusion.11.refs_11_), channel_id=1, source_target_pairs={{0,16},{4,20},{8,24},{12,28},{16,0},{20,4},{24,8},{28,12},{1,17},{... | collective-permute-start | bytes 1130504 | tf_op jit(solution)/shard_map/ppermute | solution.py:883
  75.2 6.0 %collective-permute-done.15.refs_24_ = bf16[368,512]{1,0:T(8,128)(2,1)S(1)} collective-permute-done((bf16[368,512]{1,0:T(8,128)(2,1)S(1)}, bf16[368,512]{1,0:T(8,128)(2,1)S(1)}, u32[]{:S(2)}, u32[]{:S(2)}) %collective-permute-start.15) | collective-permute-done | bytes 376864 | tf_op jit(solution)/shard_map/ppermute | solution.py:972
  81.2 5.5 %collective-permute-done.17.refs_19_ = bf16[368,512]{1,0:T(8,128)(2,1)S(1)} collective-permute-done((bf16[368,512]{1,0:T(8,128)(2,1)S(1)}, bf16[368,512]{1,0:T(8,128)(2,1)S(1)}, u32[]{:S(2)}, u32[]{:S(2)}) %collective-permute-start.17) | collective-permute-done | bytes 376864 | tf_op jit(solution)/shard_map/ppermute | solution.py:883
  90.8 7.6 %collective-permute-done.18.refs_20_ = bf16[368,512]{1,0:T(8,128)(2,1)S(1)} collective-permute-done((bf16[368,512]{1,0:T(8,128)(2,1)S(1)}, bf16[368,512]{1,0:T(8,128)(2,1)S(1)}, u32[]{:S(2)}, u32[]{:S(2)}) %collective-permute-start.18) | collective-permute-done | bytes 376864 | tf_op jit(solution)/shard_map/ppermute | solution.py:972
  99.0 8.6 %collective-permute-done.20.refs_22_ = bf16[368,512]{1,0:T(8,128)(2,1)S(1)} collective-permute-done((bf16[368,512]{1,0:T(8,128)(2,1)S(1)}, bf16[368,512]{1,0:T(8,128)(2,1)S(1)}, u32[]{:S(2)}, u32[]{:S(2)}) %collective-permute-start.20) | collective-permute-done | bytes 376864 | tf_op jit(solution)/shard_map/ppermute | solution.py:883
  120.2 29.2 %features_first.1 = (bf16[1024,512]{1,0:T(8,128)(2,1)}, bf16[1024,512]{1,0:T(8,128)(2,1)}, f32[1024,512]{1,0:T(8,128)}, bf16[1024,512]{1,0:T(8,128)(2,1)}, f32[1...) custom-call(s32[128]{0:T(128)} %broadcast_select_fusion.6.refs_0_.ga, ...), custom_call_target="tpu_custom_call" | custom-call | flops 28600000512 | bytes 37552792 | tf_op jit(solution)/shard_map/features_first/pallas_call | solution.py:735
  152.6 2.8 collective-permute-start.46
  155.5 34.1 %attend_both.1 = (bf16[768,512]{1,0:T(8,128)(2,1)}, bf16[768,512]{1,0:T(8,128)(2,1)}, f32[1024,512]{1,0:T(8,128)}, bf16[1024,512]{1,0:T(8,128)(2,1)}, bf16[2048,512]{1,0:T(8,128)(2,1)}, /*index=5*/f32[8,512]{1,0:T(8,128)}) custom-call(s32[128]{0:T(128)} %broadcast_select_fusion.6.refs_0_.gather, s32[192]{0:T(256)} %fusion.78.scatter.refs_0_.refs_1_, ...), custom_call_target="tpu_custom_call" | custom-call | flops 26400000000 | bytes 27084052 | tf_op jit(solution)/shard_map/attend_both/pallas_call | solution.py:735
  189.7 13.0 %weight_grad_two.1 = (bf16[2816,512]{1,0:T(8,128)(2,1)}, bf16[2816,512]{1,0:T(8,128)(2,1)}, bf16[1024,512]{1,0:T(8,128)(2,1)}, f32[8,512]{1,0:T(8,128)}) custom-call(s32[5]{0:T(128)} %stack.276.refs_1_.flags.refs_0_.refs_2_, bf16[1024,512]{1,0:T(8,128)(2,1)} %get-tuple-element.505.refs_1_, bf16[1024,512]{1,0:T(8,128)(2,1)} %get-tuple-element.510.refs_2_.refs_1_, ...), custom_call_target="tpu_custom_call" | custom-call | flops 13200000000 | bytes 11026452 | tf_op jit(solution)/shard_map/weight_grad_two/pallas_call | solution.py:735
  207.1 12.8 %data_grad_two.1 = (bf16[1024,512]{1,0:T(8,128)(2,1)}, f32[8,512]{1,0:T(8,128)}) custom-call(s32[5]{0:T(128)} %stack.276.refs_1_.flags.refs_0_.refs_2_, bf16[1024,512]{1,0:T(8,128)(2,1)} %get-tuple-element.510.refs_2_.refs_1_, f32[1024,512]{1,0:T(8,128)} %get-tuple-element.511.refs_2_, f32[16,512]{1,0:T(8,128)} %get-tuple-element.485.stats.refs_3_.refs_5_, ...), custom_call_target="tpu_custom_call" | custom-call | flops 13200000000 | bytes 15810580 | tf_op jit(solution)/shard_map/data_grad_two/pallas_call | solution.py:735
  220.2 2.0 fusion.98
  223.4 12.4 %weight_grad_one.1 = (bf16[2816,512]{1,0:T(8,128)(2,1)}, bf16[2816,512]{1,0:T(8,128)(2,1)}, f32[8,512]{1,0:T(8,128)}) custom-call(s32[5]{0:T(128)} %stack.276.refs_1_.flags.refs_0_.refs_2_, bf16[1024,512]{1,0:T(8,128)(2,1)} %get-tuple-element.473.refs_1_, bf16[1024,512]{1,0:T(8,128)(2,1)} %get-tuple-element.539.refs_2_, ...), custom_call_target="tpu_custom_call" | custom-call | flops 13200000000 | bytes 8929300 | tf_op jit(solution)/shard_map/weight_grad_one/pallas_call | solution.py:735
  235.9 4.0 collective-permute-done.50
  241.3 2.0 fusion.96
  252.3 3.5 collective-permute-done.58
  259.4 2.0 collective-permute-start.60
  262.0 2.0 fusion.94
  267.7 14.0 %data_grad_one.1 = (bf16[768,512]{1,0:T(8,128)(2,1)}, bf16[768,512]{1,0:T(8,128)(2,1)}, f32[8,512]{1,0:T(8,128)}) custom-call(s32[192]{0:T(256)} %fusion.78.scatter.refs_0_.refs_1_, s32[5]{0:T(128)} %stack.276.refs_1_.flags.refs_0_.refs_2_, bf16[1024,512]{1,0:T(8,128)(2,1)} %get-tuple-element.539.refs_2_, bf16[1024,512]{1,0:T(8,128)(2,1)} %get-tuple-element.540.refs_3_, ...), custom_call_target="tpu_custom_call" | custom-call | flops 13200000000 | bytes 17384212 | tf_op jit(solution)/shard_map/data_grad_one/pallas_call | solution.py:735
  282.9 2.0 fusion.92
  291.1 2.3 collective-permute-start.67
  293.4 2.6 collective-permute-start.65
  296.0 8.8 %collective-permute-done.65 = f32[16,512]{1,0:T(8,128)S(1)} collective-permute-done((f32[16,512]{1,0:T(8,128)S(1)}, f32[16,512]{1,0:T(8,128)S(1)}, u32[]{:S(2)}, u32[]{:S(2)}) %collective-permute-start.65) | collective-permute-done | bytes 32800 | tf_op jit(solution)/shard_map/ppermute | solution.py:972
  305.5 3.3 collective-permute-done.66
  312.0 3.0 collective-permute-start.69
  321.5 9.2 %collective-permute-done.70 = bf16[192,512]{1,0:T(8,128)(2,1)} collective-permute-done((bf16[192,512]{1,0:T(8,128)(2,1)}, bf16[192,512]{1,0:T(8,128)(2,1)}, u32[]{:S(2)}, u32[]{:S(2)}) %collective-permute-start.70) | collective-permute-done | bytes 196640 | tf_op jit(solution)/shard_map/ppermute | solution.py:883
  335.9 2.0 collective-permute-start.72
  339.5 3.8 collective-permute-start.76
  343.3 4.4 collective-permute-done.72.refs_13_
  347.7 7.7 %collective-permute-done.73.refs_14_ = bf16[368,512]{1,0:T(8,128)(2,1)S(1)} collective-permute-done((bf16[368,512]{1,0:T(8,128)(2,1)S(1)}, bf16[368,512]{1,0:T(8,128)(2,1)S(1)}, u32[]{:S(2)}, u32[]{:S(2)}) %collective-permute-start.73) | collective-permute-done | bytes 376864 | tf_op jit(solution)/shard_map/ppermute | solution.py:976
  360.7 2.4 collective-permute-start.81
  363.1 5.2 %collective-permute-done.77.refs_17_ = bf16[368,512]{1,0:T(8,128)(2,1)S(1)} collective-permute-done((bf16[368,512]{1,0:T(8,128)(2,1)S(1)}, bf16[368,512]{1,0:T(8,128)(2,1)S(1)}, u32[]{:S(2)}, u32[]{:S(2)}) %collective-permute-start.77) | collective-permute-done | bytes 376864 | tf_op jit(solution)/shard_map/ppermute | solution.py:972
  370.0 3.5 collective-permute-done.79.refs_25_
  381.0 6.5 %collective-permute-done.86.refs_21_ = bf16[368,512]{1,0:T(8,128)(2,1)} collective-permute-done((bf16[368,512]{1,0:T(8,128)(2,1)S(1)}, bf16[368,512]{1,0:T(8,128)(2,1)}, u32[]{:S(2)}, u32[]{:S(2)}) %collective-permute-start.86) | collective-permute-done | bytes 376864 | tf_op jit(solution)/shard_map/ppermute | solution.py:972
  389.8 7.7 %collective-permute-done.88.refs_23_ = bf16[368,512]{1,0:T(8,128)(2,1)S(1)} collective-permute-done((bf16[368,512]{1,0:T(8,128)(2,1)S(1)}, bf16[368,512]{1,0:T(8,128)(2,1)S(1)}, u32[]{:S(2)}, u32[]{:S(2)}) %collective-permute-start.88) | collective-permute-done | bytes 376864 | tf_op jit(solution)/shard_map/ppermute | solution.py:883
  408.5 4.3 collective-permute-start.104
  415.2 31.2 %forward_again.1 = (bf16[768,512]{1,0:T(8,128)(2,1)}, bf16[768,512]{1,0:T(8,128)(2,1)}) custom-call(s32[128]{0:T(128)} %broadcast_select_fusion.6.refs_0_.gather, s32[192]{0:T(256)} %fusion.78.scatter.refs_0_.refs_1_, s32[5]{0:T(128)} %stack.276.refs_1_.flags.refs_0_.refs_2_, s32[65]{0:T(128)} %pad_add_fusion.5.refs_3_, bf16[288,512]{1,0:T(8,128)(2,1)} %copy-done.28, ...), custom_call_target="tpu_custom_call" | custom-call | flops 30799998976 | bytes 15992344 | tf_op jit(solution)/shard_map/forward_again/pallas_call | solution.py:735
  452.7 1.9 collective-permute-start.109
  456.4 1.9 add_divide_fusion
  458.3 3.8 collective-permute-done.109
  462.1 20.1 %collective-permute-done.110 = bf16[288,512]{1,0:T(8,128)(2,1)S(1)} collective-permute-done((bf16[288,512]{1,0:T(8,128)(2,1)S(1)}, bf16[288,512]{1,0:T(8,128)(2,1)S(1)}, u32[]{:S(2)}, u32[]{:S(2)}) %collective-permute-start.110) | collective-permute-done | bytes 294944 | tf_op jit(solution)/shard_map/ppermute | solution.py:883
  (583 shorter events, 134.6 us)
Async XLA Ops:
  3.3 29.7 %collective-permute-start.3 = (bf16[288,512]{1,0:T(8,128)(2,1)}, bf16[288,512]{1,0:T(8,128)(2,1)}, u32[]{:S(2)}, u32[]{:S(2)}) collective-permute-start(bf16[288,512]{1,0:T(8,128)(2,1)} %get-tuple-element.784), channel_id=1, source_target_pairs={{0,8},{4,12},{8,16},{12,20},{16,24},{20,28},{24,0},{28,4},{1,9},{5... | collective-permute-start | bytes 884744 | tf_op jit(solution)/shard_map/ppermute | solution.py:883
  6.3 26.7 %collective-permute-start.4 = (bf16[288,512]{1,0:T(8,128)(2,1)S(1)}, bf16[288,512]{1,0:T(8,128)(2,1)}, u32[]{:S(2)}, u32[]{:S(2)}) collective-permute-start(bf16[288,512]{1,0:T(8,128)(2,1)S(1)} %get-tuple-element.783), channel_id=1, source_target_pairs={{0,16},{4,20},{8,24},{12,28},{16,0},{20,4},{24,8},{28,12},{1,17},{... | collective-permute-start | bytes 884744 | tf_op jit(solution)/shard_map/ppermute | solution.py:883
  8.9 24.1 %collective-permute-start.5 = (bf16[288,512]{1,0:T(8,128)(2,1)S(1)}, bf16[288,512]{1,0:T(8,128)(2,1)}, u32[]{:S(2)}, u32[]{:S(2)}) collective-permute-start(bf16[288,512]{1,0:T(8,128)(2,1)S(1)} %get-tuple-element.782), channel_id=1, source_target_pairs={{0,24},{4,28},{8,0},{12,4},{16,8},{20,12},{24,16},{28,20},{1,25},{... | collective-permute-start | bytes 884744 | tf_op jit(solution)/shard_map/ppermute | solution.py:883
  16.8 16.2 %collective-permute-start.1 = (bf16[368,512]{1,0:T(8,128)(2,1)S(1)}, bf16[368,512]{1,0:T(8,128)(2,1)}, u32[]{:S(2)}, u32[]{:S(2)}) collective-permute-start(bf16[368,512]{1,0:T(8,128)(2,1)S(1)} %pad_maximum_fusion.11.refs_11_), channel_id=1, source_target_pairs={{0,1},{1,0},{2,3},{3,2},{4,5},{5,4},{6,7},{7,6},{8,9},{9,8},{10,11... | collective-permute-start | bytes 1130504 | tf_op jit(solution)/shard_map/ppermute | solution.py:972
  33.2 22.5 %collective-permute-start.6 = (bf16[368,512]{1,0:T(8,128)(2,1)S(1)}, bf16[368,512]{1,0:T(8,128)(2,1)S(1)}, u32[]{:S(2)}, u32[]{:S(2)}) collective-permute-start(bf16[368,512]{1,0:T(8,128)(2,1)S(1)} %pad_maximum_fusion.11.refs_11_), channel_id=1, source_target_pairs={{0,3},{1,2},{2,1},{3,0},{4,7},{5,6},{6,5},{7,4},{8,11},{9,10},{10,... | collective-permute-start | bytes 1130504 | tf_op jit(solution)/shard_map/ppermute | solution.py:984
  34.1 21.7 %collective-permute-start.7 = (bf16[368,512]{1,0:T(8,128)(2,1)S(1)}, bf16[368,512]{1,0:T(8,128)(2,1)S(1)}, u32[]{:S(2)}, u32[]{:S(2)}) collective-permute-start(bf16[368,512]{1,0:T(8,128)(2,1)S(1)} %pad_maximum_fusion.11.refs_11_), channel_id=1, source_target_pairs={{0,8},{4,12},{8,16},{12,20},{16,24},{20,28},{24,0},{28,4},{1,9},{5... | collective-permute-start | bytes 1130504 | tf_op jit(solution)/shard_map/ppermute | solution.py:883
  46.8 15.6 %collective-permute-start.8 = (bf16[368,512]{1,0:T(8,128)(2,1)S(1)}, bf16[368,512]{1,0:T(8,128)(2,1)S(1)}, u32[]{:S(2)}, u32[]{:S(2)}) collective-permute-start(bf16[368,512]{1,0:T(8,128)(2,1)S(1)} %pad_maximum_fusion.11.refs_11_), channel_id=1, source_target_pairs={{0,24},{4,28},{8,0},{12,4},{16,8},{20,12},{24,16},{28,20},{1,25},{... | collective-permute-start | bytes 1130504 | tf_op jit(solution)/shard_map/ppermute | solution.py:883
  63.0 18.3 %collective-permute-start.15 = (bf16[368,512]{1,0:T(8,128)(2,1)S(1)}, bf16[368,512]{1,0:T(8,128)(2,1)S(1)}, u32[]{:S(2)}, u32[]{:S(2)}) collective-permute-start(bf16[368,512]{1,0:T(8,128)(2,1)S(1)} %collective-permute-done.8.refs_23_), channel_id=1, source_target_pairs={{0,1},{1,0},{2,3},{3,2},{4,5},{5,4},{6,7},{7,6},{8,9},{9,8},{10,11... | collective-permute-start | bytes 1130504 | tf_op jit(solution)/shard_map/ppermute | solution.py:972
  64.4 16.8 %collective-permute-start.16 = (bf16[368,512]{1,0:T(8,128)(2,1)S(1)}, bf16[368,512]{1,0:T(8,128)(2,1)S(1)}, u32[]{:S(2)}, u32[]{:S(2)}) collective-permute-start(bf16[368,512]{1,0:T(8,128)(2,1)S(1)} %collective-permute-done.8.refs_23_), channel_id=1, source_target_pairs={{0,2},{1,3},{2,0},{3,1},{4,6},{5,7},{6,4},{7,5},{8,10},{9,11},{10,... | collective-permute-start | bytes 1130504 | tf_op jit(solution)/shard_map/ppermute | solution.py:976
  66.4 20.4 %collective-permute-start.17 = (bf16[368,512]{1,0:T(8,128)(2,1)S(1)}, bf16[368,512]{1,0:T(8,128)(2,1)S(1)}, u32[]{:S(2)}, u32[]{:S(2)}) collective-permute-start(bf16[368,512]{1,0:T(8,128)(2,1)S(1)} %pad_maximum_fusion.11.refs_11_), channel_id=1, source_target_pairs={{0,16},{4,20},{8,24},{12,28},{16,0},{20,4},{24,8},{28,12},{1,17},{... | collective-permute-start | bytes 1130504 | tf_op jit(solution)/shard_map/ppermute | solution.py:883
  89.0 18.6 %collective-permute-start.20 = (bf16[368,512]{1,0:T(8,128)(2,1)S(1)}, bf16[368,512]{1,0:T(8,128)(2,1)S(1)}, u32[]{:S(2)}, u32[]{:S(2)}) collective-permute-start(bf16[368,512]{1,0:T(8,128)(2,1)S(1)} %collective-permute-done.6.refs_14_), channel_id=1, source_target_pairs={{0,16},{4,20},{8,24},{12,28},{16,0},{20,4},{24,8},{28,12},{1,17},{... | collective-permute-start | bytes 1130504 | tf_op jit(solution)/shard_map/ppermute | solution.py:883
  89.0 18.6 %collective-permute-start.21 = (bf16[368,512]{1,0:T(8,128)(2,1)S(1)}, bf16[368,512]{1,0:T(8,128)(2,1)S(1)}, u32[]{:S(2)}, u32[]{:S(2)}) collective-permute-start(bf16[368,512]{1,0:T(8,128)(2,1)S(1)} %collective-permute-done.13.refs_16_), channel_id=1, source_target_pairs={{0,2},{1,3},{2,0},{3,1},{4,6},{5,7},{6,4},{7,5},{8,10},{9,11},{10,... | collective-permute-start | bytes 1130504 | tf_op jit(solution)/shard_map/ppermute | solution.py:976
  89.3 18.9 %collective-permute-start.22 = (bf16[368,512]{1,0:T(8,128)(2,1)S(1)}, bf16[368,512]{1,0:T(8,128)(2,1)S(1)}, u32[]{:S(2)}, u32[]{:S(2)}) collective-permute-start(bf16[368,512]{1,0:T(8,128)(2,1)S(1)} %collective-permute-done.16.refs_25_), channel_id=1, source_target_pairs={{0,1},{1,0},{2,3},{3,2},{4,5},{5,4},{6,7},{7,6},{8,9},{9,8},{10,11... | collective-permute-start | bytes 1130504 | tf_op jit(solution)/shard_map/ppermute | solution.py:972
  115.3 34.1 %collective-permute-start.39 = (bf16[288,512]{1,0:T(8,128)(2,1)S(1)}, bf16[288,512]{1,0:T(8,128)(2,1)}, u32[]{:S(2)}, u32[]{:S(2)}) collective-permute-start(bf16[288,512]{1,0:T(8,128)(2,1)S(1)} %get-tuple-element.479), channel_id=1, source_target_pairs={{0,8},{4,12},{8,16},{12,20},{16,24},{20,28},{24,0},{28,4},{1,9},{5... | collective-permute-start | bytes 884744 | tf_op jit(solution)/shard_map/ppermute | solution.py:883
  115.9 33.6 %collective-permute-start.40 = (bf16[288,512]{1,0:T(8,128)(2,1)S(1)}, bf16[288,512]{1,0:T(8,128)(2,1)}, u32[]{:S(2)}, u32[]{:S(2)}) collective-permute-start(bf16[288,512]{1,0:T(8,128)(2,1)S(1)} %get-tuple-element.480), channel_id=1, source_target_pairs={{0,16},{4,20},{8,24},{12,28},{16,0},{20,4},{24,8},{28,12},{1,17},{... | collective-permute-start | bytes 884744 | tf_op jit(solution)/shard_map/ppermute | solution.py:883
  117.5 31.9 %collective-permute-start.41 = (bf16[288,512]{1,0:T(8,128)(2,1)S(1)}, bf16[288,512]{1,0:T(8,128)(2,1)}, u32[]{:S(2)}, u32[]{:S(2)}) collective-permute-start(bf16[288,512]{1,0:T(8,128)(2,1)S(1)} %get-tuple-element.481), channel_id=1, source_target_pairs={{0,24},{4,28},{8,0},{12,4},{16,8},{20,12},{24,16},{28,20},{1,25},{... | collective-permute-start | bytes 884744 | tf_op jit(solution)/shard_map/ppermute | solution.py:883
  152.6 37.0 %collective-permute-start.46 = (bf16[176,1536]{1,0:T(8,128)(2,1)S(1)}, bf16[176,1536]{1,0:T(8,128)(2,1)S(1)}, u32[]{:S(2)}, u32[]{:S(2)}) collective-permute-start(bf16[176,1536]{1,0:T(8,128)(2,1)S(1)} %pad_maximum_fusion.7), channel_id=1, source_target_pairs={{0,16},{4,20},{16,0},{20,4},{8,24},{12,28},{24,8},{28,12},{1,17},{... | collective-permute-start | bytes 1622024 | tf_op jit(solution)/shard_map/ppermute | solution.py:980
  202.7 17.2 %collective-permute-start.48 = (bf16[2816,512]{1,0:T(8,128)(2,1)}, bf16[2816,512]{1,0:T(8,128)(2,1)}, u32[]{:S(2)}, u32[]{:S(2)}) collective-permute-start(bf16[2816,512]{1,0:T(8,128)(2,1)} %get-tuple-element.514), channel_id=1, source_target_pairs={{0,4},{4,0},{8,12},{12,8},{16,20},{20,16},{24,28},{28,24},{1,5},{5... | collective-permute-start | bytes 8650760 | tf_op jit(solution)/shard_map/ppermute | solution.py:887
  204.4 31.5 %collective-permute-start.51 = (bf16[288,512]{1,0:T(8,128)(2,1)}, bf16[288,512]{1,0:T(8,128)(2,1)S(1)}, u32[]{:S(2)}, u32[]{:S(2)}) collective-permute-start(bf16[288,512]{1,0:T(8,128)(2,1)} %get-tuple-element.734), channel_id=1, source_target_pairs={{0,24},{4,28},{8,0},{12,4},{16,8},{20,12},{24,16},{28,20},{1,25},{... | collective-permute-start | bytes 884744 | tf_op jit(solution)/shard_map/ppermute | solution.py:883
  205.4 30.4 %collective-permute-start.52 = (bf16[288,512]{1,0:T(8,128)(2,1)}, bf16[288,512]{1,0:T(8,128)(2,1)S(1)}, u32[]{:S(2)}, u32[]{:S(2)}) collective-permute-start(bf16[288,512]{1,0:T(8,128)(2,1)} %get-tuple-element.735), channel_id=1, source_target_pairs={{0,16},{4,20},{8,24},{12,28},{16,0},{20,4},{24,8},{28,12},{1,17},{... | collective-permute-start | bytes 884744 | tf_op jit(solution)/shard_map/ppermute | solution.py:883
  205.4 30.5 %collective-permute-start.53 = (bf16[288,512]{1,0:T(8,128)(2,1)}, bf16[288,512]{1,0:T(8,128)(2,1)S(1)}, u32[]{:S(2)}, u32[]{:S(2)}) collective-permute-start(bf16[288,512]{1,0:T(8,128)(2,1)} %get-tuple-element.732), channel_id=1, source_target_pairs={{0,8},{4,12},{8,16},{12,20},{16,24},{20,28},{24,0},{28,4},{1,9},{5... | collective-permute-start | bytes 884744 | tf_op jit(solution)/shard_map/ppermute | solution.py:883
  222.4 17.5 %collective-permute-start.50 = (bf16[2,352,512]{2,1,0:T(8,128)(2,1)S(1)}, bf16[2,352,512]{2,1,0:T(8,128)(2,1)}, u32[]{:S(2)}, u32[]{:S(2)}) collective-permute-start(bf16[2,352,512]{2,1,0:T(8,128)(2,1)S(1)} %fusion.8), channel_id=1, source_target_pairs={{0,2},{1,3},{2,0},{3,1},{4,6},{5,7},{6,4},{7,5},{8,10},{9,11},{10,... | collective-permute-start | bytes 2162696 | tf_op jit(solution)/shard_map/ppermute | solution.py:976
  223.2 17.1 %collective-permute-start.49 = (bf16[2,352,512]{2,1,0:T(8,128)(2,1)S(1)}, bf16[2,352,512]{2,1,0:T(8,128)(2,1)S(1)}, u32[]{:S(2)}, u32[]{:S(2)}) collective-permute-start(bf16[2,352,512]{2,1,0:T(8,128)(2,1)S(1)} %fusion.7), channel_id=1, source_target_pairs={{0,1},{1,0},{2,3},{3,2},{4,5},{5,4},{6,7},{7,6},{8,9},{9,8},{10,11... | collective-permute-start | bytes 2162696 | tf_op jit(solution)/shard_map/ppermute | solution.py:972
  257.6 24.1 %collective-permute-start.59 = (bf16[176,512]{1,0:T(8,128)(2,1)}, bf16[176,512]{1,0:T(8,128)(2,1)}, u32[]{:S(2)}, u32[]{:S(2)}) collective-permute-start(bf16[176,512]{1,0:T(8,128)(2,1)} %get-tuple-element.795), channel_id=1, source_target_pairs={{0,8},{4,12},{8,16},{12,20},{16,24},{20,28},{24,0},{28,4},{1,9},{5... | collective-permute-start | bytes 540680 | tf_op jit(solution)/shard_map/ppermute | solution.py:883
  259.4 22.3 %collective-permute-start.60 = (bf16[176,512]{1,0:T(8,128)(2,1)}, bf16[176,512]{1,0:T(8,128)(2,1)}, u32[]{:S(2)}, u32[]{:S(2)}) collective-permute-start(bf16[176,512]{1,0:T(8,128)(2,1)} %get-tuple-element.794), channel_id=1, source_target_pairs={{0,24},{4,28},{8,0},{12,4},{16,8},{20,12},{24,16},{28,20},{1,25},{... | collective-permute-start | bytes 540680 | tf_op jit(solution)/shard_map/ppermute | solution.py:883
  261.4 20.3 %collective-permute-start.61 = (bf16[176,512]{1,0:T(8,128)(2,1)S(1)}, bf16[176,512]{1,0:T(8,128)(2,1)}, u32[]{:S(2)}, u32[]{:S(2)}) collective-permute-start(bf16[176,512]{1,0:T(8,128)(2,1)S(1)} %get-tuple-element.793), channel_id=1, source_target_pairs={{0,16},{4,20},{8,24},{12,28},{16,0},{20,4},{24,8},{28,12},{1,17},{... | collective-permute-start | bytes 540680 | tf_op jit(solution)/shard_map/ppermute | solution.py:883
  264.2 17.5 %collective-permute-start.56 = (bf16[2,352,512]{2,1,0:T(8,128)(2,1)S(1)}, bf16[2,352,512]{2,1,0:T(8,128)(2,1)}, u32[]{:S(2)}, u32[]{:S(2)}) collective-permute-start(bf16[2,352,512]{2,1,0:T(8,128)(2,1)S(1)} %fusion.12), channel_id=1, source_target_pairs={{0,2},{1,3},{2,0},{3,1},{4,6},{5,7},{6,4},{7,5},{8,10},{9,11},{10,... | collective-permute-start | bytes 2162696 | tf_op jit(solution)/shard_map/ppermute | solution.py:976
  266.2 16.5 %collective-permute-start.55 = (bf16[2,352,512]{2,1,0:T(8,128)(2,1)S(1)}, bf16[2,352,512]{2,1,0:T(8,128)(2,1)}, u32[]{:S(2)}, u32[]{:S(2)}) collective-permute-start(bf16[2,352,512]{2,1,0:T(8,128)(2,1)S(1)} %fusion.11), channel_id=1, source_target_pairs={{0,1},{1,0},{2,3},{3,2},{4,5},{5,4},{6,7},{7,6},{8,9},{9,8},{10,11... | collective-permute-start | bytes 2162696 | tf_op jit(solution)/shard_map/ppermute | solution.py:972
  289.0 19.7 %collective-permute-start.62 = (bf16[352,512]{1,0:T(8,128)(2,1)S(1)}, bf16[352,512]{1,0:T(8,128)(2,1)S(1)}, u32[]{:S(2)}, u32[]{:S(2)}) collective-permute-start(bf16[352,512]{1,0:T(8,128)(2,1)S(1)} %dynamic-slice_bitcast_fusion.2), channel_id=1, source_target_pairs={{0,2},{1,3},{2,0},{3,1},{4,6},{5,7},{6,4},{7,5},{8,10},{9,11},{10,... | collective-permute-start | bytes 1081352 | tf_op jit(solution)/shard_map/ppermute | solution.py:976
  289.4 19.4 %collective-permute-start.63 = (bf16[352,512]{1,0:T(8,128)(2,1)S(1)}, bf16[352,512]{1,0:T(8,128)(2,1)S(1)}, u32[]{:S(2)}, u32[]{:S(2)}) collective-permute-start(bf16[352,512]{1,0:T(8,128)(2,1)S(1)} %dynamic-slice_bitcast_fusion.1), channel_id=1, source_target_pairs={{0,1},{1,0},{2,3},{3,2},{4,5},{5,4},{6,7},{7,6},{8,9},{9,8},{10,11... | collective-permute-start | bytes 1081352 | tf_op jit(solution)/shard_map/ppermute | solution.py:972
  291.1 17.7 %collective-permute-start.67 = (f32[32,1536]{1,0:T(8,128)S(1)}, f32[32,1536]{1,0:T(8,128)S(1)}, u32[]{:S(2)}, u32[]{:S(2)}) collective-permute-start(f32[32,1536]{1,0:T(8,128)S(1)} %pad_maximum_fusion.16), channel_id=1, source_target_pairs={{0,1},{1,2},{2,3},{3,4},{4,5},{5,6},{6,7},{7,8},{8,9},{9,10},{10,1... | collective-permute-start | bytes 589832 | tf_op jit(solution)/shard_map/ppermute | solution.py:1212
  315.0 15.6 %collective-permute-start.70 = (bf16[192,512]{1,0:T(8,128)(2,1)}, bf16[192,512]{1,0:T(8,128)(2,1)}, u32[]{:S(2)}, u32[]{:S(2)}) collective-permute-start(bf16[192,512]{1,0:T(8,128)(2,1)} %get-tuple-element.831), channel_id=1, source_target_pairs={{0,16},{4,20},{8,24},{12,28},{16,0},{20,4},{24,8},{28,12},{1,17},{... | collective-permute-start | bytes 589832 | tf_op jit(solution)/shard_map/ppermute | solution.py:883
  337.9 17.5 %collective-permute-start.73 = (bf16[368,512]{1,0:T(8,128)(2,1)S(1)}, bf16[368,512]{1,0:T(8,128)(2,1)S(1)}, u32[]{:S(2)}, u32[]{:S(2)}) collective-permute-start(bf16[368,512]{1,0:T(8,128)(2,1)S(1)} %pad_maximum_fusion.12.refs_12_), channel_id=1, source_target_pairs={{0,2},{1,3},{2,0},{3,1},{4,6},{5,7},{6,4},{7,5},{8,10},{9,11},{10,... | collective-permute-start | bytes 1130504 | tf_op jit(solution)/shard_map/ppermute | solution.py:976
  339.4 16.0 %collective-permute-start.74 = (bf16[368,512]{1,0:T(8,128)(2,1)S(1)}, bf16[368,512]{1,0:T(8,128)(2,1)S(1)}, u32[]{:S(2)}, u32[]{:S(2)}) collective-permute-start(bf16[368,512]{1,0:T(8,128)(2,1)S(1)} %pad_maximum_fusion.12.refs_12_), channel_id=1, source_target_pairs={{0,3},{1,2},{2,1},{3,0},{4,7},{5,6},{6,5},{7,4},{8,11},{9,10},{10,... | collective-permute-start | bytes 1130504 | tf_op jit(solution)/shard_map/ppermute | solution.py:984
  339.5 15.9 %collective-permute-start.75 = (bf16[368,512]{1,0:T(8,128)(2,1)S(1)}, bf16[368,512]{1,0:T(8,128)(2,1)S(1)}, u32[]{:S(2)}, u32[]{:S(2)}) collective-permute-start(bf16[368,512]{1,0:T(8,128)(2,1)S(1)} %pad_maximum_fusion.12.refs_12_), channel_id=1, source_target_pairs={{0,8},{4,12},{8,16},{12,20},{16,24},{20,28},{24,0},{28,4},{1,9},{5... | collective-permute-start | bytes 1130504 | tf_op jit(solution)/shard_map/ppermute | solution.py:883
  339.5 17.2 %collective-permute-start.76 = (bf16[368,512]{1,0:T(8,128)(2,1)S(1)}, bf16[368,512]{1,0:T(8,128)(2,1)S(1)}, u32[]{:S(2)}, u32[]{:S(2)}) collective-permute-start(bf16[368,512]{1,0:T(8,128)(2,1)S(1)} %pad_maximum_fusion.12.refs_12_), channel_id=1, source_target_pairs={{0,24},{4,28},{8,0},{12,4},{16,8},{20,12},{24,16},{28,20},{1,25},{... | collective-permute-start | bytes 1130504 | tf_op jit(solution)/shard_map/ppermute | solution.py:883
  360.2 14.7 %collective-permute-start.80 = (bf16[368,512]{1,0:T(8,128)(2,1)S(1)}, bf16[368,512]{1,0:T(8,128)(2,1)S(1)}, u32[]{:S(2)}, u32[]{:S(2)}) collective-permute-start(bf16[368,512]{1,0:T(8,128)(2,1)S(1)} %collective-permute-done.76.refs_24_), channel_id=1, source_target_pairs={{0,2},{1,3},{2,0},{3,1},{4,6},{5,7},{6,4},{7,5},{8,10},{9,11},{10,... | collective-permute-start | bytes 1130504 | tf_op jit(solution)/shard_map/ppermute | solution.py:976
  360.7 15.7 %collective-permute-start.81 = (bf16[368,512]{1,0:T(8,128)(2,1)S(1)}, bf16[368,512]{1,0:T(8,128)(2,1)S(1)}, u32[]{:S(2)}, u32[]{:S(2)}) collective-permute-start(bf16[368,512]{1,0:T(8,128)(2,1)S(1)} %pad_maximum_fusion.12.refs_12_), channel_id=1, source_target_pairs={{0,16},{4,20},{8,24},{12,28},{16,0},{20,4},{24,8},{28,12},{1,17},{... | collective-permute-start | bytes 1130504 | tf_op jit(solution)/shard_map/ppermute | solution.py:883
  379.6 17.9 %collective-permute-start.88 = (bf16[368,512]{1,0:T(8,128)(2,1)S(1)}, bf16[368,512]{1,0:T(8,128)(2,1)S(1)}, u32[]{:S(2)}, u32[]{:S(2)}) collective-permute-start(bf16[368,512]{1,0:T(8,128)(2,1)S(1)} %collective-permute-done.74.refs_15_), channel_id=1, source_target_pairs={{0,16},{4,20},{8,24},{12,28},{16,0},{20,4},{24,8},{28,12},{1,17},{... | collective-permute-start | bytes 1130504 | tf_op jit(solution)/shard_map/ppermute | solution.py:883
  380.4 20.9 %collective-permute-start.97 = (bf16[768,512]{1,0:T(8,128)(2,1)S(1)}, bf16[768,512]{1,0:T(8,128)(2,1)}, u32[]{:S(2)}, u32[]{:S(2)}) collective-permute-start(bf16[768,512]{1,0:T(8,128)(2,1)S(1)} %copy-done.53), channel_id=1, source_target_pairs={{0,4},{4,0},{8,12},{12,8},{16,20},{20,16},{24,28},{28,24},{1,5},{5... | collective-permute-start | bytes 2359304 | tf_op jit(solution)/shard_map/ppermute | solution.py:887
  380.4 17.0 %collective-permute-start.89 = (bf16[368,512]{1,0:T(8,128)(2,1)S(1)}, bf16[368,512]{1,0:T(8,128)(2,1)S(1)}, u32[]{:S(2)}, u32[]{:S(2)}) collective-permute-start(bf16[368,512]{1,0:T(8,128)(2,1)S(1)} %collective-permute-done.77.refs_17_), channel_id=1, source_target_pairs={{0,2},{1,3},{2,0},{3,1},{4,6},{5,7},{6,4},{7,5},{8,10},{9,11},{10,... | collective-permute-start | bytes 1130504 | tf_op jit(solution)/shard_map/ppermute | solution.py:976
  406.5 39.9 %collective-permute-start.107 = (bf16[176,512]{1,0:T(8,128)(2,1)S(1)}, bf16[176,512]{1,0:T(8,128)(2,1)S(1)}, u32[]{:S(2)}, u32[]{:S(2)}) collective-permute-start(bf16[176,512]{1,0:T(8,128)(2,1)S(1)} %get-tuple-element.703), channel_id=1, source_target_pairs={{0,16},{4,20},{16,0},{20,4},{8,24},{12,28},{24,8},{28,12},{1,17},{... | collective-permute-start | bytes 540680 | tf_op jit(solution)/shard_map/ppermute | solution.py:980
  407.1 39.4 %collective-permute-start.71 = (f32[32,512]{1,0:T(8,128)S(1)}, f32[32,512]{1,0:T(8,128)S(1)}, u32[]{:S(2)}, u32[]{:S(2)}) collective-permute-start(f32[32,512]{1,0:T(8,128)S(1)} %slice.607), channel_id=1, source_target_pairs={{1,0},{2,1},{3,2},{4,3},{5,4},{6,5},{7,6},{8,7},{9,8},{10,9},{11,1... | collective-permute-start | bytes 196616 | tf_op jit(solution)/shard_map/ppermute | solution.py:1276
  408.5 37.9 %collective-permute-start.104 = (bf16[288,512]{1,0:T(8,128)(2,1)S(1)}, bf16[288,512]{1,0:T(8,128)(2,1)S(1)}, u32[]{:S(2)}, u32[]{:S(2)}) collective-permute-start(bf16[288,512]{1,0:T(8,128)(2,1)S(1)} %get-tuple-element.776), channel_id=1, source_target_pairs={{0,24},{4,28},{8,0},{12,4},{16,8},{20,12},{24,16},{28,20},{1,25},{... | collective-permute-start | bytes 884744 | tf_op jit(solution)/shard_map/ppermute | solution.py:883
  412.8 33.7 %collective-permute-start.105 = (bf16[288,512]{1,0:T(8,128)(2,1)S(1)}, bf16[288,512]{1,0:T(8,128)(2,1)S(1)}, u32[]{:S(2)}, u32[]{:S(2)}) collective-permute-start(bf16[288,512]{1,0:T(8,128)(2,1)S(1)} %get-tuple-element.775), channel_id=1, source_target_pairs={{0,16},{4,20},{8,24},{12,28},{16,0},{20,4},{24,8},{28,12},{1,17},{... | collective-permute-start | bytes 884744 | tf_op jit(solution)/shard_map/ppermute | solution.py:883
  413.4 33.1 %collective-permute-start.106 = (bf16[288,512]{1,0:T(8,128)(2,1)S(1)}, bf16[288,512]{1,0:T(8,128)(2,1)S(1)}, u32[]{:S(2)}, u32[]{:S(2)}) collective-permute-start(bf16[288,512]{1,0:T(8,128)(2,1)S(1)} %get-tuple-element.774), channel_id=1, source_target_pairs={{0,8},{4,12},{8,16},{12,20},{16,24},{20,28},{24,0},{28,4},{1,9},{5... | collective-permute-start | bytes 884744 | tf_op jit(solution)/shard_map/ppermute | solution.py:883
  454.5 27.7 %collective-permute-start.110 = (bf16[288,512]{1,0:T(8,128)(2,1)S(1)}, bf16[288,512]{1,0:T(8,128)(2,1)S(1)}, u32[]{:S(2)}, u32[]{:S(2)}) collective-permute-start(bf16[288,512]{1,0:T(8,128)(2,1)S(1)} %get-tuple-element.727), channel_id=1, source_target_pairs={{0,16},{4,20},{8,24},{12,28},{16,0},{20,4},{24,8},{28,12},{1,17},{... | collective-permute-start | bytes 884744 | tf_op jit(solution)/shard_map/ppermute | solution.py:883
  455.9 26.3 %collective-permute-start.111 = (bf16[288,512]{1,0:T(8,128)(2,1)S(1)}, bf16[288,512]{1,0:T(8,128)(2,1)S(1)}, u32[]{:S(2)}, u32[]{:S(2)}) collective-permute-start(bf16[288,512]{1,0:T(8,128)(2,1)S(1)} %get-tuple-element.726), channel_id=1, source_target_pairs={{0,8},{4,12},{8,16},{12,20},{16,24},{20,28},{24,0},{28,4},{1,9},{5... | collective-permute-start | bytes 884744 | tf_op jit(solution)/shard_map/ppermute | solution.py:883
  (184 other events, 2499.4 us)

commit v3 on v2

--- a/solution.py
+++ b/solution.py
@@ -13,7 +13,8 @@
 ADAM_EPSILON = 1e-08
 C = 512
 AXES = ("band", "img")
-VMEM_BYTES = 58 * 1024 * 1024
+VMEM_MARGIN = 6 * 1024 * 1024
+VMEM_MOST = 58 * 1024 * 1024
 F32, BF16 = jnp.float32, jnp.bfloat16
 
 PIX = 1024
@@ -209,9 +210,10 @@
     return out
 
 
-def norm_stats(read, gm_ref, scal):
+def norm_stats(read, gm_ref, scal, sums=None):
     zero = jnp.zeros((8, C), F32)
-    sums = line_loop(lambda seg, line, acc: acc + fold(read(line)), (zero, zero))
+    if sums is None:
+        sums = line_loop(lambda seg, line, acc: acc + fold(read(line)), (zero, zero))
     sums = [s.sum(axis=0, keepdims=True) for s in sums]
     (totals,) = group_totals(gm_ref, scal, sums)
     means = [totals[seg] * scal.inv[seg] for seg in range(2)]
@@ -261,18 +263,32 @@
         buf_ref[35 * 32 : 35 * 32 + 16, :] = buf_ref[27 * 32 + 16 : 28 * 32, :]
 
 
+def tile_at(tile):
+    return pl.ds(pl.multiple_of(tile * 256, 256), 256)
+
+
 def tile_rows(tile, shift):
-    line = (8 * tile if tile < 3 else 26) + shift
-    return slice(line * 32, line * 32 + 256)
-
-
-def conv_tiles(buf_ref, w_ref, write):
-    for tile in range(4):
+    line = 8 * tile + jnp.where(tile == 3, 2, 0) + shift
+    return pl.ds(pl.multiple_of(line * 32, 32), 256)
+
+
+def tile_loop(body):
+    def step(tile, carry):
+        body(tile)
+        return carry
+
+    lax.fori_loop(0, 4, step, 0)
+
+
+def conv_tiles(buf_ref, w_ref, out_ref):
+    def body(tile):
         acc = None
         for shift in range(3):
             term = dot(buf_ref[tile_rows(tile, shift), :], w_ref[shift * 3 * C : (shift + 1) * 3 * C, :])
             acc = term if acc is None else acc + term
-        write(tile, acc)
+        out_ref[tile_at(tile), :] = acc
+
+    tile_loop(body)
 
 
 def gather_pieces(table_ref, src_ref, dst_ref, count):
@@ -306,35 +322,39 @@
 
 
 def load_weights(pieces, parts, table, w, small16, sems):
-    copies, last = [], len(parts) * len(pieces)
+    last = len(parts) * len(pieces)
     if len(pieces) == 1:
-        copies.append(pltpu.make_async_copy(pieces[0].at[pl.ds(0, 22 * C)], w, sems.at[0]))
+        copies = [[pltpu.make_async_copy(pieces[0].at[pl.ds(0, 22 * C)], w, sems.at[0])]]
         copy = pltpu.make_async_copy(pieces[0].at[pl.ds(22 * C, 16)], small16, sems.at[1])
-        copies[0].start()
         copy.start()
+        copies[0][0].start()
         copy.wait()
     else:
         for i, piece in enumerate(pieces):
-            for start, count in parts:
-                e = len(copies)
+
+            @pl.when(table[last] == i)
+            def _():
+                pltpu.make_async_copy(
+                    piece.at[pl.ds(parts[-1][0] + parts[-1][1], 16)], small16, sems.at[last]
+                ).start()
+
+        copies = []
+        for p, (start, count) in enumerate(parts):
+            copies.append([])
+            for i, piece in enumerate(pieces):
+                e = i * len(parts) + p
                 at = pl.multiple_of(table[e] * 16, 16)
                 copy = pltpu.make_async_copy(
                     piece.at[pl.ds(start, count)], w.at[pl.ds(at, count)], sems.at[e]
                 )
                 copy.start()
-                copies.append(copy)
-
-            @pl.when(table[last] == i)
-            def _():
-                copy = pltpu.make_async_copy(
-                    piece.at[pl.ds(parts[-1][0] + parts[-1][1], 16)], small16, sems.at[last]
-                )
-                copy.start()
+                copies[p].append(copy)
+        pltpu.make_async_copy(pieces[0].at[pl.ds(0, 16)], small16, sems.at[last]).wait()
+
+    def wait(p):
+        if p < len(copies):
+            for copy in copies[p]:
                 copy.wait()
-
-    def wait():
-        for copy in copies:
-            copy.wait()
 
     return wait
 
@@ -344,33 +364,25 @@
         gather, flags, table = refs[:3]
         blocks, refs = refs[3 : 3 + sources], refs[3 + sources :]
         pieces, refs = refs[:count], refs[count:]
-        (
-            x_out,
-            a1_out,
-            h1_out,
-            a2_out,
-            y_ref,
-            z_out,
-            q_ref,
-            k_ref,
-            v_ref,
-            stats_out,
-            small,
-            w_out,
-        ) = refs[:12]
-        slots, x_ref, h_ref, z_ref, buf, w, gm, sems, small16 = refs[12:]
+        x_out, a1_out, h1_out, a2_out, y_ref, z_out, q_ref, k_ref, v_ref, stats, small, w_out = refs[:12]
+        slots, x_ref, h_ref, z_ref, buf, w, gm, sems, small16, a1, h1, a2, x16, out_sems = refs[12:]
     else:
-        gather, scatter, flags, table = refs[:4]
-        blocks, refs = refs[4 : 4 + sources], refs[4 + sources :]
-        pieces, refs = refs[:count], refs[count:]
+        scatter, flags, table, x_in, stats = refs[:5]
+        pieces, refs = refs[5 : 5 + count], refs[5 + count :]
         own_out, oth_out = refs[:2]
         slots, x_ref, h_ref, z_ref, buf, w, gm, sems, small16, small, y_ref, q_ref, k_ref, v_ref = refs[2:]
     wait_weights = load_weights(pieces, parts, table, w, small16, sems)
     scal = Scalars(flags)
     fill_group_matrix(gm)
-    slots_to_image(gather, scal, blocks, slots, x_ref)
     small[...] = small16[...].astype(F32)
     col = columns()
+    saves = []
+
+    def save(value, out):
+        if first:
+            copy = pltpu.make_async_copy(value, out, out_sems.at[len(saves)])
+            copy.start()
+            saves.append(copy)
 
     def row(i):
         return small[i : i + 1, :]
@@ -390,84 +402,100 @@
     def read_x(line):
         return x_ref[line_rows(line), :]
 
-    means1, rstds1 = norm_stats(read_x, gm, scal)
-    activate(read_x, means1, rstds1, row(0), row(1), a1_out if first else None)
     if first:
+        slots_to_image(gather, scal, blocks, slots, x_ref)
+        means1, rstds1 = norm_stats(read_x, gm, scal)
 
         def keep_x(seg, line, carry):
-            x_out[line_rows(line), :] = read_x(line).astype(BF16)
+            x16[line_rows(line), :] = read_x(line).astype(BF16)
             return carry
 
         line_loop(keep_x, (0, 0))
-
-    wait_weights()
+        save(x16, x_out)
+    else:
+
+        def widen_x(seg, line, carry):
+            x_ref[line_rows(line), :] = x_in[line_rows(line), :].astype(F32)
+            return carry
+
+        line_loop(widen_x, (0, 0))
+        means1, rstds1 = [stats[0:1, :], stats[1:2, :]], [stats[2:3, :], stats[3:4, :]]
+    activate(read_x, means1, rstds1, row(0), row(1), a1 if first else None)
     if first:
-        save = pltpu.make_async_copy(w, w_out, sems.at[0])
-        save.start()
-
-    def write_h(tile, acc):
-        h_ref[tile * 256 : (tile + 1) * 256, :] = acc
-
-    conv_tiles(buf, w.at[0 : 9 * C], write_h)
+        save(a1, a1_out)
+    wait_weights(0)
+    if first:
+        save(w, w_out)
+
+    conv_tiles(buf, w.at[0 : 9 * C], h_ref)
 
     def finish_h(seg, line, carry):
         value = jnp.where(col < scal.lims[seg], h_ref[line_rows(line), :] + row(2), 0.0)
         h_ref[line_rows(line), :] = value
         if first:
-            h1_out[line_rows(line), :] = value
-        return carry
-
-    line_loop(finish_h, (0, 0))
+            h1[line_rows(line), :] = value
+        return carry + fold(value)
+
+    zero = jnp.zeros((8, C), F32)
 
     def read_h(line):
         return h_ref[line_rows(line), :]
 
-    means2, rstds2 = norm_stats(read_h, gm, scal)
-    activate(read_h, means2, rstds2, row(3), row(4), a2_out if first else None)
-    conv_tiles(buf, w.at[9 * C : 18 * C], write_h)
+    means2, rstds2 = norm_stats(read_h, gm, scal, line_loop(finish_h, (zero, zero)))
+    if first:
+        save(h1, h1_out)
+    activate(read_h, means2, rstds2, row(3), row(4), a2 if first else None)
+    if first:
+        save(a2, a2_out)
+    wait_weights(1)
+    conv_tiles(buf, w.at[9 * C : 18 * C], h_ref)
 
     def finish_y(seg, line, carry):
         value = jnp.where(
             col < scal.lims[seg], read_x(line) + (h_ref[line_rows(line), :] + row(5)), 0.0
         )
         y_ref[line_rows(line), :] = value
-        return carry
-
-    line_loop(finish_y, (0, 0))
+        return carry + fold(value)
 
     def read_y(line):
         return y_ref[line_rows(line), :]
 
-    means3, rstds3 = norm_stats(read_y, gm, scal)
+    means3, rstds3 = norm_stats(read_y, gm, scal, line_loop(finish_y, (zero, zero)))
 
     def third(seg, line, carry):
         normed = (read_y(line) - means3[seg]) * rstds3[seg] * row(6) + row(7)
-        value = jnp.where(col < scal.lims[seg], normed, 0.0).astype(BF16)
-        z_ref[line_rows(line), :] = value
-        if first:
-            z_out[line_rows(line), :] = value
+        z_ref[line_rows(line), :] = jnp.where(col < scal.lims[seg], normed, 0.0).astype(BF16)
         return carry
 
     line_loop(third, (0, 0))
-    for tile in range(4):
-        at = slice(tile * 256, (tile + 1) * 256)
+    if first:
+        save(z_ref, z_out)
+
+    def project(tile):
+        at = tile_at(tile)
         rows = z_ref[at, :]
         q_ref[at, :] = (dot(rows, w[18 * C : 19 * C, :]) + row(8)).astype(BF16)
         k_ref[at, :] = dot(rows, w[19 * C : 20 * C, :]).astype(BF16)
         v_ref[at, :] = (dot(rows, w[20 * C : 21 * C, :]) + row(9)).astype(BF16)
+
+    tile_loop(project)
     if first:
         for i, pair in enumerate((means1, rstds1, means2, rstds2, means3, rstds3)):
-            stats_out[2 * i : 2 * i + 1, :] = pair[0]
-            stats_out[2 * i + 1 : 2 * i + 2, :] = pair[1]
-        stats_out[12:16, :] = jnp.zeros((4, C), F32)
-        save.wait()
+            stats[2 * i : 2 * i + 1, :] = pair[0]
+            stats[2 * i + 1 : 2 * i + 2, :] = pair[1]
+        stats[12:16, :] = jnp.zeros((4, C), F32)
+        for copy in saves:
+            copy.wait()
         return
-    biases = key_bias(scal)
-    for tile in range(4):
-        at = slice(tile * 256, (tile + 1) * 256)
-        prob = probabilities(q_ref[at, :], k_ref, biases[tile // 3]).astype(BF16)
+    bias = key_bias(scal)
+
+    def attend(tile):
+        at = tile_at(tile)
+        prob = probabilities(q_ref[at, :], k_ref, bias(tile)).astype(BF16)
         mixed = dot(prob, v_ref[...]).astype(BF16)
         y_ref[at, :] = y_ref[at, :] + (dot(mixed, w[21 * C : 22 * C, :]) + row(10))
+
+    tile_loop(attend)
     y_ref[PIX : PIX + 8, :] = jnp.zeros((8, C), F32)
     image_to_slots(scatter, y_ref, slots, own_out, oth_out)
 
@@ -481,7 +509,7 @@
     large = scal.is_l == 1
     row0 = jnp.where(ok0 | (ok1 & large), 0.0, -1e30).astype(F32)
     row1 = jnp.where(ok1 | (ok0 & large), 0.0, -1e30).astype(F32)
-    return row0, row1
+    return lambda tile: jnp.where(tile == 3, row1, row0)
 
 
 def probabilities(q, k_ref, bias):
@@ -505,21 +533,39 @@
     weights,
     *refs,
 ):
-    blocks = refs[:-16]
-    own_out, oth_out, dy_out, dy16_out, grads_out, sums_out = refs[-16:-10]
-    image, slots, g_ref, o_ref, d_ref, dk_acc, dv_acc, wp, gm, sems = refs[-10:]
-    copy = pltpu.make_async_copy(weights.at[pl.ds(18 * C, 4 * C)], wp, sems.at[0])
-    copy.start()
+    blocks = refs[:-23]
+    own_out, oth_out, dy_out, dy16_out, grads_out, sums_out = refs[-23:-17]
+    image, slots, g_ref, o_ref, d_ref, dk_acc, dv_acc, wp, gm, sems = refs[-17:-7]
+    loaded = [
+        (weights.at[pl.ds(18 * C, 4 * C)], wp),
+        (q, refs[-7]),
+        (k, refs[-6]),
+        (v, refs[-5]),
+        (y, refs[-4]),
+        (z, refs[-3]),
+    ]
+    loads = [pltpu.make_async_copy(a, b, sems.at[i]) for i, (a, b) in enumerate(loaded)]
+    for load in loads:
+        load.start()
+    q, k, v, y, z, grads, own_rows = refs[-7:]
+    oth_rows = own_rows.at[pl.ds(own_out.shape[0], own_out.shape[0])]
+    own_rows = own_rows.at[pl.ds(0, own_out.shape[0])]
+    stores = [(own_rows, own_out), (oth_rows, oth_out), (grads, grads_out)]
+    stores = [pltpu.make_async_copy(a, b, sems.at[6 + i]) for i, (a, b) in enumerate(stores)]
     scal = Scalars(flags)
     fill_group_matrix(gm)
-    biases = key_bias(scal)
+    bias = key_bias(scal)
     slots_to_image(gather, scal, blocks, slots, g_ref)
-    copy.wait()
+    for load in loads[:5]:
+        load.wait()
     scaling = C**-0.5
-    for tile in range(4):
-        at = slice(tile * 256, (tile + 1) * 256)
+    dk_acc[...] = jnp.zeros(MAP, F32)
+    dv_acc[...] = jnp.zeros(MAP, F32)
+
+    def attend(tile):
+        at = tile_at(tile)
         q_t = q[at, :]
-        prob = probabilities(q_t, k, biases[tile // 3])
+        prob = probabilities(q_t, k, bias(tile))
         prob16 = prob.astype(BF16)
         mixed = dot(prob16, v[...]).astype(BF16)
         o_ref[at, :] = mixed
@@ -529,28 +575,30 @@
         inner = jnp.sum(prob * d_prob, axis=1, keepdims=True)
         d_score = (prob * (d_prob - inner)).astype(BF16)
         d_ref[at, 0:C] = (scaling * dot(d_score, k[...])).astype(BF16)
-        dk = dot_tn(d_score, q_t)
-        dv = dot_tn(prob16, d_mixed)
-        if tile == 0:
-            dk_acc[...] = dk
-            dv_acc[...] = dv
-        else:
-            dk_acc[...] += dk
-            dv_acc[...] += dv
+        dk_acc[...] += dot_tn(d_score, q_t)
+        dv_acc[...] += dot_tn(prob16, d_mixed)
+
+    tile_loop(attend)
     d_ref[:, C : 2 * C] = (scaling * dk_acc[...]).astype(BF16)
     d_ref[:, 2 * C : 3 * C] = dv_acc[...].astype(BF16)
     image[PIX : PIX + 8, :] = jnp.zeros((8, C), F32)
-    image_to_slots(scatter, image, slots, own_out, oth_out)
+    image_to_slots(scatter, image, slots, own_rows, oth_rows)
+    stores[0].start()
+    stores[1].start()
+    loads[5].wait()
     for part in range(3):
-        grads_out[part * C : (part + 1) * C, :] = dot_tn(
-            z[...], d_ref[:, part * C : (part + 1) * C]
-        ).astype(BF16)
-    grads_out[3 * C : 4 * C, :] = dot_tn(o_ref[...], g_ref[...].astype(BF16)).astype(BF16)
-    for tile in range(4):
-        at = slice(tile * 256, (tile + 1) * 256)
+        grads[part * C : (part + 1) * C, :] = dot_tn(z[...], d_ref[:, part * C : (part + 1) * C]).astype(
+            BF16
+        )
+    grads[3 * C : 4 * C, :] = dot_tn(o_ref[...], g_ref[...].astype(BF16)).astype(BF16)
+    stores[2].start()
+    def back_to_norm(tile):
+        at = tile_at(tile)
         acc = dot_nt(d_ref[at, 0:C], wp[0:C, :])
         acc = acc + dot_nt(d_ref[at, C : 2 * C], wp[C : 2 * C, :])
         image[at, :] = acc + dot_nt(d_ref[at, 2 * C : 3 * C], wp[2 * C : 3 * C, :])
+
+    tile_loop(back_to_norm)
     col = columns()
     means = (stats[8:9, :], stats[9:10, :])
     rstds = (stats[10:11, :], stats[11:12, :])
@@ -575,9 +623,9 @@
     ones, cross = group_totals(
         gm, scal, [got[0][0] * gain, got[1][0] * gain, got[0][1] * gain, got[1][1] * gain]
     )
+    sums_out[...] = jnp.zeros((16, C), F32)
     for i, part in enumerate((1, 0, 2, 3, 4)):
-        sums_out[i : i + 1, :] = got[0][part] + got[1][part]
-    sums_out[5:8, :] = jnp.zeros((3, C), F32)
+        sums_out[6 + i : 7 + i, :] = got[0][part] + got[1][part]
 
     def back(seg, line, carry):
         at = line_rows(line)
@@ -591,6 +639,8 @@
         return carry
 
     line_loop(back, (0, 0))
+    for store in stores:
+        store.wait()
 
 
 def fill_gradient_buffer(buf, scal, grad_ref):
@@ -605,73 +655,85 @@
 def weight_grad_kernel(conv, split, *refs):
     if not split:
         flags, act, grad, w_out, sums_out, buf, act_t = refs
-    elif conv == 1:
-        flags, act, grad, proj, kept, sent, early, sums_out, buf, act_t = refs
     else:
-        flags, act, grad, early, kept, sent, sums_out, buf, act_t = refs
+        flags, act, grad, more = refs[:4]
+        planes, refs = refs[4:8], refs[8:]
+        early_out = refs[0] if conv == 1 else None
+        sums_out, buf, act_t, rows, sems = refs[conv:]
+        kept, sent = planes[:2], planes[2:]
+        offset = 2 * C if conv == 1 else 0
+        more_at = 9 * C - offset
+        load = pltpu.make_async_copy(more, rows.at[pl.ds(more_at, more.shape[0])], sems.at[4])
+        load.start()
     scal = Scalars(flags)
-
-    def put(unit, value16):
-        if split and conv == 1 and unit < 44:
-            early[(unit - 36) * 128 : (unit - 35) * 128, :] = value16
-            return
-        if not split:
-            unit -= 36 * conv
-            w_out[unit * 128 : (unit + 1) * 128, :] = value16
-            return
-        row = (unit // 22 % 2) * 1408 + unit % 11 * 128
-        mine = scal.core == unit % 22 // 11
-
-        @pl.when(mine)
-        def _():
-            kept[row : row + 128, :] = value16
-
-        @pl.when(jnp.logical_not(mine))
-        def _():
-            sent[row : row + 128, :] = value16
-
-    if split and conv == 1:
-        for i in range(16):
-            put(72 + i, proj[i * 128 : (i + 1) * 128, :])
-    elif split:
-        for i in range(8):
-            put(36 + i, early[i * 128 : (i + 1) * 128, :])
     fill_gradient_buffer(buf, scal, grad)
     for tile in range(4):
         at = slice(tile * 256, (tile + 1) * 256)
         act_t[:, at] = act[at, :].T
+
+    def send_out(run):
+        plane, core = run // 2, run % 2
+        source = rows.at[pl.ds(run * 1408, 1408)]
+
+        @pl.when(scal.core == core)
+        def _():
+            pltpu.make_async_copy(source, kept[plane], sems.at[run]).start()
+
+        @pl.when(scal.core != core)
+        def _():
+            pltpu.make_async_copy(source, sent[plane], sems.at[run]).start()
+
+    ready = {0: (3,) if conv == 0 else (2, 3), 1: (2,) if conv == 0 else (1,), 2: (0, 1) if conv == 0 else (0,)}
     for shift in range(3):
         seg0 = slice(shift * 32, shift * 32 + 768)
         seg1 = slice((26 + shift) * 32, (26 + shift) * 32 + 256)
         for part in range(3):
             cols = slice(part * C, (part + 1) * C)
+            value = dot(act_t[:, 0:768], buf[seg0, cols]) + dot(act_t[:, 768:1024], buf[seg1, cols])
             tap = 3 * (2 - shift) + (2 - part)
-            value = dot(act_t[:, 0:768], buf[seg0, cols]) + dot(act_t[:, 768:1024], buf[seg1, cols])
-            value16 = value.astype(BF16)
-            for i in range(4):
-                put(36 * conv + 4 * tap + i, value16[i * 128 : (i + 1) * 128])
+            if not split:
+                w_out[tap * C : (tap + 1) * C, :] = value.astype(BF16)
+            elif conv == 1 and tap < 2:
+                early_out[tap * C : (tap + 1) * C, :] = value.astype(BF16)
+            else:
+                rows[tap * C - offset : (tap + 1) * C - offset, :] = value.astype(BF16)
+        if split:
+            if shift == 0:
+                load.wait()
+            for run in ready[shift]:
+                send_out(run)
     zero = jnp.zeros((8, C), F32)
     got = line_loop(
         lambda seg, line, acc: acc + fold(grad[line_rows(line), :].astype(F32)), (zero, zero)
     )
-    sums_out[...] = jnp.zeros((8, C), F32)
-    sums_out[0:1, :] = (got[0] + got[1]).sum(axis=0, keepdims=True)
+    sums_out[...] = jnp.zeros((16, C), F32)
+    sums_out[3 * conv + 2 : 3 * conv + 3, :] = (got[0] + got[1]).sum(axis=0, keepdims=True)
+    if split:
+        for run in range(4):
+            pltpu.make_async_copy(rows.at[pl.ds(run * 1408, 1408)], kept[run // 2], sems.at[run]).wait()
 
 
 def data_grad_kernel(last, conv, *refs):
     if last:
         scatter, flags, grad, feat, dy, stats, small, weights, own_out, oth_out, sums_out = refs[:11]
-        dn, slots, buf, w, gm, sems = refs[11:]
+        dn, slots, buf, w, gm, sems, feat_v, dy_v = refs[11:]
     else:
         flags, grad, feat, stats, small, weights, grad_out, sums_out = refs[:8]
-        dn, buf, w, gm, sems = refs[8:]
-    copy = pltpu.make_async_copy(weights.at[pl.ds(conv * 9 * C, 9 * C)], w, sems.at[0])
-    copy.start()
+        dn, buf, w, gm, sems, feat_v = refs[8:]
+    copies = [pltpu.make_async_copy(weights.at[pl.ds(conv * 9 * C, 9 * C)], w, sems.at[0])]
+    copies.append(pltpu.make_async_copy(feat, feat_v, sems.at[1]))
+    if last:
+        copies.append(pltpu.make_async_copy(dy, dy_v, sems.at[2]))
+        dy = dy_v
+    feat = feat_v
+    for copy in copies:
+        copy.start()
     scal = Scalars(flags)
     fill_group_matrix(gm)
     fill_gradient_buffer(buf, scal, grad)
-    copy.wait()
-    for tile in range(4):
+    copies[0].wait()
+
+    def transposed(tile):
         acc = None
         for shift in range(3):
             for part in range(3):
@@ -680,7 +742,11 @@
                     buf[tile_rows(tile, shift), part * C : (part + 1) * C], w[tap * C : (tap + 1) * C, :]
                 )
                 acc = term if acc is None else acc + term
-        dn[tile * 256 : (tile + 1) * 256, :] = acc
+        dn[tile_at(tile), :] = acc
+
+    tile_loop(transposed)
+    for copy in copies[1:]:
+        copy.wait()
     base = 4 * conv
     means = (stats[base : base + 1, :], stats[base + 1 : base + 2, :])
     rstds = (stats[base + 2 : base + 3, :], stats[base + 3 : base + 4, :])
@@ -701,9 +767,9 @@
     ones, cross = group_totals(
         gm, scal, [got[0][0] * gain, got[1][0] * gain, got[0][1] * gain, got[1][1] * gain]
     )
-    sums_out[...] = jnp.zeros((8, C), F32)
-    sums_out[0:1, :] = got[0][1] + got[1][1]
-    sums_out[1:2, :] = got[0][0] + got[1][0]
+    sums_out[...] = jnp.zeros((16, C), F32)
+    sums_out[3 * conv : 3 * conv + 1, :] = got[0][1] + got[1][1]
+    sums_out[3 * conv + 1 : 3 * conv + 2, :] = got[0][0] + got[1][0]
 
     def back(seg, line, carry):
         at = line_rows(line)
@@ -726,20 +792,25 @@
 
 SMEM = pl.BlockSpec(memory_space=pltpu.SMEM)
 VMEM = pl.BlockSpec(memory_space=pltpu.VMEM)
-ANY = pl.BlockSpec(memory_space=pl.ANY)
-
-
-def call(kernel, name, in_specs, outs, scratch, flops, args, out_specs=None):
+HBM = pl.BlockSpec(memory_space=pltpu.HBM)
+
+
+def call(kernel, name, in_specs, outs, scratch, flops, args, out_specs=None, limit=None):
     moved = sum(int(np.prod(a.shape)) * a.dtype.itemsize for a in args)
     moved += sum(int(np.prod(s)) * jnp.dtype(d).itemsize for s, d in outs)
+    out_specs = out_specs or [VMEM] * len(outs)
+    held = [(a.shape, a.dtype) for a, spec in zip(args, in_specs) if spec is VMEM]
+    held += [out for out, spec in zip(outs, out_specs) if spec is VMEM]
+    held += [(s.shape, s.dtype) for s in scratch if s.memory_space == pltpu.VMEM]
+    used = sum(int(np.prod(s)) * jnp.dtype(d).itemsize for s, d in held)
     return pl.pallas_call(
         kernel,
         name=name,
         out_shape=[jax.ShapeDtypeStruct(s, d) for s, d in outs],
         in_specs=in_specs,
-        out_specs=out_specs or [VMEM] * len(outs),
+        out_specs=out_specs,
         scratch_shapes=scratch,
-        compiler_params=pltpu.CompilerParams(vmem_limit_bytes=VMEM_BYTES),
+        compiler_params=pltpu.CompilerParams(vmem_limit_bytes=limit or used + VMEM_MARGIN),
         cost_estimate=pl.CostEstimate(flops=int(flops), bytes_accessed=moved, transcendentals=0),
     )(*args)
 
@@ -749,9 +820,10 @@
 BUF = pltpu.VMEM((BUF_LINES * 32, 3 * C), BF16)
 
 
-def run_features(first, plan, tables, blocks, pieces, parts, table):
+def run_features(first, plan, tables, x, pieces, parts, table):
     gather, scatter, flags = tables
     slot_rows = plan.n_band * plan.piece
+    count = len(pieces)
     scratch = [
         pltpu.VMEM((slot_rows + SLOT_PAD, C), F32),
         pltpu.VMEM(MAP, F32),
@@ -760,10 +832,9 @@
         BUF,
         pltpu.VMEM((22 * C, C), BF16),
         pltpu.VMEM((C, C), BF16),
-        pltpu.SemaphoreType.DMA((len(parts) * len(pieces) + 1,)),
+        pltpu.SemaphoreType.DMA((len(parts) * count + 1,)),
         pltpu.VMEM((16, C), BF16),
     ]
-    count = len(pieces)
     if first:
         outs = [
             (MAP, BF16),
@@ -780,19 +851,27 @@
             ((22 * C, C), BF16),
         ]
         return call(
-            functools.partial(features_kernel, True, len(blocks), count, parts),
+            functools.partial(features_kernel, True, len(x), count, parts),
             "features_first",
-            [SMEM] * 3 + [VMEM] * len(blocks) + [ANY] * count,
+            [SMEM] * 3 + [VMEM] * len(x) + [HBM] * count,
             outs,
-            scratch,
+            scratch
+            + [
+                pltpu.VMEM(MAP, BF16),
+                pltpu.VMEM(MAP, F32),
+                pltpu.VMEM(MAP, BF16),
+                pltpu.VMEM(MAP, BF16),
+                pltpu.SemaphoreType.DMA((6,)),
+            ],
             26 * MICROSECOND,
-            (gather, flags, table, *blocks, *pieces),
-            out_specs=[VMEM] * 11 + [ANY],
+            (gather, flags, table, *x, *pieces),
+            out_specs=[HBM] * 4 + [VMEM, HBM] + [VMEM] * 5 + [HBM],
+            limit=VMEM_MOST,
         )
     return call(
-        functools.partial(features_kernel, False, len(blocks), count, parts),
+        functools.partial(features_kernel, False, 0, count, parts),
         "forward_again",
-        [SMEM] * 4 + [VMEM] * len(blocks) + [ANY] * count,
+        [SMEM] * 3 + [VMEM] * 2 + [HBM] * count,
         [((slot_rows // 2, C), BF16)] * 2,
         scratch
         + [
@@ -803,7 +882,8 @@
             pltpu.VMEM(MAP, BF16),
         ],
         28 * MICROSECOND,
-        (gather, scatter, flags, table, *blocks, *pieces),
+        (scatter, flags, table, *x, *pieces),
+        limit=VMEM_MOST,
     )
 
 
@@ -813,14 +893,14 @@
     return call(
         attend_both_kernel,
         "attend_both",
-        [SMEM] * 3 + [VMEM] * 7 + [ANY] + [VMEM] * len(blocks),
+        [SMEM] * 3 + [HBM] * 5 + [VMEM] * 2 + [HBM] + [VMEM] * len(blocks),
         [
             ((slot_rows // 2, C), BF16),
             ((slot_rows // 2, C), BF16),
             (MAP, F32),
             (MAP, BF16),
             ((4 * C, C), BF16),
-            ((8, C), F32),
+            ((16, C), F32),
         ],
         [
             pltpu.VMEM((PIX + 8, C), F32),
@@ -832,50 +912,73 @@
             pltpu.VMEM(MAP, F32),
             pltpu.VMEM((4 * C, C), BF16),
             pltpu.VMEM((C, C), BF16),
-            pltpu.SemaphoreType.DMA((1,)),
+            pltpu.SemaphoreType.DMA((9,)),
+            pltpu.VMEM(MAP, BF16),
+            pltpu.VMEM(MAP, BF16),
+            pltpu.VMEM(MAP, BF16),
+            pltpu.VMEM(MAP, F32),
+            pltpu.VMEM(MAP, BF16),
+            pltpu.VMEM((4 * C, C), BF16),
+            pltpu.VMEM((slot_rows, C), BF16),
         ],
         24 * MICROSECOND,
         (gather, scatter, flags, q, k, v, y, z, stats, small, weights, *blocks),
+        out_specs=[HBM] * 2 + [VMEM] * 2 + [HBM, VMEM],
+        limit=VMEM_MOST,
     )
 
 
 def run_weight_grad(tables, conv, act, grad, more=None):
-    split = more is not None
-    outs = [((2816, C), BF16)] * 2 if split else [((9 * C, C), BF16)]
-    if split and conv == 1:
-        outs.append(((2 * C, C), BF16))
+    scratch = [BUF, pltpu.VMEM((C, PIX), BF16)]
+    name = "weight_grad_one" if conv == 0 else "weight_grad_two"
+    if more is None:
+        return call(
+            functools.partial(weight_grad_kernel, conv, False),
+            name,
+            [SMEM, VMEM, VMEM],
+            [((9 * C, C), BF16), ((16, C), F32)],
+            scratch,
+            9 * MICROSECOND,
+            (tables[2], act, grad),
+        )
+    early = [((2 * C, C), BF16)] if conv == 1 else []
     return call(
-        functools.partial(weight_grad_kernel, conv, split),
-        "weight_grad_one" if conv == 0 else "weight_grad_two",
-        [SMEM, VMEM, VMEM] + [VMEM] * split,
-        outs + [((8, C), F32)],
-        [BUF, pltpu.VMEM((C, PIX), BF16)],
-        12 * MICROSECOND,
-        (tables[2], act, grad) + ((more,) if split else ()),
+        functools.partial(weight_grad_kernel, conv, True),
+        name,
+        [SMEM, VMEM, VMEM, HBM],
+        [((1408, C), BF16)] * 4 + early + [((16, C), F32)],
+        scratch + [pltpu.VMEM((5632, C), BF16), pltpu.SemaphoreType.DMA((5,))],
+        9 * MICROSECOND,
+        (tables[2], act, grad, more),
+        out_specs=[HBM] * 4 + [VMEM] * len(early) + [VMEM],
+        limit=VMEM_MOST,
     )
 
 
 def run_data_grad(tables, conv, grad, feat, stats, small, weights, dy=None, half=None):
     last = dy is not None
-    scratch = [BUF, pltpu.VMEM((9 * C, C), BF16), pltpu.VMEM((C, C), BF16), pltpu.SemaphoreType.DMA((1,))]
+    scratch = [BUF, pltpu.VMEM((9 * C, C), BF16), pltpu.VMEM((C, C), BF16), pltpu.SemaphoreType.DMA((3,))]
+    scratch.append(pltpu.VMEM(MAP, feat.dtype))
     if last:
         outs = [((half, C), BF16)] * 2
         scratch = [pltpu.VMEM((PIX + 8, C), F32), pltpu.VMEM((2 * half, C), F32)] + scratch
+        scratch.append(pltpu.VMEM(MAP, F32))
         args = (tables[1], tables[2], grad, feat, dy, stats, small, weights)
-        specs = [SMEM, SMEM] + [VMEM] * 5 + [ANY]
+        specs = [SMEM, SMEM, VMEM, HBM, HBM, VMEM, VMEM, HBM]
     else:
         outs = [(MAP, BF16)]
         scratch = [pltpu.VMEM(MAP, F32)] + scratch
         args = (tables[2], grad, feat, stats, small, weights)
-        specs = [SMEM] + [VMEM] * 4 + [ANY]
+        specs = [SMEM, VMEM, HBM, VMEM, VMEM, HBM]
     return call(
         functools.partial(data_grad_kernel, last, conv),
         "data_grad_one" if conv == 0 else "data_grad_two",
         specs,
-        outs + [((8, C), F32)],
+        outs + [((16, C), F32)],
         scratch,
         12 * MICROSECOND,
         args,
+        limit=VMEM_MOST,
     )
 
 
@@ -1030,22 +1133,22 @@
     return lax.dynamic_index_in_dim(value, index, axis, keepdims=False)
 
 
-def planes_of(rows):
-    return rows.reshape(2, 2, 2, 352, C)
-
-
-def add_part(kept, got, plane, axis, index):
-    both = part(planes_of(kept)[plane], axis, index).astype(F32)
-    return (both + part(planes_of(got)[plane], axis, index).astype(F32)).astype(BF16)
-
-
-def send_halves(here, kept, got):
-    return over_x(add_part(kept, got, 0, 1, 1 - here.x)), over_y(add_part(kept, got, 1, 0, 1 - here.y))
+def add_part(kept, got, axis, index):
+    both = [part(value.reshape(2, 2, 352, C), axis, index).astype(F32) for value in (kept, got)]
+    return (both[0] + both[1]).astype(BF16)
+
+
+def halves_to_send(here, kept, got):
+    return add_part(kept[0], got[0], 1, 1 - here.x), add_part(kept[1], got[1], 0, 1 - here.y)
+
+
+def send_halves(a, b):
+    return over_x(a), over_y(b)
 
 
 def add_halves(here, kept, got, got_a, got_b):
-    a = add_part(kept, got, 0, 1, here.x).astype(F32) + got_a.astype(F32)
-    b = add_part(kept, got, 1, 0, here.y).astype(F32) + got_b.astype(F32)
+    a = add_part(kept[0], got[0], 1, here.x).astype(F32) + got_a.astype(F32)
+    b = add_part(kept[1], got[1], 0, here.y).astype(F32) + got_b.astype(F32)
     return a.astype(BF16), b.astype(BF16)
 
 
@@ -1092,8 +1195,7 @@
 
 def sum_over_plane(value):
     value = value + over_core(value)
-    value = value + over_x(value)
-    return value + over_y(value)
+    return (value + over_x(value)) + (over_y(value) + over_corner(value))
 
 
 def adam(params, first, second, grad, step_count, rate):
@@ -1151,7 +1253,19 @@
         )
         state = (params, first_moment, second_moment)
         far = [lax.dynamic_slice_in_dim(rows_of, 176 - here.owner, 176, 0).astype(BF16) for rows_of in state]
-        values, far = stage((gather.second(values), jnp.concatenate(far, axis=1)))
+        head = jnp.concatenate([rows_of[rows - count :] for rows_of in state], axis=1)
+        near = [rows_of[:176] for rows_of in state]
+        single_state = [rows_of[singles : singles + 16] for rows_of in state]
+        table_again = gather_table(
+            here,
+            lambda z, place: [
+                (8 * (z & 1) + place) * 22 + jnp.where(z < 2, 0, 11),
+                (8 * (z | 2) + place) * 22 + jnp.where(z < 2, 11, 0),
+            ],
+        )
+        values, far, head, near, single_state, table_again = stage(
+            (gather.second(values), jnp.concatenate(far, axis=1), head, near, single_state, table_again)
+        )
         values, others = stage((gather.third(values), gather.others(values, 4)))
         cot_sent, values = stage((cot_sent, values))
         cot_got = to_chips(plan, cot_sent)
@@ -1169,8 +1283,9 @@
     cot_got, y = stage((cot_got, y))
     cot_blocks = to_cores(plan, cot_got)
     if here.planes:
-        cot_blocks, far = stage((cot_blocks, far))
+        cot_blocks, far, head = stage((cot_blocks, far, head))
         far = over_two_planes(far)
+        before = lax.ppermute(head, AXES, [(o, o + 1) for o in range(last)])
     out_own, out_oth, dy, dy16, g_proj, sums3 = run_attend_both(
         plan, tables, q, k, v, y, z, cot_blocks, stats, small, weights
     )
@@ -1180,73 +1295,65 @@
             update, _, _ = adam(*state, grad, step_count, step_rate)
             return (state[0] - update).astype(BF16)
 
-        dy16, far, out_oth = stage((dy16, far, out_oth))
+        dy16, far, before, out_oth = stage((dy16, far, before, out_oth))
         out_got = over_core(out_oth)
-        kept, sent, early, sums_b2 = run_weight_grad(tables, 1, a2, dy16, g_proj)
+        *kept, early, sums_b2 = run_weight_grad(tables, 1, a2, dy16, g_proj)
+        kept, sent = kept[:2], kept[2:]
         dy16, kept, sent, out_got = stage((dy16, kept, sent, out_got))
-        got = over_core(sent)
+        got = [over_core(value) for value in sent]
         out_got = from_chips(plan, merge_cores(plan, position, out_own, out_got))
         dh1, sums_n2 = run_data_grad(tables, 1, dy16, h1, stats, small, weights)
         dh1, kept, got = stage((dh1, kept, got))
-        halves = send_halves(here, kept, got)
+        halves = send_halves(*halves_to_send(here, kept, got))
         high = kept, got
-        kept, sent, sums_b1 = run_weight_grad(tables, 0, a1, dh1, early)
+        *kept, sums_b1 = run_weight_grad(tables, 0, a1, dh1, early)
+        kept, sent = kept[:2], kept[2:]
         kept, sent, high, halves, out_got = stage((kept, sent, high, halves, out_got))
-        got = over_core(sent)
+        got = [over_core(value) for value in sent]
         high = add_halves(here, *high, *halves)
         quarters = send_quarters(*quarters_to_send(here, *high))
-        kept, got, high = stage((kept, got, high))
         low = kept, got
-        halves = send_halves(here, *low)
-        high, quarters, dh1 = stage((high, quarters, dh1))
+        low, halves, high, quarters, dh1 = stage((low, halves_to_send(here, *low), high, quarters, dh1))
+        halves = send_halves(*halves)
         high = by_plane(False, *add_quarters(here, *high, *quarters))
-        high, dh1, head = stage((high, dh1, [rows_of[rows - count :] for rows_of in state]))
+        high, dh1 = stage((high, dh1))
         high_got = send_planes(here, high)
         dx_own, dx_oth, sums_n1 = run_data_grad(
             tables, 0, dh1, x_img, stats, small, weights, dy=dy, half=out_own.shape[0]
         )
-        low, halves, high, high_got, sums_n1, head = stage((low, halves, high, high_got, sums_n1, head))
+        low, halves, high, high_got, sums_n1 = stage((low, halves, high, high_got, sums_n1))
         low = add_halves(here, *low, *halves)
-        low, low_sent, sums_n1, head = stage((low, quarters_to_send(here, *low), sums_n1, head))
+        low, low_sent, sums_n1 = stage((low, quarters_to_send(here, *low), sums_n1))
         quarters = send_quarters(*low_sent)
-        before = lax.ppermute(jnp.concatenate(head, axis=1), AXES, [(o, o + 1) for o in range(last)])
-        small_rows = jnp.concatenate(
-            [sums_n1[0:2], sums_b1[0:1], sums_n2[0:2], sums_b2[0:1], sums3[0:5]], axis=0
-        )
-        small_sum = sum_over_plane(jnp.pad(small_rows, ((0, 5), (0, 0))))
-        low, quarters, small_sum, before = stage((low, quarters, small_sum, before))
+        small_sum = sum_over_plane(sums_n1 + sums_b1 + sums_n2 + sums_b2 + sums3)
+        low, quarters, small_sum = stage((low, quarters, small_sum))
         low = by_plane(True, *add_quarters(here, *low, *quarters))
         low_got = send_planes(here, low, small_sum)
         low, low_got, before, far, high, high_got = stage((low, low_got, before, far, high, high_got))
         low, high = add_planes(here, low, low_got, small_sum), add_planes(here, high, high_got)
         low, small_sum = low[:176], low[176:]
         own = [
-            aligned(before[:, i * C : (i + 1) * C], rows_of[:176], 176) for i, rows_of in enumerate(state)
+            aligned(before[:, i * C : (i + 1) * C], rows_of, 176) for i, rows_of in enumerate(near)
         ]
         far = [far[:, i * C : (i + 1) * C].astype(F32) for i in range(3)]
         first_two = here.z < 2
         block = [
             stepped([jnp.where(first_two, a, b) for a, b in zip(own, far)], low),
             stepped([jnp.where(first_two, b, a) for a, b in zip(own, far)], high),
-            stepped([rows_of[singles : singles + 16] for rows_of in state], small_sum),
+            stepped(single_state, small_sum),
         ]
         gather = Gather(jnp.concatenate(block, axis=0))
-        values = stage(gather.first())
-        values, others, dx_oth = stage((gather.second(values), gather.others(values, 4), dx_oth))
-        values, more, dx_got = stage((gather.third(values), gather.others(values[4:], 6), over_core(dx_oth)))
-        others = others + more
+        values, dx_got = stage((gather.first(), over_core(dx_oth)))
         dx_sent = merge_cores(plan, position, dx_own, dx_got)
-        pieces = gather.pieces(values, others + gather.others(values[10:], 6))
+        values, others, dx_sent, first_out = stage(
+            (gather.second(values), gather.others(values, 4), dx_sent, to_bands(plan, position, out_got))
+        )
+        values, more = stage((gather.third(values), gather.others(values[4:], 6)))
+        pieces = gather.pieces(values, others + more + gather.others(values[10:], 6))
         pieces, dx_sent = stage((pieces, dx_sent))
         dx_got = from_chips(plan, dx_sent)
         far = over_two_planes(jnp.where(here.z < 2, high, low).astype(BF16))
-        table = gather_table(
-            here,
-            lambda z, place: [
-                (8 * (z & 1) + place) * 22 + jnp.where(z < 2, 0, 11),
-                (8 * (z | 2) + place) * 22 + jnp.where(z < 2, 11, 0),
-            ],
-        )
+        table = table_again
         parts = ((0, 176), (176, 176))
     else:
         out_got = from_chips(plan, merge_cores(plan, position, out_own, over_core(out_oth)))
@@ -1257,9 +1364,7 @@
             tables, 0, dh1, x_img, stats, small, weights, dy=dy, half=out_own.shape[0]
         )
         dx_got = from_chips(plan, merge_cores(plan, position, dx_own, over_core(dx_oth)))
-        small_rows = jnp.concatenate(
-            [sums_n1[0:2], sums_b1[0:1], sums_n2[0:2], sums_b2[0:1], sums3[0:5]], axis=0
-        )
+        small_rows = sums_n1 + sums_b1 + sums_n2 + sums_b2 + sums3
         full = jnp.concatenate([g_w1, g_w2, g_proj, small_rows.astype(BF16)], axis=0)
         full = jnp.pad(full, ((0, rows * count - full.shape[0]), (0, 0)))
         grad = lax.psum_scatter(full, AXES, scatter_dimension=0, tiled=True).astype(F32)
@@ -1267,20 +1372,21 @@
             params, first_moment, second_moment, grad, step_count, step_rate
         )
         pieces = [lax.all_gather((params - weight_update).astype(BF16), AXES, axis=0, tiled=True)]
-    again_own, again_oth = run_features(False, plan, tables, x_blocks, pieces, parts, table)
+    again_own, again_oth = run_features(False, plan, tables, (x_img, stats), pieces, parts, table)
     if here.planes:
-        again_own, again_oth, out_got, dx_got, far = stage((again_own, again_oth, out_got, dx_got, far))
+        again_own, again_oth, dx_got, far = stage((again_own, again_oth, dx_got, far))
     again = from_chips(plan, merge_cores(plan, position, again_own, over_core(again_oth)))
     if here.planes:
         mine = jnp.concatenate([jnp.where(here.z < 2, low, high), far.astype(F32)], axis=0)
         follow = lax.ppermute(mine[:count], AXES, [(o, o - 1) for o in range(1, count)])
-        follow, dx_got, out_got = stage((follow, dx_got, out_got))
+        follow, dx_got = stage((follow, dx_got))
         follow = jnp.where(here.owner == last, jnp.pad(small_sum, ((0, count - 16), (0, 0))), follow)
         grad = lax.dynamic_slice_in_dim(jnp.concatenate([mine, follow], axis=0), here.owner, rows, 0)
         weight_update, new_first, new_second = adam(
             params, first_moment, second_moment, grad, step_count, step_rate
         )
-    first_out = to_bands(plan, position, out_got)
+    else:
+        first_out = to_bands(plan, position, out_got)
     input_grads = to_bands(plan, position, dx_got)
     second_out = to_bands(plan, position, again)
     return (*first_out, *second_out, *input_grads, weight_update, new_first, new_second)

time: 490 us -> 459 us (0.937)
  Pallas kernels: 147 us -> 127 us
  local copies, waits for them, and re-layouts: 36.3 us -> 16.7 us
  waiting for transfers between devices: 142 us -> 147 us
    pallas_call x7, Pallas kernels: 147 us -> 127 us  [call(): pl.pallas_call(kernel, name=name, out_shape=[jax.ShapeDtypeStruct(s, d) f...]
    slice x15 -> x6, local copies, waits for them, and re-layouts: 14.6 us -> 1.92 us  [the longest x3 1.85 us: body(): single_state = [rows_of[singles:singles + 16] for rows_of in state]]
    ppermute x29, waiting for transfers between devices: 64.4 us -> 71.1 us  [z_shift(): lax.ppermute(value, 'band', [(2 * z + c, 2 * ((z + k) % nz) + c) for z in...]
    convert_element_type x4, other arithmetic: 0.84 us -> 7.14 us  [add_part(): return (both[0] + both[1]).astype(BF16)]
    ppermute x46 -> x48, waiting for transfers between devices: 10.5 us -> 11.8 us  [core_swap(): return lax.ppermute(value, 'band', [(b, b ^ 1) for b in range(n_band)])]
    ppermute x46 -> x48, starting transfers between devices: 10.3 us -> 10.6 us  [core_swap(): return lax.ppermute(value, 'band', [(b, b ^ 1) for b in range(n_band)])]
  transfers between devices with their start and end apart: 112 -> 115, of which waited for: 50 -> 58; matrix products, arithmetic and copies ran while one was open for 9% -> 8% of each run, Pallas kernels for 30% -> 28%
where the time goes in v3:
time: 459 us; the launch traced here: 450 us
  waiting for transfers between devices  147 us (32%)
  Pallas kernels  127 us (28%)
  starting transfers between devices  116 us (25%)
  other arithmetic  35.5 us (8%)
  local copies, waits for them, and re-layouts  16.7 us (4%)
  between operations  8.66 us (2%)
    pallas_call x7, Pallas kernels, call(): pl.pallas_call(kernel, name=name, out_shape=[jax.ShapeDtypeStruct(s, d) f...  127 us
    ppermute x29, waiting for transfers between devices, z_shift(): lax.ppermute(value, 'band', [(2 * z + c, 2 * ((z + k) % nz) + c) for z in...  71.1 us
    ppermute x29, starting transfers between devices, z_shift(): lax.ppermute(value, 'band', [(2 * z + c, 2 * ((z + k) % nz) + c) for z in...  58.5 us
    ppermute x15, waiting for transfers between devices, over_x(): return lax.ppermute(value, 'img', [(i, i ^ 1) for i in range(4)])  42.7 us
    ppermute x15, starting transfers between devices, over_x(): return lax.ppermute(value, 'img', [(i, i ^ 1) for i in range(4)])  19.6 us
    ppermute x15, waiting for transfers between devices, over_y(): return lax.ppermute(value, 'img', [(i, i ^ 2) for i in range(4)])  19.4 us
    ppermute x15, starting transfers between devices, over_y(): return lax.ppermute(value, 'img', [(i, i ^ 2) for i in range(4)])  13.8 us
    ppermute x48, waiting for transfers between devices, core_swap(): return lax.ppermute(value, 'band', [(b, b ^ 1) for b in range(n_band)])  11.8 us
  transfers between devices with their start and end apart: 115, of which 58 were waited for; matrix products, arithmetic and copies ran while one was open for 8% of the time, Pallas kernels for 28%

profile of v3, /device:TPU:0, one launch (start us, length us, event | category | flops | bytes accessed | tf_op | source)
XLA Modules:
  0.0 450.0 jit_solution(1845292865470084129)
XLA Ops:
  3.4 3.0 collective-permute-start.3
  6.5 2.6 collective-permute-start.4
  10.6 3.5 collective-permute-start
  16.7 2.3 collective-permute-start.1
  31.5 12.6 %collective-permute-start.7 = (bf16[368,512]{1,0:T(8,128)(2,1)}, bf16[368,512]{1,0:T(8,128)(2,1)S(1)}, u32[]{:S(2)}, u32[]{:S(2)}) collective-permute-start(bf16[368,512]{1,0:T(8,128)(2,1)} %pad_maximum_fusion.11.refs_11_), channel_id=1, source_target_pairs={{0,8},{4,12},{8,16},{12,20},{16,24},{20,28},{24,0},{28,4},{1,9},{5... | collective-permute-start | bytes 1130504 | tf_op jit(solution)/shard_map/ppermute | solution.py:986
  46.6 2.4 collective-permute-start.10
  53.7 6.3 %collective-permute-done.8.refs_23_ = bf16[368,512]{1,0:T(8,128)(2,1)S(1)} collective-permute-done((bf16[368,512]{1,0:T(8,128)(2,1)}, bf16[368,512]{1,0:T(8,128)(2,1)S(1)}, u32[]{:S(2)}, u32[]{:S(2)}) %collective-permute-start.8) | collective-permute-done | bytes 376864 | tf_op jit(solution)/shard_map/ppermute | solution.py:986
  62.0 2.0 collective-permute-start.16
  64.0 7.4 %collective-permute-start.17 = (bf16[368,512]{1,0:T(8,128)(2,1)}, bf16[368,512]{1,0:T(8,128)(2,1)S(1)}, u32[]{:S(2)}, u32[]{:S(2)}) collective-permute-start(bf16[368,512]{1,0:T(8,128)(2,1)} %pad_maximum_fusion.11.refs_11_), channel_id=1, source_target_pairs={{0,16},{4,20},{8,24},{12,28},{16,0},{20,4},{24,8},{28,12},{1,17},{... | collective-permute-start | bytes 1130504 | tf_op jit(solution)/shard_map/ppermute | solution.py:986
  74.7 4.1 collective-permute-done.15.refs_24_
  78.9 5.7 %collective-permute-done.17.refs_19_ = bf16[368,512]{1,0:T(8,128)(2,1)S(1)} collective-permute-done((bf16[368,512]{1,0:T(8,128)(2,1)}, bf16[368,512]{1,0:T(8,128)(2,1)S(1)}, u32[]{:S(2)}, u32[]{:S(2)}) %collective-permute-start.17) | collective-permute-done | bytes 376864 | tf_op jit(solution)/shard_map/ppermute | solution.py:986
  88.6 7.6 %collective-permute-done.18.refs_20_ = bf16[368,512]{1,0:T(8,128)(2,1)S(1)} collective-permute-done((bf16[368,512]{1,0:T(8,128)(2,1)S(1)}, bf16[368,512]{1,0:T(8,128)(2,1)S(1)}, u32[]{:S(2)}, u32[]{:S(2)}) %collective-permute-start.18) | collective-permute-done | bytes 376864 | tf_op jit(solution)/shard_map/ppermute | solution.py:1075
  96.8 8.6 %collective-permute-done.20.refs_22_ = bf16[368,512]{1,0:T(8,128)(2,1)S(1)} collective-permute-done((bf16[368,512]{1,0:T(8,128)(2,1)S(1)}, bf16[368,512]{1,0:T(8,128)(2,1)S(1)}, u32[]{:S(2)}, u32[]{:S(2)}) %collective-permute-start.20) | collective-permute-done | bytes 376864 | tf_op jit(solution)/shard_map/ppermute | solution.py:986
  115.0 2.0 collective-permute-start.41
  118.0 26.5 %features_first.1 = (bf16[1024,512]{1,0:T(8,128)(2,1)}, bf16[1024,512]{1,0:T(8,128)(2,1)}, f32[1024,512]{1,0:T(8,128)}, bf16[1024,512]{1,0:T(8,128)(2,1)}, f32[1...) custom-call(s32[128]{0:T(128)} %broadcast_select_fusion.6.refs_0_.ga, ...), custom_call_target="tpu_custom_call" | custom-call | flops 28600000512 | bytes 37552792 | tf_op jit(solution)/shard_map/features_first/pallas_call | solution.py:806
  147.7 2.0 collective-permute-start.46
  149.7 2.5 collective-permute-start.47
  152.2 26.1 %attend_both.1 = (bf16[768,512]{1,0:T(8,128)(2,1)}, bf16[768,512]{1,0:T(8,128)(2,1)}, f32[1024,512]{1,0:T(8,128)}, bf16[1024,512]{1,0:T(8,128)(2,1)}, bf16[2048,512]{1,0:T(8,128)(2,1)}, /*index=5*/f32[16,512]{1,0:T(8,128)}) custom-call(s32[128]{0:T(128)} %broadcast_select_fusion.6.refs_0_.gather, s32[192]{0:T(256)} %fusion.78.scatter.refs_0_, ...), custom_call_target="tpu_custom_call" | custom-call | flops 26400000000 | bytes 27100436 | tf_op jit(solution)/shard_map/attend_both/pallas_call | solution.py:806
  178.4 9.0 %weight_grad_two.1 = (bf16[1408,512]{1,0:T(8,128)(2,1)}, bf16[1408,512]{1,0:T(8,128)(2,1)}, bf16[1408,512]{1,0:T(8,128)(2,1)}, bf16[1408,512]{1,0:T(8,128)(2,1)}...) custom-call(s32[5]{0:T(128)} %stack.276.refs_1_.flags.refs_0_, bf16[1024,512]{1,0:T(8,128)(2,1)} %get-tuple-element.519.refs_1_, ...), custom_call_target="tpu_custom_call" | custom-call | flops 9900000256 | bytes 11042836 | tf_op jit(solution)/shard_map/weight_grad_two/pallas_call | solution.py:806
  192.1 12.5 %data_grad_two.1 = (bf16[1024,512]{1,0:T(8,128)(2,1)}, f32[16,512]{1,0:T(8,128)}) custom-call(s32[5]{0:T(128)} %stack.276.refs_1_.flags.refs_0_, bf16[1024,512]{1,0:T(8,128)(2,1)} %get-tuple-element.526.refs_2_.refs_1_, f32[1024,512]{1,0:T(8,128)} %get-tuple-element.527.refs_2_, f32[16,512]{1,0:T(8,128)} %get-tuple-element.497.stats.refs_3_.refs_5_.refs_4_, ...), custom_call_target="tpu_custom_call" | custom-call | flops 13200000000 | bytes 15826964 | tf_op jit(solution)/shard_map/data_grad_two/pallas_call | solution.py:806
  207.8 3.3 collective-permute-start.51
  211.1 9.8 %weight_grad_one.1 = (bf16[1408,512]{1,0:T(8,128)(2,1)}, bf16[1408,512]{1,0:T(8,128)(2,1)}, bf16[1408,512]{1,0:T(8,128)(2,1)}, bf16[1408,512]{1,0:T(8,128)(2,1)}, f32[16,512]{1,0:T(8,128)}) custom-call(s32[5]{0:T(128)} %stack.276.refs_1_.flags.refs_0_, bf16[1024,512]{1,0:T(8,128)(2,1)} %get-tuple-element.485.refs_1_, ...), custom_call_target="tpu_custom_call" | custom-call | flops 9900000256 | bytes 8945684 | tf_op jit(solution)/shard_map/weight_grad_one/pallas_call | solution.py:806
  220.9 2.9 collective-permute-done.52
  223.9 2.5 collective-permute-done.51
  236.0 2.3 fusion.10
  238.3 2.2 fusion.9
  241.5 3.0 collective-permute-done.58
  247.1 2.6 collective-permute-start.63
  250.6 13.6 %data_grad_one.1 = (bf16[768,512]{1,0:T(8,128)(2,1)}, bf16[768,512]{1,0:T(8,128)(2,1)}, f32[16,512]{1,0:T(8,128)}) custom-call(s32[192]{0:T(256)} %fusion.78.scatter.refs_0_, s32[5]{0:T(128)} %stack.276.refs_1_.flags.refs_0_, bf16[1024,512]{1,0:T(8,128)(2,1)} %get-tuple-element.567.refs_2_, bf16[1024,512]{1,0:T(8,128)(2,1)} %get-tuple-element.568.refs_3_, ...), custom_call_target="tpu_custom_call" | custom-call | flops 13200000000 | bytes 17400596 | tf_op jit(solution)/shard_map/data_grad_one/pallas_call | solution.py:806
  264.3 2.0 collective-permute-done.60
  275.8 6.3 %collective-permute-done.68 = f32[16,512]{1,0:T(8,128)S(1)} collective-permute-done((f32[16,512]{1,0:T(8,128)S(1)}, f32[16,512]{1,0:T(8,128)S(1)}, u32[]{:S(2)}, u32[]{:S(2)}) %collective-permute-start.68) | collective-permute-done | bytes 32800 | tf_op jit(solution)/shard_map/ppermute | solution.py:1075
  285.4 2.8 collective-permute-start.72
  289.4 4.5 %collective-permute-done.71 = bf16[192,512]{1,0:T(8,128)(2,1)S(1)} collective-permute-done((bf16[192,512]{1,0:T(8,128)(2,1)S(1)}, bf16[192,512]{1,0:T(8,128)(2,1)S(1)}, u32[]{:S(2)}, u32[]{:S(2)}) %collective-permute-start.71) | collective-permute-done | bytes 196640 | tf_op jit(solution)/shard_map/ppermute | solution.py:986
  295.7 8.8 %collective-permute-done.73 = bf16[192,512]{1,0:T(8,128)(2,1)S(1)} collective-permute-done((bf16[192,512]{1,0:T(8,128)(2,1)S(1)}, bf16[192,512]{1,0:T(8,128)(2,1)S(1)}, u32[]{:S(2)}, u32[]{:S(2)}) %collective-permute-start.73) | collective-permute-done | bytes 196640 | tf_op jit(solution)/shard_map/ppermute | solution.py:986
  310.5 3.8 collective-permute-start.78
  314.4 4.3 collective-permute-done.74.refs_6_
  318.7 8.1 %collective-permute-done.75.refs_7_ = bf16[368,512]{1,0:T(8,128)(2,1)S(1)} collective-permute-done((bf16[368,512]{1,0:T(8,128)(2,1)S(1)}, bf16[368,512]{1,0:T(8,128)(2,1)S(1)}, u32[]{:S(2)}, u32[]{:S(2)}) %collective-permute-start.75) | collective-permute-done | bytes 376864 | tf_op jit(solution)/shard_map/ppermute | solution.py:1079
  333.7 2.4 collective-permute-start.84
  336.1 3.7 collective-permute-done.80.refs_10_
  341.4 3.5 collective-permute-done.82.refs_18_
  346.6 3.3 collective-permute-done.84.refs_13_
  354.2 7.7 %collective-permute-done.89.refs_14_ = bf16[368,512]{1,0:T(8,128)(2,1)S(1)} collective-permute-done((bf16[368,512]{1,0:T(8,128)(2,1)}, bf16[368,512]{1,0:T(8,128)(2,1)S(1)}, u32[]{:S(2)}, u32[]{:S(2)}) %collective-permute-start.89) | collective-permute-done | bytes 376864 | tf_op jit(solution)/shard_map/ppermute | solution.py:1075
  363.6 6.6 %collective-permute-done.91.refs_16_ = bf16[368,512]{1,0:T(8,128)(2,1)} collective-permute-done((bf16[368,512]{1,0:T(8,128)(2,1)S(1)}, bf16[368,512]{1,0:T(8,128)(2,1)}, u32[]{:S(2)}, u32[]{:S(2)}) %collective-permute-start.91) | collective-permute-done | bytes 376864 | tf_op jit(solution)/shard_map/ppermute | solution.py:986
  378.4 5.1 %collective-permute-start.106 = (bf16[288,512]{1,0:T(8,128)(2,1)S(1)}, bf16[288,512]{1,0:T(8,128)(2,1)S(1)}, u32[]{:S(2)}, u32[]{:S(2)}) collective-permute-start(bf16[288,512]{1,0:T(8,128)(2,1)S(1)} %get-tuple-element.770), channel_id=1, source_target_pairs={{0,24},{4,28},{8,0},{12,4},{16,8},{20,12},{24,16},{28,20},{1,25},{... | collective-permute-start | bytes 884744 | tf_op jit(solution)/shard_map/ppermute | solution.py:986
  385.4 29.2 %forward_again.1 = (bf16[768,512]{1,0:T(8,128)(2,1)}, bf16[768,512]{1,0:T(8,128)(2,1)}) custom-call(s32[192]{0:T(256)} %fusion.78.scatter.refs_0_, s32[5]{0:T(128)} %stack.276.refs_1_.flags.refs_0_, s32[65]{0:T(128)} %pad_add_fusion.5.refs_2_, bf16[1024,512]{1,0:T(8,128)(2,1)} %get-tuple-element.568.refs_3_, ...), custom_call_target="tpu_custom_call" | custom-call | flops 30799998976 | bytes 14713880 | tf_op jit(solution)/shard_map/forward_again/pallas_call | solution.py:806
  418.5 2.0 collective-permute-start.111
  423.5 4.4 collective-permute-done.111
  427.9 19.7 %collective-permute-done.112 = bf16[288,512]{1,0:T(8,128)(2,1)S(1)} collective-permute-done((bf16[288,512]{1,0:T(8,128)(2,1)S(1)}, bf16[288,512]{1,0:T(8,128)(2,1)S(1)}, u32[]{:S(2)}, u32[]{:S(2)}) %collective-permute-start.112) | collective-permute-done | bytes 294944 | tf_op jit(solution)/shard_map/ppermute | solution.py:986
  (563 shorter events, 122.4 us)
Async XLA Ops:
  3.4 27.0 %collective-permute-start.3 = (bf16[288,512]{1,0:T(8,128)(2,1)}, bf16[288,512]{1,0:T(8,128)(2,1)}, u32[]{:S(2)}, u32[]{:S(2)}) collective-permute-start(bf16[288,512]{1,0:T(8,128)(2,1)} %get-tuple-element.790), channel_id=1, source_target_pairs={{0,8},{4,12},{8,16},{12,20},{16,24},{20,28},{24,0},{28,4},{1,9},{5... | collective-permute-start | bytes 884744 | tf_op jit(solution)/shard_map/ppermute | solution.py:986
  6.5 23.9 %collective-permute-start.4 = (bf16[288,512]{1,0:T(8,128)(2,1)}, bf16[288,512]{1,0:T(8,128)(2,1)}, u32[]{:S(2)}, u32[]{:S(2)}) collective-permute-start(bf16[288,512]{1,0:T(8,128)(2,1)} %get-tuple-element.789), channel_id=1, source_target_pairs={{0,16},{4,20},{8,24},{12,28},{16,0},{20,4},{24,8},{28,12},{1,17},{... | collective-permute-start | bytes 884744 | tf_op jit(solution)/shard_map/ppermute | solution.py:986
  9.1 21.3 %collective-permute-start.5 = (bf16[288,512]{1,0:T(8,128)(2,1)}, bf16[288,512]{1,0:T(8,128)(2,1)}, u32[]{:S(2)}, u32[]{:S(2)}) collective-permute-start(bf16[288,512]{1,0:T(8,128)(2,1)} %get-tuple-element.788), channel_id=1, source_target_pairs={{0,24},{4,28},{8,0},{12,4},{16,8},{20,12},{24,16},{28,20},{1,25},{... | collective-permute-start | bytes 884744 | tf_op jit(solution)/shard_map/ppermute | solution.py:986
  30.6 23.0 %collective-permute-start.6 = (bf16[368,512]{1,0:T(8,128)(2,1)}, bf16[368,512]{1,0:T(8,128)(2,1)S(1)}, u32[]{:S(2)}, u32[]{:S(2)}) collective-permute-start(bf16[368,512]{1,0:T(8,128)(2,1)} %pad_maximum_fusion.11.refs_11_), channel_id=1, source_target_pairs={{0,3},{1,2},{2,1},{3,0},{4,7},{5,6},{6,5},{7,4},{8,11},{9,10},{10,... | collective-permute-start | bytes 1130504 | tf_op jit(solution)/shard_map/ppermute | solution.py:1087
  31.5 22.2 %collective-permute-start.7 = (bf16[368,512]{1,0:T(8,128)(2,1)}, bf16[368,512]{1,0:T(8,128)(2,1)S(1)}, u32[]{:S(2)}, u32[]{:S(2)}) collective-permute-start(bf16[368,512]{1,0:T(8,128)(2,1)} %pad_maximum_fusion.11.refs_11_), channel_id=1, source_target_pairs={{0,8},{4,12},{8,16},{12,20},{16,24},{20,28},{24,0},{28,4},{1,9},{5... | collective-permute-start | bytes 1130504 | tf_op jit(solution)/shard_map/ppermute | solution.py:986
  44.1 15.9 %collective-permute-start.8 = (bf16[368,512]{1,0:T(8,128)(2,1)}, bf16[368,512]{1,0:T(8,128)(2,1)S(1)}, u32[]{:S(2)}, u32[]{:S(2)}) collective-permute-start(bf16[368,512]{1,0:T(8,128)(2,1)} %pad_maximum_fusion.11.refs_11_), channel_id=1, source_target_pairs={{0,24},{4,28},{8,0},{12,4},{16,8},{20,12},{24,16},{28,20},{1,25},{... | collective-permute-start | bytes 1130504 | tf_op jit(solution)/shard_map/ppermute | solution.py:986
  60.0 14.7 %collective-permute-start.14 = (bf16[368,512]{1,0:T(8,128)(2,1)S(1)}, bf16[368,512]{1,0:T(8,128)(2,1)S(1)}, u32[]{:S(2)}, u32[]{:S(2)}) collective-permute-start(bf16[368,512]{1,0:T(8,128)(2,1)S(1)} %collective-permute-done.7.refs_15_), channel_id=1, source_target_pairs={{0,2},{1,3},{2,0},{3,1},{4,6},{5,7},{6,4},{7,5},{8,10},{9,11},{10,... | collective-permute-start | bytes 1130504 | tf_op jit(solution)/shard_map/ppermute | solution.py:1079
  60.5 18.3 %collective-permute-start.15 = (bf16[368,512]{1,0:T(8,128)(2,1)S(1)}, bf16[368,512]{1,0:T(8,128)(2,1)S(1)}, u32[]{:S(2)}, u32[]{:S(2)}) collective-permute-start(bf16[368,512]{1,0:T(8,128)(2,1)S(1)} %collective-permute-done.8.refs_23_), channel_id=1, source_target_pairs={{0,1},{1,0},{2,3},{3,2},{4,5},{5,4},{6,7},{7,6},{8,9},{9,8},{10,11... | collective-permute-start | bytes 1130504 | tf_op jit(solution)/shard_map/ppermute | solution.py:1075
  62.0 16.9 %collective-permute-start.16 = (bf16[368,512]{1,0:T(8,128)(2,1)S(1)}, bf16[368,512]{1,0:T(8,128)(2,1)S(1)}, u32[]{:S(2)}, u32[]{:S(2)}) collective-permute-start(bf16[368,512]{1,0:T(8,128)(2,1)S(1)} %collective-permute-done.8.refs_23_), channel_id=1, source_target_pairs={{0,2},{1,3},{2,0},{3,1},{4,6},{5,7},{6,4},{7,5},{8,10},{9,11},{10,... | collective-permute-start | bytes 1130504 | tf_op jit(solution)/shard_map/ppermute | solution.py:1079
  64.0 20.6 %collective-permute-start.17 = (bf16[368,512]{1,0:T(8,128)(2,1)}, bf16[368,512]{1,0:T(8,128)(2,1)S(1)}, u32[]{:S(2)}, u32[]{:S(2)}) collective-permute-start(bf16[368,512]{1,0:T(8,128)(2,1)} %pad_maximum_fusion.11.refs_11_), channel_id=1, source_target_pairs={{0,16},{4,20},{8,24},{12,28},{16,0},{20,4},{24,8},{28,12},{1,17},{... | collective-permute-start | bytes 1130504 | tf_op jit(solution)/shard_map/ppermute | solution.py:986
  86.8 18.6 %collective-permute-start.20 = (bf16[368,512]{1,0:T(8,128)(2,1)S(1)}, bf16[368,512]{1,0:T(8,128)(2,1)S(1)}, u32[]{:S(2)}, u32[]{:S(2)}) collective-permute-start(bf16[368,512]{1,0:T(8,128)(2,1)S(1)} %collective-permute-done.6.refs_14_), channel_id=1, source_target_pairs={{0,16},{4,20},{8,24},{12,28},{16,0},{20,4},{24,8},{28,12},{1,17},{... | collective-permute-start | bytes 1130504 | tf_op jit(solution)/shard_map/ppermute | solution.py:986
  86.8 18.6 %collective-permute-start.21 = (bf16[368,512]{1,0:T(8,128)(2,1)S(1)}, bf16[368,512]{1,0:T(8,128)(2,1)S(1)}, u32[]{:S(2)}, u32[]{:S(2)}) collective-permute-start(bf16[368,512]{1,0:T(8,128)(2,1)S(1)} %collective-permute-done.13.refs_16_), channel_id=1, source_target_pairs={{0,2},{1,3},{2,0},{3,1},{4,6},{5,7},{6,4},{7,5},{8,10},{9,11},{10,... | collective-permute-start | bytes 1130504 | tf_op jit(solution)/shard_map/ppermute | solution.py:1079
  87.1 18.9 %collective-permute-start.22 = (bf16[368,512]{1,0:T(8,128)(2,1)S(1)}, bf16[368,512]{1,0:T(8,128)(2,1)S(1)}, u32[]{:S(2)}, u32[]{:S(2)}) collective-permute-start(bf16[368,512]{1,0:T(8,128)(2,1)S(1)} %collective-permute-done.16.refs_25_), channel_id=1, source_target_pairs={{0,1},{1,0},{2,3},{3,2},{4,5},{5,4},{6,7},{7,6},{8,9},{9,8},{10,11... | collective-permute-start | bytes 1130504 | tf_op jit(solution)/shard_map/ppermute | solution.py:1075
  113.1 31.3 %collective-permute-start.39 = (bf16[288,512]{1,0:T(8,128)(2,1)S(1)}, bf16[288,512]{1,0:T(8,128)(2,1)}, u32[]{:S(2)}, u32[]{:S(2)}) collective-permute-start(bf16[288,512]{1,0:T(8,128)(2,1)S(1)} %get-tuple-element.491), channel_id=1, source_target_pairs={{0,8},{4,12},{8,16},{12,20},{16,24},{20,28},{24,0},{28,4},{1,9},{5... | collective-permute-start | bytes 884744 | tf_op jit(solution)/shard_map/ppermute | solution.py:986
  113.6 30.8 %collective-permute-start.40 = (bf16[288,512]{1,0:T(8,128)(2,1)S(1)}, bf16[288,512]{1,0:T(8,128)(2,1)}, u32[]{:S(2)}, u32[]{:S(2)}) collective-permute-start(bf16[288,512]{1,0:T(8,128)(2,1)S(1)} %get-tuple-element.492), channel_id=1, source_target_pairs={{0,16},{4,20},{8,24},{12,28},{16,0},{20,4},{24,8},{28,12},{1,17},{... | collective-permute-start | bytes 884744 | tf_op jit(solution)/shard_map/ppermute | solution.py:986
  115.0 29.5 %collective-permute-start.41 = (bf16[288,512]{1,0:T(8,128)(2,1)S(1)}, bf16[288,512]{1,0:T(8,128)(2,1)}, u32[]{:S(2)}, u32[]{:S(2)}) collective-permute-start(bf16[288,512]{1,0:T(8,128)(2,1)S(1)} %get-tuple-element.493), channel_id=1, source_target_pairs={{0,24},{4,28},{8,0},{12,4},{16,8},{20,12},{24,16},{28,20},{1,25},{... | collective-permute-start | bytes 884744 | tf_op jit(solution)/shard_map/ppermute | solution.py:986
  147.7 30.6 %collective-permute-start.46 = (bf16[176,1536]{1,0:T(8,128)(2,1)S(1)}, bf16[176,1536]{1,0:T(8,128)(2,1)S(1)}, u32[]{:S(2)}, u32[]{:S(2)}) collective-permute-start(bf16[176,1536]{1,0:T(8,128)(2,1)S(1)} %pad_maximum_fusion.7), channel_id=1, source_target_pairs={{0,16},{4,20},{16,0},{20,4},{8,24},{12,28},{24,8},{28,12},{1,17},{... | collective-permute-start | bytes 1622024 | tf_op jit(solution)/shard_map/ppermute | solution.py:1083
  149.7 28.6 %collective-permute-start.47 = (f32[32,1536]{1,0:T(8,128)S(1)}, f32[32,1536]{1,0:T(8,128)S(1)}, u32[]{:S(2)}, u32[]{:S(2)}) collective-permute-start(f32[32,1536]{1,0:T(8,128)S(1)} %copy-done.22), channel_id=1, source_target_pairs={{0,1},{1,2},{2,3},{3,4},{4,5},{5,6},{6,7},{7,8},{8,9},{9,10},{10,1... | collective-permute-start | bytes 589832 | tf_op jit(solution)/shard_map/ppermute | solution.py:1288
  187.4 17.2 %collective-permute-start.49 = (bf16[1408,512]{1,0:T(8,128)(2,1)}, bf16[1408,512]{1,0:T(8,128)(2,1)}, u32[]{:S(2)}, u32[]{:S(2)}) collective-permute-start(bf16[1408,512]{1,0:T(8,128)(2,1)} %get-tuple-element.531), channel_id=1, source_target_pairs={{0,4},{4,0},{8,12},{12,8},{16,20},{20,16},{24,28},{28,24},{1,5},{5... | collective-permute-start | bytes 4325384 | tf_op jit(solution)/shard_map/ppermute | solution.py:990
  187.9 16.7 %collective-permute-start.50 = (bf16[1408,512]{1,0:T(8,128)(2,1)}, bf16[1408,512]{1,0:T(8,128)(2,1)}, u32[]{:S(2)}, u32[]{:S(2)}) collective-permute-start(bf16[1408,512]{1,0:T(8,128)(2,1)} %get-tuple-element.532), channel_id=1, source_target_pairs={{0,4},{4,0},{8,12},{12,8},{16,20},{20,16},{24,28},{28,24},{1,5},{5... | collective-permute-start | bytes 4325384 | tf_op jit(solution)/shard_map/ppermute | solution.py:990
  189.1 31.8 %collective-permute-start.53 = (bf16[288,512]{1,0:T(8,128)(2,1)}, bf16[288,512]{1,0:T(8,128)(2,1)S(1)}, u32[]{:S(2)}, u32[]{:S(2)}) collective-permute-start(bf16[288,512]{1,0:T(8,128)(2,1)} %get-tuple-element.740), channel_id=1, source_target_pairs={{0,24},{4,28},{8,0},{12,4},{16,8},{20,12},{24,16},{28,20},{1,25},{... | collective-permute-start | bytes 884744 | tf_op jit(solution)/shard_map/ppermute | solution.py:986
  190.6 30.3 %collective-permute-start.54 = (bf16[288,512]{1,0:T(8,128)(2,1)}, bf16[288,512]{1,0:T(8,128)(2,1)}, u32[]{:S(2)}, u32[]{:S(2)}) collective-permute-start(bf16[288,512]{1,0:T(8,128)(2,1)} %get-tuple-element.741), channel_id=1, source_target_pairs={{0,16},{4,20},{8,24},{12,28},{16,0},{20,4},{24,8},{28,12},{1,17},{... | collective-permute-start | bytes 884744 | tf_op jit(solution)/shard_map/ppermute | solution.py:986
  190.6 30.3 %collective-permute-start.55 = (bf16[288,512]{1,0:T(8,128)(2,1)}, bf16[288,512]{1,0:T(8,128)(2,1)}, u32[]{:S(2)}, u32[]{:S(2)}) collective-permute-start(bf16[288,512]{1,0:T(8,128)(2,1)} %get-tuple-element.738), channel_id=1, source_target_pairs={{0,8},{4,12},{8,16},{12,20},{16,24},{20,28},{24,0},{28,4},{1,9},{5... | collective-permute-start | bytes 884744 | tf_op jit(solution)/shard_map/ppermute | solution.py:986
  206.0 17.8 %collective-permute-start.52 = (bf16[2,352,512]{2,1,0:T(8,128)(2,1)S(1)}, bf16[2,352,512]{2,1,0:T(8,128)(2,1)}, u32[]{:S(2)}, u32[]{:S(2)}) collective-permute-start(bf16[2,352,512]{2,1,0:T(8,128)(2,1)S(1)} %fusion.8), channel_id=1, source_target_pairs={{0,2},{1,3},{2,0},{3,1},{4,6},{5,7},{6,4},{7,5},{8,10},{9,11},{10,... | collective-permute-start | bytes 2162696 | tf_op jit(solution)/shard_map/ppermute | solution.py:1079
  207.8 18.5 %collective-permute-start.51 = (bf16[2,352,512]{2,1,0:T(8,128)(2,1)S(1)}, bf16[2,352,512]{2,1,0:T(8,128)(2,1)S(1)}, u32[]{:S(2)}, u32[]{:S(2)}) collective-permute-start(bf16[2,352,512]{2,1,0:T(8,128)(2,1)S(1)} %fusion.7), channel_id=1, source_target_pairs={{0,1},{1,0},{2,3},{3,2},{4,5},{5,4},{6,7},{7,6},{8,9},{9,8},{10,11... | collective-permute-start | bytes 2162696 | tf_op jit(solution)/shard_map/ppermute | solution.py:1075
  245.9 18.4 %collective-permute-start.62 = (bf16[176,512]{1,0:T(8,128)(2,1)}, bf16[176,512]{1,0:T(8,128)(2,1)}, u32[]{:S(2)}, u32[]{:S(2)}) collective-permute-start(bf16[176,512]{1,0:T(8,128)(2,1)} %get-tuple-element.801), channel_id=1, source_target_pairs={{0,8},{4,12},{8,16},{12,20},{16,24},{20,28},{24,0},{28,4},{1,9},{5... | collective-permute-start | bytes 540680 | tf_op jit(solution)/shard_map/ppermute | solution.py:986
  247.1 17.1 %collective-permute-start.63 = (bf16[176,512]{1,0:T(8,128)(2,1)}, bf16[176,512]{1,0:T(8,128)(2,1)}, u32[]{:S(2)}, u32[]{:S(2)}) collective-permute-start(bf16[176,512]{1,0:T(8,128)(2,1)} %get-tuple-element.800), channel_id=1, source_target_pairs={{0,24},{4,28},{8,0},{12,4},{16,8},{20,12},{24,16},{28,20},{1,25},{... | collective-permute-start | bytes 540680 | tf_op jit(solution)/shard_map/ppermute | solution.py:986
  249.7 16.6 %collective-permute-start.60 = (bf16[2,352,512]{2,1,0:T(8,128)(2,1)}, bf16[2,352,512]{2,1,0:T(8,128)(2,1)}, u32[]{:S(2)}, u32[]{:S(2)}) collective-permute-start(bf16[2,352,512]{2,1,0:T(8,128)(2,1)} %fusion.9), channel_id=1, source_target_pairs={{0,1},{1,0},{2,3},{3,2},{4,5},{5,4},{6,7},{7,6},{8,9},{9,8},{10,11... | collective-permute-start | bytes 2162696 | tf_op jit(solution)/shard_map/ppermute | solution.py:1075
  250.0 16.4 %collective-permute-start.61 = (bf16[2,352,512]{2,1,0:T(8,128)(2,1)}, bf16[2,352,512]{2,1,0:T(8,128)(2,1)}, u32[]{:S(2)}, u32[]{:S(2)}) collective-permute-start(bf16[2,352,512]{2,1,0:T(8,128)(2,1)} %fusion.10), channel_id=1, source_target_pairs={{0,2},{1,3},{2,0},{3,1},{4,6},{5,7},{6,4},{7,5},{8,10},{9,11},{10,... | collective-permute-start | bytes 2162696 | tf_op jit(solution)/shard_map/ppermute | solution.py:1079
  288.3 16.2 %collective-permute-start.73 = (bf16[192,512]{1,0:T(8,128)(2,1)S(1)}, bf16[192,512]{1,0:T(8,128)(2,1)S(1)}, u32[]{:S(2)}, u32[]{:S(2)}) collective-permute-start(bf16[192,512]{1,0:T(8,128)(2,1)S(1)} %get-tuple-element.835), channel_id=1, source_target_pairs={{0,16},{4,20},{8,24},{12,28},{16,0},{20,4},{24,8},{28,12},{1,17},{... | collective-permute-start | bytes 589832 | tf_op jit(solution)/shard_map/ppermute | solution.py:986
  289.1 21.4 %collective-permute-start.79 = (bf16[768,512]{1,0:T(8,128)(2,1)S(1)}, bf16[768,512]{1,0:T(8,128)(2,1)S(1)}, u32[]{:S(2)}, u32[]{:S(2)}) collective-permute-start(bf16[768,512]{1,0:T(8,128)(2,1)S(1)} %copy-done.48), channel_id=1, source_target_pairs={{0,4},{4,0},{8,12},{12,8},{16,20},{20,16},{24,28},{28,24},{1,5},{5... | collective-permute-start | bytes 2359304 | tf_op jit(solution)/shard_map/ppermute | solution.py:990
  308.7 18.1 %collective-permute-start.75 = (bf16[368,512]{1,0:T(8,128)(2,1)S(1)}, bf16[368,512]{1,0:T(8,128)(2,1)S(1)}, u32[]{:S(2)}, u32[]{:S(2)}) collective-permute-start(bf16[368,512]{1,0:T(8,128)(2,1)S(1)} %pad_maximum_fusion.12.refs_5_), channel_id=1, source_target_pairs={{0,2},{1,3},{2,0},{3,1},{4,6},{5,7},{6,4},{7,5},{8,10},{9,11},{10,... | collective-permute-start | bytes 1130504 | tf_op jit(solution)/shard_map/ppermute | solution.py:1079
  309.0 17.7 %collective-permute-start.76 = (bf16[368,512]{1,0:T(8,128)(2,1)S(1)}, bf16[368,512]{1,0:T(8,128)(2,1)S(1)}, u32[]{:S(2)}, u32[]{:S(2)}) collective-permute-start(bf16[368,512]{1,0:T(8,128)(2,1)S(1)} %pad_maximum_fusion.12.refs_5_), channel_id=1, source_target_pairs={{0,3},{1,2},{2,1},{3,0},{4,7},{5,6},{6,5},{7,4},{8,11},{9,10},{10,... | collective-permute-start | bytes 1130504 | tf_op jit(solution)/shard_map/ppermute | solution.py:1087
  310.5 16.3 %collective-permute-start.77 = (bf16[368,512]{1,0:T(8,128)(2,1)S(1)}, bf16[368,512]{1,0:T(8,128)(2,1)S(1)}, u32[]{:S(2)}, u32[]{:S(2)}) collective-permute-start(bf16[368,512]{1,0:T(8,128)(2,1)S(1)} %pad_maximum_fusion.12.refs_5_), channel_id=1, source_target_pairs={{0,8},{4,12},{8,16},{12,20},{16,24},{20,28},{24,0},{28,4},{1,9},{5... | collective-permute-start | bytes 1130504 | tf_op jit(solution)/shard_map/ppermute | solution.py:986
  310.5 17.5 %collective-permute-start.78 = (bf16[368,512]{1,0:T(8,128)(2,1)S(1)}, bf16[368,512]{1,0:T(8,128)(2,1)S(1)}, u32[]{:S(2)}, u32[]{:S(2)}) collective-permute-start(bf16[368,512]{1,0:T(8,128)(2,1)S(1)} %pad_maximum_fusion.12.refs_5_), channel_id=1, source_target_pairs={{0,24},{4,28},{8,0},{12,4},{16,8},{20,12},{24,16},{28,20},{1,25},{... | collective-permute-start | bytes 1130504 | tf_op jit(solution)/shard_map/ppermute | solution.py:986
  330.1 14.9 %collective-permute-start.82 = (bf16[368,512]{1,0:T(8,128)(2,1)S(1)}, bf16[368,512]{1,0:T(8,128)(2,1)S(1)}, u32[]{:S(2)}, u32[]{:S(2)}) collective-permute-start(bf16[368,512]{1,0:T(8,128)(2,1)S(1)} %collective-permute-done.78.refs_17_), channel_id=1, source_target_pairs={{0,1},{1,0},{2,3},{3,2},{4,5},{5,4},{6,7},{7,6},{8,9},{9,8},{10,11... | collective-permute-start | bytes 1130504 | tf_op jit(solution)/shard_map/ppermute | solution.py:1075
  330.6 15.7 %collective-permute-start.83 = (bf16[368,512]{1,0:T(8,128)(2,1)S(1)}, bf16[368,512]{1,0:T(8,128)(2,1)S(1)}, u32[]{:S(2)}, u32[]{:S(2)}) collective-permute-start(bf16[368,512]{1,0:T(8,128)(2,1)S(1)} %collective-permute-done.78.refs_17_), channel_id=1, source_target_pairs={{0,2},{1,3},{2,0},{3,1},{4,6},{5,7},{6,4},{7,5},{8,10},{9,11},{10,... | collective-permute-start | bytes 1130504 | tf_op jit(solution)/shard_map/ppermute | solution.py:1079
  333.7 16.2 %collective-permute-start.84 = (bf16[368,512]{1,0:T(8,128)(2,1)S(1)}, bf16[368,512]{1,0:T(8,128)(2,1)}, u32[]{:S(2)}, u32[]{:S(2)}) collective-permute-start(bf16[368,512]{1,0:T(8,128)(2,1)S(1)} %pad_maximum_fusion.12.refs_5_), channel_id=1, source_target_pairs={{0,16},{4,20},{8,24},{12,28},{16,0},{20,4},{24,8},{28,12},{1,17},{... | collective-permute-start | bytes 1130504 | tf_op jit(solution)/shard_map/ppermute | solution.py:986
  352.1 18.1 %collective-permute-start.91 = (bf16[368,512]{1,0:T(8,128)(2,1)S(1)}, bf16[368,512]{1,0:T(8,128)(2,1)}, u32[]{:S(2)}, u32[]{:S(2)}) collective-permute-start(bf16[368,512]{1,0:T(8,128)(2,1)S(1)} %collective-permute-done.76.refs_8_), channel_id=1, source_target_pairs={{0,16},{4,20},{8,24},{12,28},{16,0},{20,4},{24,8},{28,12},{1,17},{... | collective-permute-start | bytes 1130504 | tf_op jit(solution)/shard_map/ppermute | solution.py:986
  352.1 18.3 %collective-permute-start.92 = (bf16[368,512]{1,0:T(8,128)(2,1)S(1)}, bf16[368,512]{1,0:T(8,128)(2,1)S(1)}, u32[]{:S(2)}, u32[]{:S(2)}) collective-permute-start(bf16[368,512]{1,0:T(8,128)(2,1)S(1)} %collective-permute-done.80.refs_10_), channel_id=1, source_target_pairs={{0,2},{1,3},{2,0},{3,1},{4,6},{5,7},{6,4},{7,5},{8,10},{9,11},{10,... | collective-permute-start | bytes 1130504 | tf_op jit(solution)/shard_map/ppermute | solution.py:1079
  353.7 17.1 %collective-permute-start.93 = (bf16[368,512]{1,0:T(8,128)(2,1)S(1)}, bf16[368,512]{1,0:T(8,128)(2,1)}, u32[]{:S(2)}, u32[]{:S(2)}) collective-permute-start(bf16[368,512]{1,0:T(8,128)(2,1)S(1)} %collective-permute-done.83.refs_19_), channel_id=1, source_target_pairs={{0,1},{1,0},{2,3},{3,2},{4,5},{5,4},{6,7},{7,6},{8,9},{9,8},{10,11... | collective-permute-start | bytes 1130504 | tf_op jit(solution)/shard_map/ppermute | solution.py:1075
  376.7 38.0 %collective-permute-start.109 = (bf16[176,512]{1,0:T(8,128)(2,1)S(1)}, bf16[176,512]{1,0:T(8,128)(2,1)S(1)}, u32[]{:S(2)}, u32[]{:S(2)}) collective-permute-start(bf16[176,512]{1,0:T(8,128)(2,1)S(1)} %select_convert_fusion), channel_id=1, source_target_pairs={{0,16},{4,20},{16,0},{20,4},{8,24},{12,28},{24,8},{28,12},{1,17},{... | collective-permute-start | bytes 540680 | tf_op jit(solution)/shard_map/ppermute | solution.py:1083
  376.7 38.0 %collective-permute-start.114 = (f32[32,512]{1,0:T(8,128)S(1)}, f32[32,512]{1,0:T(8,128)S(1)}, u32[]{:S(2)}, u32[]{:S(2)}) collective-permute-start(f32[32,512]{1,0:T(8,128)S(1)} %slice.514), channel_id=1, source_target_pairs={{1,0},{2,1},{3,2},{4,3},{5,4},{6,5},{7,6},{8,7},{9,8},{10,9},{11,1... | collective-permute-start | bytes 196616 | tf_op jit(solution)/shard_map/ppermute | solution.py:1381
  378.4 36.3 %collective-permute-start.106 = (bf16[288,512]{1,0:T(8,128)(2,1)S(1)}, bf16[288,512]{1,0:T(8,128)(2,1)S(1)}, u32[]{:S(2)}, u32[]{:S(2)}) collective-permute-start(bf16[288,512]{1,0:T(8,128)(2,1)S(1)} %get-tuple-element.770), channel_id=1, source_target_pairs={{0,24},{4,28},{8,0},{12,4},{16,8},{20,12},{24,16},{28,20},{1,25},{... | collective-permute-start | bytes 884744 | tf_op jit(solution)/shard_map/ppermute | solution.py:986
  383.5 31.1 %collective-permute-start.107 = (bf16[288,512]{1,0:T(8,128)(2,1)S(1)}, bf16[288,512]{1,0:T(8,128)(2,1)S(1)}, u32[]{:S(2)}, u32[]{:S(2)}) collective-permute-start(bf16[288,512]{1,0:T(8,128)(2,1)S(1)} %get-tuple-element.769), channel_id=1, source_target_pairs={{0,16},{4,20},{8,24},{12,28},{16,0},{20,4},{24,8},{28,12},{1,17},{... | collective-permute-start | bytes 884744 | tf_op jit(solution)/shard_map/ppermute | solution.py:986
  383.5 31.1 %collective-permute-start.108 = (bf16[288,512]{1,0:T(8,128)(2,1)S(1)}, bf16[288,512]{1,0:T(8,128)(2,1)S(1)}, u32[]{:S(2)}, u32[]{:S(2)}) collective-permute-start(bf16[288,512]{1,0:T(8,128)(2,1)S(1)} %get-tuple-element.768), channel_id=1, source_target_pairs={{0,8},{4,12},{8,16},{12,20},{16,24},{20,28},{24,0},{28,4},{1,9},{5... | collective-permute-start | bytes 884744 | tf_op jit(solution)/shard_map/ppermute | solution.py:986
  420.4 27.1 %collective-permute-start.112 = (bf16[288,512]{1,0:T(8,128)(2,1)S(1)}, bf16[288,512]{1,0:T(8,128)(2,1)S(1)}, u32[]{:S(2)}, u32[]{:S(2)}) collective-permute-start(bf16[288,512]{1,0:T(8,128)(2,1)S(1)} %get-tuple-element.733), channel_id=1, source_target_pairs={{0,16},{4,20},{8,24},{12,28},{16,0},{20,4},{24,8},{28,12},{1,17},{... | collective-permute-start | bytes 884744 | tf_op jit(solution)/shard_map/ppermute | solution.py:986
  421.6 26.0 %collective-permute-start.113 = (bf16[288,512]{1,0:T(8,128)(2,1)S(1)}, bf16[288,512]{1,0:T(8,128)(2,1)S(1)}, u32[]{:S(2)}, u32[]{:S(2)}) collective-permute-start(bf16[288,512]{1,0:T(8,128)(2,1)S(1)} %get-tuple-element.732), channel_id=1, source_target_pairs={{0,8},{4,12},{8,16},{12,20},{16,24},{20,28},{24,0},{28,4},{1,9},{5... | collective-permute-start | bytes 884744 | tf_op jit(solution)/shard_map/ppermute | solution.py:986
  (179 other events, 2033.3 us)

commit v4 on v3

--- a/solution.py
+++ b/solution.py
@@ -277,7 +277,7 @@
         body(tile)
         return carry
 
-    lax.fori_loop(0, 4, step, 0)
+    lax.fori_loop(0, 4, step, 0, unroll=2)
 
 
 def conv_tiles(buf_ref, w_ref, out_ref):
@@ -1121,9 +1121,9 @@
 GATHERED = [(side, k, flip) for side in range(2) for k in (0, 1, 2, 3) for flip in range(4)]
 
 
-def gather_table(here, block_rows):
+def gather_table(here, core, block_rows):
     side, k, flip = np.array(GATHERED, np.int32).T
-    core, z, img = here.core ^ side, (here.z - k) % 4, here.img ^ flip
+    core, z, img = core ^ side, (here.z - k) % 4, here.img ^ flip
     last = (core == 1) & (z == 3) & (img == 3)
     rows = jnp.stack(block_rows(z, 4 * core + img), axis=1).reshape(-1)
     return jnp.concatenate([rows, jnp.argmax(last)[None]]).astype(jnp.int32)
@@ -1134,8 +1134,8 @@
 
 
 def add_part(kept, got, axis, index):
-    both = [part(value.reshape(2, 2, 352, C), axis, index).astype(F32) for value in (kept, got)]
-    return (both[0] + both[1]).astype(BF16)
+    both = [part(value.reshape(2, 2, 352, C), axis, index) for value in (kept, got)]
+    return both[0] + both[1]
 
 
 def halves_to_send(here, kept, got):
@@ -1147,9 +1147,9 @@
 
 
 def add_halves(here, kept, got, got_a, got_b):
-    a = add_part(kept[0], got[0], 1, here.x).astype(F32) + got_a.astype(F32)
-    b = add_part(kept[1], got[1], 0, here.y).astype(F32) + got_b.astype(F32)
-    return a.astype(BF16), b.astype(BF16)
+    a = add_part(kept[0], got[0], 1, here.x) + got_a
+    b = add_part(kept[1], got[1], 0, here.y) + got_b
+    return a, b
 
 
 def quarters_to_send(here, a, b):
@@ -1193,8 +1193,7 @@
     return along_z(value, [(0, 2), (2, 0), (1, 3), (3, 1)])
 
 
-def sum_over_plane(value):
-    value = value + over_core(value)
+def sum_over_img(value):
     return (value + over_x(value)) + (over_y(value) + over_corner(value))
 
 
@@ -1244,32 +1243,49 @@
 
         gather = Gather(jnp.concatenate([aligned(before, shard16, rows - 1), shard16[singles : singles + 16]], axis=0))
         x_got = to_chips(plan, chip_blocks(plan, position, images))
-        values, x_got, band_rows, cots = stage((gather.beside(), x_got, band_rows, cots))
-        tables = make_tables(plan, band_rows, position)
-        cot_sent = chip_blocks(plan, position, cots)
-        table = gather_table(here, lambda z, place: [(8 * z + place) * 22])
-        values, x_blocks, cot_sent, tables, table = stage(
-            (gather.first(values), to_cores(plan, x_got), cot_sent, tables, table)
+        values = gather.beside()
+        values[1], later, core, band_rows = stage((values[1], position, here.core, band_rows))
+        tables = make_tables(plan, band_rows, later)
+        values, x_got, tables, core, cots, params, first_moment, second_moment = stage(
+            (values, x_got, tables, core, cots, params, first_moment, second_moment)
+        )
+        values = gather.first(values)
+        values[3], core, later, cots = stage((values[3], core, position, cots))
+        cot_sent = chip_blocks(plan, later, cots)
+        table = gather_table(here, core, lambda z, place: [(8 * z + place) * 22])
+        values, x_blocks, cot_sent, table = stage((values, to_cores(plan, x_got), cot_sent, table))
+        values = gather.second(values)
+        values[6], params, first_moment, second_moment, later = stage(
+            (values[6], params, first_moment, second_moment, here.owner)
         )
         state = (params, first_moment, second_moment)
-        far = [lax.dynamic_slice_in_dim(rows_of, 176 - here.owner, 176, 0).astype(BF16) for rows_of in state]
+        far = [lax.dynamic_slice_in_dim(rows_of, 176 - later, 176, 0).astype(BF16) for rows_of in state]
         head = jnp.concatenate([rows_of[rows - count :] for rows_of in state], axis=1)
         near = [rows_of[:176] for rows_of in state]
         single_state = [rows_of[singles : singles + 16] for rows_of in state]
         table_again = gather_table(
             here,
+            core,
             lambda z, place: [
                 (8 * (z & 1) + place) * 22 + jnp.where(z < 2, 0, 11),
                 (8 * (z | 2) + place) * 22 + jnp.where(z < 2, 11, 0),
             ],
         )
-        values, far, head, near, single_state, table_again = stage(
-            (gather.second(values), jnp.concatenate(far, axis=1), head, near, single_state, table_again)
-        )
-        values, others = stage((gather.third(values), gather.others(values, 4)))
+        values, others, far, head, near, single_state, table_again = stage(
+            (
+                values,
+                gather.others(values, 4),
+                jnp.concatenate(far, axis=1),
+                head,
+                near,
+                single_state,
+                table_again,
+            )
+        )
+        values, more = stage((gather.third(values), gather.others(values[4:], 6)))
         cot_sent, values = stage((cot_sent, values))
         cot_got = to_chips(plan, cot_sent)
-        pieces, parts = gather.pieces(values, others + gather.others(values[4:], 12)), ((0, rows - 1),)
+        pieces, parts = gather.pieces(values, others + more + gather.others(values[10:], 6)), ((0, rows - 1),)
         pieces, x_blocks = stage((pieces, x_blocks))
     else:
         pieces, parts = [lax.all_gather(params.astype(BF16), AXES, axis=0, tiled=True)], ((0, rows),)
@@ -1302,9 +1318,10 @@
         dy16, kept, sent, out_got = stage((dy16, kept, sent, out_got))
         got = [over_core(value) for value in sent]
         out_got = from_chips(plan, merge_cores(plan, position, out_own, out_got))
+        dy16, kept, got, halves = stage((dy16, kept, got, halves_to_send(here, kept, got)))
+        halves = send_halves(*halves)
         dh1, sums_n2 = run_data_grad(tables, 1, dy16, h1, stats, small, weights)
-        dh1, kept, got = stage((dh1, kept, got))
-        halves = send_halves(*halves_to_send(here, kept, got))
+        dh1, kept, got, halves = stage((dh1, kept, got, halves))
         high = kept, got
         *kept, sums_b1 = run_weight_grad(tables, 0, a1, dh1, early)
         kept, sent = kept[:2], kept[2:]
@@ -1323,9 +1340,10 @@
         )
         low, halves, high, high_got, sums_n1 = stage((low, halves, high, high_got, sums_n1))
         low = add_halves(here, *low, *halves)
-        low, low_sent, sums_n1 = stage((low, quarters_to_send(here, *low), sums_n1))
+        sums = sums_n1 + sums_b1 + sums_n2 + sums_b2 + sums3
+        low, low_sent, sums = stage((low, quarters_to_send(here, *low), sums + over_core(sums)))
         quarters = send_quarters(*low_sent)
-        small_sum = sum_over_plane(sums_n1 + sums_b1 + sums_n2 + sums_b2 + sums3)
+        small_sum = sum_over_img(sums)
         low, quarters, small_sum = stage((low, quarters, small_sum))
         low = by_plane(True, *add_quarters(here, *low, *quarters))
         low_got = send_planes(here, low, small_sum)

time: 459 us -> 451 us (0.983)
  starting transfers between devices: 116 us -> 104 us
  waiting for transfers between devices: 147 us -> 159 us
    convert_element_type x8 -> x0, other arithmetic: 13.9 us -> none  [the longest x4 7.14 us: add_part(): return (both[0] + both[1]).astype(BF16)]
    ppermute x29, starting transfers between devices: 58.5 us -> 45 us  [z_shift(): lax.ppermute(value, 'band', [(2 * z + c, 2 * ((z + k) % nz) + c) for z in...]
    add x3 -> x11, other arithmetic: 0.03 us -> 12.7 us  [the longest x4 5.78 us: add_part(): return both[0] + both[1]]
    ppermute x15, waiting for transfers between devices: 42.7 us -> 54.1 us  [over_x(): return lax.ppermute(value, 'img', [(i, i ^ 1) for i in range(4)])]
  transfers between devices with their start and end apart: 115 -> 115, of which waited for: 58 -> 57; matrix products, arithmetic and copies ran while one was open for 8% -> 8% of each run, Pallas kernels for 28% -> 28%
where the time goes in v4:
time: 451 us; the launch traced here: 443 us
  waiting for transfers between devices  159 us (35%)
  Pallas kernels  123 us (27%)
  starting transfers between devices  104 us (23%)
  other arithmetic  34.9 us (8%)
  local copies, waits for them, and re-layouts  14 us (3%)
  between operations  8.59 us (2%)
    pallas_call x7, Pallas kernels, call(): pl.pallas_call(kernel, name=name, out_shape=[jax.ShapeDtypeStruct(s, d) f...  123 us
    ppermute x29, waiting for transfers between devices, z_shift(): lax.ppermute(value, 'band', [(2 * z + c, 2 * ((z + k) % nz) + c) for z in...  75.4 us
    ppermute x15, waiting for transfers between devices, over_x(): return lax.ppermute(value, 'img', [(i, i ^ 1) for i in range(4)])  54.1 us
    ppermute x29, starting transfers between devices, z_shift(): lax.ppermute(value, 'band', [(2 * z + c, 2 * ((z + k) % nz) + c) for z in...  45 us
    ppermute x15, starting transfers between devices, over_x(): return lax.ppermute(value, 'img', [(i, i ^ 1) for i in range(4)])  17.4 us
    ppermute x15, starting transfers between devices, over_y(): return lax.ppermute(value, 'img', [(i, i ^ 2) for i in range(4)])  16 us
    ppermute x15, waiting for transfers between devices, over_y(): return lax.ppermute(value, 'img', [(i, i ^ 2) for i in range(4)])  15.4 us
    ppermute x48, waiting for transfers between devices, core_swap(): return lax.ppermute(value, 'band', [(b, b ^ 1) for b in range(n_band)])  10.2 us
  transfers between devices with their start and end apart: 115, of which 57 were waited for; matrix products, arithmetic and copies ran while one was open for 8% of the time, Pallas kernels for 28%

profile of v4, /device:TPU:0, one launch (start us, length us, event | category | flops | bytes accessed | tf_op | source)
XLA Modules:
  0.0 443.1 jit_solution(17147160080535130544)
XLA Ops:
  2.0 4.8 %collective-permute-start = (bf16[32,512]{1,0:T(8,128)(2,1)S(1)}, bf16[32,512]{1,0:T(8,128)(2,1)S(1)}, u32[]{:S(2)}, u32[]{:S(2)}) collective-permute-start(bf16[32,512]{1,0:T(8,128)(2,1)S(1)} %slice.490), channel_id=1, source_target_pairs={{0,1},{1,2},{2,3},{3,4},{4,5},{5,6},{6,7},{7,8},{8,9},{9,10},{10,1... | collective-permute-start | bytes 98312 | tf_op jit(solution)/shard_map/ppermute | solution.py:1238
  9.3 2.3 collective-permute-start.1
  14.5 2.6 collective-permute-start.4
  32.3 3.0 collective-permute-done.4.refs_5_
  35.3 2.1 collective-permute-start.6
  37.4 6.8 %collective-permute-start.7 = (bf16[368,512]{1,0:T(8,128)(2,1)}, bf16[368,512]{1,0:T(8,128)(2,1)}, u32[]{:S(2)}, u32[]{:S(2)}) collective-permute-start(bf16[368,512]{1,0:T(8,128)(2,1)} %pad_maximum_fusion.11.refs_11_), channel_id=1, source_target_pairs={{0,8},{4,12},{8,16},{12,20},{16,24},{20,28},{24,0},{28,4},{1,9},{5... | collective-permute-start | bytes 1130504 | tf_op jit(solution)/shard_map/ppermute | solution.py:986
  51.2 4.1 collective-permute-done.7.refs_15_
  55.3 5.2 %collective-permute-done.8.refs_23_ = bf16[368,512]{1,0:T(8,128)(2,1)} collective-permute-done((bf16[368,512]{1,0:T(8,128)(2,1)}, bf16[368,512]{1,0:T(8,128)(2,1)}, u32[]{:S(2)}, u32[]{:S(2)}) %collective-permute-start.8) | collective-permute-done | bytes 376864 | tf_op jit(solution)/shard_map/ppermute | solution.py:986
  66.1 6.3 %collective-permute-done.13.refs_16_ = bf16[368,512]{1,0:T(8,128)(2,1)S(1)} collective-permute-done((bf16[368,512]{1,0:T(8,128)(2,1)}, bf16[368,512]{1,0:T(8,128)(2,1)S(1)}, u32[]{:S(2)}, u32[]{:S(2)}) %collective-permute-start.13) | collective-permute-done | bytes 376864 | tf_op jit(solution)/shard_map/ppermute | solution.py:1075
  73.9 5.0 %collective-permute-done.15.refs_24_ = bf16[368,512]{1,0:T(8,128)(2,1)} collective-permute-done((bf16[368,512]{1,0:T(8,128)(2,1)}, bf16[368,512]{1,0:T(8,128)(2,1)}, u32[]{:S(2)}, u32[]{:S(2)}) %collective-permute-start.15) | collective-permute-done | bytes 376864 | tf_op jit(solution)/shard_map/ppermute | solution.py:1075
  81.5 2.7 collective-permute-done.17.refs_19_
  88.4 7.9 %collective-permute-done.22.refs_20_ = bf16[368,512]{1,0:T(8,128)(2,1)S(1)} collective-permute-done((bf16[368,512]{1,0:T(8,128)(2,1)}, bf16[368,512]{1,0:T(8,128)(2,1)S(1)}, u32[]{:S(2)}, u32[]{:S(2)}) %collective-permute-start.22) | collective-permute-done | bytes 376864 | tf_op jit(solution)/shard_map/ppermute | solution.py:1075
  96.9 7.7 %collective-permute-done.24.refs_22_ = bf16[368,512]{1,0:T(8,128)(2,1)S(1)} collective-permute-done((bf16[368,512]{1,0:T(8,128)(2,1)}, bf16[368,512]{1,0:T(8,128)(2,1)S(1)}, u32[]{:S(2)}, u32[]{:S(2)}) %collective-permute-start.24) | collective-permute-done | bytes 376864 | tf_op jit(solution)/shard_map/ppermute | solution.py:986
  111.2 1.8 collective-permute-start.40
  113.0 2.2 collective-permute-start.41
  116.0 25.9 %features_first.1 = (bf16[1024,512]{1,0:T(8,128)(2,1)}, bf16[1024,512]{1,0:T(8,128)(2,1)}, f32[1024,512]{1,0:T(8,128)}, bf16[1024,512]{1,0:T(8,128)(2,1)}, f32[1...) custom-call(s32[128]{0:T(128)} %broadcast_select_fusion.6.refs_0_.ga, ...), custom_call_target="tpu_custom_call" | custom-call | flops 28600000512 | bytes 37552792 | tf_op jit(solution)/shard_map/features_first/pallas_call | solution.py:806
  145.1 2.0 collective-permute-start.46
  147.1 3.0 collective-permute-start.47
  150.2 25.2 %attend_both.1 = (bf16[768,512]{1,0:T(8,128)(2,1)}, bf16[768,512]{1,0:T(8,128)(2,1)}, f32[1024,512]{1,0:T(8,128)}, bf16[1024,512]{1,0:T(8,128)(2,1)}, bf16[2048,512]{1,0:T(8,128)(2,1)}, /*index=5*/f32[16,512]{1,0:T(8,128)}) custom-call(s32[128]{0:T(128)} %broadcast_select_fusion.6.refs_0_.gather, s32[192]{0:T(256)} %fusion.72.scatter.refs_0_, ...), custom_call_target="tpu_custom_call" | custom-call | flops 26400000000 | bytes 27100436 | tf_op jit(solution)/shard_map/attend_both/pallas_call | solution.py:806
  175.6 9.0 %weight_grad_two.1 = (bf16[1408,512]{1,0:T(8,128)(2,1)}, bf16[1408,512]{1,0:T(8,128)(2,1)}, bf16[1408,512]{1,0:T(8,128)(2,1)}, bf16[1408,512]{1,0:T(8,128)(2,1)}...) custom-call(s32[5]{0:T(128)} %stack.271.refs_1_.flags.refs_0_, bf16[1024,512]{1,0:T(8,128)(2,1)} %get-tuple-element.576.refs_1_, ...), custom_call_target="tpu_custom_call" | custom-call | flops 9900000256 | bytes 11042836 | tf_op jit(solution)/shard_map/weight_grad_two/pallas_call | solution.py:806
  192.6 2.1 collective-permute-start.52
  194.7 12.0 %data_grad_two.1 = (bf16[1024,512]{1,0:T(8,128)(2,1)}, f32[16,512]{1,0:T(8,128)}) custom-call(s32[5]{0:T(128)} %stack.271.refs_1_.flags.refs_0_, bf16[1024,512]{1,0:T(8,128)(2,1)} %get-tuple-element.588.refs_2_.refs_1_, f32[1024,512]{1,0:T(8,128)} %get-tuple-element.589.refs_2_, f32[16,512]{1,0:T(8,128)} %get-tuple-element.554.stats.refs_3_.refs_5_.refs_4_, ...), custom_call_target="tpu_custom_call" | custom-call | flops 13200000000 | bytes 15826964 | tf_op jit(solution)/shard_map/data_grad_two/pallas_call | solution.py:806
  206.7 3.4 collective-permute-done.51
  210.7 10.0 %weight_grad_one.1 = (bf16[1408,512]{1,0:T(8,128)(2,1)}, bf16[1408,512]{1,0:T(8,128)(2,1)}, bf16[1408,512]{1,0:T(8,128)(2,1)}, bf16[1408,512]{1,0:T(8,128)(2,1)}, f32[16,512]{1,0:T(8,128)}) custom-call(s32[5]{0:T(128)} %stack.271.refs_1_.flags.refs_0_, bf16[1024,512]{1,0:T(8,128)(2,1)} %get-tuple-element.542.refs_1_, ...), custom_call_target="tpu_custom_call" | custom-call | flops 9900000256 | bytes 8945684 | tf_op jit(solution)/shard_map/weight_grad_one/pallas_call | solution.py:806
  230.9 2.0 fusion.7
  232.9 2.0 collective-permute-done.59
  235.0 2.3 collective-permute-done.58
  239.9 2.7 collective-permute-start.63
  244.5 13.2 %data_grad_one.1 = (bf16[768,512]{1,0:T(8,128)(2,1)}, bf16[768,512]{1,0:T(8,128)(2,1)}, f32[16,512]{1,0:T(8,128)}) custom-call(s32[192]{0:T(256)} %fusion.72.scatter.refs_0_, s32[5]{0:T(128)} %stack.271.refs_1_.flags.refs_0_, bf16[1024,512]{1,0:T(8,128)(2,1)} %get-tuple-element.633.refs_2_, bf16[1024,512]{1,0:T(8,128)(2,1)} %get-tuple-element.634.refs_3_, ...), custom_call_target="tpu_custom_call" | custom-call | flops 13200000000 | bytes 17400596 | tf_op jit(solution)/shard_map/data_grad_one/pallas_call | solution.py:806
  269.6 7.1 %collective-permute-done.68 = f32[16,512]{1,0:T(8,128)S(1)} collective-permute-done((f32[16,512]{1,0:T(8,128)S(1)}, f32[16,512]{1,0:T(8,128)S(1)}, u32[]{:S(2)}, u32[]{:S(2)}) %collective-permute-start.68) | collective-permute-done | bytes 32800 | tf_op jit(solution)/shard_map/ppermute | solution.py:1075
  278.8 3.2 collective-permute-start.72
  283.0 4.8 %collective-permute-done.71 = bf16[192,512]{1,0:T(8,128)(2,1)S(1)} collective-permute-done((bf16[192,512]{1,0:T(8,128)(2,1)S(1)}, bf16[192,512]{1,0:T(8,128)(2,1)S(1)}, u32[]{:S(2)}, u32[]{:S(2)}) %collective-permute-start.71) | collective-permute-done | bytes 196640 | tf_op jit(solution)/shard_map/ppermute | solution.py:986
  289.4 9.0 %collective-permute-done.73 = bf16[192,512]{1,0:T(8,128)(2,1)S(1)} collective-permute-done((bf16[192,512]{1,0:T(8,128)(2,1)S(1)}, bf16[192,512]{1,0:T(8,128)(2,1)S(1)}, u32[]{:S(2)}, u32[]{:S(2)}) %collective-permute-start.73) | collective-permute-done | bytes 196640 | tf_op jit(solution)/shard_map/ppermute | solution.py:986
  304.5 3.8 collective-permute-start.78
  308.4 4.2 collective-permute-done.74.refs_6_
  312.7 7.8 %collective-permute-done.75.refs_7_ = bf16[368,512]{1,0:T(8,128)(2,1)S(1)} collective-permute-done((bf16[368,512]{1,0:T(8,128)(2,1)S(1)}, bf16[368,512]{1,0:T(8,128)(2,1)S(1)}, u32[]{:S(2)}, u32[]{:S(2)}) %collective-permute-start.75) | collective-permute-done | bytes 376864 | tf_op jit(solution)/shard_map/ppermute | solution.py:1079
  328.0 2.4 collective-permute-start.84
  330.4 3.6 collective-permute-done.80.refs_10_
  335.2 4.0 collective-permute-done.82.refs_18_
  340.4 3.9 collective-permute-done.84.refs_13_
  348.5 7.7 %collective-permute-done.89.refs_14_ = bf16[368,512]{1,0:T(8,128)(2,1)} collective-permute-done((bf16[368,512]{1,0:T(8,128)(2,1)S(1)}, bf16[368,512]{1,0:T(8,128)(2,1)}, u32[]{:S(2)}, u32[]{:S(2)}) %collective-permute-start.89) | collective-permute-done | bytes 376864 | tf_op jit(solution)/shard_map/ppermute | solution.py:1075
  357.4 7.2 %collective-permute-done.91.refs_16_ = bf16[368,512]{1,0:T(8,128)(2,1)} collective-permute-done((bf16[368,512]{1,0:T(8,128)(2,1)S(1)}, bf16[368,512]{1,0:T(8,128)(2,1)}, u32[]{:S(2)}, u32[]{:S(2)}) %collective-permute-start.91) | collective-permute-done | bytes 376864 | tf_op jit(solution)/shard_map/ppermute | solution.py:986
  372.7 5.1 %collective-permute-start.106 = (bf16[288,512]{1,0:T(8,128)(2,1)S(1)}, bf16[288,512]{1,0:T(8,128)(2,1)S(1)}, u32[]{:S(2)}, u32[]{:S(2)}) collective-permute-start(bf16[288,512]{1,0:T(8,128)(2,1)S(1)} %get-tuple-element.836), channel_id=1, source_target_pairs={{0,24},{4,28},{8,0},{12,4},{16,8},{20,12},{24,16},{28,20},{1,25},{... | collective-permute-start | bytes 884744 | tf_op jit(solution)/shard_map/ppermute | solution.py:986
  377.8 1.9 collective-permute-start.108
  379.7 27.8 %forward_again.1 = (bf16[768,512]{1,0:T(8,128)(2,1)}, bf16[768,512]{1,0:T(8,128)(2,1)}) custom-call(s32[192]{0:T(256)} %fusion.72.scatter.refs_0_, s32[5]{0:T(128)} %stack.271.refs_1_.flags.refs_0_, s32[65]{0:T(128)} %pad_add_fusion.5.refs_2_, bf16[1024,512]{1,0:T(8,128)(2,1)} %get-tuple-element.634.refs_3_, ...), custom_call_target="tpu_custom_call" | custom-call | flops 30799998976 | bytes 14713880 | tf_op jit(solution)/shard_map/forward_again/pallas_call | solution.py:806
  414.6 1.9 add_divide_fusion
  416.5 4.4 collective-permute-done.111
  420.9 19.7 %collective-permute-done.112 = bf16[288,512]{1,0:T(8,128)(2,1)S(1)} collective-permute-done((bf16[288,512]{1,0:T(8,128)(2,1)S(1)}, bf16[288,512]{1,0:T(8,128)(2,1)S(1)}, u32[]{:S(2)}, u32[]{:S(2)}) %collective-permute-start.112) | collective-permute-done | bytes 294944 | tf_op jit(solution)/shard_map/ppermute | solution.py:986
  (558 shorter events, 125.4 us)
Async XLA Ops:
  12.9 19.4 %collective-permute-start.3 = (bf16[288,512]{1,0:T(8,128)(2,1)S(1)}, bf16[288,512]{1,0:T(8,128)(2,1)S(1)}, u32[]{:S(2)}, u32[]{:S(2)}) collective-permute-start(bf16[288,512]{1,0:T(8,128)(2,1)S(1)} %get-tuple-element.856), channel_id=1, source_target_pairs={{0,8},{4,12},{8,16},{12,20},{16,24},{20,28},{24,0},{28,4},{1,9},{5... | collective-permute-start | bytes 884744 | tf_op jit(solution)/shard_map/ppermute | solution.py:986
  14.5 20.8 %collective-permute-start.4 = (bf16[288,512]{1,0:T(8,128)(2,1)S(1)}, bf16[288,512]{1,0:T(8,128)(2,1)}, u32[]{:S(2)}, u32[]{:S(2)}) collective-permute-start(bf16[288,512]{1,0:T(8,128)(2,1)S(1)} %get-tuple-element.855), channel_id=1, source_target_pairs={{0,16},{4,20},{8,24},{12,28},{16,0},{20,4},{24,8},{28,12},{1,17},{... | collective-permute-start | bytes 884744 | tf_op jit(solution)/shard_map/ppermute | solution.py:986
  17.0 18.3 %collective-permute-start.5 = (bf16[288,512]{1,0:T(8,128)(2,1)S(1)}, bf16[288,512]{1,0:T(8,128)(2,1)}, u32[]{:S(2)}, u32[]{:S(2)}) collective-permute-start(bf16[288,512]{1,0:T(8,128)(2,1)S(1)} %get-tuple-element.854), channel_id=1, source_target_pairs={{0,24},{4,28},{8,0},{12,4},{16,8},{20,12},{24,16},{28,20},{1,25},{... | collective-permute-start | bytes 884744 | tf_op jit(solution)/shard_map/ppermute | solution.py:986
  18.4 16.9 %collective-permute-start.2 = (bf16[368,512]{1,0:T(8,128)(2,1)}, bf16[368,512]{1,0:T(8,128)(2,1)}, u32[]{:S(2)}, u32[]{:S(2)}) collective-permute-start(bf16[368,512]{1,0:T(8,128)(2,1)} %pad_maximum_fusion.11.refs_11_), channel_id=1, source_target_pairs={{0,2},{1,3},{2,0},{3,1},{4,6},{5,7},{6,4},{7,5},{8,10},{9,11},{10,... | collective-permute-start | bytes 1130504 | tf_op jit(solution)/shard_map/ppermute | solution.py:1079
  37.4 17.9 %collective-permute-start.7 = (bf16[368,512]{1,0:T(8,128)(2,1)}, bf16[368,512]{1,0:T(8,128)(2,1)}, u32[]{:S(2)}, u32[]{:S(2)}) collective-permute-start(bf16[368,512]{1,0:T(8,128)(2,1)} %pad_maximum_fusion.11.refs_11_), channel_id=1, source_target_pairs={{0,8},{4,12},{8,16},{12,20},{16,24},{20,28},{24,0},{28,4},{1,9},{5... | collective-permute-start | bytes 1130504 | tf_op jit(solution)/shard_map/ppermute | solution.py:986
  44.2 16.3 %collective-permute-start.8 = (bf16[368,512]{1,0:T(8,128)(2,1)}, bf16[368,512]{1,0:T(8,128)(2,1)}, u32[]{:S(2)}, u32[]{:S(2)}) collective-permute-start(bf16[368,512]{1,0:T(8,128)(2,1)} %pad_maximum_fusion.11.refs_11_), channel_id=1, source_target_pairs={{0,24},{4,28},{8,0},{12,4},{16,8},{20,12},{24,16},{28,20},{1,25},{... | collective-permute-start | bytes 1130504 | tf_op jit(solution)/shard_map/ppermute | solution.py:986
  62.0 16.9 %collective-permute-start.15 = (bf16[368,512]{1,0:T(8,128)(2,1)}, bf16[368,512]{1,0:T(8,128)(2,1)}, u32[]{:S(2)}, u32[]{:S(2)}) collective-permute-start(bf16[368,512]{1,0:T(8,128)(2,1)} %collective-permute-done.8.refs_23_), channel_id=1, source_target_pairs={{0,1},{1,0},{2,3},{3,2},{4,5},{5,4},{6,7},{7,6},{8,9},{9,8},{10,11... | collective-permute-start | bytes 1130504 | tf_op jit(solution)/shard_map/ppermute | solution.py:1075
  63.7 15.5 %collective-permute-start.16 = (bf16[368,512]{1,0:T(8,128)(2,1)}, bf16[368,512]{1,0:T(8,128)(2,1)}, u32[]{:S(2)}, u32[]{:S(2)}) collective-permute-start(bf16[368,512]{1,0:T(8,128)(2,1)} %collective-permute-done.8.refs_23_), channel_id=1, source_target_pairs={{0,2},{1,3},{2,0},{3,1},{4,6},{5,7},{6,4},{7,5},{8,10},{9,11},{10,... | collective-permute-start | bytes 1130504 | tf_op jit(solution)/shard_map/ppermute | solution.py:1079
  66.1 18.1 %collective-permute-start.17 = (bf16[368,512]{1,0:T(8,128)(2,1)}, bf16[368,512]{1,0:T(8,128)(2,1)}, u32[]{:S(2)}, u32[]{:S(2)}) collective-permute-start(bf16[368,512]{1,0:T(8,128)(2,1)} %pad_maximum_fusion.11.refs_11_), channel_id=1, source_target_pairs={{0,16},{4,20},{8,24},{12,28},{16,0},{20,4},{24,8},{28,12},{1,17},{... | collective-permute-start | bytes 1130504 | tf_op jit(solution)/shard_map/ppermute | solution.py:986
  86.2 18.5 %collective-permute-start.24 = (bf16[368,512]{1,0:T(8,128)(2,1)}, bf16[368,512]{1,0:T(8,128)(2,1)S(1)}, u32[]{:S(2)}, u32[]{:S(2)}) collective-permute-start(bf16[368,512]{1,0:T(8,128)(2,1)} %collective-permute-done.6.refs_14_), channel_id=1, source_target_pairs={{0,16},{4,20},{8,24},{12,28},{16,0},{20,4},{24,8},{28,12},{1,17},{... | collective-permute-start | bytes 1130504 | tf_op jit(solution)/shard_map/ppermute | solution.py:986
  86.2 18.5 %collective-permute-start.25 = (bf16[368,512]{1,0:T(8,128)(2,1)S(1)}, bf16[368,512]{1,0:T(8,128)(2,1)S(1)}, u32[]{:S(2)}, u32[]{:S(2)}) collective-permute-start(bf16[368,512]{1,0:T(8,128)(2,1)S(1)} %copy-done.61), channel_id=1, source_target_pairs={{0,2},{1,3},{2,0},{3,1},{4,6},{5,7},{6,4},{7,5},{8,10},{9,11},{10,... | collective-permute-start | bytes 1130504 | tf_op jit(solution)/shard_map/ppermute | solution.py:1079
  87.0 18.2 %collective-permute-start.26 = (bf16[368,512]{1,0:T(8,128)(2,1)}, bf16[368,512]{1,0:T(8,128)(2,1)S(1)}, u32[]{:S(2)}, u32[]{:S(2)}) collective-permute-start(bf16[368,512]{1,0:T(8,128)(2,1)} %collective-permute-done.16.refs_25_), channel_id=1, source_target_pairs={{0,1},{1,0},{2,3},{3,2},{4,5},{5,4},{6,7},{7,6},{8,9},{9,8},{10,11... | collective-permute-start | bytes 1130504 | tf_op jit(solution)/shard_map/ppermute | solution.py:1075
  111.1 30.8 %collective-permute-start.39 = (bf16[288,512]{1,0:T(8,128)(2,1)S(1)}, bf16[288,512]{1,0:T(8,128)(2,1)}, u32[]{:S(2)}, u32[]{:S(2)}) collective-permute-start(bf16[288,512]{1,0:T(8,128)(2,1)S(1)} %copy-done.23), channel_id=1, source_target_pairs={{0,8},{4,12},{8,16},{12,20},{16,24},{20,28},{24,0},{28,4},{1,9},{5... | collective-permute-start | bytes 884744 | tf_op jit(solution)/shard_map/ppermute | solution.py:986
  111.2 30.8 %collective-permute-start.40 = (bf16[288,512]{1,0:T(8,128)(2,1)S(1)}, bf16[288,512]{1,0:T(8,128)(2,1)}, u32[]{:S(2)}, u32[]{:S(2)}) collective-permute-start(bf16[288,512]{1,0:T(8,128)(2,1)S(1)} %copy-done.22), channel_id=1, source_target_pairs={{0,16},{4,20},{8,24},{12,28},{16,0},{20,4},{24,8},{28,12},{1,17},{... | collective-permute-start | bytes 884744 | tf_op jit(solution)/shard_map/ppermute | solution.py:986
  113.0 29.0 %collective-permute-start.41 = (bf16[288,512]{1,0:T(8,128)(2,1)S(1)}, bf16[288,512]{1,0:T(8,128)(2,1)}, u32[]{:S(2)}, u32[]{:S(2)}) collective-permute-start(bf16[288,512]{1,0:T(8,128)(2,1)S(1)} %copy-done.21), channel_id=1, source_target_pairs={{0,24},{4,28},{8,0},{12,4},{16,8},{20,12},{24,16},{28,20},{1,25},{... | collective-permute-start | bytes 884744 | tf_op jit(solution)/shard_map/ppermute | solution.py:986
  145.1 30.3 %collective-permute-start.46 = (bf16[176,1536]{1,0:T(8,128)(2,1)S(1)}, bf16[176,1536]{1,0:T(8,128)(2,1)S(1)}, u32[]{:S(2)}, u32[]{:S(2)}) collective-permute-start(bf16[176,1536]{1,0:T(8,128)(2,1)S(1)} %pad_maximum_fusion.7), channel_id=1, source_target_pairs={{0,16},{4,20},{16,0},{20,4},{8,24},{12,28},{24,8},{28,12},{1,17},{... | collective-permute-start | bytes 1622024 | tf_op jit(solution)/shard_map/ppermute | solution.py:1083
  147.1 28.3 %collective-permute-start.47 = (f32[32,1536]{1,0:T(8,128)S(1)}, f32[32,1536]{1,0:T(8,128)S(1)}, u32[]{:S(2)}, u32[]{:S(2)}) collective-permute-start(f32[32,1536]{1,0:T(8,128)S(1)} %pad_maximum_fusion.16), channel_id=1, source_target_pairs={{0,1},{1,2},{2,3},{3,4},{4,5},{5,6},{6,7},{7,8},{8,9},{9,10},{10,1... | collective-permute-start | bytes 589832 | tf_op jit(solution)/shard_map/ppermute | solution.py:1304
  186.2 34.5 %collective-permute-start.53 = (bf16[288,512]{1,0:T(8,128)(2,1)}, bf16[288,512]{1,0:T(8,128)(2,1)S(1)}, u32[]{:S(2)}, u32[]{:S(2)}) collective-permute-start(bf16[288,512]{1,0:T(8,128)(2,1)} %get-tuple-element.806), channel_id=1, source_target_pairs={{0,24},{4,28},{8,0},{12,4},{16,8},{20,12},{24,16},{28,20},{1,25},{... | collective-permute-start | bytes 884744 | tf_op jit(solution)/shard_map/ppermute | solution.py:986
  187.7 33.0 %collective-permute-start.54 = (bf16[288,512]{1,0:T(8,128)(2,1)S(1)}, bf16[288,512]{1,0:T(8,128)(2,1)}, u32[]{:S(2)}, u32[]{:S(2)}) collective-permute-start(bf16[288,512]{1,0:T(8,128)(2,1)S(1)} %get-tuple-element.807), channel_id=1, source_target_pairs={{0,16},{4,20},{8,24},{12,28},{16,0},{20,4},{24,8},{28,12},{1,17},{... | collective-permute-start | bytes 884744 | tf_op jit(solution)/shard_map/ppermute | solution.py:986
  187.7 33.0 %collective-permute-start.55 = (bf16[288,512]{1,0:T(8,128)(2,1)S(1)}, bf16[288,512]{1,0:T(8,128)(2,1)}, u32[]{:S(2)}, u32[]{:S(2)}) collective-permute-start(bf16[288,512]{1,0:T(8,128)(2,1)S(1)} %get-tuple-element.804), channel_id=1, source_target_pairs={{0,8},{4,12},{8,16},{12,20},{16,24},{20,28},{24,0},{28,4},{1,9},{5... | collective-permute-start | bytes 884744 | tf_op jit(solution)/shard_map/ppermute | solution.py:986
  191.6 18.4 %collective-permute-start.51 = (bf16[2,352,512]{2,1,0:T(8,128)(2,1)S(1)}, bf16[2,352,512]{2,1,0:T(8,128)(2,1)S(1)}, u32[]{:S(2)}, u32[]{:S(2)}) collective-permute-start(bf16[2,352,512]{2,1,0:T(8,128)(2,1)S(1)} %fusion.8), channel_id=1, source_target_pairs={{0,1},{1,0},{2,3},{3,2},{4,5},{5,4},{6,7},{7,6},{8,9},{9,8},{10,11... | collective-permute-start | bytes 2162696 | tf_op jit(solution)/shard_map/ppermute | solution.py:1075
  192.6 18.1 %collective-permute-start.52 = (bf16[2,352,512]{2,1,0:T(8,128)(2,1)S(1)}, bf16[2,352,512]{2,1,0:T(8,128)(2,1)S(1)}, u32[]{:S(2)}, u32[]{:S(2)}) collective-permute-start(bf16[2,352,512]{2,1,0:T(8,128)(2,1)S(1)} %add_bitcast_fusion.1), channel_id=1, source_target_pairs={{0,2},{1,3},{2,0},{3,1},{4,6},{5,7},{6,4},{7,5},{8,10},{9,11},{10,... | collective-permute-start | bytes 2162696 | tf_op jit(solution)/shard_map/ppermute | solution.py:1079
  238.6 19.2 %collective-permute-start.62 = (bf16[176,512]{1,0:T(8,128)(2,1)}, bf16[176,512]{1,0:T(8,128)(2,1)}, u32[]{:S(2)}, u32[]{:S(2)}) collective-permute-start(bf16[176,512]{1,0:T(8,128)(2,1)} %get-tuple-element.867), channel_id=1, source_target_pairs={{0,8},{4,12},{8,16},{12,20},{16,24},{20,28},{24,0},{28,4},{1,9},{5... | collective-permute-start | bytes 540680 | tf_op jit(solution)/shard_map/ppermute | solution.py:986
  239.9 17.9 %collective-permute-start.63 = (bf16[176,512]{1,0:T(8,128)(2,1)S(1)}, bf16[176,512]{1,0:T(8,128)(2,1)}, u32[]{:S(2)}, u32[]{:S(2)}) collective-permute-start(bf16[176,512]{1,0:T(8,128)(2,1)S(1)} %get-tuple-element.866), channel_id=1, source_target_pairs={{0,24},{4,28},{8,0},{12,4},{16,8},{20,12},{24,16},{28,20},{1,25},{... | collective-permute-start | bytes 540680 | tf_op jit(solution)/shard_map/ppermute | solution.py:986
  242.6 15.2 %collective-permute-start.64 = (bf16[176,512]{1,0:T(8,128)(2,1)S(1)}, bf16[176,512]{1,0:T(8,128)(2,1)}, u32[]{:S(2)}, u32[]{:S(2)}) collective-permute-start(bf16[176,512]{1,0:T(8,128)(2,1)S(1)} %get-tuple-element.865), channel_id=1, source_target_pairs={{0,16},{4,20},{8,24},{12,28},{16,0},{20,4},{24,8},{28,12},{1,17},{... | collective-permute-start | bytes 540680 | tf_op jit(solution)/shard_map/ppermute | solution.py:986
  242.6 16.6 %collective-permute-start.60 = (bf16[2,352,512]{2,1,0:T(8,128)(2,1)}, bf16[2,352,512]{2,1,0:T(8,128)(2,1)S(1)}, u32[]{:S(2)}, u32[]{:S(2)}) collective-permute-start(bf16[2,352,512]{2,1,0:T(8,128)(2,1)} %fusion.7), channel_id=1, source_target_pairs={{0,1},{1,0},{2,3},{3,2},{4,5},{5,4},{6,7},{7,6},{8,9},{9,8},{10,11... | collective-permute-start | bytes 2162696 | tf_op jit(solution)/shard_map/ppermute | solution.py:1075
  243.5 16.2 %collective-permute-start.61 = (bf16[2,352,512]{2,1,0:T(8,128)(2,1)S(1)}, bf16[2,352,512]{2,1,0:T(8,128)(2,1)}, u32[]{:S(2)}, u32[]{:S(2)}) collective-permute-start(bf16[2,352,512]{2,1,0:T(8,128)(2,1)S(1)} %add_bitcast_fusion), channel_id=1, source_target_pairs={{0,2},{1,3},{2,0},{3,1},{4,6},{5,7},{6,4},{7,5},{8,10},{9,11},{10,... | collective-permute-start | bytes 2162696 | tf_op jit(solution)/shard_map/ppermute | solution.py:1079
  263.9 13.5 %collective-permute-start.66 = (bf16[352,512]{1,0:T(8,128)(2,1)S(1)}, bf16[352,512]{1,0:T(8,128)(2,1)S(1)}, u32[]{:S(2)}, u32[]{:S(2)}) collective-permute-start(bf16[352,512]{1,0:T(8,128)(2,1)S(1)} %dynamic-slice_bitcast_fusion.2), channel_id=1, source_target_pairs={{0,2},{1,3},{2,0},{3,1},{4,6},{5,7},{6,4},{7,5},{8,10},{9,11},{10,... | collective-permute-start | bytes 1081352 | tf_op jit(solution)/shard_map/ppermute | solution.py:1079
  265.0 12.4 %collective-permute-start.67 = (bf16[352,512]{1,0:T(8,128)(2,1)S(1)}, bf16[352,512]{1,0:T(8,128)(2,1)S(1)}, u32[]{:S(2)}, u32[]{:S(2)}) collective-permute-start(bf16[352,512]{1,0:T(8,128)(2,1)S(1)} %dynamic-slice_bitcast_fusion.1), channel_id=1, source_target_pairs={{0,1},{1,0},{2,3},{3,2},{4,5},{5,4},{6,7},{7,6},{8,9},{9,8},{10,11... | collective-permute-start | bytes 1081352 | tf_op jit(solution)/shard_map/ppermute | solution.py:1075
  281.9 16.5 %collective-permute-start.73 = (bf16[192,512]{1,0:T(8,128)(2,1)S(1)}, bf16[192,512]{1,0:T(8,128)(2,1)S(1)}, u32[]{:S(2)}, u32[]{:S(2)}) collective-permute-start(bf16[192,512]{1,0:T(8,128)(2,1)S(1)} %get-tuple-element.901), channel_id=1, source_target_pairs={{0,16},{4,20},{8,24},{12,28},{16,0},{20,4},{24,8},{28,12},{1,17},{... | collective-permute-start | bytes 589832 | tf_op jit(solution)/shard_map/ppermute | solution.py:986
  282.8 21.7 %collective-permute-start.79 = (bf16[768,512]{1,0:T(8,128)(2,1)S(1)}, bf16[768,512]{1,0:T(8,128)(2,1)S(1)}, u32[]{:S(2)}, u32[]{:S(2)}) collective-permute-start(bf16[768,512]{1,0:T(8,128)(2,1)S(1)} %copy-done.52), channel_id=1, source_target_pairs={{0,4},{4,0},{8,12},{12,8},{16,20},{20,16},{24,28},{28,24},{1,5},{5... | collective-permute-start | bytes 2359304 | tf_op jit(solution)/shard_map/ppermute | solution.py:990
  302.2 18.3 %collective-permute-start.75 = (bf16[368,512]{1,0:T(8,128)(2,1)S(1)}, bf16[368,512]{1,0:T(8,128)(2,1)S(1)}, u32[]{:S(2)}, u32[]{:S(2)}) collective-permute-start(bf16[368,512]{1,0:T(8,128)(2,1)S(1)} %pad_maximum_fusion.12.refs_5_), channel_id=1, source_target_pairs={{0,2},{1,3},{2,0},{3,1},{4,6},{5,7},{6,4},{7,5},{8,10},{9,11},{10,... | collective-permute-start | bytes 1130504 | tf_op jit(solution)/shard_map/ppermute | solution.py:1079
  303.0 17.5 %collective-permute-start.76 = (bf16[368,512]{1,0:T(8,128)(2,1)S(1)}, bf16[368,512]{1,0:T(8,128)(2,1)S(1)}, u32[]{:S(2)}, u32[]{:S(2)}) collective-permute-start(bf16[368,512]{1,0:T(8,128)(2,1)S(1)} %pad_maximum_fusion.12.refs_5_), channel_id=1, source_target_pairs={{0,3},{1,2},{2,1},{3,0},{4,7},{5,6},{6,5},{7,4},{8,11},{9,10},{10,... | collective-permute-start | bytes 1130504 | tf_op jit(solution)/shard_map/ppermute | solution.py:1087
  304.5 16.0 %collective-permute-start.77 = (bf16[368,512]{1,0:T(8,128)(2,1)S(1)}, bf16[368,512]{1,0:T(8,128)(2,1)S(1)}, u32[]{:S(2)}, u32[]{:S(2)}) collective-permute-start(bf16[368,512]{1,0:T(8,128)(2,1)S(1)} %pad_maximum_fusion.12.refs_5_), channel_id=1, source_target_pairs={{0,8},{4,12},{8,16},{12,20},{16,24},{20,28},{24,0},{28,4},{1,9},{5... | collective-permute-start | bytes 1130504 | tf_op jit(solution)/shard_map/ppermute | solution.py:986
  304.5 17.8 %collective-permute-start.78 = (bf16[368,512]{1,0:T(8,128)(2,1)S(1)}, bf16[368,512]{1,0:T(8,128)(2,1)S(1)}, u32[]{:S(2)}, u32[]{:S(2)}) collective-permute-start(bf16[368,512]{1,0:T(8,128)(2,1)S(1)} %pad_maximum_fusion.12.refs_5_), channel_id=1, source_target_pairs={{0,24},{4,28},{8,0},{12,4},{16,8},{20,12},{24,16},{28,20},{1,25},{... | collective-permute-start | bytes 1130504 | tf_op jit(solution)/shard_map/ppermute | solution.py:986
  324.2 14.9 %collective-permute-start.82 = (bf16[368,512]{1,0:T(8,128)(2,1)S(1)}, bf16[368,512]{1,0:T(8,128)(2,1)S(1)}, u32[]{:S(2)}, u32[]{:S(2)}) collective-permute-start(bf16[368,512]{1,0:T(8,128)(2,1)S(1)} %collective-permute-done.78.refs_17_), channel_id=1, source_target_pairs={{0,1},{1,0},{2,3},{3,2},{4,5},{5,4},{6,7},{7,6},{8,9},{9,8},{10,11... | collective-permute-start | bytes 1130504 | tf_op jit(solution)/shard_map/ppermute | solution.py:1075
  325.4 14.7 %collective-permute-start.83 = (bf16[368,512]{1,0:T(8,128)(2,1)S(1)}, bf16[368,512]{1,0:T(8,128)(2,1)S(1)}, u32[]{:S(2)}, u32[]{:S(2)}) collective-permute-start(bf16[368,512]{1,0:T(8,128)(2,1)S(1)} %collective-permute-done.78.refs_17_), channel_id=1, source_target_pairs={{0,2},{1,3},{2,0},{3,1},{4,6},{5,7},{6,4},{7,5},{8,10},{9,11},{10,... | collective-permute-start | bytes 1130504 | tf_op jit(solution)/shard_map/ppermute | solution.py:1079
  328.0 16.4 %collective-permute-start.84 = (bf16[368,512]{1,0:T(8,128)(2,1)S(1)}, bf16[368,512]{1,0:T(8,128)(2,1)S(1)}, u32[]{:S(2)}, u32[]{:S(2)}) collective-permute-start(bf16[368,512]{1,0:T(8,128)(2,1)S(1)} %pad_maximum_fusion.12.refs_5_), channel_id=1, source_target_pairs={{0,16},{4,20},{8,24},{12,28},{16,0},{20,4},{24,8},{28,12},{1,17},{... | collective-permute-start | bytes 1130504 | tf_op jit(solution)/shard_map/ppermute | solution.py:986
  346.4 18.1 %collective-permute-start.91 = (bf16[368,512]{1,0:T(8,128)(2,1)S(1)}, bf16[368,512]{1,0:T(8,128)(2,1)}, u32[]{:S(2)}, u32[]{:S(2)}) collective-permute-start(bf16[368,512]{1,0:T(8,128)(2,1)S(1)} %collective-permute-done.76.refs_8_), channel_id=1, source_target_pairs={{0,16},{4,20},{8,24},{12,28},{16,0},{20,4},{24,8},{28,12},{1,17},{... | collective-permute-start | bytes 1130504 | tf_op jit(solution)/shard_map/ppermute | solution.py:986
  346.4 18.2 %collective-permute-start.92 = (bf16[368,512]{1,0:T(8,128)(2,1)S(1)}, bf16[368,512]{1,0:T(8,128)(2,1)S(1)}, u32[]{:S(2)}, u32[]{:S(2)}) collective-permute-start(bf16[368,512]{1,0:T(8,128)(2,1)S(1)} %collective-permute-done.80.refs_10_), channel_id=1, source_target_pairs={{0,2},{1,3},{2,0},{3,1},{4,6},{5,7},{6,4},{7,5},{8,10},{9,11},{10,... | collective-permute-start | bytes 1130504 | tf_op jit(solution)/shard_map/ppermute | solution.py:1079
  347.6 17.5 %collective-permute-start.93 = (bf16[368,512]{1,0:T(8,128)(2,1)S(1)}, bf16[368,512]{1,0:T(8,128)(2,1)}, u32[]{:S(2)}, u32[]{:S(2)}) collective-permute-start(bf16[368,512]{1,0:T(8,128)(2,1)S(1)} %collective-permute-done.83.refs_19_), channel_id=1, source_target_pairs={{0,1},{1,0},{2,3},{3,2},{4,5},{5,4},{6,7},{7,6},{8,9},{9,8},{10,11... | collective-permute-start | bytes 1130504 | tf_op jit(solution)/shard_map/ppermute | solution.py:1075
  370.8 36.7 %collective-permute-start.109 = (bf16[176,512]{1,0:T(8,128)(2,1)S(1)}, bf16[176,512]{1,0:T(8,128)(2,1)S(1)}, u32[]{:S(2)}, u32[]{:S(2)}) collective-permute-start(bf16[176,512]{1,0:T(8,128)(2,1)S(1)} %select_convert_fusion), channel_id=1, source_target_pairs={{0,16},{4,20},{16,0},{20,4},{8,24},{12,28},{24,8},{28,12},{1,17},{... | collective-permute-start | bytes 540680 | tf_op jit(solution)/shard_map/ppermute | solution.py:1083
  371.0 36.9 %collective-permute-start.114 = (f32[32,512]{1,0:T(8,128)S(1)}, f32[32,512]{1,0:T(8,128)S(1)}, u32[]{:S(2)}, u32[]{:S(2)}) collective-permute-start(f32[32,512]{1,0:T(8,128)S(1)} %slice.514), channel_id=1, source_target_pairs={{1,0},{2,1},{3,2},{4,3},{5,4},{6,5},{7,6},{8,7},{9,8},{10,9},{11,1... | collective-permute-start | bytes 196616 | tf_op jit(solution)/shard_map/ppermute | solution.py:1399
  372.7 34.8 %collective-permute-start.106 = (bf16[288,512]{1,0:T(8,128)(2,1)S(1)}, bf16[288,512]{1,0:T(8,128)(2,1)S(1)}, u32[]{:S(2)}, u32[]{:S(2)}) collective-permute-start(bf16[288,512]{1,0:T(8,128)(2,1)S(1)} %get-tuple-element.836), channel_id=1, source_target_pairs={{0,24},{4,28},{8,0},{12,4},{16,8},{20,12},{24,16},{28,20},{1,25},{... | collective-permute-start | bytes 884744 | tf_op jit(solution)/shard_map/ppermute | solution.py:986
  377.8 30.1 %collective-permute-start.107 = (bf16[288,512]{1,0:T(8,128)(2,1)S(1)}, bf16[288,512]{1,0:T(8,128)(2,1)S(1)}, u32[]{:S(2)}, u32[]{:S(2)}) collective-permute-start(bf16[288,512]{1,0:T(8,128)(2,1)S(1)} %get-tuple-element.835), channel_id=1, source_target_pairs={{0,16},{4,20},{8,24},{12,28},{16,0},{20,4},{24,8},{28,12},{1,17},{... | collective-permute-start | bytes 884744 | tf_op jit(solution)/shard_map/ppermute | solution.py:986
  377.8 30.1 %collective-permute-start.108 = (bf16[288,512]{1,0:T(8,128)(2,1)S(1)}, bf16[288,512]{1,0:T(8,128)(2,1)S(1)}, u32[]{:S(2)}, u32[]{:S(2)}) collective-permute-start(bf16[288,512]{1,0:T(8,128)(2,1)S(1)} %get-tuple-element.834), channel_id=1, source_target_pairs={{0,8},{4,12},{8,16},{12,20},{16,24},{20,28},{24,0},{28,4},{1,9},{5... | collective-permute-start | bytes 884744 | tf_op jit(solution)/shard_map/ppermute | solution.py:986
  413.5 27.1 %collective-permute-start.112 = (bf16[288,512]{1,0:T(8,128)(2,1)S(1)}, bf16[288,512]{1,0:T(8,128)(2,1)S(1)}, u32[]{:S(2)}, u32[]{:S(2)}) collective-permute-start(bf16[288,512]{1,0:T(8,128)(2,1)S(1)} %get-tuple-element.799), channel_id=1, source_target_pairs={{0,16},{4,20},{8,24},{12,28},{16,0},{20,4},{24,8},{28,12},{1,17},{... | collective-permute-start | bytes 884744 | tf_op jit(solution)/shard_map/ppermute | solution.py:986
  414.6 26.0 %collective-permute-start.113 = (bf16[288,512]{1,0:T(8,128)(2,1)S(1)}, bf16[288,512]{1,0:T(8,128)(2,1)S(1)}, u32[]{:S(2)}, u32[]{:S(2)}) collective-permute-start(bf16[288,512]{1,0:T(8,128)(2,1)S(1)} %get-tuple-element.798), channel_id=1, source_target_pairs={{0,8},{4,12},{8,16},{12,20},{16,24},{20,28},{24,0},{28,4},{1,9},{5... | collective-permute-start | bytes 884744 | tf_op jit(solution)/shard_map/ppermute | solution.py:986
  (176 other events, 1970.8 us)

commit v5 on v4

--- a/solution.py
+++ b/solution.py
@@ -1235,16 +1235,18 @@
     images, cots = (x_small, x_medium, x_large), (cot_small, cot_medium, cot_large)
     if here.planes:
         shard16 = params.astype(BF16)
-        before = lax.ppermute(shard16[rows - count :], AXES, [(o, o + 1) for o in range(last)])
+        before = lax.ppermute(params[rows - count :].astype(BF16), AXES, [(o, o + 1) for o in range(last)])
 
         def aligned(head, shard, size):
             both = jnp.concatenate([head, shard], axis=0)
             return lax.dynamic_slice_in_dim(both, count - here.owner, size, 0)
 
-        gather = Gather(jnp.concatenate([aligned(before, shard16, rows - 1), shard16[singles : singles + 16]], axis=0))
-        x_got = to_chips(plan, chip_blocks(plan, position, images))
+        before, x_sent = stage((before, chip_blocks(plan, position, images)))
+        x_got = to_chips(plan, x_sent)
+        x_got[1], before, later, core, band_rows = stage((x_got[1], before, position, here.core, band_rows))
+        block = aligned(before, shard16, rows - 1)
+        gather = Gather(jnp.concatenate([block, shard16[singles : singles + 16]], axis=0))
         values = gather.beside()
-        values[1], later, core, band_rows = stage((values[1], position, here.core, band_rows))
         tables = make_tables(plan, band_rows, later)
         values, x_got, tables, core, cots, params, first_moment, second_moment = stage(
             (values, x_got, tables, core, cots, params, first_moment, second_moment)
@@ -1299,9 +1301,8 @@
     cot_got, y = stage((cot_got, y))
     cot_blocks = to_cores(plan, cot_got)
     if here.planes:
-        cot_blocks, far, head = stage((cot_blocks, far, head))
+        cot_blocks, far = stage((cot_blocks, far))
         far = over_two_planes(far)
-        before = lax.ppermute(head, AXES, [(o, o + 1) for o in range(last)])
     out_own, out_oth, dy, dy16, g_proj, sums3 = run_attend_both(
         plan, tables, q, k, v, y, z, cot_blocks, stats, small, weights
     )
@@ -1311,7 +1312,7 @@
             update, _, _ = adam(*state, grad, step_count, step_rate)
             return (state[0] - update).astype(BF16)
 
-        dy16, far, before, out_oth = stage((dy16, far, before, out_oth))
+        dy16, far, out_oth = stage((dy16, far, out_oth))
         out_got = over_core(out_oth)
         *kept, early, sums_b2 = run_weight_grad(tables, 1, a2, dy16, g_proj)
         kept, sent = kept[:2], kept[2:]
@@ -1344,7 +1345,8 @@
         low, low_sent, sums = stage((low, quarters_to_send(here, *low), sums + over_core(sums)))
         quarters = send_quarters(*low_sent)
         small_sum = sum_over_img(sums)
-        low, quarters, small_sum = stage((low, quarters, small_sum))
+        low, quarters, small_sum, head = stage((low, quarters, small_sum, head))
+        before = lax.ppermute(head, AXES, [(o, o + 1) for o in range(last)])
         low = by_plane(True, *add_quarters(here, *low, *quarters))
         low_got = send_planes(here, low, small_sum)
         low, low_got, before, far, high, high_got = stage((low, low_got, before, far, high, high_got))

time: 451 us -> 449 us (level)
  waiting for transfers between devices: 159 us -> 150 us
  starting transfers between devices: 104 us -> 109 us
    ppermute x15, waiting for transfers between devices: 54.1 us -> 44.4 us  [over_x(): return lax.ppermute(value, 'img', [(i, i ^ 1) for i in range(4)])]
    ppermute x29, starting transfers between devices: 45 us -> 53.8 us  [z_shift(): lax.ppermute(value, 'band', [(2 * z + c, 2 * ((z + k) % nz) + c) for z in...]
  transfers between devices with their start and end apart: 115 -> 115, of which waited for: 57 -> 56; matrix products, arithmetic and copies ran while one was open for 8% -> 9% of each run, Pallas kernels for 28% -> 28%
where the time goes in v5:
time: 449 us; the launch traced here: 441 us
  waiting for transfers between devices  150 us (33%)
  Pallas kernels  123 us (27%)
  starting transfers between devices  109 us (24%)
  other arithmetic  35.6 us (8%)
  local copies, waits for them, and re-layouts  14.6 us (3%)
  between operations  8.54 us (2%)
    pallas_call x7, Pallas kernels, call(): pl.pallas_call(kernel, name=name, out_shape=[jax.ShapeDtypeStruct(s, d) f...  123 us
    ppermute x29, waiting for transfers between devices, z_shift(): lax.ppermute(value, 'band', [(2 * z + c, 2 * ((z + k) % nz) + c) for z in...  77 us
    ppermute x29, starting transfers between devices, z_shift(): lax.ppermute(value, 'band', [(2 * z + c, 2 * ((z + k) % nz) + c) for z in...  53.8 us
    ppermute x15, waiting for transfers between devices, over_x(): return lax.ppermute(value, 'img', [(i, i ^ 1) for i in range(4)])  44.4 us
    ppermute x15, waiting for transfers between devices, over_y(): return lax.ppermute(value, 'img', [(i, i ^ 2) for i in range(4)])  17.3 us
    ppermute x15, starting transfers between devices, over_y(): return lax.ppermute(value, 'img', [(i, i ^ 2) for i in range(4)])  16.8 us
    ppermute x15, starting transfers between devices, over_x(): return lax.ppermute(value, 'img', [(i, i ^ 1) for i in range(4)])  14.4 us
    ppermute x48, waiting for transfers between devices, core_swap(): return lax.ppermute(value, 'band', [(b, b ^ 1) for b in range(n_band)])  10.7 us
  transfers between devices with their start and end apart: 115, of which 56 were waited for; matrix products, arithmetic and copies ran while one was open for 9% of the time, Pallas kernels for 28%

profile of v5, /device:TPU:0, one launch (start us, length us, event | category | flops | bytes accessed | tf_op | source)
XLA Modules:
  0.0 440.9 jit_solution(14421083548184815006)
XLA Ops:
  2.0 4.8 %collective-permute-start = (bf16[32,512]{1,0:T(8,128)(2,1)S(1)}, bf16[32,512]{1,0:T(8,128)(2,1)S(1)}, u32[]{:S(2)}, u32[]{:S(2)}) collective-permute-start(bf16[32,512]{1,0:T(8,128)(2,1)S(1)} %slice.491), channel_id=1, source_target_pairs={{0,1},{1,2},{2,3},{3,4},{4,5},{5,6},{6,7},{7,8},{8,9},{9,10},{10,1... | collective-permute-start | bytes 98312 | tf_op jit(solution)/shard_map/ppermute | solution.py:1238
  8.4 3.6 collective-permute-start.1
  12.0 2.6 collective-permute-start.4
  16.0 6.1 %collective-permute-done.1.refs_4_ = bf16[288,512]{1,0:T(8,128)(2,1)S(1)} collective-permute-done((bf16[288,512]{1,0:T(8,128)(2,1)S(1)}, bf16[288,512]{1,0:T(8,128)(2,1)S(1)}, u32[]{:S(2)}, u32[]{:S(2)}) %collective-permute-start.1) | collective-permute-done | bytes 294944 | tf_op jit(solution)/shard_map/ppermute | solution.py:986
  37.4 12.0 %collective-permute-start.7 = (bf16[368,512]{1,0:T(8,128)(2,1)}, bf16[368,512]{1,0:T(8,128)(2,1)}, u32[]{:S(2)}, u32[]{:S(2)}) collective-permute-start(bf16[368,512]{1,0:T(8,128)(2,1)} %pad_maximum_fusion.11.refs_11_), channel_id=1, source_target_pairs={{0,8},{4,12},{8,16},{12,20},{16,24},{20,28},{24,0},{28,4},{1,9},{5... | collective-permute-start | bytes 1130504 | tf_op jit(solution)/shard_map/ppermute | solution.py:986
  54.9 4.1 collective-permute-done.8.refs_23_
  64.6 4.4 collective-permute-start.17
  70.9 2.7 collective-permute-done.15.refs_24_
  76.2 7.7 %collective-permute-done.17.refs_19_ = bf16[368,512]{1,0:T(8,128)(2,1)} collective-permute-done((bf16[368,512]{1,0:T(8,128)(2,1)}, bf16[368,512]{1,0:T(8,128)(2,1)}, u32[]{:S(2)}, u32[]{:S(2)}) %collective-permute-start.17) | collective-permute-done | bytes 376864 | tf_op jit(solution)/shard_map/ppermute | solution.py:986
  88.7 7.2 %collective-permute-done.22.refs_20_ = bf16[368,512]{1,0:T(8,128)(2,1)S(1)} collective-permute-done((bf16[368,512]{1,0:T(8,128)(2,1)}, bf16[368,512]{1,0:T(8,128)(2,1)S(1)}, u32[]{:S(2)}, u32[]{:S(2)}) %collective-permute-start.22) | collective-permute-done | bytes 376864 | tf_op jit(solution)/shard_map/ppermute | solution.py:1075
  97.4 6.2 %collective-permute-done.24.refs_22_ = bf16[368,512]{1,0:T(8,128)(2,1)S(1)} collective-permute-done((bf16[368,512]{1,0:T(8,128)(2,1)}, bf16[368,512]{1,0:T(8,128)(2,1)S(1)}, u32[]{:S(2)}, u32[]{:S(2)}) %collective-permute-start.24) | collective-permute-done | bytes 376864 | tf_op jit(solution)/shard_map/ppermute | solution.py:986
  111.0 3.1 collective-permute-start.41
  115.0 25.9 %features_first.1 = (bf16[1024,512]{1,0:T(8,128)(2,1)}, bf16[1024,512]{1,0:T(8,128)(2,1)}, f32[1024,512]{1,0:T(8,128)}, bf16[1024,512]{1,0:T(8,128)(2,1)}, f32[1...) custom-call(s32[128]{0:T(128)} %broadcast_select_fusion.6.refs_0_.ga, ...), custom_call_target="tpu_custom_call" | custom-call | flops 28600000512 | bytes 37552792 | tf_op jit(solution)/shard_map/features_first/pallas_call | solution.py:806
  144.1 2.0 collective-permute-start.46
  146.1 25.3 %attend_both.1 = (bf16[768,512]{1,0:T(8,128)(2,1)}, bf16[768,512]{1,0:T(8,128)(2,1)}, f32[1024,512]{1,0:T(8,128)}, bf16[1024,512]{1,0:T(8,128)(2,1)}, bf16[2048,512]{1,0:T(8,128)(2,1)}, /*index=5*/f32[16,512]{1,0:T(8,128)}) custom-call(s32[128]{0:T(128)} %broadcast_select_fusion.6.refs_0_.gather, s32[192]{0:T(256)} %fusion.72.scatter.refs_0_, ...), custom_call_target="tpu_custom_call" | custom-call | flops 26400000000 | bytes 27100436 | tf_op jit(solution)/shard_map/attend_both/pallas_call | solution.py:806
  171.5 9.1 %weight_grad_two.1 = (bf16[1408,512]{1,0:T(8,128)(2,1)}, bf16[1408,512]{1,0:T(8,128)(2,1)}, bf16[1408,512]{1,0:T(8,128)(2,1)}, bf16[1408,512]{1,0:T(8,128)(2,1)}...) custom-call(s32[5]{0:T(128)} %stack.271.refs_1_.flags.refs_0_, bf16[1024,512]{1,0:T(8,128)(2,1)} %get-tuple-element.585.refs_1_, ...), custom_call_target="tpu_custom_call" | custom-call | flops 9900000256 | bytes 11042836 | tf_op jit(solution)/shard_map/weight_grad_two/pallas_call | solution.py:806
  187.7 1.7 collective-permute-start.50
  190.3 12.0 %data_grad_two.1 = (bf16[1024,512]{1,0:T(8,128)(2,1)}, f32[16,512]{1,0:T(8,128)}) custom-call(s32[5]{0:T(128)} %stack.271.refs_1_.flags.refs_0_, bf16[1024,512]{1,0:T(8,128)(2,1)} %get-tuple-element.597.refs_2_.refs_1_, f32[1024,512]{1,0:T(8,128)} %get-tuple-element.598.refs_2_, f32[16,512]{1,0:T(8,128)} %get-tuple-element.565.stats.refs_3_.refs_5_.refs_4_, ...), custom_call_target="tpu_custom_call" | custom-call | flops 13200000000 | bytes 15826964 | tf_op jit(solution)/shard_map/data_grad_two/pallas_call | solution.py:806
  202.3 3.8 collective-permute-done.50
  207.6 9.8 %weight_grad_one.1 = (bf16[1408,512]{1,0:T(8,128)(2,1)}, bf16[1408,512]{1,0:T(8,128)(2,1)}, bf16[1408,512]{1,0:T(8,128)(2,1)}, bf16[1408,512]{1,0:T(8,128)(2,1)}, f32[16,512]{1,0:T(8,128)}) custom-call(s32[5]{0:T(128)} %stack.271.refs_1_.flags.refs_0_, bf16[1024,512]{1,0:T(8,128)(2,1)} %get-tuple-element.553.refs_1_, ...), custom_call_target="tpu_custom_call" | custom-call | flops 9900000256 | bytes 8945684 | tf_op jit(solution)/shard_map/weight_grad_one/pallas_call | solution.py:806
  226.2 2.2 add_bitcast_fusion
  228.4 2.0 fusion.7
  232.1 1.7 collective-permute-done.57
  236.6 2.6 collective-permute-start.62
  241.5 13.2 %data_grad_one.1 = (bf16[768,512]{1,0:T(8,128)(2,1)}, bf16[768,512]{1,0:T(8,128)(2,1)}, f32[16,512]{1,0:T(8,128)}) custom-call(s32[192]{0:T(256)} %fusion.72.scatter.refs_0_, s32[5]{0:T(128)} %stack.271.refs_1_.flags.refs_0_, bf16[1024,512]{1,0:T(8,128)(2,1)} %get-tuple-element.642.refs_2_, bf16[1024,512]{1,0:T(8,128)(2,1)} %get-tuple-element.643.refs_3_, ...), custom_call_target="tpu_custom_call" | custom-call | flops 13200000000 | bytes 17400596 | tf_op jit(solution)/shard_map/data_grad_one/pallas_call | solution.py:806
  266.6 7.3 %collective-permute-done.67 = f32[16,512]{1,0:T(8,128)S(1)} collective-permute-done((f32[16,512]{1,0:T(8,128)S(1)}, f32[16,512]{1,0:T(8,128)S(1)}, u32[]{:S(2)}, u32[]{:S(2)}) %collective-permute-start.67) | collective-permute-done | bytes 32800 | tf_op jit(solution)/shard_map/ppermute | solution.py:1075
  276.2 3.2 collective-permute-start.71
  280.2 2.6 collective-permute-start.73
  283.0 2.2 collective-permute-done.70
  286.9 9.0 %collective-permute-done.72 = bf16[192,512]{1,0:T(8,128)(2,1)S(1)} collective-permute-done((bf16[192,512]{1,0:T(8,128)(2,1)S(1)}, bf16[192,512]{1,0:T(8,128)(2,1)S(1)}, u32[]{:S(2)}, u32[]{:S(2)}) %collective-permute-start.72) | collective-permute-done | bytes 196640 | tf_op jit(solution)/shard_map/ppermute | solution.py:986
  300.0 2.0 collective-permute-start.76
  302.0 3.8 collective-permute-start.78
  305.9 4.2 collective-permute-done.74.refs_6_
  310.1 7.3 %collective-permute-done.75.refs_7_ = bf16[368,512]{1,0:T(8,128)(2,1)S(1)} collective-permute-done((bf16[368,512]{1,0:T(8,128)(2,1)S(1)}, bf16[368,512]{1,0:T(8,128)(2,1)S(1)}, u32[]{:S(2)}, u32[]{:S(2)}) %collective-permute-start.75) | collective-permute-done | bytes 376864 | tf_op jit(solution)/shard_map/ppermute | solution.py:1079
  317.5 2.3 collective-permute-done.78.refs_17_
  320.5 1.7 collective-permute-start.81
  325.4 2.4 collective-permute-start.84
  327.8 3.6 collective-permute-done.80.refs_10_
  332.2 4.4 collective-permute-done.82.refs_18_
  338.3 3.5 collective-permute-done.84.refs_13_
  343.5 1.7 collective-permute-start.90
  346.1 7.8 %collective-permute-done.89.refs_14_ = bf16[368,512]{1,0:T(8,128)(2,1)S(1)} collective-permute-done((bf16[368,512]{1,0:T(8,128)(2,1)}, bf16[368,512]{1,0:T(8,128)(2,1)S(1)}, u32[]{:S(2)}, u32[]{:S(2)}) %collective-permute-start.89) | collective-permute-done | bytes 376864 | tf_op jit(solution)/shard_map/ppermute | solution.py:1075
  355.4 8.3 %collective-permute-done.91.refs_16_ = bf16[368,512]{1,0:T(8,128)(2,1)} collective-permute-done((bf16[368,512]{1,0:T(8,128)(2,1)S(1)}, bf16[368,512]{1,0:T(8,128)(2,1)}, u32[]{:S(2)}, u32[]{:S(2)}) %collective-permute-start.91) | collective-permute-done | bytes 376864 | tf_op jit(solution)/shard_map/ppermute | solution.py:986
  371.9 3.8 collective-permute-start.106
  377.4 27.8 %forward_again.1 = (bf16[768,512]{1,0:T(8,128)(2,1)}, bf16[768,512]{1,0:T(8,128)(2,1)}) custom-call(s32[192]{0:T(256)} %fusion.72.scatter.refs_0_, s32[5]{0:T(128)} %stack.271.refs_1_.flags.refs_0_, s32[65]{0:T(128)} %pad_add_fusion.5.refs_2_, bf16[1024,512]{1,0:T(8,128)(2,1)} %get-tuple-element.643.refs_3_, ...), custom_call_target="tpu_custom_call" | custom-call | flops 30799998976 | bytes 14713880 | tf_op jit(solution)/shard_map/forward_again/pallas_call | solution.py:806
  413.1 1.9 add_divide_fusion
  415.0 5.2 %collective-permute-done.111 = bf16[288,512]{1,0:T(8,128)(2,1)S(1)} collective-permute-done((bf16[288,512]{1,0:T(8,128)(2,1)S(1)}, bf16[288,512]{1,0:T(8,128)(2,1)S(1)}, u32[]{:S(2)}, u32[]{:S(2)}) %collective-permute-start.111) | collective-permute-done | bytes 294944 | tf_op jit(solution)/shard_map/ppermute | solution.py:986
  420.2 18.2 %collective-permute-done.112 = bf16[288,512]{1,0:T(8,128)(2,1)S(1)} collective-permute-done((bf16[288,512]{1,0:T(8,128)(2,1)S(1)}, bf16[288,512]{1,0:T(8,128)(2,1)S(1)}, u32[]{:S(2)}, u32[]{:S(2)}) %collective-permute-start.112) | collective-permute-done | bytes 294944 | tf_op jit(solution)/shard_map/ppermute | solution.py:986
  (562 shorter events, 122.1 us)
Async XLA Ops:
  8.4 13.7 %collective-permute-start.1 = (bf16[288,512]{1,0:T(8,128)(2,1)S(1)}, bf16[288,512]{1,0:T(8,128)(2,1)S(1)}, u32[]{:S(2)}, u32[]{:S(2)}) collective-permute-start(bf16[288,512]{1,0:T(8,128)(2,1)S(1)} %get-tuple-element.402), channel_id=1, source_target_pairs={{0,8},{4,12},{8,16},{12,20},{16,24},{20,28},{24,0},{28,4},{1,9},{5... | collective-permute-start | bytes 884744 | tf_op jit(solution)/shard_map/ppermute | solution.py:986
  12.0 23.8 %collective-permute-start.4 = (bf16[288,512]{1,0:T(8,128)(2,1)S(1)}, bf16[288,512]{1,0:T(8,128)(2,1)}, u32[]{:S(2)}, u32[]{:S(2)}) collective-permute-start(bf16[288,512]{1,0:T(8,128)(2,1)S(1)} %get-tuple-element.407), channel_id=1, source_target_pairs={{0,16},{4,20},{8,24},{12,28},{16,0},{20,4},{24,8},{28,12},{1,17},{... | collective-permute-start | bytes 884744 | tf_op jit(solution)/shard_map/ppermute | solution.py:986
  14.7 21.2 %collective-permute-start.5 = (bf16[288,512]{1,0:T(8,128)(2,1)S(1)}, bf16[288,512]{1,0:T(8,128)(2,1)}, u32[]{:S(2)}, u32[]{:S(2)}) collective-permute-start(bf16[288,512]{1,0:T(8,128)(2,1)S(1)} %get-tuple-element.408), channel_id=1, source_target_pairs={{0,24},{4,28},{8,0},{12,4},{16,8},{20,12},{24,16},{28,20},{1,25},{... | collective-permute-start | bytes 884744 | tf_op jit(solution)/shard_map/ppermute | solution.py:986
  23.3 12.6 %collective-permute-start.2 = (bf16[368,512]{1,0:T(8,128)(2,1)}, bf16[368,512]{1,0:T(8,128)(2,1)}, u32[]{:S(2)}, u32[]{:S(2)}) collective-permute-start(bf16[368,512]{1,0:T(8,128)(2,1)} %pad_maximum_fusion.11.refs_11_), channel_id=1, source_target_pairs={{0,1},{1,0},{2,3},{3,2},{4,5},{5,4},{6,7},{7,6},{8,9},{9,8},{10,11... | collective-permute-start | bytes 1130504 | tf_op jit(solution)/shard_map/ppermute | solution.py:1075
  35.9 14.1 %collective-permute-start.6 = (bf16[368,512]{1,0:T(8,128)(2,1)}, bf16[368,512]{1,0:T(8,128)(2,1)}, u32[]{:S(2)}, u32[]{:S(2)}) collective-permute-start(bf16[368,512]{1,0:T(8,128)(2,1)} %pad_maximum_fusion.11.refs_11_), channel_id=1, source_target_pairs={{0,3},{1,2},{2,1},{3,0},{4,7},{5,6},{6,5},{7,4},{8,11},{9,10},{10,... | collective-permute-start | bytes 1130504 | tf_op jit(solution)/shard_map/ppermute | solution.py:1087
  37.4 17.5 %collective-permute-start.7 = (bf16[368,512]{1,0:T(8,128)(2,1)}, bf16[368,512]{1,0:T(8,128)(2,1)}, u32[]{:S(2)}, u32[]{:S(2)}) collective-permute-start(bf16[368,512]{1,0:T(8,128)(2,1)} %pad_maximum_fusion.11.refs_11_), channel_id=1, source_target_pairs={{0,8},{4,12},{8,16},{12,20},{16,24},{20,28},{24,0},{28,4},{1,9},{5... | collective-permute-start | bytes 1130504 | tf_op jit(solution)/shard_map/ppermute | solution.py:986
  60.3 13.2 %collective-permute-start.15 = (bf16[368,512]{1,0:T(8,128)(2,1)}, bf16[368,512]{1,0:T(8,128)(2,1)}, u32[]{:S(2)}, u32[]{:S(2)}) collective-permute-start(bf16[368,512]{1,0:T(8,128)(2,1)} %collective-permute-done.8.refs_23_), channel_id=1, source_target_pairs={{0,1},{1,0},{2,3},{3,2},{4,5},{5,4},{6,7},{7,6},{8,9},{9,8},{10,11... | collective-permute-start | bytes 1130504 | tf_op jit(solution)/shard_map/ppermute | solution.py:1075
  64.6 19.4 %collective-permute-start.17 = (bf16[368,512]{1,0:T(8,128)(2,1)}, bf16[368,512]{1,0:T(8,128)(2,1)}, u32[]{:S(2)}, u32[]{:S(2)}) collective-permute-start(bf16[368,512]{1,0:T(8,128)(2,1)} %pad_maximum_fusion.11.refs_11_), channel_id=1, source_target_pairs={{0,16},{4,20},{8,24},{12,28},{16,0},{20,4},{24,8},{28,12},{1,17},{... | collective-permute-start | bytes 1130504 | tf_op jit(solution)/shard_map/ppermute | solution.py:986
  70.2 13.8 %collective-permute-start.18 = (bf16[368,512]{1,0:T(8,128)(2,1)}, bf16[368,512]{1,0:T(8,128)(2,1)}, u32[]{:S(2)}, u32[]{:S(2)}) collective-permute-start(bf16[368,512]{1,0:T(8,128)(2,1)} %pad_maximum_fusion.11.refs_11_), channel_id=1, source_target_pairs={{0,4},{4,0},{8,12},{12,8},{16,20},{20,16},{24,28},{28,24},{1,5},{5... | collective-permute-start | bytes 1130504 | tf_op jit(solution)/shard_map/ppermute | solution.py:990
  70.3 13.6 %collective-permute-start.19 = (bf16[368,512]{1,0:T(8,128)(2,1)}, bf16[368,512]{1,0:T(8,128)(2,1)S(1)}, u32[]{:S(2)}, u32[]{:S(2)}) collective-permute-start(bf16[368,512]{1,0:T(8,128)(2,1)} %collective-permute-done.2.refs_12_), channel_id=1, source_target_pairs={{0,4},{4,0},{8,12},{12,8},{16,20},{20,16},{24,28},{28,24},{1,5},{5... | collective-permute-start | bytes 1130504 | tf_op jit(solution)/shard_map/ppermute | solution.py:990
  86.8 16.8 %collective-permute-start.24 = (bf16[368,512]{1,0:T(8,128)(2,1)}, bf16[368,512]{1,0:T(8,128)(2,1)S(1)}, u32[]{:S(2)}, u32[]{:S(2)}) collective-permute-start(bf16[368,512]{1,0:T(8,128)(2,1)} %collective-permute-done.6.refs_14_), channel_id=1, source_target_pairs={{0,16},{4,20},{8,24},{12,28},{16,0},{20,4},{24,8},{28,12},{1,17},{... | collective-permute-start | bytes 1130504 | tf_op jit(solution)/shard_map/ppermute | solution.py:986
  86.8 17.2 %collective-permute-start.25 = (bf16[368,512]{1,0:T(8,128)(2,1)S(1)}, bf16[368,512]{1,0:T(8,128)(2,1)S(1)}, u32[]{:S(2)}, u32[]{:S(2)}) collective-permute-start(bf16[368,512]{1,0:T(8,128)(2,1)S(1)} %copy-done.61), channel_id=1, source_target_pairs={{0,2},{1,3},{2,0},{3,1},{4,6},{5,7},{6,4},{7,5},{8,10},{9,11},{10,... | collective-permute-start | bytes 1130504 | tf_op jit(solution)/shard_map/ppermute | solution.py:1079
  87.5 16.7 %collective-permute-start.26 = (bf16[368,512]{1,0:T(8,128)(2,1)}, bf16[368,512]{1,0:T(8,128)(2,1)S(1)}, u32[]{:S(2)}, u32[]{:S(2)}) collective-permute-start(bf16[368,512]{1,0:T(8,128)(2,1)} %collective-permute-done.16.refs_25_), channel_id=1, source_target_pairs={{0,1},{1,0},{2,3},{3,2},{4,5},{5,4},{6,7},{7,6},{8,9},{9,8},{10,11... | collective-permute-start | bytes 1130504 | tf_op jit(solution)/shard_map/ppermute | solution.py:1075
  110.1 30.8 %collective-permute-start.39 = (bf16[288,512]{1,0:T(8,128)(2,1)S(1)}, bf16[288,512]{1,0:T(8,128)(2,1)}, u32[]{:S(2)}, u32[]{:S(2)}) collective-permute-start(bf16[288,512]{1,0:T(8,128)(2,1)S(1)} %copy-done.26), channel_id=1, source_target_pairs={{0,8},{4,12},{8,16},{12,20},{16,24},{20,28},{24,0},{28,4},{1,9},{5... | collective-permute-start | bytes 884744 | tf_op jit(solution)/shard_map/ppermute | solution.py:986
  110.2 30.8 %collective-permute-start.40 = (bf16[288,512]{1,0:T(8,128)(2,1)S(1)}, bf16[288,512]{1,0:T(8,128)(2,1)}, u32[]{:S(2)}, u32[]{:S(2)}) collective-permute-start(bf16[288,512]{1,0:T(8,128)(2,1)S(1)} %copy-done.25), channel_id=1, source_target_pairs={{0,16},{4,20},{8,24},{12,28},{16,0},{20,4},{24,8},{28,12},{1,17},{... | collective-permute-start | bytes 884744 | tf_op jit(solution)/shard_map/ppermute | solution.py:986
  111.0 29.9 %collective-permute-start.41 = (bf16[288,512]{1,0:T(8,128)(2,1)S(1)}, bf16[288,512]{1,0:T(8,128)(2,1)}, u32[]{:S(2)}, u32[]{:S(2)}) collective-permute-start(bf16[288,512]{1,0:T(8,128)(2,1)S(1)} %copy-done.24), channel_id=1, source_target_pairs={{0,24},{4,28},{8,0},{12,4},{16,8},{20,12},{24,16},{28,20},{1,25},{... | collective-permute-start | bytes 884744 | tf_op jit(solution)/shard_map/ppermute | solution.py:986
  144.1 27.3 %collective-permute-start.46 = (bf16[176,1536]{1,0:T(8,128)(2,1)S(1)}, bf16[176,1536]{1,0:T(8,128)(2,1)S(1)}, u32[]{:S(2)}, u32[]{:S(2)}) collective-permute-start(bf16[176,1536]{1,0:T(8,128)(2,1)S(1)} %pad_maximum_fusion.7), channel_id=1, source_target_pairs={{0,16},{4,20},{16,0},{20,4},{8,24},{12,28},{24,8},{28,12},{1,17},{... | collective-permute-start | bytes 1622024 | tf_op jit(solution)/shard_map/ppermute | solution.py:1083
  182.3 35.1 %collective-permute-start.52 = (bf16[288,512]{1,0:T(8,128)(2,1)}, bf16[288,512]{1,0:T(8,128)(2,1)S(1)}, u32[]{:S(2)}, u32[]{:S(2)}) collective-permute-start(bf16[288,512]{1,0:T(8,128)(2,1)} %get-tuple-element.816), channel_id=1, source_target_pairs={{0,24},{4,28},{8,0},{12,4},{16,8},{20,12},{24,16},{28,20},{1,25},{... | collective-permute-start | bytes 884744 | tf_op jit(solution)/shard_map/ppermute | solution.py:986
  183.9 34.2 %collective-permute-start.53 = (bf16[288,512]{1,0:T(8,128)(2,1)}, bf16[288,512]{1,0:T(8,128)(2,1)}, u32[]{:S(2)}, u32[]{:S(2)}) collective-permute-start(bf16[288,512]{1,0:T(8,128)(2,1)} %get-tuple-element.817), channel_id=1, source_target_pairs={{0,16},{4,20},{8,24},{12,28},{16,0},{20,4},{24,8},{28,12},{1,17},{... | collective-permute-start | bytes 884744 | tf_op jit(solution)/shard_map/ppermute | solution.py:986
  183.9 34.2 %collective-permute-start.54 = (bf16[288,512]{1,0:T(8,128)(2,1)}, bf16[288,512]{1,0:T(8,128)(2,1)}, u32[]{:S(2)}, u32[]{:S(2)}) collective-permute-start(bf16[288,512]{1,0:T(8,128)(2,1)} %get-tuple-element.814), channel_id=1, source_target_pairs={{0,8},{4,12},{8,16},{12,20},{16,24},{20,28},{24,0},{28,4},{1,9},{5... | collective-permute-start | bytes 884744 | tf_op jit(solution)/shard_map/ppermute | solution.py:986
  187.7 18.4 %collective-permute-start.50 = (bf16[2,352,512]{2,1,0:T(8,128)(2,1)S(1)}, bf16[2,352,512]{2,1,0:T(8,128)(2,1)S(1)}, u32[]{:S(2)}, u32[]{:S(2)}) collective-permute-start(bf16[2,352,512]{2,1,0:T(8,128)(2,1)S(1)} %fusion.8), channel_id=1, source_target_pairs={{0,1},{1,0},{2,3},{3,2},{4,5},{5,4},{6,7},{7,6},{8,9},{9,8},{10,11... | collective-permute-start | bytes 2162696 | tf_op jit(solution)/shard_map/ppermute | solution.py:1075
  189.4 18.2 %collective-permute-start.51 = (bf16[2,352,512]{2,1,0:T(8,128)(2,1)S(1)}, bf16[2,352,512]{2,1,0:T(8,128)(2,1)}, u32[]{:S(2)}, u32[]{:S(2)}) collective-permute-start(bf16[2,352,512]{2,1,0:T(8,128)(2,1)S(1)} %add_bitcast_fusion.1), channel_id=1, source_target_pairs={{0,2},{1,3},{2,0},{3,1},{4,6},{5,7},{6,4},{7,5},{8,10},{9,11},{10,... | collective-permute-start | bytes 2162696 | tf_op jit(solution)/shard_map/ppermute | solution.py:1079
  235.2 19.6 %collective-permute-start.61 = (bf16[176,512]{1,0:T(8,128)(2,1)}, bf16[176,512]{1,0:T(8,128)(2,1)}, u32[]{:S(2)}, u32[]{:S(2)}) collective-permute-start(bf16[176,512]{1,0:T(8,128)(2,1)} %get-tuple-element.877), channel_id=1, source_target_pairs={{0,8},{4,12},{8,16},{12,20},{16,24},{20,28},{24,0},{28,4},{1,9},{5... | collective-permute-start | bytes 540680 | tf_op jit(solution)/shard_map/ppermute | solution.py:986
  236.6 18.2 %collective-permute-start.62 = (bf16[176,512]{1,0:T(8,128)(2,1)}, bf16[176,512]{1,0:T(8,128)(2,1)}, u32[]{:S(2)}, u32[]{:S(2)}) collective-permute-start(bf16[176,512]{1,0:T(8,128)(2,1)} %get-tuple-element.876), channel_id=1, source_target_pairs={{0,24},{4,28},{8,0},{12,4},{16,8},{20,12},{24,16},{28,20},{1,25},{... | collective-permute-start | bytes 540680 | tf_op jit(solution)/shard_map/ppermute | solution.py:986
  239.2 15.6 %collective-permute-start.63 = (bf16[176,512]{1,0:T(8,128)(2,1)S(1)}, bf16[176,512]{1,0:T(8,128)(2,1)}, u32[]{:S(2)}, u32[]{:S(2)}) collective-permute-start(bf16[176,512]{1,0:T(8,128)(2,1)S(1)} %get-tuple-element.875), channel_id=1, source_target_pairs={{0,16},{4,20},{8,24},{12,28},{16,0},{20,4},{24,8},{28,12},{1,17},{... | collective-permute-start | bytes 540680 | tf_op jit(solution)/shard_map/ppermute | solution.py:986
  239.2 16.8 %collective-permute-start.59 = (bf16[2,352,512]{2,1,0:T(8,128)(2,1)}, bf16[2,352,512]{2,1,0:T(8,128)(2,1)}, u32[]{:S(2)}, u32[]{:S(2)}) collective-permute-start(bf16[2,352,512]{2,1,0:T(8,128)(2,1)} %fusion.7), channel_id=1, source_target_pairs={{0,1},{1,0},{2,3},{3,2},{4,5},{5,4},{6,7},{7,6},{8,9},{9,8},{10,11... | collective-permute-start | bytes 2162696 | tf_op jit(solution)/shard_map/ppermute | solution.py:1075
  240.7 16.4 %collective-permute-start.60 = (bf16[2,352,512]{2,1,0:T(8,128)(2,1)}, bf16[2,352,512]{2,1,0:T(8,128)(2,1)}, u32[]{:S(2)}, u32[]{:S(2)}) collective-permute-start(bf16[2,352,512]{2,1,0:T(8,128)(2,1)} %add_bitcast_fusion), channel_id=1, source_target_pairs={{0,2},{1,3},{2,0},{3,1},{4,6},{5,7},{6,4},{7,5},{8,10},{9,11},{10,... | collective-permute-start | bytes 2162696 | tf_op jit(solution)/shard_map/ppermute | solution.py:1079
  261.4 13.5 %collective-permute-start.65 = (bf16[352,512]{1,0:T(8,128)(2,1)S(1)}, bf16[352,512]{1,0:T(8,128)(2,1)S(1)}, u32[]{:S(2)}, u32[]{:S(2)}) collective-permute-start(bf16[352,512]{1,0:T(8,128)(2,1)S(1)} %dynamic-slice_bitcast_fusion.2), channel_id=1, source_target_pairs={{0,2},{1,3},{2,0},{3,1},{4,6},{5,7},{6,4},{7,5},{8,10},{9,11},{10,... | collective-permute-start | bytes 1081352 | tf_op jit(solution)/shard_map/ppermute | solution.py:1079
  279.4 16.5 %collective-permute-start.72 = (bf16[192,512]{1,0:T(8,128)(2,1)S(1)}, bf16[192,512]{1,0:T(8,128)(2,1)S(1)}, u32[]{:S(2)}, u32[]{:S(2)}) collective-permute-start(bf16[192,512]{1,0:T(8,128)(2,1)S(1)} %get-tuple-element.911), channel_id=1, source_target_pairs={{0,16},{4,20},{8,24},{12,28},{16,0},{20,4},{24,8},{28,12},{1,17},{... | collective-permute-start | bytes 589832 | tf_op jit(solution)/shard_map/ppermute | solution.py:986
  280.2 15.7 %collective-permute-start.73 = (f32[32,1536]{1,0:T(8,128)S(1)}, f32[32,1536]{1,0:T(8,128)S(1)}, u32[]{:S(2)}, u32[]{:S(2)}) collective-permute-start(f32[32,1536]{1,0:T(8,128)S(1)} %pad_maximum_fusion.16), channel_id=1, source_target_pairs={{0,1},{1,2},{2,3},{3,4},{4,5},{5,6},{6,7},{7,8},{8,9},{9,10},{10,1... | collective-permute-start | bytes 589832 | tf_op jit(solution)/shard_map/ppermute | solution.py:1349
  282.8 19.1 %collective-permute-start.79 = (bf16[768,512]{1,0:T(8,128)(2,1)S(1)}, bf16[768,512]{1,0:T(8,128)(2,1)S(1)}, u32[]{:S(2)}, u32[]{:S(2)}) collective-permute-start(bf16[768,512]{1,0:T(8,128)(2,1)S(1)} %copy-done.52), channel_id=1, source_target_pairs={{0,4},{4,0},{8,12},{12,8},{16,20},{20,16},{24,28},{28,24},{1,5},{5... | collective-permute-start | bytes 2359304 | tf_op jit(solution)/shard_map/ppermute | solution.py:990
  299.1 18.3 %collective-permute-start.75 = (bf16[368,512]{1,0:T(8,128)(2,1)S(1)}, bf16[368,512]{1,0:T(8,128)(2,1)S(1)}, u32[]{:S(2)}, u32[]{:S(2)}) collective-permute-start(bf16[368,512]{1,0:T(8,128)(2,1)S(1)} %pad_maximum_fusion.12.refs_5_), channel_id=1, source_target_pairs={{0,2},{1,3},{2,0},{3,1},{4,6},{5,7},{6,4},{7,5},{8,10},{9,11},{10,... | collective-permute-start | bytes 1130504 | tf_op jit(solution)/shard_map/ppermute | solution.py:1079
  300.0 17.5 %collective-permute-start.76 = (bf16[368,512]{1,0:T(8,128)(2,1)S(1)}, bf16[368,512]{1,0:T(8,128)(2,1)S(1)}, u32[]{:S(2)}, u32[]{:S(2)}) collective-permute-start(bf16[368,512]{1,0:T(8,128)(2,1)S(1)} %pad_maximum_fusion.12.refs_5_), channel_id=1, source_target_pairs={{0,3},{1,2},{2,1},{3,0},{4,7},{5,6},{6,5},{7,4},{8,11},{9,10},{10,... | collective-permute-start | bytes 1130504 | tf_op jit(solution)/shard_map/ppermute | solution.py:1087
  301.9 15.5 %collective-permute-start.77 = (bf16[368,512]{1,0:T(8,128)(2,1)S(1)}, bf16[368,512]{1,0:T(8,128)(2,1)S(1)}, u32[]{:S(2)}, u32[]{:S(2)}) collective-permute-start(bf16[368,512]{1,0:T(8,128)(2,1)S(1)} %pad_maximum_fusion.12.refs_5_), channel_id=1, source_target_pairs={{0,8},{4,12},{8,16},{12,20},{16,24},{20,28},{24,0},{28,4},{1,9},{5... | collective-permute-start | bytes 1130504 | tf_op jit(solution)/shard_map/ppermute | solution.py:986
  302.0 17.8 %collective-permute-start.78 = (bf16[368,512]{1,0:T(8,128)(2,1)S(1)}, bf16[368,512]{1,0:T(8,128)(2,1)S(1)}, u32[]{:S(2)}, u32[]{:S(2)}) collective-permute-start(bf16[368,512]{1,0:T(8,128)(2,1)S(1)} %pad_maximum_fusion.12.refs_5_), channel_id=1, source_target_pairs={{0,24},{4,28},{8,0},{12,4},{16,8},{20,12},{24,16},{28,20},{1,25},{... | collective-permute-start | bytes 1130504 | tf_op jit(solution)/shard_map/ppermute | solution.py:986
  322.2 14.4 %collective-permute-start.82 = (bf16[368,512]{1,0:T(8,128)(2,1)S(1)}, bf16[368,512]{1,0:T(8,128)(2,1)S(1)}, u32[]{:S(2)}, u32[]{:S(2)}) collective-permute-start(bf16[368,512]{1,0:T(8,128)(2,1)S(1)} %collective-permute-done.78.refs_17_), channel_id=1, source_target_pairs={{0,1},{1,0},{2,3},{3,2},{4,5},{5,4},{6,7},{7,6},{8,9},{9,8},{10,11... | collective-permute-start | bytes 1130504 | tf_op jit(solution)/shard_map/ppermute | solution.py:1075
  322.6 15.4 %collective-permute-start.83 = (bf16[368,512]{1,0:T(8,128)(2,1)S(1)}, bf16[368,512]{1,0:T(8,128)(2,1)S(1)}, u32[]{:S(2)}, u32[]{:S(2)}) collective-permute-start(bf16[368,512]{1,0:T(8,128)(2,1)S(1)} %collective-permute-done.78.refs_17_), channel_id=1, source_target_pairs={{0,2},{1,3},{2,0},{3,1},{4,6},{5,7},{6,4},{7,5},{8,10},{9,11},{10,... | collective-permute-start | bytes 1130504 | tf_op jit(solution)/shard_map/ppermute | solution.py:1079
  325.4 16.5 %collective-permute-start.84 = (bf16[368,512]{1,0:T(8,128)(2,1)S(1)}, bf16[368,512]{1,0:T(8,128)(2,1)}, u32[]{:S(2)}, u32[]{:S(2)}) collective-permute-start(bf16[368,512]{1,0:T(8,128)(2,1)S(1)} %pad_maximum_fusion.12.refs_5_), channel_id=1, source_target_pairs={{0,16},{4,20},{8,24},{12,28},{16,0},{20,4},{24,8},{28,12},{1,17},{... | collective-permute-start | bytes 1130504 | tf_op jit(solution)/shard_map/ppermute | solution.py:986
  345.2 18.5 %collective-permute-start.91 = (bf16[368,512]{1,0:T(8,128)(2,1)S(1)}, bf16[368,512]{1,0:T(8,128)(2,1)}, u32[]{:S(2)}, u32[]{:S(2)}) collective-permute-start(bf16[368,512]{1,0:T(8,128)(2,1)S(1)} %collective-permute-done.76.refs_8_), channel_id=1, source_target_pairs={{0,16},{4,20},{8,24},{12,28},{16,0},{20,4},{24,8},{28,12},{1,17},{... | collective-permute-start | bytes 1130504 | tf_op jit(solution)/shard_map/ppermute | solution.py:986
  345.2 18.5 %collective-permute-start.92 = (bf16[368,512]{1,0:T(8,128)(2,1)S(1)}, bf16[368,512]{1,0:T(8,128)(2,1)S(1)}, u32[]{:S(2)}, u32[]{:S(2)}) collective-permute-start(bf16[368,512]{1,0:T(8,128)(2,1)S(1)} %collective-permute-done.80.refs_10_), channel_id=1, source_target_pairs={{0,2},{1,3},{2,0},{3,1},{4,6},{5,7},{6,4},{7,5},{8,10},{9,11},{10,... | collective-permute-start | bytes 1130504 | tf_op jit(solution)/shard_map/ppermute | solution.py:1079
  345.5 18.8 %collective-permute-start.93 = (bf16[368,512]{1,0:T(8,128)(2,1)S(1)}, bf16[368,512]{1,0:T(8,128)(2,1)}, u32[]{:S(2)}, u32[]{:S(2)}) collective-permute-start(bf16[368,512]{1,0:T(8,128)(2,1)S(1)} %collective-permute-done.83.refs_19_), channel_id=1, source_target_pairs={{0,1},{1,0},{2,3},{3,2},{4,5},{5,4},{6,7},{7,6},{8,9},{9,8},{10,11... | collective-permute-start | bytes 1130504 | tf_op jit(solution)/shard_map/ppermute | solution.py:1075
  370.1 35.0 %collective-permute-start.109 = (bf16[176,512]{1,0:T(8,128)(2,1)S(1)}, bf16[176,512]{1,0:T(8,128)(2,1)S(1)}, u32[]{:S(2)}, u32[]{:S(2)}) collective-permute-start(bf16[176,512]{1,0:T(8,128)(2,1)S(1)} %select_convert_fusion), channel_id=1, source_target_pairs={{0,16},{4,20},{16,0},{20,4},{8,24},{12,28},{24,8},{28,12},{1,17},{... | collective-permute-start | bytes 540680 | tf_op jit(solution)/shard_map/ppermute | solution.py:1083
  370.2 36.7 %collective-permute-start.114 = (f32[32,512]{1,0:T(8,128)S(1)}, f32[32,512]{1,0:T(8,128)S(1)}, u32[]{:S(2)}, u32[]{:S(2)}) collective-permute-start(f32[32,512]{1,0:T(8,128)S(1)} %slice.515), channel_id=1, source_target_pairs={{1,0},{2,1},{3,2},{4,3},{5,4},{6,5},{7,6},{8,7},{9,8},{10,9},{11,1... | collective-permute-start | bytes 196616 | tf_op jit(solution)/shard_map/ppermute | solution.py:1401
  371.9 33.3 %collective-permute-start.106 = (bf16[288,512]{1,0:T(8,128)(2,1)S(1)}, bf16[288,512]{1,0:T(8,128)(2,1)S(1)}, u32[]{:S(2)}, u32[]{:S(2)}) collective-permute-start(bf16[288,512]{1,0:T(8,128)(2,1)S(1)} %get-tuple-element.846), channel_id=1, source_target_pairs={{0,24},{4,28},{8,0},{12,4},{16,8},{20,12},{24,16},{28,20},{1,25},{... | collective-permute-start | bytes 884744 | tf_op jit(solution)/shard_map/ppermute | solution.py:986
  375.7 31.1 %collective-permute-start.107 = (bf16[288,512]{1,0:T(8,128)(2,1)S(1)}, bf16[288,512]{1,0:T(8,128)(2,1)S(1)}, u32[]{:S(2)}, u32[]{:S(2)}) collective-permute-start(bf16[288,512]{1,0:T(8,128)(2,1)S(1)} %get-tuple-element.845), channel_id=1, source_target_pairs={{0,16},{4,20},{8,24},{12,28},{16,0},{20,4},{24,8},{28,12},{1,17},{... | collective-permute-start | bytes 884744 | tf_op jit(solution)/shard_map/ppermute | solution.py:986
  376.2 30.6 %collective-permute-start.108 = (bf16[288,512]{1,0:T(8,128)(2,1)S(1)}, bf16[288,512]{1,0:T(8,128)(2,1)S(1)}, u32[]{:S(2)}, u32[]{:S(2)}) collective-permute-start(bf16[288,512]{1,0:T(8,128)(2,1)S(1)} %get-tuple-element.844), channel_id=1, source_target_pairs={{0,8},{4,12},{8,16},{12,20},{16,24},{20,28},{24,0},{28,4},{1,9},{5... | collective-permute-start | bytes 884744 | tf_op jit(solution)/shard_map/ppermute | solution.py:986
  411.9 26.6 %collective-permute-start.112 = (bf16[288,512]{1,0:T(8,128)(2,1)S(1)}, bf16[288,512]{1,0:T(8,128)(2,1)S(1)}, u32[]{:S(2)}, u32[]{:S(2)}) collective-permute-start(bf16[288,512]{1,0:T(8,128)(2,1)S(1)} %get-tuple-element.809), channel_id=1, source_target_pairs={{0,16},{4,20},{8,24},{12,28},{16,0},{20,4},{24,8},{28,12},{1,17},{... | collective-permute-start | bytes 884744 | tf_op jit(solution)/shard_map/ppermute | solution.py:986
  412.5 26.0 %collective-permute-start.113 = (bf16[288,512]{1,0:T(8,128)(2,1)S(1)}, bf16[288,512]{1,0:T(8,128)(2,1)S(1)}, u32[]{:S(2)}, u32[]{:S(2)}) collective-permute-start(bf16[288,512]{1,0:T(8,128)(2,1)S(1)} %get-tuple-element.808), channel_id=1, source_target_pairs={{0,8},{4,12},{8,16},{12,20},{16,24},{20,28},{24,0},{28,4},{1,9},{5... | collective-permute-start | bytes 884744 | tf_op jit(solution)/shard_map/ppermute | solution.py:986
  (177 other events, 2083.2 us)

commit v6 on v5

--- a/solution.py
+++ b/solution.py
@@ -57,10 +57,12 @@
         self.block = max(self.sizes[2 * j] + self.sizes[2 * j + 1] for j in range(self.n_chip))
         self.piece = max(self.sizes)
         self.offs = [0 if b % 2 == 0 else self.piece - self.sizes[b] for b in range(n_band)]
-        self.is_l = np.array([int("l" in h) for h in holders], np.int32)
-        self.has_m = np.array([int("m" in h) for h in holders], np.int32)
-        self.has_s = np.array([int("s" in h) for h in holders], np.int32)
-        self.off = np.array(self.offs, np.int32)
+        rows, flags = [], []
+        for b, h in enumerate(holders):
+            large, middle, small = int("l" in h), int("m" in h), int("s" in h)
+            rows.append([large, middle, small, self.offs[b]])
+            flags.append([large, 32 if large else 24 * middle, 32 if large else 32 * small, 16 - 16 * large, b % 2])
+        self.rows, self.flags = np.array(rows, np.int32), np.array(flags, np.int32)
 
 
 def pick(table, index):
@@ -70,7 +72,8 @@
 def make_tables(plan, band_rows, position):
     nz = plan.n_chip
     z, core = position // 2, position % 2
-    is_l, has_m, has_s, off = (pick(t, position) for t in (plan.is_l, plan.has_m, plan.has_s, plan.off))
+    own = pick(plan.rows, position)
+    is_l, has_m, has_s, off = own[0], own[1], own[2], own[3]
     starts = jnp.cumsum(band_rows, axis=1) - band_rows
     zero_in = plan.n_band * plan.piece // 8
 
@@ -128,15 +131,7 @@
         jnp.where(ok_l, out_l, 128),
         jnp.where(ok_m, out_m, jnp.where(ok_s, out_s, 128)),
     ).astype(jnp.int32)
-    flags = jnp.stack(
-        [
-            is_l,
-            jnp.where(is_l == 1, 32, 24 * has_m),
-            jnp.where(is_l == 1, 32, 32 * has_s),
-            jnp.where(is_l == 1, 0, 16),
-            core,
-        ]
-    ).astype(jnp.int32)
+    flags = pick(plan.flags, position)
     return gather, scatter, flags
 
 
@@ -272,12 +267,12 @@
     return pl.ds(pl.multiple_of(line * 32, 32), 256)
 
 
-def tile_loop(body):
+def tile_loop(body, unroll=2):
     def step(tile, carry):
         body(tile)
         return carry
 
-    lax.fori_loop(0, 4, step, 0, unroll=2)
+    lax.fori_loop(0, 4, step, 0, unroll=unroll)
 
 
 def conv_tiles(buf_ref, w_ref, out_ref):
@@ -288,7 +283,7 @@
             acc = term if acc is None else acc + term
         out_ref[tile_at(tile), :] = acc
 
-    tile_loop(body)
+    tile_loop(body, 4)
 
 
 def gather_pieces(table_ref, src_ref, dst_ref, count):

time: 449 us -> 449 us (level)
  no operation moved by 1% of the time
where the time goes in v6:
time: 449 us; the launch traced here: 440 us
  waiting for transfers between devices  150 us (33%)
  Pallas kernels  122 us (27%)
  starting transfers between devices  111 us (25%)
  other arithmetic  35.5 us (8%)
  local copies, waits for them, and re-layouts  13.4 us (3%)
  between operations  7.22 us (2%)
    pallas_call x7, Pallas kernels, call(): pl.pallas_call(kernel, name=name, out_shape=[jax.ShapeDtypeStruct(s, d) f...  122 us
    ppermute x29, waiting for transfers between devices, z_shift(): lax.ppermute(value, 'band', [(2 * z + c, 2 * ((z + k) % nz) + c) for z in...  76.7 us
    ppermute x29, starting transfers between devices, z_shift(): lax.ppermute(value, 'band', [(2 * z + c, 2 * ((z + k) % nz) + c) for z in...  56.2 us
    ppermute x15, waiting for transfers between devices, over_x(): return lax.ppermute(value, 'img', [(i, i ^ 1) for i in range(4)])  44.3 us
    ppermute x15, waiting for transfers between devices, over_y(): return lax.ppermute(value, 'img', [(i, i ^ 2) for i in range(4)])  17.6 us
    ppermute x15, starting transfers between devices, over_y(): return lax.ppermute(value, 'img', [(i, i ^ 2) for i in range(4)])  16.3 us
    ppermute x15, starting transfers between devices, over_x(): return lax.ppermute(value, 'img', [(i, i ^ 1) for i in range(4)])  15.2 us
    ppermute x48, waiting for transfers between devices, core_swap(): return lax.ppermute(value, 'band', [(b, b ^ 1) for b in range(n_band)])  10.7 us
  transfers between devices with their start and end apart: 115, of which 56 were waited for; matrix products, arithmetic and copies ran while one was open for 9% of the time, Pallas kernels for 28%

profile of v6, /device:TPU:0, one launch (start us, length us, event | category | flops | bytes accessed | tf_op | source)
XLA Modules:
  0.0 440.2 jit_solution(6366261676961992205)
XLA Ops:
  2.0 4.8 %collective-permute-start = (bf16[32,512]{1,0:T(8,128)(2,1)S(1)}, bf16[32,512]{1,0:T(8,128)(2,1)S(1)}, u32[]{:S(2)}, u32[]{:S(2)}) collective-permute-start(bf16[32,512]{1,0:T(8,128)(2,1)S(1)} %slice.511), channel_id=1, source_target_pairs={{0,1},{1,2},{2,3},{3,4},{4,5},{5,6},{6,7},{7,8},{8,9},{9,10},{10,1... | collective-permute-start | bytes 98312 | tf_op jit(solution)/shard_map/ppermute | solution.py:1233
  8.4 3.6 collective-permute-start.1
  12.0 2.6 collective-permute-start.4
  16.0 6.1 %collective-permute-done.1.refs_4_ = bf16[288,512]{1,0:T(8,128)(2,1)S(1)} collective-permute-done((bf16[288,512]{1,0:T(8,128)(2,1)S(1)}, bf16[288,512]{1,0:T(8,128)(2,1)S(1)}, u32[]{:S(2)}, u32[]{:S(2)}) %collective-permute-start.1) | collective-permute-done | bytes 294944 | tf_op jit(solution)/shard_map/ppermute | solution.py:981
  35.0 14.5 %collective-permute-start.7 = (bf16[368,512]{1,0:T(8,128)(2,1)}, bf16[368,512]{1,0:T(8,128)(2,1)}, u32[]{:S(2)}, u32[]{:S(2)}) collective-permute-start(bf16[368,512]{1,0:T(8,128)(2,1)} %pad_maximum_fusion.11.refs_11_), channel_id=1, source_target_pairs={{0,8},{4,12},{8,16},{12,20},{16,24},{20,28},{24,0},{28,4},{1,9},{5... | collective-permute-start | bytes 1130504 | tf_op jit(solution)/shard_map/ppermute | solution.py:981
  54.9 4.1 collective-permute-done.8.refs_23_
  59.8 2.0 collective-permute-start.15
  64.5 4.4 collective-permute-start.17
  70.9 2.7 collective-permute-done.15.refs_24_
  76.2 7.4 %collective-permute-done.17.refs_19_ = bf16[368,512]{1,0:T(8,128)(2,1)} collective-permute-done((bf16[368,512]{1,0:T(8,128)(2,1)}, bf16[368,512]{1,0:T(8,128)(2,1)}, u32[]{:S(2)}, u32[]{:S(2)}) %collective-permute-start.17) | collective-permute-done | bytes 376864 | tf_op jit(solution)/shard_map/ppermute | solution.py:981
  88.7 7.0 %collective-permute-done.22.refs_20_ = bf16[368,512]{1,0:T(8,128)(2,1)S(1)} collective-permute-done((bf16[368,512]{1,0:T(8,128)(2,1)}, bf16[368,512]{1,0:T(8,128)(2,1)S(1)}, u32[]{:S(2)}, u32[]{:S(2)}) %collective-permute-start.22) | collective-permute-done | bytes 376864 | tf_op jit(solution)/shard_map/ppermute | solution.py:1070
  97.4 6.2 %collective-permute-done.24.refs_22_ = bf16[368,512]{1,0:T(8,128)(2,1)S(1)} collective-permute-done((bf16[368,512]{1,0:T(8,128)(2,1)}, bf16[368,512]{1,0:T(8,128)(2,1)S(1)}, u32[]{:S(2)}, u32[]{:S(2)}) %collective-permute-start.24) | collective-permute-done | bytes 376864 | tf_op jit(solution)/shard_map/ppermute | solution.py:981
  111.1 3.1 collective-permute-start.41
  115.0 25.6 %features_first.1 = (bf16[1024,512]{1,0:T(8,128)(2,1)}, bf16[1024,512]{1,0:T(8,128)(2,1)}, f32[1024,512]{1,0:T(8,128)}, bf16[1024,512]{1,0:T(8,128)(2,1)}, f32[1...) custom-call(s32[128]{0:T(128)} %broadcast_select_fusion.6.refs_0_.ga, ...), custom_call_target="tpu_custom_call" | custom-call | flops 28600000512 | bytes 37552792 | tf_op jit(solution)/shard_map/features_first/pallas_call | solution.py:801
  143.8 2.0 collective-permute-start.46
  145.8 25.3 %attend_both.1 = (bf16[768,512]{1,0:T(8,128)(2,1)}, bf16[768,512]{1,0:T(8,128)(2,1)}, f32[1024,512]{1,0:T(8,128)}, bf16[1024,512]{1,0:T(8,128)(2,1)}, bf16[2048,512]{1,0:T(8,128)(2,1)}, /*index=5*/f32[16,512]{1,0:T(8,128)}) custom-call(s32[128]{0:T(128)} %broadcast_select_fusion.6.refs_0_.gather, s32[192]{0:T(256)} %fusion.72.scatter.refs_0_, ...), custom_call_target="tpu_custom_call" | custom-call | flops 26400000000 | bytes 27100436 | tf_op jit(solution)/shard_map/attend_both/pallas_call | solution.py:801
  171.3 9.0 %weight_grad_two.1 = (bf16[1408,512]{1,0:T(8,128)(2,1)}, bf16[1408,512]{1,0:T(8,128)(2,1)}, bf16[1408,512]{1,0:T(8,128)(2,1)}, bf16[1408,512]{1,0:T(8,128)(2,1)}...) custom-call(s32[5]{0:T(128)} %fusion.80.refs_1_.flags.refs_0_, bf16[1024,512]{1,0:T(8,128)(2,1)} %get-tuple-element.585.refs_1_, ...), custom_call_target="tpu_custom_call" | custom-call | flops 9900000256 | bytes 11042836 | tf_op jit(solution)/shard_map/weight_grad_two/pallas_call | solution.py:801
  190.0 12.0 %data_grad_two.1 = (bf16[1024,512]{1,0:T(8,128)(2,1)}, f32[16,512]{1,0:T(8,128)}) custom-call(s32[5]{0:T(128)} %fusion.80.refs_1_.flags.refs_0_, bf16[1024,512]{1,0:T(8,128)(2,1)} %get-tuple-element.597.refs_2_.refs_1_, f32[1024,512]{1,0:T(8,128)} %get-tuple-element.598.refs_2_, f32[16,512]{1,0:T(8,128)} %get-tuple-element.565.stats.refs_3_.refs_5_.refs_4_, ...), custom_call_target="tpu_custom_call" | custom-call | flops 13200000000 | bytes 15826964 | tf_op jit(solution)/shard_map/data_grad_two/pallas_call | solution.py:801
  202.0 3.8 collective-permute-done.50
  207.3 9.7 %weight_grad_one.1 = (bf16[1408,512]{1,0:T(8,128)(2,1)}, bf16[1408,512]{1,0:T(8,128)(2,1)}, bf16[1408,512]{1,0:T(8,128)(2,1)}, bf16[1408,512]{1,0:T(8,128)(2,1)}, f32[16,512]{1,0:T(8,128)}) custom-call(s32[5]{0:T(128)} %fusion.80.refs_1_.flags.refs_0_, bf16[1024,512]{1,0:T(8,128)(2,1)} %get-tuple-element.553.refs_1_, ...), custom_call_target="tpu_custom_call" | custom-call | flops 9900000256 | bytes 8945684 | tf_op jit(solution)/shard_map/weight_grad_one/pallas_call | solution.py:801
  225.9 2.2 add_bitcast_fusion
  228.0 2.0 fusion.7
  236.2 2.7 collective-permute-start.62
  241.2 13.2 %data_grad_one.1 = (bf16[768,512]{1,0:T(8,128)(2,1)}, bf16[768,512]{1,0:T(8,128)(2,1)}, f32[16,512]{1,0:T(8,128)}) custom-call(s32[192]{0:T(256)} %fusion.72.scatter.refs_0_, s32[5]{0:T(128)} %fusion.80.refs_1_.flags.refs_0_, bf16[1024,512]{1,0:T(8,128)(2,1)} %get-tuple-element.642.refs_2_, bf16[1024,512]{1,0:T(8,128)(2,1)} %get-tuple-element.643.refs_3_, ...), custom_call_target="tpu_custom_call" | custom-call | flops 13200000000 | bytes 17400596 | tf_op jit(solution)/shard_map/data_grad_one/pallas_call | solution.py:801
  266.2 7.3 %collective-permute-done.67 = f32[16,512]{1,0:T(8,128)S(1)} collective-permute-done((f32[16,512]{1,0:T(8,128)S(1)}, f32[16,512]{1,0:T(8,128)S(1)}, u32[]{:S(2)}, u32[]{:S(2)}) %collective-permute-start.67) | collective-permute-done | bytes 32800 | tf_op jit(solution)/shard_map/ppermute | solution.py:1070
  275.8 3.2 collective-permute-start.71
  279.9 2.6 collective-permute-start.73
  282.7 2.2 collective-permute-done.70
  286.5 9.0 %collective-permute-done.72 = bf16[192,512]{1,0:T(8,128)(2,1)S(1)} collective-permute-done((bf16[192,512]{1,0:T(8,128)(2,1)S(1)}, bf16[192,512]{1,0:T(8,128)(2,1)S(1)}, u32[]{:S(2)}, u32[]{:S(2)}) %collective-permute-start.72) | collective-permute-done | bytes 196640 | tf_op jit(solution)/shard_map/ppermute | solution.py:981
  299.6 2.0 collective-permute-start.76
  301.6 3.8 collective-permute-start.78
  305.5 4.2 collective-permute-done.74.refs_6_
  309.7 7.4 %collective-permute-done.75.refs_7_ = bf16[368,512]{1,0:T(8,128)(2,1)S(1)} collective-permute-done((bf16[368,512]{1,0:T(8,128)(2,1)S(1)}, bf16[368,512]{1,0:T(8,128)(2,1)S(1)}, u32[]{:S(2)}, u32[]{:S(2)}) %collective-permute-start.75) | collective-permute-done | bytes 376864 | tf_op jit(solution)/shard_map/ppermute | solution.py:1074
  317.1 2.2 collective-permute-done.78.refs_17_
  320.1 1.7 collective-permute-start.81
  325.0 2.4 collective-permute-start.84
  327.4 3.7 collective-permute-done.80.refs_10_
  331.8 4.4 collective-permute-done.82.refs_18_
  338.0 3.5 collective-permute-done.84.refs_13_
  343.1 1.7 collective-permute-start.90
  345.7 7.8 %collective-permute-done.89.refs_14_ = bf16[368,512]{1,0:T(8,128)(2,1)S(1)} collective-permute-done((bf16[368,512]{1,0:T(8,128)(2,1)}, bf16[368,512]{1,0:T(8,128)(2,1)S(1)}, u32[]{:S(2)}, u32[]{:S(2)}) %collective-permute-start.89) | collective-permute-done | bytes 376864 | tf_op jit(solution)/shard_map/ppermute | solution.py:1070
  355.0 8.3 %collective-permute-done.91.refs_16_ = bf16[368,512]{1,0:T(8,128)(2,1)} collective-permute-done((bf16[368,512]{1,0:T(8,128)(2,1)S(1)}, bf16[368,512]{1,0:T(8,128)(2,1)}, u32[]{:S(2)}, u32[]{:S(2)}) %collective-permute-start.91) | collective-permute-done | bytes 376864 | tf_op jit(solution)/shard_map/ppermute | solution.py:981
  371.5 3.8 collective-permute-start.106
  377.0 27.5 %forward_again.1 = (bf16[768,512]{1,0:T(8,128)(2,1)}, bf16[768,512]{1,0:T(8,128)(2,1)}) custom-call(s32[192]{0:T(256)} %fusion.72.scatter.refs_0_, s32[5]{0:T(128)} %fusion.80.refs_1_.flags.refs_0_, s32[65]{0:T(128)} %pad_add_fusion.5.refs_2_, bf16[1024,512]{1,0:T(8,128)(2,1)} %get-tuple-element.643.refs_3_, ...), custom_call_target="tpu_custom_call" | custom-call | flops 30799998976 | bytes 14713880 | tf_op jit(solution)/shard_map/forward_again/pallas_call | solution.py:801
  404.5 1.9 collective-permute-done.107
  412.7 1.9 add_divide_fusion
  414.6 5.4 %collective-permute-done.111 = bf16[288,512]{1,0:T(8,128)(2,1)S(1)} collective-permute-done((bf16[288,512]{1,0:T(8,128)(2,1)S(1)}, bf16[288,512]{1,0:T(8,128)(2,1)S(1)}, u32[]{:S(2)}, u32[]{:S(2)}) %collective-permute-start.111) | collective-permute-done | bytes 294944 | tf_op jit(solution)/shard_map/ppermute | solution.py:981
  420.1 17.7 %collective-permute-done.112 = bf16[288,512]{1,0:T(8,128)(2,1)S(1)} collective-permute-done((bf16[288,512]{1,0:T(8,128)(2,1)S(1)}, bf16[288,512]{1,0:T(8,128)(2,1)S(1)}, u32[]{:S(2)}, u32[]{:S(2)}) %collective-permute-start.112) | collective-permute-done | bytes 294944 | tf_op jit(solution)/shard_map/ppermute | solution.py:981
  (552 shorter events, 121.1 us)
Async XLA Ops:
  8.4 13.7 %collective-permute-start.1 = (bf16[288,512]{1,0:T(8,128)(2,1)S(1)}, bf16[288,512]{1,0:T(8,128)(2,1)S(1)}, u32[]{:S(2)}, u32[]{:S(2)}) collective-permute-start(bf16[288,512]{1,0:T(8,128)(2,1)S(1)} %get-tuple-element.402), channel_id=1, source_target_pairs={{0,8},{4,12},{8,16},{12,20},{16,24},{20,28},{24,0},{28,4},{1,9},{5... | collective-permute-start | bytes 884744 | tf_op jit(solution)/shard_map/ppermute | solution.py:981
  12.0 21.4 %collective-permute-start.4 = (bf16[288,512]{1,0:T(8,128)(2,1)S(1)}, bf16[288,512]{1,0:T(8,128)(2,1)}, u32[]{:S(2)}, u32[]{:S(2)}) collective-permute-start(bf16[288,512]{1,0:T(8,128)(2,1)S(1)} %get-tuple-element.407), channel_id=1, source_target_pairs={{0,16},{4,20},{8,24},{12,28},{16,0},{20,4},{24,8},{28,12},{1,17},{... | collective-permute-start | bytes 884744 | tf_op jit(solution)/shard_map/ppermute | solution.py:981
  14.7 18.7 %collective-permute-start.5 = (bf16[288,512]{1,0:T(8,128)(2,1)S(1)}, bf16[288,512]{1,0:T(8,128)(2,1)}, u32[]{:S(2)}, u32[]{:S(2)}) collective-permute-start(bf16[288,512]{1,0:T(8,128)(2,1)S(1)} %get-tuple-element.408), channel_id=1, source_target_pairs={{0,24},{4,28},{8,0},{12,4},{16,8},{20,12},{24,16},{28,20},{1,25},{... | collective-permute-start | bytes 884744 | tf_op jit(solution)/shard_map/ppermute | solution.py:981
  33.4 16.6 %collective-permute-start.6 = (bf16[368,512]{1,0:T(8,128)(2,1)}, bf16[368,512]{1,0:T(8,128)(2,1)}, u32[]{:S(2)}, u32[]{:S(2)}) collective-permute-start(bf16[368,512]{1,0:T(8,128)(2,1)} %pad_maximum_fusion.11.refs_11_), channel_id=1, source_target_pairs={{0,3},{1,2},{2,1},{3,0},{4,7},{5,6},{6,5},{7,4},{8,11},{9,10},{10,... | collective-permute-start | bytes 1130504 | tf_op jit(solution)/shard_map/ppermute | solution.py:1082
  35.0 19.9 %collective-permute-start.7 = (bf16[368,512]{1,0:T(8,128)(2,1)}, bf16[368,512]{1,0:T(8,128)(2,1)}, u32[]{:S(2)}, u32[]{:S(2)}) collective-permute-start(bf16[368,512]{1,0:T(8,128)(2,1)} %pad_maximum_fusion.11.refs_11_), channel_id=1, source_target_pairs={{0,8},{4,12},{8,16},{12,20},{16,24},{20,28},{24,0},{28,4},{1,9},{5... | collective-permute-start | bytes 1130504 | tf_op jit(solution)/shard_map/ppermute | solution.py:981
  59.8 13.8 %collective-permute-start.15 = (bf16[368,512]{1,0:T(8,128)(2,1)}, bf16[368,512]{1,0:T(8,128)(2,1)}, u32[]{:S(2)}, u32[]{:S(2)}) collective-permute-start(bf16[368,512]{1,0:T(8,128)(2,1)} %collective-permute-done.8.refs_23_), channel_id=1, source_target_pairs={{0,1},{1,0},{2,3},{3,2},{4,5},{5,4},{6,7},{7,6},{8,9},{9,8},{10,11... | collective-permute-start | bytes 1130504 | tf_op jit(solution)/shard_map/ppermute | solution.py:1070
  64.5 19.1 %collective-permute-start.17 = (bf16[368,512]{1,0:T(8,128)(2,1)}, bf16[368,512]{1,0:T(8,128)(2,1)}, u32[]{:S(2)}, u32[]{:S(2)}) collective-permute-start(bf16[368,512]{1,0:T(8,128)(2,1)} %pad_maximum_fusion.11.refs_11_), channel_id=1, source_target_pairs={{0,16},{4,20},{8,24},{12,28},{16,0},{20,4},{24,8},{28,12},{1,17},{... | collective-permute-start | bytes 1130504 | tf_op jit(solution)/shard_map/ppermute | solution.py:981
  70.2 13.5 %collective-permute-start.18 = (bf16[368,512]{1,0:T(8,128)(2,1)}, bf16[368,512]{1,0:T(8,128)(2,1)}, u32[]{:S(2)}, u32[]{:S(2)}) collective-permute-start(bf16[368,512]{1,0:T(8,128)(2,1)} %pad_maximum_fusion.11.refs_11_), channel_id=1, source_target_pairs={{0,4},{4,0},{8,12},{12,8},{16,20},{20,16},{24,28},{28,24},{1,5},{5... | collective-permute-start | bytes 1130504 | tf_op jit(solution)/shard_map/ppermute | solution.py:985
  70.4 13.3 %collective-permute-start.19 = (bf16[368,512]{1,0:T(8,128)(2,1)}, bf16[368,512]{1,0:T(8,128)(2,1)S(1)}, u32[]{:S(2)}, u32[]{:S(2)}) collective-permute-start(bf16[368,512]{1,0:T(8,128)(2,1)} %collective-permute-done.2.refs_12_), channel_id=1, source_target_pairs={{0,4},{4,0},{8,12},{12,8},{16,20},{20,16},{24,28},{28,24},{1,5},{5... | collective-permute-start | bytes 1130504 | tf_op jit(solution)/shard_map/ppermute | solution.py:985
  86.8 16.9 %collective-permute-start.24 = (bf16[368,512]{1,0:T(8,128)(2,1)}, bf16[368,512]{1,0:T(8,128)(2,1)S(1)}, u32[]{:S(2)}, u32[]{:S(2)}) collective-permute-start(bf16[368,512]{1,0:T(8,128)(2,1)} %collective-permute-done.6.refs_14_), channel_id=1, source_target_pairs={{0,16},{4,20},{8,24},{12,28},{16,0},{20,4},{24,8},{28,12},{1,17},{... | collective-permute-start | bytes 1130504 | tf_op jit(solution)/shard_map/ppermute | solution.py:981
  86.8 17.1 %collective-permute-start.25 = (bf16[368,512]{1,0:T(8,128)(2,1)S(1)}, bf16[368,512]{1,0:T(8,128)(2,1)S(1)}, u32[]{:S(2)}, u32[]{:S(2)}) collective-permute-start(bf16[368,512]{1,0:T(8,128)(2,1)S(1)} %copy-done.61), channel_id=1, source_target_pairs={{0,2},{1,3},{2,0},{3,1},{4,6},{5,7},{6,4},{7,5},{8,10},{9,11},{10,... | collective-permute-start | bytes 1130504 | tf_op jit(solution)/shard_map/ppermute | solution.py:1074
  87.5 16.7 %collective-permute-start.26 = (bf16[368,512]{1,0:T(8,128)(2,1)}, bf16[368,512]{1,0:T(8,128)(2,1)S(1)}, u32[]{:S(2)}, u32[]{:S(2)}) collective-permute-start(bf16[368,512]{1,0:T(8,128)(2,1)} %collective-permute-done.16.refs_25_), channel_id=1, source_target_pairs={{0,1},{1,0},{2,3},{3,2},{4,5},{5,4},{6,7},{7,6},{8,9},{9,8},{10,11... | collective-permute-start | bytes 1130504 | tf_op jit(solution)/shard_map/ppermute | solution.py:1070
  110.1 30.5 %collective-permute-start.39 = (bf16[288,512]{1,0:T(8,128)(2,1)S(1)}, bf16[288,512]{1,0:T(8,128)(2,1)}, u32[]{:S(2)}, u32[]{:S(2)}) collective-permute-start(bf16[288,512]{1,0:T(8,128)(2,1)S(1)} %copy-done.26), channel_id=1, source_target_pairs={{0,8},{4,12},{8,16},{12,20},{16,24},{20,28},{24,0},{28,4},{1,9},{5... | collective-permute-start | bytes 884744 | tf_op jit(solution)/shard_map/ppermute | solution.py:981
  110.2 30.5 %collective-permute-start.40 = (bf16[288,512]{1,0:T(8,128)(2,1)S(1)}, bf16[288,512]{1,0:T(8,128)(2,1)}, u32[]{:S(2)}, u32[]{:S(2)}) collective-permute-start(bf16[288,512]{1,0:T(8,128)(2,1)S(1)} %copy-done.25), channel_id=1, source_target_pairs={{0,16},{4,20},{8,24},{12,28},{16,0},{20,4},{24,8},{28,12},{1,17},{... | collective-permute-start | bytes 884744 | tf_op jit(solution)/shard_map/ppermute | solution.py:981
  111.1 29.6 %collective-permute-start.41 = (bf16[288,512]{1,0:T(8,128)(2,1)S(1)}, bf16[288,512]{1,0:T(8,128)(2,1)}, u32[]{:S(2)}, u32[]{:S(2)}) collective-permute-start(bf16[288,512]{1,0:T(8,128)(2,1)S(1)} %copy-done.24), channel_id=1, source_target_pairs={{0,24},{4,28},{8,0},{12,4},{16,8},{20,12},{24,16},{28,20},{1,25},{... | collective-permute-start | bytes 884744 | tf_op jit(solution)/shard_map/ppermute | solution.py:981
  143.8 27.4 %collective-permute-start.46 = (bf16[176,1536]{1,0:T(8,128)(2,1)S(1)}, bf16[176,1536]{1,0:T(8,128)(2,1)S(1)}, u32[]{:S(2)}, u32[]{:S(2)}) collective-permute-start(bf16[176,1536]{1,0:T(8,128)(2,1)S(1)} %pad_maximum_fusion.7), channel_id=1, source_target_pairs={{0,16},{4,20},{16,0},{20,4},{8,24},{12,28},{24,8},{28,12},{1,17},{... | collective-permute-start | bytes 1622024 | tf_op jit(solution)/shard_map/ppermute | solution.py:1078
  182.0 35.0 %collective-permute-start.52 = (bf16[288,512]{1,0:T(8,128)(2,1)}, bf16[288,512]{1,0:T(8,128)(2,1)S(1)}, u32[]{:S(2)}, u32[]{:S(2)}) collective-permute-start(bf16[288,512]{1,0:T(8,128)(2,1)} %get-tuple-element.816), channel_id=1, source_target_pairs={{0,24},{4,28},{8,0},{12,4},{16,8},{20,12},{24,16},{28,20},{1,25},{... | collective-permute-start | bytes 884744 | tf_op jit(solution)/shard_map/ppermute | solution.py:981
  183.5 34.2 %collective-permute-start.53 = (bf16[288,512]{1,0:T(8,128)(2,1)}, bf16[288,512]{1,0:T(8,128)(2,1)}, u32[]{:S(2)}, u32[]{:S(2)}) collective-permute-start(bf16[288,512]{1,0:T(8,128)(2,1)} %get-tuple-element.817), channel_id=1, source_target_pairs={{0,16},{4,20},{8,24},{12,28},{16,0},{20,4},{24,8},{28,12},{1,17},{... | collective-permute-start | bytes 884744 | tf_op jit(solution)/shard_map/ppermute | solution.py:981
  183.5 34.2 %collective-permute-start.54 = (bf16[288,512]{1,0:T(8,128)(2,1)}, bf16[288,512]{1,0:T(8,128)(2,1)}, u32[]{:S(2)}, u32[]{:S(2)}) collective-permute-start(bf16[288,512]{1,0:T(8,128)(2,1)} %get-tuple-element.814), channel_id=1, source_target_pairs={{0,8},{4,12},{8,16},{12,20},{16,24},{20,28},{24,0},{28,4},{1,9},{5... | collective-permute-start | bytes 884744 | tf_op jit(solution)/shard_map/ppermute | solution.py:981
  187.4 18.4 %collective-permute-start.50 = (bf16[2,352,512]{2,1,0:T(8,128)(2,1)S(1)}, bf16[2,352,512]{2,1,0:T(8,128)(2,1)S(1)}, u32[]{:S(2)}, u32[]{:S(2)}) collective-permute-start(bf16[2,352,512]{2,1,0:T(8,128)(2,1)S(1)} %fusion.8), channel_id=1, source_target_pairs={{0,1},{1,0},{2,3},{3,2},{4,5},{5,4},{6,7},{7,6},{8,9},{9,8},{10,11... | collective-permute-start | bytes 2162696 | tf_op jit(solution)/shard_map/ppermute | solution.py:1070
  189.1 18.1 %collective-permute-start.51 = (bf16[2,352,512]{2,1,0:T(8,128)(2,1)S(1)}, bf16[2,352,512]{2,1,0:T(8,128)(2,1)}, u32[]{:S(2)}, u32[]{:S(2)}) collective-permute-start(bf16[2,352,512]{2,1,0:T(8,128)(2,1)S(1)} %add_bitcast_fusion.1), channel_id=1, source_target_pairs={{0,2},{1,3},{2,0},{3,1},{4,6},{5,7},{6,4},{7,5},{8,10},{9,11},{10,... | collective-permute-start | bytes 2162696 | tf_op jit(solution)/shard_map/ppermute | solution.py:1074
  234.8 19.6 %collective-permute-start.61 = (bf16[176,512]{1,0:T(8,128)(2,1)}, bf16[176,512]{1,0:T(8,128)(2,1)}, u32[]{:S(2)}, u32[]{:S(2)}) collective-permute-start(bf16[176,512]{1,0:T(8,128)(2,1)} %get-tuple-element.877), channel_id=1, source_target_pairs={{0,8},{4,12},{8,16},{12,20},{16,24},{20,28},{24,0},{28,4},{1,9},{5... | collective-permute-start | bytes 540680 | tf_op jit(solution)/shard_map/ppermute | solution.py:981
  236.2 18.2 %collective-permute-start.62 = (bf16[176,512]{1,0:T(8,128)(2,1)}, bf16[176,512]{1,0:T(8,128)(2,1)}, u32[]{:S(2)}, u32[]{:S(2)}) collective-permute-start(bf16[176,512]{1,0:T(8,128)(2,1)} %get-tuple-element.876), channel_id=1, source_target_pairs={{0,24},{4,28},{8,0},{12,4},{16,8},{20,12},{24,16},{28,20},{1,25},{... | collective-permute-start | bytes 540680 | tf_op jit(solution)/shard_map/ppermute | solution.py:981
  238.8 15.6 %collective-permute-start.63 = (bf16[176,512]{1,0:T(8,128)(2,1)S(1)}, bf16[176,512]{1,0:T(8,128)(2,1)}, u32[]{:S(2)}, u32[]{:S(2)}) collective-permute-start(bf16[176,512]{1,0:T(8,128)(2,1)S(1)} %get-tuple-element.875), channel_id=1, source_target_pairs={{0,16},{4,20},{8,24},{12,28},{16,0},{20,4},{24,8},{28,12},{1,17},{... | collective-permute-start | bytes 540680 | tf_op jit(solution)/shard_map/ppermute | solution.py:981
  238.8 16.8 %collective-permute-start.59 = (bf16[2,352,512]{2,1,0:T(8,128)(2,1)}, bf16[2,352,512]{2,1,0:T(8,128)(2,1)}, u32[]{:S(2)}, u32[]{:S(2)}) collective-permute-start(bf16[2,352,512]{2,1,0:T(8,128)(2,1)} %fusion.7), channel_id=1, source_target_pairs={{0,1},{1,0},{2,3},{3,2},{4,5},{5,4},{6,7},{7,6},{8,9},{9,8},{10,11... | collective-permute-start | bytes 2162696 | tf_op jit(solution)/shard_map/ppermute | solution.py:1070
  240.3 16.4 %collective-permute-start.60 = (bf16[2,352,512]{2,1,0:T(8,128)(2,1)}, bf16[2,352,512]{2,1,0:T(8,128)(2,1)}, u32[]{:S(2)}, u32[]{:S(2)}) collective-permute-start(bf16[2,352,512]{2,1,0:T(8,128)(2,1)} %add_bitcast_fusion), channel_id=1, source_target_pairs={{0,2},{1,3},{2,0},{3,1},{4,6},{5,7},{6,4},{7,5},{8,10},{9,11},{10,... | collective-permute-start | bytes 2162696 | tf_op jit(solution)/shard_map/ppermute | solution.py:1074
  261.0 13.5 %collective-permute-start.65 = (bf16[352,512]{1,0:T(8,128)(2,1)S(1)}, bf16[352,512]{1,0:T(8,128)(2,1)S(1)}, u32[]{:S(2)}, u32[]{:S(2)}) collective-permute-start(bf16[352,512]{1,0:T(8,128)(2,1)S(1)} %dynamic-slice_bitcast_fusion.2), channel_id=1, source_target_pairs={{0,2},{1,3},{2,0},{3,1},{4,6},{5,7},{6,4},{7,5},{8,10},{9,11},{10,... | collective-permute-start | bytes 1081352 | tf_op jit(solution)/shard_map/ppermute | solution.py:1074
  261.9 12.6 %collective-permute-start.66 = (bf16[352,512]{1,0:T(8,128)(2,1)S(1)}, bf16[352,512]{1,0:T(8,128)(2,1)S(1)}, u32[]{:S(2)}, u32[]{:S(2)}) collective-permute-start(bf16[352,512]{1,0:T(8,128)(2,1)S(1)} %dynamic-slice_bitcast_fusion.1), channel_id=1, source_target_pairs={{0,1},{1,0},{2,3},{3,2},{4,5},{5,4},{6,7},{7,6},{8,9},{9,8},{10,11... | collective-permute-start | bytes 1081352 | tf_op jit(solution)/shard_map/ppermute | solution.py:1070
  279.0 16.5 %collective-permute-start.72 = (bf16[192,512]{1,0:T(8,128)(2,1)S(1)}, bf16[192,512]{1,0:T(8,128)(2,1)S(1)}, u32[]{:S(2)}, u32[]{:S(2)}) collective-permute-start(bf16[192,512]{1,0:T(8,128)(2,1)S(1)} %get-tuple-element.911), channel_id=1, source_target_pairs={{0,16},{4,20},{8,24},{12,28},{16,0},{20,4},{24,8},{28,12},{1,17},{... | collective-permute-start | bytes 589832 | tf_op jit(solution)/shard_map/ppermute | solution.py:981
  279.9 15.7 %collective-permute-start.73 = (f32[32,1536]{1,0:T(8,128)S(1)}, f32[32,1536]{1,0:T(8,128)S(1)}, u32[]{:S(2)}, u32[]{:S(2)}) collective-permute-start(f32[32,1536]{1,0:T(8,128)S(1)} %pad_maximum_fusion.16), channel_id=1, source_target_pairs={{0,1},{1,2},{2,3},{3,4},{4,5},{5,6},{6,7},{7,8},{8,9},{9,10},{10,1... | collective-permute-start | bytes 589832 | tf_op jit(solution)/shard_map/ppermute | solution.py:1344
  282.5 19.1 %collective-permute-start.79 = (bf16[768,512]{1,0:T(8,128)(2,1)S(1)}, bf16[768,512]{1,0:T(8,128)(2,1)S(1)}, u32[]{:S(2)}, u32[]{:S(2)}) collective-permute-start(bf16[768,512]{1,0:T(8,128)(2,1)S(1)} %copy-done.52), channel_id=1, source_target_pairs={{0,4},{4,0},{8,12},{12,8},{16,20},{20,16},{24,28},{28,24},{1,5},{5... | collective-permute-start | bytes 2359304 | tf_op jit(solution)/shard_map/ppermute | solution.py:985
  298.7 18.3 %collective-permute-start.75 = (bf16[368,512]{1,0:T(8,128)(2,1)S(1)}, bf16[368,512]{1,0:T(8,128)(2,1)S(1)}, u32[]{:S(2)}, u32[]{:S(2)}) collective-permute-start(bf16[368,512]{1,0:T(8,128)(2,1)S(1)} %pad_maximum_fusion.12.refs_5_), channel_id=1, source_target_pairs={{0,2},{1,3},{2,0},{3,1},{4,6},{5,7},{6,4},{7,5},{8,10},{9,11},{10,... | collective-permute-start | bytes 1130504 | tf_op jit(solution)/shard_map/ppermute | solution.py:1074
  299.6 17.5 %collective-permute-start.76 = (bf16[368,512]{1,0:T(8,128)(2,1)S(1)}, bf16[368,512]{1,0:T(8,128)(2,1)S(1)}, u32[]{:S(2)}, u32[]{:S(2)}) collective-permute-start(bf16[368,512]{1,0:T(8,128)(2,1)S(1)} %pad_maximum_fusion.12.refs_5_), channel_id=1, source_target_pairs={{0,3},{1,2},{2,1},{3,0},{4,7},{5,6},{6,5},{7,4},{8,11},{9,10},{10,... | collective-permute-start | bytes 1130504 | tf_op jit(solution)/shard_map/ppermute | solution.py:1082
  301.6 15.5 %collective-permute-start.77 = (bf16[368,512]{1,0:T(8,128)(2,1)S(1)}, bf16[368,512]{1,0:T(8,128)(2,1)S(1)}, u32[]{:S(2)}, u32[]{:S(2)}) collective-permute-start(bf16[368,512]{1,0:T(8,128)(2,1)S(1)} %pad_maximum_fusion.12.refs_5_), channel_id=1, source_target_pairs={{0,8},{4,12},{8,16},{12,20},{16,24},{20,28},{24,0},{28,4},{1,9},{5... | collective-permute-start | bytes 1130504 | tf_op jit(solution)/shard_map/ppermute | solution.py:981
  301.6 17.8 %collective-permute-start.78 = (bf16[368,512]{1,0:T(8,128)(2,1)S(1)}, bf16[368,512]{1,0:T(8,128)(2,1)S(1)}, u32[]{:S(2)}, u32[]{:S(2)}) collective-permute-start(bf16[368,512]{1,0:T(8,128)(2,1)S(1)} %pad_maximum_fusion.12.refs_5_), channel_id=1, source_target_pairs={{0,24},{4,28},{8,0},{12,4},{16,8},{20,12},{24,16},{28,20},{1,25},{... | collective-permute-start | bytes 1130504 | tf_op jit(solution)/shard_map/ppermute | solution.py:981
  321.9 14.4 %collective-permute-start.82 = (bf16[368,512]{1,0:T(8,128)(2,1)S(1)}, bf16[368,512]{1,0:T(8,128)(2,1)S(1)}, u32[]{:S(2)}, u32[]{:S(2)}) collective-permute-start(bf16[368,512]{1,0:T(8,128)(2,1)S(1)} %collective-permute-done.78.refs_17_), channel_id=1, source_target_pairs={{0,1},{1,0},{2,3},{3,2},{4,5},{5,4},{6,7},{7,6},{8,9},{9,8},{10,11... | collective-permute-start | bytes 1130504 | tf_op jit(solution)/shard_map/ppermute | solution.py:1070
  322.2 15.4 %collective-permute-start.83 = (bf16[368,512]{1,0:T(8,128)(2,1)S(1)}, bf16[368,512]{1,0:T(8,128)(2,1)S(1)}, u32[]{:S(2)}, u32[]{:S(2)}) collective-permute-start(bf16[368,512]{1,0:T(8,128)(2,1)S(1)} %collective-permute-done.78.refs_17_), channel_id=1, source_target_pairs={{0,2},{1,3},{2,0},{3,1},{4,6},{5,7},{6,4},{7,5},{8,10},{9,11},{10,... | collective-permute-start | bytes 1130504 | tf_op jit(solution)/shard_map/ppermute | solution.py:1074
  325.0 16.5 %collective-permute-start.84 = (bf16[368,512]{1,0:T(8,128)(2,1)S(1)}, bf16[368,512]{1,0:T(8,128)(2,1)}, u32[]{:S(2)}, u32[]{:S(2)}) collective-permute-start(bf16[368,512]{1,0:T(8,128)(2,1)S(1)} %pad_maximum_fusion.12.refs_5_), channel_id=1, source_target_pairs={{0,16},{4,20},{8,24},{12,28},{16,0},{20,4},{24,8},{28,12},{1,17},{... | collective-permute-start | bytes 1130504 | tf_op jit(solution)/shard_map/ppermute | solution.py:981
  344.8 18.5 %collective-permute-start.91 = (bf16[368,512]{1,0:T(8,128)(2,1)S(1)}, bf16[368,512]{1,0:T(8,128)(2,1)}, u32[]{:S(2)}, u32[]{:S(2)}) collective-permute-start(bf16[368,512]{1,0:T(8,128)(2,1)S(1)} %collective-permute-done.76.refs_8_), channel_id=1, source_target_pairs={{0,16},{4,20},{8,24},{12,28},{16,0},{20,4},{24,8},{28,12},{1,17},{... | collective-permute-start | bytes 1130504 | tf_op jit(solution)/shard_map/ppermute | solution.py:981
  344.8 18.5 %collective-permute-start.92 = (bf16[368,512]{1,0:T(8,128)(2,1)S(1)}, bf16[368,512]{1,0:T(8,128)(2,1)S(1)}, u32[]{:S(2)}, u32[]{:S(2)}) collective-permute-start(bf16[368,512]{1,0:T(8,128)(2,1)S(1)} %collective-permute-done.80.refs_10_), channel_id=1, source_target_pairs={{0,2},{1,3},{2,0},{3,1},{4,6},{5,7},{6,4},{7,5},{8,10},{9,11},{10,... | collective-permute-start | bytes 1130504 | tf_op jit(solution)/shard_map/ppermute | solution.py:1074
  345.1 18.8 %collective-permute-start.93 = (bf16[368,512]{1,0:T(8,128)(2,1)S(1)}, bf16[368,512]{1,0:T(8,128)(2,1)}, u32[]{:S(2)}, u32[]{:S(2)}) collective-permute-start(bf16[368,512]{1,0:T(8,128)(2,1)S(1)} %collective-permute-done.83.refs_19_), channel_id=1, source_target_pairs={{0,1},{1,0},{2,3},{3,2},{4,5},{5,4},{6,7},{7,6},{8,9},{9,8},{10,11... | collective-permute-start | bytes 1130504 | tf_op jit(solution)/shard_map/ppermute | solution.py:1070
  369.7 34.7 %collective-permute-start.109 = (bf16[176,512]{1,0:T(8,128)(2,1)S(1)}, bf16[176,512]{1,0:T(8,128)(2,1)S(1)}, u32[]{:S(2)}, u32[]{:S(2)}) collective-permute-start(bf16[176,512]{1,0:T(8,128)(2,1)S(1)} %select_convert_fusion), channel_id=1, source_target_pairs={{0,16},{4,20},{16,0},{20,4},{8,24},{12,28},{24,8},{28,12},{1,17},{... | collective-permute-start | bytes 540680 | tf_op jit(solution)/shard_map/ppermute | solution.py:1078
  369.8 36.7 %collective-permute-start.114 = (f32[32,512]{1,0:T(8,128)S(1)}, f32[32,512]{1,0:T(8,128)S(1)}, u32[]{:S(2)}, u32[]{:S(2)}) collective-permute-start(f32[32,512]{1,0:T(8,128)S(1)} %slice.535), channel_id=1, source_target_pairs={{1,0},{2,1},{3,2},{4,3},{5,4},{6,5},{7,6},{8,7},{9,8},{10,9},{11,1... | collective-permute-start | bytes 196616 | tf_op jit(solution)/shard_map/ppermute | solution.py:1396
  371.5 33.0 %collective-permute-start.106 = (bf16[288,512]{1,0:T(8,128)(2,1)S(1)}, bf16[288,512]{1,0:T(8,128)(2,1)S(1)}, u32[]{:S(2)}, u32[]{:S(2)}) collective-permute-start(bf16[288,512]{1,0:T(8,128)(2,1)S(1)} %get-tuple-element.846), channel_id=1, source_target_pairs={{0,24},{4,28},{8,0},{12,4},{16,8},{20,12},{24,16},{28,20},{1,25},{... | collective-permute-start | bytes 884744 | tf_op jit(solution)/shard_map/ppermute | solution.py:981
  375.3 31.1 %collective-permute-start.107 = (bf16[288,512]{1,0:T(8,128)(2,1)S(1)}, bf16[288,512]{1,0:T(8,128)(2,1)S(1)}, u32[]{:S(2)}, u32[]{:S(2)}) collective-permute-start(bf16[288,512]{1,0:T(8,128)(2,1)S(1)} %get-tuple-element.845), channel_id=1, source_target_pairs={{0,16},{4,20},{8,24},{12,28},{16,0},{20,4},{24,8},{28,12},{1,17},{... | collective-permute-start | bytes 884744 | tf_op jit(solution)/shard_map/ppermute | solution.py:981
  375.8 30.6 %collective-permute-start.108 = (bf16[288,512]{1,0:T(8,128)(2,1)S(1)}, bf16[288,512]{1,0:T(8,128)(2,1)S(1)}, u32[]{:S(2)}, u32[]{:S(2)}) collective-permute-start(bf16[288,512]{1,0:T(8,128)(2,1)S(1)} %get-tuple-element.844), channel_id=1, source_target_pairs={{0,8},{4,12},{8,16},{12,20},{16,24},{20,28},{24,0},{28,4},{1,9},{5... | collective-permute-start | bytes 884744 | tf_op jit(solution)/shard_map/ppermute | solution.py:981
  411.1 26.6 %collective-permute-start.112 = (bf16[288,512]{1,0:T(8,128)(2,1)S(1)}, bf16[288,512]{1,0:T(8,128)(2,1)S(1)}, u32[]{:S(2)}, u32[]{:S(2)}) collective-permute-start(bf16[288,512]{1,0:T(8,128)(2,1)S(1)} %get-tuple-element.809), channel_id=1, source_target_pairs={{0,16},{4,20},{8,24},{12,28},{16,0},{20,4},{24,8},{28,12},{1,17},{... | collective-permute-start | bytes 884744 | tf_op jit(solution)/shard_map/ppermute | solution.py:981
  411.8 26.0 %collective-permute-start.113 = (bf16[288,512]{1,0:T(8,128)(2,1)S(1)}, bf16[288,512]{1,0:T(8,128)(2,1)S(1)}, u32[]{:S(2)}, u32[]{:S(2)}) collective-permute-start(bf16[288,512]{1,0:T(8,128)(2,1)S(1)} %get-tuple-element.808), channel_id=1, source_target_pairs={{0,8},{4,12},{8,16},{12,20},{16,24},{20,28},{24,0},{28,4},{1,9},{5... | collective-permute-start | bytes 884744 | tf_op jit(solution)/shard_map/ppermute | solution.py:981
  (173 other events, 1998.2 us)
